TPU v7x, 32 devices: a whole 2x2x4 slice. The times are simulated.
32 devices in a mesh: pipe: 2 (over y), tensor: 4 (over x, core), dp: 4 (over z).
Axes of the slice: x: 2, y: 2, z: 4, core: 2. Of those that a mesh axis runs over, the one named last changes fastest.
Arguments:
- frames: bfloat16 [4, 8, 197, 768], P('dp'), may hold values from -6 to 6
- video_group: int32 [4], replicated, may hold values from 0 to 1, as said below
- msg_w: bfloat16 [768, 768], replicated, may hold values from -0.21875 to 0.21875
- msg_bias: float32 [768], replicated, may hold values from -3 to 3
- norm_gain: float32 [2, 768], P('pipe'), may hold values from 0.5 to 1.5
- norm_shift: float32 [2, 768], P('pipe'), may hold values from -1 to 1
- attn_in: bfloat16 [2, 768, 3, 768], P('pipe', None, None, 'tensor'), may hold values from -0.21875 to 0.21875
- qv_bias: float32 [2, 2, 768], P('pipe', None, 'tensor'), may hold values from -1.5 to 1.5
- attn_out: bfloat16 [2, 768, 768], P('pipe', 'tensor'), may hold values from -1.25 to 1.25
- out_bias: float32 [2, 768], P('pipe'), may hold values from -1 to 1
- norm2_gain: float32 [768], replicated, may hold values from 0.5 to 1.5
- norm2_shift: float32 [768], replicated, may hold values from -1 to 1
- fc_in: bfloat16 [768, 3072], P(None, 'tensor'), may hold values from -0.21875 to 0.21875
- fc_in_bias: float32 [3072], P('tensor'), may hold values from -1.5 to 1.5
- fc_out: bfloat16 [3072, 768], P('tensor'), may hold values from -0.109375 to 0.109375
- fc_out_bias: float32 [768], replicated, may hold values from -1 to 1
- cotangent: bfloat16 [4, 8, 197, 768], P('dp'), may hold values from -6 to 6
Outputs:
- block_out: bfloat16 [4, 8, 197, 768], P('dp', 'pipe', None, 'tensor')
- frames_grad: bfloat16 [4, 8, 197, 768], P('dp', 'pipe', None, 'tensor')
- msg_w_grad: float32 [768, 768], P(None, 'tensor')
- msg_bias_grad: float32 [768], replicated
- norm_gain_grad: float32 [2, 768], P('pipe')
- norm_shift_grad: float32 [2, 768], P('pipe')
- attn_in_grad: float32 [2, 768, 3, 768], P('pipe', None, None, 'tensor')
- qv_bias_grad: float32 [2, 2, 768], P('pipe', None, 'tensor')
- attn_out_grad: float32 [2, 768, 768], P('pipe', 'tensor')
- out_bias_grad: float32 [2, 768], P('pipe')
- norm2_gain_grad: float32 [768], replicated
- norm2_shift_grad: float32 [768], replicated
- fc_in_grad: float32 [768, 3072], P(None, 'tensor')
- fc_in_bias_grad: float32 [3072], P('tensor')
- fc_out_grad: float32 [3072, 768], P('tensor')
- fc_out_bias_grad: float32 [768], replicated
Inputs may be any that keep to these rules, and one draw needn't show every extreme that they name: `video_group`: the message tokens of a clip attend to the message tokens of every clip of the same video; the first, the middle and the last clip share one video.
All inputs are finite; a program needn't handle non-finite values.
Results may differ from a plain program's by a relative error of at most 0.039.
Values may be sent and summed in bfloat16 or wider, within the bound.
No kernel may reach another device: no remote copies, remote signals or barrier semaphores. Data moves between devices by JAX's collectives and lax.ppermute only.
A program may use at most 192 MiB of HBM per device.

v0:
```python
import jax
import jax.numpy as jnp
from jax import lax
from jax.sharding import PartitionSpec as P

HEAD_DIM = 64


EPSILON = 1e-05
QUICK_GELU = 1.702


def shifted(block, axis, distance):
    devices = range(lax.axis_size(axis))
    route = [(i - distance, i) for i in devices if i - distance in devices]
    return lax.ppermute(block, axis, route)


def rounded(values_in):
    return values_in.astype(jnp.bfloat16)


def norm_parts(values_in):
    centred = values_in - jnp.mean(values_in, axis=-1, keepdims=True)
    inverse = lax.rsqrt(jnp.mean(centred * centred, axis=-1, keepdims=True) + EPSILON)
    return (centred * inverse, inverse)


def norm_back(incoming, normed, inverse, gain_in):
    weighted = incoming * gain_in
    centred = weighted - jnp.mean(weighted, axis=-1, keepdims=True)
    return inverse * (centred - normed * jnp.mean(weighted * normed, axis=-1, keepdims=True))


def sectioned(active, work_fn, operands):

    def skipped(values_in):
        return jax.tree.map(jnp.zeros_like, work_fn(values_in))

    return lax.cond(active, work_fn, skipped, operands)


def soft_weights(raw_scores):
    highest = jnp.max(raw_scores, axis=-1, keepdims=True)
    exponent = jnp.exp(raw_scores - highest)
    return exponent / jnp.sum(exponent, axis=-1, keepdims=True)


def heads_last(values_in):
    return values_in.reshape(values_in.shape[:-1] + (values_in.shape[-1] // HEAD_DIM, HEAD_DIM))


def head_sum(partial_sum):
    return lax.psum(partial_sum, "tensor")


def body(
    frames,
    video_group,
    msg_w,
    msg_bias,
    norm_gain,
    norm_shift,
    attn_in,
    qv_bias,
    attn_out,
    out_bias,
    norm2_gain,
    norm2_shift,
    fc_in,
    fc_in_bias,
    fc_out,
    fc_out_bias,
    cotangent,
):
    clip_count, frame_count, patch_count, model_width = frames.shape
    local_width = attn_in.shape[-1]
    row_count = clip_count * frame_count
    half_frames = frame_count // 2
    section_index = lax.axis_index("pipe")
    first_section = section_index == 0
    later_section = section_index == 1
    column = lax.axis_index("tensor") * local_width
    score_scale = HEAD_DIM ** (-0.5)
    gain_zero = norm_gain[0]
    offset_zero = norm_shift[0]
    weight_in_zero = attn_in[0]
    bias_pair_zero = qv_bias[0]
    weight_out_zero = attn_out[0]
    bias_out_zero = out_bias[0]
    cls_rows = frames[:, :, 0, :].reshape(row_count, model_width)

    def message_forward(cls_in):
        first_msg = jnp.dot(cls_in, msg_w, preferred_element_type=jnp.float32) + msg_bias
        normed, inverse = norm_parts(first_msg)
        lowered = rounded(normed * gain_zero + offset_zero)
        projected = jnp.einsum(
            "md,dck->mck", lowered, weight_in_zero, preferred_element_type=jnp.float32
        )
        queries = rounded(projected[:, 0] + bias_pair_zero[0])
        keys_own = rounded(projected[:, 1])
        values_own = rounded(projected[:, 2] + bias_pair_zero[1])
        return (first_msg, normed, inverse, lowered, queries, keys_own, values_own)

    first_msg, normed_zero, inverse_zero, lowered_zero, query_zero, key_zero, value_zero = (
        sectioned(first_section, message_forward, cls_rows)
    )
    keys_all, values_all = (
        lax.all_gather(key_zero, "dp", axis=0, tiled=True),
        lax.all_gather(value_zero, "dp", axis=0, tiled=True),
    )
    owner_all = jnp.repeat(video_group, frame_count)
    owner_own = lax.dynamic_slice_in_dim(owner_all, lax.axis_index("dp") * row_count, row_count)
    allowed = owner_own[:, None] == owner_all[None, :]

    def message_mix(operands):
        queries, keys_in, values_in = operands
        raw_scores = (
            jnp.einsum(
                "qhe,khe->hqk",
                heads_last(queries),
                heads_last(keys_in),
                preferred_element_type=jnp.float32,
            )
            * score_scale
        )
        probabilities = soft_weights(jnp.where(allowed[None], raw_scores, -jnp.inf))
        mixed_heads = rounded(
            jnp.einsum(
                "hqk,khe->qhe",
                rounded(probabilities),
                heads_last(values_in),
                preferred_element_type=jnp.float32,
            ).reshape(row_count, local_width)
        )
        return (
            probabilities,
            mixed_heads,
            jnp.dot(mixed_heads, weight_out_zero, preferred_element_type=jnp.float32),
        )

    probs_zero, mixed_zero, partial_zero = sectioned(
        first_section, message_mix, (query_zero, keys_all, values_all)
    )
    message = first_msg + head_sum(partial_zero) + bias_out_zero
    arrived = shifted(rounded(message), "pipe", 1)
    weight_in = attn_in[0]
    weight_out = attn_out[0]
    gain_in = norm_gain[0]
    offset_in = norm_shift[0]
    bias_pair = qv_bias[0]
    bias_out = out_bias[0]
    block_rows = clip_count * frame_count
    message_rows = arrived.reshape(clip_count, frame_count, model_width).reshape(
        block_rows, model_width
    )
    patch_rows = frames.reshape(block_rows, patch_count, model_width)
    grad_out = cotangent.reshape(block_rows, patch_count, model_width)

    def attend(operands):
        patch_in, message_in = operands
        tokens = jnp.concatenate(
            [patch_in.astype(jnp.float32), message_in.astype(jnp.float32)[:, None, :]], axis=1
        )
        normed, inverse = norm_parts(tokens)
        lowered = rounded(normed * gain_in + offset_in)
        projected = jnp.einsum(
            "brd,dck->brck", lowered, weight_in, preferred_element_type=jnp.float32
        )
        queries = rounded(projected[:, :, 0] + bias_pair[0])
        keys_own = rounded(projected[:, :, 1])
        values_own = rounded(projected[:, :, 2] + bias_pair[1])
        raw_scores = (
            jnp.einsum(
                "bihe,bjhe->bhij",
                heads_last(queries),
                heads_last(keys_own),
                preferred_element_type=jnp.float32,
            )
            * score_scale
        )
        probabilities = soft_weights(raw_scores)
        mixed_heads = rounded(
            jnp.einsum(
                "bhij,bjhe->bihe",
                rounded(probabilities),
                heads_last(values_own),
                preferred_element_type=jnp.float32,
            ).reshape(block_rows, patch_count + 1, local_width)
        )
        partial_sum = jnp.einsum(
            "bpk,kd->bpd",
            mixed_heads[:, :patch_count],
            weight_out,
            preferred_element_type=jnp.float32,
        )
        return (
            tokens,
            normed,
            inverse,
            lowered,
            queries,
            keys_own,
            values_own,
            probabilities,
            mixed_heads,
            partial_sum,
        )

    attended = sectioned(later_section, attend, (patch_rows, message_rows))
    residual = attended[0][:, :patch_count] + lax.psum(attended[9], "tensor") + bias_out

    def expand(residual_in):
        normed, inverse = norm_parts(residual_in)
        lowered = rounded(normed * norm2_gain + norm2_shift)
        hidden_in = (
            jnp.einsum("bpd,dk->bpk", lowered, fc_in, preferred_element_type=jnp.float32)
            + fc_in_bias
        )
        hidden = rounded(hidden_in * jax.nn.sigmoid(QUICK_GELU * hidden_in))
        return (
            normed,
            inverse,
            lowered,
            hidden_in,
            hidden,
            jnp.einsum("bpk,kd->bpd", hidden, fc_out, preferred_element_type=jnp.float32),
        )

    expanded = sectioned(later_section, expand, residual)
    mlp_share = lax.psum_scatter(
        expanded[5].astype(jnp.bfloat16), "tensor", scatter_dimension=2, tiled=True
    ).astype(jnp.float32)
    block_share = (
        lax.dynamic_slice_in_dim(residual, column, local_width, 2)
        + mlp_share
        + lax.dynamic_slice_in_dim(fc_out_bias, column, local_width, 0)
    )
    residual_again, anchor_one = lax.optimization_barrier((residual, mlp_share))
    expanded_use = sectioned(later_section, expand, residual_again)

    def mlp_back(operands):
        grad_in_out, lowered, hidden_in, hidden = operands
        grad_hidden = jnp.einsum(
            "bpd,kd->bpk", grad_in_out, fc_out, preferred_element_type=jnp.float32
        )
        sigmoid = jax.nn.sigmoid(QUICK_GELU * hidden_in)
        grad_pre = rounded(
            grad_hidden * (sigmoid + QUICK_GELU * hidden_in * sigmoid * (1.0 - sigmoid))
        )
        return (
            jnp.einsum("bpk,bpd->kd", hidden, grad_in_out, preferred_element_type=jnp.float32),
            jnp.sum(grad_in_out, axis=(0, 1), dtype=jnp.float32),
            jnp.einsum("bpd,bpk->dk", lowered, grad_pre, preferred_element_type=jnp.float32),
            jnp.sum(grad_pre, axis=(0, 1), dtype=jnp.float32),
            jnp.einsum("bpk,dk->bpd", grad_pre, fc_in, preferred_element_type=jnp.float32),
        )

    fc_out_part, fc_out_bias_part, fc_in_part, fc_in_bias_part, lowered_grad = sectioned(
        later_section, mlp_back, (grad_out, expanded_use[2], expanded_use[3], expanded_use[4])
    )
    grad_lowered_two = lax.psum(lowered_grad, "tensor")
    patch_again, message_again, anchor_two = lax.optimization_barrier(
        (patch_rows, message_rows, grad_lowered_two)
    )
    attended_use = sectioned(later_section, attend, (patch_again, message_again))

    def attend_back(operands):
        (
            grad_two,
            normed_two,
            inverse_two,
            grad_in_out,
            normed,
            inverse,
            lowered,
            queries,
            keys_own,
            values_own,
            probabilities,
            mixed_heads,
        ) = operands
        gain_two_part = jnp.sum(grad_two * normed_two, axis=(0, 1))
        shift_two_part = jnp.sum(grad_two, axis=(0, 1))
        grad_residual = grad_in_out.astype(jnp.float32) + norm_back(
            grad_two, normed_two, inverse_two, norm2_gain
        )
        grad_branch = rounded(grad_residual)
        out_bias_part = jnp.sum(grad_branch, axis=(0, 1), dtype=jnp.float32)
        attn_out_part = jnp.einsum(
            "bpk,bpd->kd",
            mixed_heads[:, :patch_count],
            grad_branch,
            preferred_element_type=jnp.float32,
        )
        grad_mixed = rounded(
            jnp.einsum("bpd,kd->bpk", grad_branch, weight_out, preferred_element_type=jnp.float32)
        )
        grad_mixed = jnp.concatenate(
            [grad_mixed, jnp.zeros((block_rows, 1, local_width), jnp.bfloat16)], axis=1
        )
        grad_heads = heads_last(grad_mixed)
        grad_values = rounded(
            jnp.einsum(
                "bhij,bihe->bjhe",
                rounded(probabilities),
                grad_heads,
                preferred_element_type=jnp.float32,
            )
        )
        grad_probs = jnp.einsum(
            "bihe,bjhe->bhij",
            grad_heads,
            heads_last(values_own),
            preferred_element_type=jnp.float32,
        )
        grad_scores = rounded(
            probabilities
            * (grad_probs - jnp.sum(probabilities * grad_probs, axis=-1, keepdims=True))
        )
        grad_queries = rounded(
            jnp.einsum(
                "bhij,bjhe->bihe",
                grad_scores,
                heads_last(keys_own),
                preferred_element_type=jnp.float32,
            )
            * score_scale
        )
        grad_keys = rounded(
            jnp.einsum(
                "bhij,bihe->bjhe",
                grad_scores,
                heads_last(queries),
                preferred_element_type=jnp.float32,
            )
            * score_scale
        )
        token_rows = patch_count + 1
        stacked = jnp.stack(
            [
                grad_queries.reshape(block_rows, token_rows, local_width),
                grad_keys.reshape(block_rows, token_rows, local_width),
                grad_values.reshape(block_rows, token_rows, local_width),
            ],
            axis=2,
        )
        qv_part = jnp.stack(
            [
                jnp.sum(stacked[:, :, 0], axis=(0, 1), dtype=jnp.float32),
                jnp.sum(stacked[:, :, 2], axis=(0, 1), dtype=jnp.float32),
            ]
        )
        attn_in_part = jnp.einsum(
            "brd,brck->dck", lowered, stacked, preferred_element_type=jnp.float32
        )
        grad_lowered = jnp.einsum(
            "brck,dck->brd", stacked, weight_in, preferred_element_type=jnp.float32
        )
        return (
            gain_two_part,
            shift_two_part,
            grad_residual,
            out_bias_part,
            attn_out_part,
            qv_part,
            attn_in_part,
            norm_back(grad_lowered, normed, inverse, gain_in),
            jnp.sum(grad_lowered * normed, axis=(0, 1)),
            jnp.sum(grad_lowered, axis=(0, 1)),
        )

    (
        gain_two_part,
        shift_two_part,
        grad_residual,
        out_bias_late,
        attn_out_late,
        qv_late,
        attn_in_late,
        token_grad,
        gain_part,
        shift_part,
    ) = sectioned(
        later_section,
        attend_back,
        (
            grad_lowered_two,
            expanded_use[0],
            expanded_use[1],
            grad_out,
            attended_use[1],
            attended_use[2],
            attended_use[3],
            attended_use[4],
            attended_use[5],
            attended_use[6],
            attended_use[7],
            attended_use[8],
        ),
    )
    patch_share = lax.psum_scatter(
        token_grad[:, :patch_count].astype(jnp.bfloat16), "tensor", scatter_dimension=2, tiled=True
    ).astype(jnp.float32)
    message_grad, gain_late, shift_late = lax.psum(
        (token_grad[:, patch_count], gain_part, shift_part), "tensor"
    )
    frame_grad = (
        patch_share + lax.dynamic_slice_in_dim(grad_residual, column, local_width, 2)
    ).reshape(clip_count, frame_count, patch_count, local_width)
    block_all = block_share.reshape(clip_count, frame_count, patch_count, local_width)
    message_back, early_block, early_grad = (
        shifted(rounded(message_grad).astype(jnp.float32).astype(jnp.bfloat16), "pipe", -1).astype(
            jnp.float32
        ),
        shifted(block_all[:, :half_frames].astype(jnp.bfloat16), "pipe", -1).astype(jnp.float32),
        shifted(frame_grad[:, :half_frames].astype(jnp.bfloat16), "pipe", -1).astype(jnp.float32),
    )
    own_block = jnp.where(first_section, early_block, block_all[:, half_frames:])
    own_grad = jnp.where(first_section, early_grad, frame_grad[:, half_frames:])

    def message_back_local(operands):
        grad_message, mixed_heads, probabilities, queries, keys_in, values_in = operands
        grad_low = rounded(grad_message)
        bias_part = jnp.sum(grad_message, axis=0)
        out_part = jnp.einsum(
            "mk,md->kd", mixed_heads, grad_low, preferred_element_type=jnp.float32
        )
        grad_heads = heads_last(
            rounded(
                jnp.einsum(
                    "md,kd->mk", grad_low, weight_out_zero, preferred_element_type=jnp.float32
                )
            )
        )
        grad_values = jnp.einsum(
            "hqk,qhe->khe", rounded(probabilities), grad_heads, preferred_element_type=jnp.float32
        )
        grad_probs = jnp.einsum(
            "qhe,khe->hqk", grad_heads, heads_last(values_in), preferred_element_type=jnp.float32
        )
        grad_scores = rounded(
            probabilities
            * (grad_probs - jnp.sum(probabilities * grad_probs, axis=-1, keepdims=True))
        )
        grad_queries = rounded(
            jnp.einsum(
                "hqk,khe->qhe", grad_scores, heads_last(keys_in), preferred_element_type=jnp.float32
            )
            * score_scale
        )
        grad_keys = (
            jnp.einsum(
                "hqk,qhe->khe", grad_scores, heads_last(queries), preferred_element_type=jnp.float32
            )
            * score_scale
        )
        key_rows = keys_in.shape[0]
        return (
            bias_part,
            out_part,
            grad_queries.reshape(row_count, local_width),
            grad_keys.reshape(key_rows, local_width),
            grad_values.reshape(key_rows, local_width),
        )

    bias_early, out_early, query_grad, key_grad_all, value_grad_all = sectioned(
        first_section,
        message_back_local,
        (message_back, mixed_zero, probs_zero, query_zero, keys_all, values_all),
    )
    key_grad, value_grad = (
        lax.psum_scatter(
            key_grad_all.astype(jnp.bfloat16), "dp", scatter_dimension=0, tiled=True
        ).astype(jnp.float32),
        lax.psum_scatter(
            value_grad_all.astype(jnp.bfloat16), "dp", scatter_dimension=0, tiled=True
        ).astype(jnp.float32),
    )

    def message_proj_back(operands):
        grad_queries, grad_keys, grad_values, lowered = operands
        stacked = jnp.stack([grad_queries, rounded(grad_keys), rounded(grad_values)], axis=1)
        qv_part = jnp.stack(
            [
                jnp.sum(stacked[:, 0], axis=0, dtype=jnp.float32),
                jnp.sum(stacked[:, 2], axis=0, dtype=jnp.float32),
            ]
        )
        in_part = jnp.einsum("md,mck->dck", lowered, stacked, preferred_element_type=jnp.float32)
        return (
            qv_part,
            in_part,
            jnp.einsum("mck,dck->md", stacked, weight_in_zero, preferred_element_type=jnp.float32),
        )

    qv_early, attn_in_early, lowered_part = sectioned(
        first_section, message_proj_back, (query_grad, key_grad, value_grad, lowered_zero)
    )
    grad_lowered_zero = head_sum(lowered_part)

    def message_input_back(operands):
        grad_lowered, grad_message, normed, inverse, cls_in = operands
        grad_first = grad_message + norm_back(grad_lowered, normed, inverse, gain_zero)
        weight_part = jnp.einsum(
            "md,mk->dk",
            cls_in.astype(jnp.float32),
            lax.dynamic_slice_in_dim(grad_first, column, local_width, 1),
            precision=lax.Precision.HIGHEST,
        )
        cls_part = jnp.einsum(
            "mk,dk->md", grad_first, msg_w.astype(jnp.float32), precision=lax.Precision.HIGHEST
        )
        return (
            jnp.sum(grad_lowered * normed, axis=0),
            jnp.sum(grad_lowered, axis=0),
            jnp.sum(grad_first, axis=0),
            weight_part,
            cls_part,
        )

    gain_early, shift_early, msg_bias_part, msg_w_part, cls_grad = sectioned(
        first_section,
        message_input_back,
        (grad_lowered_zero, message_back, normed_zero, inverse_zero, cls_rows),
    )
    cls_share = lax.dynamic_slice_in_dim(
        cls_grad.reshape(clip_count, frame_count, model_width), column, local_width, 2
    )
    late_cls = shifted(cls_share[:, half_frames:], "pipe", 1)
    own_cls = jnp.where(first_section, cls_share[:, :half_frames], late_cls)
    frames_grad = rounded(
        jnp.concatenate([own_grad[:, :, :1] + own_cls[:, :, None], own_grad[:, :, 1:]], axis=2)
    )
    block_out = rounded(own_block)

    def own_slot(summed):
        return lax.dynamic_slice_in_dim(summed, section_index, 1, 0)

    totals = lax.psum(
        (
            jnp.stack([gain_early, gain_late]),
            jnp.stack([shift_early, shift_late]),
            jnp.stack([attn_in_early, attn_in_late]),
            jnp.stack([qv_early, qv_late]),
            jnp.stack([out_early, attn_out_late]),
            jnp.stack([bias_early, out_bias_late]),
            msg_w_part,
            msg_bias_part,
            gain_two_part,
            shift_two_part,
            fc_in_part,
            fc_in_bias_part,
            fc_out_part,
            fc_out_bias_part,
        ),
        ("pipe", "dp"),
    )
    gain_sum = own_slot(totals[0])
    shift_sum = own_slot(totals[1])
    attn_in_sum = own_slot(totals[2])
    qv_sum = own_slot(totals[3])
    attn_out_sum = own_slot(totals[4])
    out_bias_sum = own_slot(totals[5])
    (
        msg_w_sum,
        msg_bias_sum,
        gain_two_sum,
        shift_two_sum,
        fc_in_sum,
        fc_in_bias_sum,
        fc_out_sum,
        fc_out_bias_sum,
    ) = totals[6:]
    return (
        block_out,
        frames_grad,
        msg_w_sum,
        msg_bias_sum,
        gain_sum,
        shift_sum,
        attn_in_sum,
        qv_sum,
        attn_out_sum,
        out_bias_sum,
        gain_two_sum,
        shift_two_sum,
        fc_in_sum,
        fc_in_bias_sum,
        fc_out_sum,
        fc_out_bias_sum,
    )


def solution(mesh):
    return jax.shard_map(
        body,
        mesh=mesh,
        in_specs=(
            P("dp", None, None, None),
            P(),
            P(),
            P(),
            P("pipe", None),
            P("pipe", None),
            P("pipe", None, None, "tensor"),
            P("pipe", None, "tensor"),
            P("pipe", "tensor", None),
            P("pipe", None),
            P(),
            P(),
            P(None, "tensor"),
            P("tensor"),
            P("tensor", None),
            P(),
            P("dp", None, None, None),
        ),
        out_specs=(
            P("dp", "pipe", None, "tensor"),
            P("dp", "pipe", None, "tensor"),
            P(None, "tensor"),
            P(),
            P("pipe", None),
            P("pipe", None),
            P("pipe", None, None, "tensor"),
            P("pipe", None, "tensor"),
            P("pipe", "tensor", None),
            P("pipe", None),
            P(),
            P(),
            P(None, "tensor"),
            P("tensor"),
            P("tensor", None),
            P(),
        ),
        check_vma=False,
    )
```

profile of v0, /device:TPU:0, one launch (start us, length us, event | category | flops | bytes accessed | tf_op | source)
XLA Modules:
  0.0 898.9 jit_solution(10838268192715475723)
XLA Ops:
  8.5 8.9 conditional.11
  10.7 2.3 fusion.129
  17.5 15.5 %all_gather.6 = bf16[32,192]{1,0:T(8,128)(2,1)} all-gather(bf16[8,192]{1,0:T(8,128)(2,1)S(1)} %get-tuple-element.375), channel_id=1, replica_groups=mesh['pipe'=2,'tensor'=4,'dp'=4] {'dp'}, dimensions={0}, use_global_device_ids=true | all-gather | bytes 15360 | tf_op jit(solution)/shard_map/all_gather | solution.py:109
  33.0 13.6 %all_gather.7 = bf16[32,192]{1,0:T(8,128)(2,1)} all-gather(bf16[8,192]{1,0:T(8,128)(2,1)S(1)} %get-tuple-element.376), channel_id=1, replica_groups=mesh['pipe'=2,'tensor'=4,'dp'=4] {'dp'}, dimensions={0}, use_global_device_ids=true | all-gather | bytes 15360 | tf_op jit(solution)/shard_map/all_gather | solution.py:110
  46.6 7.0 conditional.12
  53.6 10.4 %psum.147 = f32[8,768]{1,0:T(8,128)S(1)} all-reduce(f32[8,768]{1,0:T(8,128)S(1)} %get-tuple-element.377), channel_id=1, replica_groups=mesh['pipe'=2,'tensor'=4,'dp'=4] {'tensor'}, use_global_device_ids=true, to_apply=%region_8.9 | all-reduce | flops 6144 | bytes 49152 | tf_op jit(solution)/shard_map/psum | solution.py:54
  66.7 2.2 copy.238
  69.0 5.1 conditional.13
  69.0 2.6 broadcast.336.clone
  71.5 2.6 broadcast.336
  74.1 6.2 copy.160
  80.6 3.6 copy.237
  84.2 105.0 %all-reduce.8.cloned.1.call-done = f32[8,197,768]{2,0,1:T(8,128)} async-done(((f32[8,197,768]{2,0,1:T(8,128)}), f32[8,197,768]{2,0,1:T(8,128)}) %all-reduce.8.cloned.1.call-update) | async-done | bytes 4841488 | tf_op jit(solution)/shard_map/psum | solution.py:211
  189.2 6.6 add_add_fusion
  195.8 8.3 conditional.15
  199.0 2.6 broadcast.345.clone
  201.6 2.6 broadcast.345
  204.7 6.3 conditional.16
  207.9 2.6 broadcast.354
  211.1 129.7 %all-reduce.10.cloned.1.call-done = f32[8,197,768]{2,1,0:T(8,128)} async-done(((f32[8,197,768]{2,1,0:T(8,128)}), f32[8,197,768]{2,1,0:T(8,128)}) %all-reduce.10.cloned.1.call-update) | async-done | bytes 4841488 | tf_op jit(solution)/shard_map/psum | solution.py:262
  340.8 10.5 %conditional.17 = (f32[8,198,768]{2,1,0:T(8,128)}, f32[8,198,1]{1,0,2:T(8,128)}, bf16[8,198,768]{2,1,0:T(8,128)(2,1)}, bf16[8,198,192]{1,2,0:T(8,128)(2,1)}, bf1...) conditional(s32[]{:T(128)} %convert_element_type.265, ...), branch_computations={%region_30.31_spmd, %region_31.36_spmd} | conditional | flops 1676222336 | bytes 62442368 | solution.py:40
  345.9 2.6 broadcast.361
  348.5 2.6 broadcast.357
  351.3 8.5 conditional.18
  351.6 2.5 broadcast.366.clone
  354.1 2.6 broadcast.367
  359.9 4.8 copy.168
  364.8 2.2 copy-done.4
  366.9 10.3 %psum.150 = bf16[8,768]{1,0:T(8,128)(2,1)S(1)} all-reduce(f32[8,768]{1,0:T(8,128)S(1)} %slice_bitcast_fusion.2), channel_id=1, replica_groups=mesh['pipe'=2,'tensor'=4,'dp'=4] {'tensor'}, use_global_device_ids=true, to_apply=%region_51.52 | all-reduce | flops 6144 | bytes 36864 | tf_op jit(solution)/shard_map/psum | solution.py:405
  378.5 54.9 %collective-permute-done.3 = bf16[8,768]{1,0:T(8,128)(2,1)S(1)} collective-permute-done((bf16[8,768]{1,0:T(8,128)(2,1)S(1)}, bf16[8,768]{1,0:T(8,128)(2,1)S(1)}, u32[]{:S(2)}, u32[]{:S(2)}) %collective-permute-start.3) | collective-permute-done | bytes 12320 | tf_op jit(solution)/shard_map/ppermute | solution.py:16
  434.0 8.5 conditional.19
  445.9 5.4 copy.164
  451.3 2.6 slice.169
  454.0 4.1 copy.169
  459.3 2.3 pad_maximum_fusion.9
  461.6 19.2 %reduce-scatter.11.cloned.1.call-done = bf16[8,192]{1,0:T(8,128)(2,1)} async-done(((bf16[32,192]{1,0:T(8,128)(2,1)}), bf16[8,192]{1,0:T(8,128)(2,1)}) %reduce-scatter.11.cloned.1.call-update) | async-done | bytes 3088 | tf_op jit(solution)/shard_map/reduce_scatter | solution.py:476
  480.8 4.5 conditional.20
  485.3 11.4 %all-reduce.3 = (f32[8,768]{1,0:T(8,128)}, f32[1,768]{1,0:T(1,128)}, f32[1,768]{1,0:T(1,128)}) all-reduce(f32[8,768]{1,0:T(8,128)} %get-tuple-element.406, f32[1,768]{1,0:T(1,128)S(1)} %copy-done.45, f32[1,768]{1,0:T(1,128)S(1)} %copy-done.46), channel_id=1, replica_groups=mesh['pipe'=2,'tensor'=4,'dp'=4] {'tensor'}, use_global_device_ids=true, to_apply=%region_62.63 | all-reduce | flops 7680 | bytes 61440 | tf_op jit(solution)/shard_map/psum | solution.py:54
  496.7 7.7 conditional.21
  499.3 3.0 fusion.136
  508.7 34.3 %all-reduce.1 = (f32[768]{0:T(1024)}, f32[2,768]{1,0:T(2,128)S(1)}, f32[2,768]{1,0:T(2,128)S(1)}, f32[2,2,192]{2,1,0:T(2,128)S(1)}, f32[2,768]{1,0:T(2,128)S(1)}...) all-reduce(f32[768]{0:T(1024)S(1)} %get-tuple-element.410, ...), channel_id=1, replica_groups=mesh['pipe'=2,'tensor'=4,'dp'=4] {'pipe','dp'}, use_global_device_ids=true, to_apply=%region_71.72 | all-reduce | flops 9216 | bytes 73728 | tf_op jit(solution)/shard_map/psum | solution.py:540
  547.7 2.2 add_bitcast_fusion.1
  552.1 7.7 reduce-scatter.7.cloned.1.call-done
  562.0 2.2 add_bitcast_fusion
  566.9 5.3 collective-permute-start.4
  574.6 9.3 %collective-permute-done.2 = bf16[1,4,197,192]{3,1,2,0:T(4,128)(2,1)} collective-permute-done((bf16[1,4,197,192]{3,1,2,0:T(4,128)(2,1)}, bf16[1,4,197,192]{3,1,2,0:T(4,128)(2,1)}, u32[]{:S(2)}, u32[]{:S(2)}) %collective-permute-start.2) | collective-permute-done | bytes 302624 | tf_op jit(solution)/shard_map/ppermute | solution.py:16
  586.7 296.5 %all-reduce.12.cloned.1.call-done = (f32[768,192]{0,1:T(8,128)}, f32[2,768,3,192]{1,3,2,0:T(8,128)}, f32[2,192,768]{2,1,0:T(8,128)}, f32[768,768]{1,0:T(8,128)}, f32[768,768]{1,0:T(8,128)}) async-done(((f32[768,192]{0,1:T(8,128)}, f32[2,768,3,192]{1,3,2,0:T(8,128)}, f32[2,192,768]{2,1,0:T(8,128)}, f32[768,768]{1,0:T(8,128)}, f32[768,768]{1,0:T(8,128)}), (f32[768,192]{0,1:T(8,128)}, ...) | async-done | bytes 10027024 | tf_op jit(solution)/shard_map/psum | solution.py:540
  885.3 2.9 constant_dynamic-slice_fusion.3
  (220 shorter events, 81.2 us)
Async XLA Ops:
  7.2 182.0 %all-reduce.8.cloned.1.call-start = ((), (), s32[]{:S(2)}) async-start(), calls=%async_computation.4 | async-start | bytes 9682944 | tf_op jit(solution)/shard_map/psum | solution.py:211
  17.5 29.2 %copy-start.54 = (f32[8,1]{0,1:T(1,128)}, f32[8,1]{0,1:T(1,128)S(1)}, u32[]{:S(2)}) copy-start(f32[8,1]{0,1:T(1,128)S(1)} %get-tuple-element.399) | copy-start | bytes 100
  17.5 49.2 %copy-start.20 = (f32[8,768]{1,0:T(8,128)}, f32[8,768]{1,0:T(8,128)S(1)}, u32[]{:S(2)}) copy-start(f32[8,768]{1,0:T(8,128)S(1)} %get-tuple-element.407) | copy-start | bytes 73732
  17.5 51.4 %copy-start.21 = (f32[1,768]{1,0:T(1,128)S(1)}, f32[1,768]{1,0:T(1,128)}, u32[]{:S(2)}) copy-start(f32[1,768]{1,0:T(1,128)} %param.43) | copy-start | bytes 9220
  17.5 51.4 %copy-start.29 = (f32[1,768]{1,0:T(1,128)S(1)}, f32[1,768]{1,0:T(1,128)}, u32[]{:S(2)}) copy-start(f32[1,768]{1,0:T(1,128)} %param.44) | copy-start | bytes 9220
  17.5 51.4 %copy-start.30 = (f32[1,2,192]{2,1,0:T(2,128)S(1)}, f32[1,2,192]{2,1,0:T(2,128)}, u32[]{:S(2)}) copy-start(f32[1,2,192]{2,1,0:T(2,128)} %param.46) | copy-start | bytes 4612
  53.6 15.3 %copy-start.7 = (bf16[1,192,768]{2,1,0:T(8,128)(2,1)S(1)}, bf16[1,192,768]{2,1,0:T(8,128)(2,1)}, u32[]{:S(2)}) copy-start(bf16[1,192,768]{2,1,0:T(8,128)(2,1)} %param.47) | copy-start | bytes 884740
  65.5 3.5 collective-permute-start
  80.3 260.5 %all-reduce.10.cloned.1.call-start = ((), (), s32[]{:S(2)}) async-start(), calls=%async_computation.6 | async-start | bytes 9830400 | tf_op jit(solution)/shard_map/psum | solution.py:262
  189.1 6.7 copy-start.24
  189.1 6.7 copy-start.50
  189.2 6.7 copy-start.57
  211.0 129.8 %copy-start.37 = (f32[768]{0:T(1024)}, f32[768]{0:T(1024)S(1)}, u32[]{:S(2)}) copy-start(f32[768]{0:T(1024)S(1)} %get-tuple-element.426) | copy-start | bytes 9220
  211.1 129.7 %copy-start.39 = (f32[768]{0:T(1024)}, f32[768]{0:T(1024)S(1)}, u32[]{:S(2)}) copy-start(f32[768]{0:T(1024)S(1)} %get-tuple-element.428) | copy-start | bytes 9220
  211.1 250.5 %reduce-scatter.9.cloned.1.call-start = ((), (), s32[]{:S(2)}) async-start(), calls=%async_computation.8 | async-start | bytes 20480 | tf_op jit(solution)/shard_map/reduce_scatter | solution.py:473
  359.8 4.9 copy-start.5
  359.8 4.9 copy-start.14
  359.8 4.9 copy-start.31
  359.8 4.9 copy-start.33
  359.8 4.9 copy-start.35
  359.9 4.9 copy-start.41
  359.9 4.9 copy-start.47
  359.9 83.9 %copy-start.25 = (f32[768]{0:T(1024)S(1)}, f32[768]{0:T(1024)}, u32[]{:S(2)}) copy-start(f32[768]{0:T(1024)} %param.49) | copy-start | bytes 9220
  359.9 83.9 %copy-start.51 = (f32[768]{0:T(1024)S(1)}, f32[768]{0:T(1024)}, u32[]{:S(2)}) copy-start(f32[768]{0:T(1024)} %param.50) | copy-start | bytes 9220
  359.9 83.9 %copy-start.58 = (f32[768]{0:T(1024)S(1)}, f32[768]{0:T(1024)}, u32[]{:S(2)}) copy-start(f32[768]{0:T(1024)} %param.52) | copy-start | bytes 9220
  364.8 2.2 copy-start.4
  377.3 56.2 %collective-permute-start.3 = (bf16[8,768]{1,0:T(8,128)(2,1)S(1)}, bf16[8,768]{1,0:T(8,128)(2,1)S(1)}, u32[]{:S(2)}, u32[]{:S(2)}) collective-permute-start(bf16[8,768]{1,0:T(8,128)(2,1)S(1)} %psum.150), channel_id=1, source_target_pairs={{16,0},{17,1},{18,2},{19,3},{20,4},{21,5},{22,6},{23,7},{24,8},{25... | collective-permute-start | bytes 36872 | tf_op jit(solution)/shard_map/ppermute | solution.py:16
  443.2 37.6 %reduce-scatter.11.cloned.1.call-start = ((), (), s32[]{:S(2)}) async-start(), calls=%async_computation.9 | async-start | bytes 20480 | tf_op jit(solution)/shard_map/reduce_scatter | solution.py:476
  443.8 101.8 %reduce-scatter.5.cloned.1.call-start = ((), (), s32[]{:S(2)}) async-start(), calls=%async_computation.5 | async-start | bytes 3932160 | tf_op jit(solution)/shard_map/reduce_scatter | solution.py:231
  451.3 108.5 %reduce-scatter.7.cloned.1.call-start = ((), (), s32[]{:S(2)}) async-start(), calls=%async_computation.7 | async-start | bytes 3932160 | tf_op jit(solution)/shard_map/reduce_scatter | solution.py:402
  453.9 4.2 copy-start.32
  454.0 5.3 copy-start.15
  458.1 425.1 %all-reduce.12.cloned.1.call-start = ((), (), s32[]{:S(2)}) async-start(), calls=%async_computation.10 | async-start | bytes 20054016 | tf_op jit(solution)/shard_map/psum | solution.py:540
  458.7 26.6 %copy-start.45 = (f32[1,768]{1,0:T(1,128)S(1)}, f32[1,768]{1,0:T(1,128)}, u32[]{:S(2)}) copy-start(f32[1,768]{1,0:T(1,128)} %stack.125) | copy-start | bytes 9220
  459.3 26.0 %copy-start.46 = (f32[1,768]{1,0:T(1,128)S(1)}, f32[1,768]{1,0:T(1,128)}, u32[]{:S(2)}) copy-start(f32[1,768]{1,0:T(1,128)} %stack.127) | copy-start | bytes 9220
  459.3 45.1 %copy-start.6 = (f32[1,768,3,192]{1,3,2,0:T(8,128)S(1)}, f32[1,768,3,192]{1,3,2,0:T(8,128)}, u32[]{:S(2)}) copy-start(f32[1,768,3,192]{1,3,2,0:T(8,128)} %copy-done.5) | copy-start | bytes 5308420
  506.4 1.6 copy-start.52
  506.4 1.6 copy-start.53
  506.4 2.3 copy-start.34
  506.4 2.3 copy-start.36
  506.4 2.3 copy-start.38
  506.4 2.3 copy-start.40
  550.8 21.4 %collective-permute-start.1 = (bf16[1,4,197,192]{3,1,2,0:T(4,128)(2,1)}, bf16[1,4,197,192]{3,1,2,0:T(4,128)(2,1)}, u32[]{:S(2)}, u32[]{:S(2)}) collective-permute-start(bf16[1,4,197,192]{3,1,2,0:T(4,128)(2,1)} %slice.171), channel_id=1, source_target_pairs={{16,0},{17,1},{18,2},{19,3},{20,4},{21,5},{22,6},{23,7},{24,8},{25... | collective-permute-start | bytes 907784 | tf_op jit(solution)/shard_map/ppermute | solution.py:16
  565.0 18.9 %collective-permute-start.2 = (bf16[1,4,197,192]{3,1,2,0:T(4,128)(2,1)}, bf16[1,4,197,192]{3,1,2,0:T(4,128)(2,1)}, u32[]{:S(2)}, u32[]{:S(2)}) collective-permute-start(bf16[1,4,197,192]{3,1,2,0:T(4,128)(2,1)} %slice.170), channel_id=1, source_target_pairs={{16,0},{17,1},{18,2},{19,3},{20,4},{21,5},{22,6},{23,7},{24,8},{25... | collective-permute-start | bytes 907784 | tf_op jit(solution)/shard_map/ppermute | solution.py:16
  566.9 18.4 %collective-permute-start.4 = (f32[1,4,192]{2,1,0:T(4,128)S(1)}, f32[1,4,192]{2,1,0:T(4,128)S(1)}, u32[]{:S(2)}, u32[]{:S(2)}) collective-permute-start(f32[1,4,192]{2,1,0:T(4,128)S(1)} %slice.122), channel_id=1, source_target_pairs={{0,16},{1,17},{2,18},{3,19},{4,20},{5,21},{6,22},{7,23},{8,24},{9,... | collective-permute-start | bytes 9224 | tf_op jit(solution)/shard_map/ppermute | solution.py:16
  883.2 5.0 copy-start.19
  883.2 5.8 copy-start.13
  885.3 5.2 copy-start.12
  (8 other events, 7.0 us)
Sparse Core Ops, SparseCore 0:
  80.4 108.7 all-reduce.7
  211.2 129.5 all-reduce.9
  443.3 18.2 reduce-scatter.8
  463.7 17.0 reduce-scatter.10
  483.3 36.1 reduce-scatter.4
  521.9 37.8 reduce-scatter.6
  566.1 317.0 all-reduce.11
where the time goes:
time: 909 us; the launch traced here: 899 us
  waiting for transfers between devices  623 us (69%)
  local copies, waits for them, and re-layouts  100 us (11%)
  blocking collectives  95.6 us (11%)
  other arithmetic  31.5 us (3%)
  matrix products  18.4 us (2%)
  between operations  15 us (2%)
  starting transfers between devices  11 us (1%)
    psum x1, waiting for transfers between devices, body(): lax.psum((jnp.stack([gain_early, gain_late]), jnp.stack([shift_early, shi...  296 us
    psum x1, waiting for transfers between devices, body(): grad_lowered_two = lax.psum(lowered_grad, 'tensor')  130 us
    psum x1, waiting for transfers between devices, body(): lax.psum(attended[9], 'tensor')  105 us
    ppermute x5, waiting for transfers between devices, shifted(): return lax.ppermute(block, axis, route)  64.2 us
    another operation x27, local copies, waits for them, and re-layouts  34.8 us
    psum x1, blocking collectives, body(): lax.psum((jnp.stack([gain_early, gain_late]), jnp.stack([shift_early, shi...  34.3 us
    psum x2, blocking collectives, head_sum(): return lax.psum(partial_sum, 'tensor')  21.8 us
    reduce_scatter x1, waiting for transfers between devices, body(): lax.psum_scatter(value_grad_all.astype(jnp.bfloat16), 'dp', scatter_dimen...  19.2 us
  transfers between devices with their start and end apart: 12, of which 7 were waited for; matrix products, arithmetic and copies ran while one was open for 6% of the time, Pallas kernels for 0%

commit v1 on v0

v1 whole, which is shorter than its diff:
```python
import functools

import jax
import jax.numpy as jnp
from jax import lax
from jax.experimental import pallas as pl
from jax.experimental.pallas import tpu as pltpu
from jax.sharding import PartitionSpec as P

HEAD_DIM = 64
EPSILON = 1e-05
QUICK_GELU = 1.702
F32 = jnp.float32
BF16 = jnp.bfloat16
VMEM_BYTES = 56 * 1024 * 1024


def nn(left, right):
    return lax.dot_general(left, right, (((1,), (0,)), ((), ())), preferred_element_type=F32)


def nt(left, right):
    return lax.dot_general(left, right, (((1,), (1,)), ((), ())), preferred_element_type=F32)


def tn(left, right):
    return lax.dot_general(left, right, (((0,), (0,)), ((), ())), preferred_element_type=F32)


def norm_parts(values_in):
    centred = values_in - jnp.mean(values_in, axis=-1, keepdims=True)
    inverse = lax.rsqrt(jnp.mean(centred * centred, axis=-1, keepdims=True) + EPSILON)
    return centred * inverse, inverse


def norm_back(incoming, normed, inverse, gain):
    weighted = incoming * gain
    centred = weighted - jnp.mean(weighted, axis=-1, keepdims=True)
    return inverse * (centred - normed * jnp.mean(weighted * normed, axis=-1, keepdims=True))


def row_sum(values_in):
    return jnp.sum(values_in, axis=0, keepdims=True)


def block_of(shape, place):
    return pl.BlockSpec(shape, lambda i, info: place)


def run(kernel, info, ins, outs, scratch=(), flops=0):
    arrays, specs, moved = [], [], 0
    for item in ins:
        if isinstance(item, tuple):
            array, shape, place = item
        else:
            array, shape, place = item, item.shape, (0,) * item.ndim
        arrays.append(array)
        specs.append(block_of(shape, place))
        size = array.dtype.itemsize
        for n in shape:
            size *= n
        moved += size
    out_specs = [block_of(o.shape, (0,) * len(o.shape)) for o in outs]
    return pl.pallas_call(
        kernel,
        out_shape=outs,
        grid_spec=pltpu.PrefetchScalarGridSpec(
            num_scalar_prefetch=1,
            grid=(1,),
            in_specs=specs,
            out_specs=out_specs,
            scratch_shapes=list(scratch),
        ),
        compiler_params=pltpu.CompilerParams(vmem_limit_bytes=VMEM_BYTES),
        cost_estimate=pl.CostEstimate(flops=flops, bytes_accessed=moved, transcendentals=0),
    )(info, *arrays)


def shape_of(shape, kind):
    return jax.ShapeDtypeStruct(shape, kind)


def body(
    frames,
    video_group,
    msg_w,
    msg_bias,
    norm_gain,
    norm_shift,
    attn_in,
    qv_bias,
    attn_out,
    out_bias,
    norm2_gain,
    norm2_shift,
    fc_in,
    fc_in_bias,
    fc_out,
    fc_out_bias,
    cotangent,
):
    _, frame_count, patch, model = frames.shape
    width = attn_in.shape[-1]
    hidden_width = fc_in.shape[-1]
    heads = width // HEAD_DIM
    clips = lax.axis_size("dp")
    half = frame_count // 2
    rows = -(-(patch + 1) // 16) * 16
    all_rows = clips * frame_count
    scale = HEAD_DIM ** (-0.5)
    pipe = lax.axis_index("pipe")
    tensor = lax.axis_index("tensor")
    clip = lax.axis_index("dp")
    ring = clips == 4
    info = jnp.stack([pipe, tensor, clip if ring else jnp.zeros_like(clip)]).astype(jnp.int32)
    first_section = pipe == 0

    def core_swap(v):
        return lax.ppermute(v, "tensor", [(i, i ^ 1) for i in range(4)])

    def x_swap(v):
        return lax.ppermute(v, "tensor", [(i, i ^ 2) for i in range(4)])

    def y_swap(v):
        return lax.ppermute(v, "pipe", [(0, 1), (1, 0)])

    def y_late(v):
        return lax.ppermute(v, "pipe", [(0, 1)])

    def y_early(v):
        return lax.ppermute(v, "pipe", [(1, 0)])

    def z_up(v, distance=1):
        return lax.ppermute(v, "dp", [(i, (i + distance) % clips) for i in range(clips)])

    def z_down(v):
        return lax.ppermute(v, "dp", [(i, (i - 1) % clips) for i in range(clips)])

    def gather_clips(v):
        if ring:
            return jnp.stack([v, z_down(v), z_up(v, 2), z_up(v)])
        every = lax.all_gather(v, "dp")
        return lax.dynamic_slice_in_dim(jnp.concatenate([every, every]), clip, clips, 0)

    own_in = jnp.transpose(attn_in[0], (1, 2, 0))
    own_out = attn_out[0]
    vectors = jnp.concatenate(
        [norm_gain, norm_shift, out_bias, jnp.pad(qv_bias[0], ((0, 0), (0, model - width)))]
    )

    cls_rows = frames[0, :, 0, :]
    cls_all = gather_clips(cls_rows).reshape(all_rows, model)
    w_in = jnp.where(first_section, y_early(own_in), own_in)
    w_out = jnp.where(first_section, y_early(own_out), own_out)
    vec = jnp.where(first_section, y_early(vectors), vectors)
    owner = jnp.repeat(
        video_group[(clip + jnp.arange(clips)) % clips], frame_count
    )

    msg_bias_row = msg_bias[None]
    gain_two, shift_two = norm2_gain[None], norm2_shift[None]
    fc_in_bias_row, fc_out_bias_row = fc_in_bias[None], fc_out_bias[None]

    def head_masks(n):
        lane = lax.broadcasted_iota(jnp.int32, (n, width), 1)
        return [(lane >= h * HEAD_DIM) & (lane < (h + 1) * HEAD_DIM) for h in range(heads)]

    def only(mask, v):
        return jnp.where(mask, v, jnp.zeros_like(v))

    def message_forward(
        info_ref, cls, mw, mb, gain, shift, w, bias, wo, ob, col, line,
        first_o, low_o, q_o, k_o, v_o, probs_o, mixed_o, part_o,
    ):
        first = nn(cls[...], mw[...]) + mb[...]
        first_o[...] = first
        normed, _ = norm_parts(first)
        low = (normed * gain[...] + shift[...]).astype(BF16)
        low_o[...] = low
        q = (nt(low, w[0]) + bias[0, 0:1]).astype(BF16)
        k = nt(low, w[1]).astype(BF16)
        v = (nt(low, w[2]) + bias[0, 1:2]).astype(BF16)
        q_o[...] = q
        k_o[...] = k
        v_o[...] = v
        allowed = col[...] == line[...]
        mixed = jnp.zeros((all_rows, width), F32)
        for h, mask in enumerate(head_masks(all_rows)):
            scores = jnp.where(allowed, nt(only(mask, q), k) * scale, -jnp.inf)
            exponent = jnp.exp(scores - jnp.max(scores, axis=-1, keepdims=True))
            probs = exponent / jnp.sum(exponent, axis=-1, keepdims=True)
            probs_o[h] = probs
            mixed = mixed + only(mask, nn(probs.astype(BF16), v))
        mixed = mixed.astype(BF16)
        mixed_o[...] = mixed
        part = nn(mixed, wo[...]) + jnp.where(info_ref[1] == 0, ob[...], 0.0)
        part_o[...] = part[:frame_count]

    (first_msg, low_zero, q_zero, k_zero, v_zero, probs_zero, mixed_zero, part_zero) = run(
        message_forward,
        info,
        [
            cls_all, msg_w, msg_bias_row, norm_gain, norm_shift, own_in, qv_bias, own_out, out_bias,
            owner[:, None], owner[None, :],
        ],
        [
            shape_of((all_rows, model), F32),
            shape_of((all_rows, model), BF16),
            shape_of((all_rows, width), BF16),
            shape_of((all_rows, width), BF16),
            shape_of((all_rows, width), BF16),
            shape_of((heads, all_rows, all_rows), F32),
            shape_of((all_rows, width), BF16),
            shape_of((frame_count, model), F32),
        ],
    )
    part_zero = part_zero + core_swap(part_zero)
    part_zero = part_zero + x_swap(part_zero)
    part_late = y_late(part_zero)

    def slots(v):
        picked = [
            lax.dynamic_index_in_dim(v[0], pipe * half + (tensor ^ s), 0, keepdims=False)
            for s in range(half)
        ]
        return jnp.pad(jnp.stack(picked), ((0, 0), (0, rows - patch), (0, 0)))

    x_slots = slots(frames)
    g_slots = slots(cotangent)

    def grad_hidden_kernel(info_ref, g, w, out):
        for s in range(half):
            out[s] = nt(g[s], w[...]).astype(BF16)

    (g_hidden,) = run(
        grad_hidden_kernel, info, [g_slots, fc_out],
        [shape_of((half, rows, hidden_width), BF16)],
        flops=2 * half * rows * model * hidden_width,
    )

    def project_kernel(info_ref, x, w, v, q_o, k_o, v_o):
        gain, shift = v[0:1], v[1:2]
        for s in range(half):
            normed, _ = norm_parts(x[s].astype(F32))
            low = (normed * gain + shift).astype(BF16)
            q_o[s] = (nt(low, w[0]) + v[3:4, :width]).astype(BF16)
            k_o[s] = nt(low, w[1]).astype(BF16)
            v_o[s] = (nt(low, w[2]) + v[4:5, :width]).astype(BF16)

    q_one, k_one, v_one = run(
        project_kernel, info, [x_slots, w_in, vec],
        [shape_of((half, rows, width), BF16)] * 3,
        flops=2 * half * rows * model * 3 * width,
    )

    def attend_kernel(
        base, info_ref, q, k, v, first, part, late, w, vrow, wo,
        pa_o, pb_o, mixed_o, probs_o, k_o, v_o, msg_o,
    ):
        sec, ten = info_ref[0], info_ref[1]
        msg_o[...] = jnp.zeros_like(msg_o)
        for j in range(2):
            at = pl.ds(sec * half + (ten ^ (base + j)), 1)
            summed = jnp.where(sec == 0, part[at, :], late[at, :])
            msg_o[j : j + 1, :] = (first[at, :] + summed).astype(BF16).astype(F32)
        normed, _ = norm_parts(msg_o[...])
        low = (normed * vrow[0:1] + vrow[1:2]).astype(BF16)
        k_msg = nt(low, w[1])
        v_msg = nt(low, w[2]) + vrow[4:5, :width]
        here = lax.broadcasted_iota(jnp.int32, (rows, width), 0) == patch
        key_here = lax.broadcasted_iota(jnp.int32, (rows, rows), 1) <= patch
        masks = head_masks(rows)
        for j in (1, 0):
            kk = jnp.where(here, k_msg[j : j + 1], k[j].astype(F32)).astype(BF16)
            vv = jnp.where(here, v_msg[j : j + 1], v[j].astype(F32)).astype(BF16)
            k_o[j] = kk
            v_o[j] = vv
            mixed = jnp.zeros((rows, width), F32)
            for h in range(heads):
                scores = nt(only(masks[h], q[j]), kk) * scale
                scores = jnp.where(key_here, scores, -jnp.inf)
                exponent = jnp.exp(scores - jnp.max(scores, axis=-1, keepdims=True))
                probs = exponent * (1.0 / jnp.sum(exponent, axis=-1, keepdims=True))
                probs = probs.astype(BF16)
                probs_o[j, h] = probs
                mixed = mixed + only(masks[h], nn(probs, vv))
            mixed = mixed.astype(BF16)
            mixed_o[j] = mixed
            (pa_o, pb_o)[j][...] = nn(mixed, wo[...]).astype(BF16)

    def attend(pair):
        return run(
            functools.partial(attend_kernel, 2 * pair),
            info,
            [
                (q_one, (2, rows, width), (pair, 0, 0)),
                (k_one, (2, rows, width), (pair, 0, 0)),
                (v_one, (2, rows, width), (pair, 0, 0)),
                first_msg, part_zero, part_late, w_in, vec, w_out,
            ],
            [
                shape_of((rows, model), BF16),
                shape_of((rows, model), BF16),
                shape_of((2, rows, width), BF16),
                shape_of((2, heads, rows, rows), BF16),
                shape_of((2, rows, width), BF16),
                shape_of((2, rows, width), BF16),
                shape_of((16, model), F32),
            ],
            flops=2 * 2 * rows * (width * model + 2 * heads * rows * HEAD_DIM),
        )

    def own_sum(part0, part1, part2, part3):
        two = part2 + core_swap(part3)
        return part0, core_swap(part1), x_swap(two)

    def spread(own):
        one = core_swap(own)
        two = x_swap(own)
        return own, one, two, core_swap(two)

    part2, part3, mixed23, probs23, k23, v23, msg23 = attend(1)
    part0, part1, mixed01, probs01, k01, v01, msg01 = attend(0)
    branch_parts = own_sum(part0, part1, part2, part3)

    def residual_kernel(info_ref, a, b, c, x, vrow, gain, shift, resid_o, low_o):
        summed = a[...].astype(F32) + b[...].astype(F32) + c[...].astype(F32)
        resid = x[0].astype(F32) + summed + vrow[2:3]
        resid_o[...] = resid
        normed, _ = norm_parts(resid)
        low_o[...] = (normed * gain[...] + shift[...]).astype(BF16)

    resid_own, low_own = run(
        residual_kernel, info,
        [*branch_parts, (x_slots, (1, rows, model), (0, 0, 0)), vec, gain_two, shift_two],
        [shape_of((rows, model), F32), shape_of((rows, model), BF16)],
    )
    low_two = spread(low_own)

    def feed_kernel(info_ref, low_a, low_b, gh, w, bias, hid_o, pre_o, ga_o, gb_o):
        for j in (1, 0):
            hidden_in = nn((low_a, low_b)[j][...], w[...]) + bias[...]
            sig = 1.0 / (1.0 + jnp.exp(-QUICK_GELU * hidden_in))
            hid_o[j] = (hidden_in * sig).astype(BF16)
            slope = sig + QUICK_GELU * hidden_in * sig * (1.0 - sig)
            pre = (gh[j].astype(F32) * slope).astype(BF16)
            pre_o[j] = pre
            (ga_o, gb_o)[j][...] = nt(pre, w[...]).astype(BF16)

    def feed(pair):
        return run(
            feed_kernel, info,
            [
                low_two[2 * pair], low_two[2 * pair + 1],
                (g_hidden, (2, rows, hidden_width), (pair, 0, 0)),
                fc_in, fc_in_bias_row,
            ],
            [
                shape_of((2, rows, hidden_width), BF16),
                shape_of((2, rows, hidden_width), BF16),
                shape_of((rows, model), BF16),
                shape_of((rows, model), BF16),
            ],
            flops=2 * 4 * rows * model * hidden_width,
        )

    hid01, pre01, gl0, gl1 = feed(0)
    hid23, pre23, gl2, gl3 = feed(1)
    low_parts = own_sum(gl0, gl1, gl2, gl3)

    def residual_back_kernel(info_ref, a, b, c, resid, g, gain, grad_o, low_o, small_o):
        incoming = a[...].astype(F32) + b[...].astype(F32) + c[...].astype(F32)
        normed, inverse = norm_parts(resid[...])
        real = lax.broadcasted_iota(jnp.int32, (rows, model), 0) < patch
        incoming = jnp.where(real, incoming, 0.0)
        grad = g[0].astype(F32) + norm_back(incoming, normed, inverse, gain[...])
        grad = jnp.where(real, grad, 0.0)
        grad_o[...] = grad
        low = grad.astype(BF16)
        low_o[...] = low
        small_o[...] = jnp.zeros_like(small_o)
        small_o[0:1, :] = row_sum(incoming * normed)
        small_o[1:2, :] = row_sum(incoming)
        small_o[2:3, :] = row_sum(low.astype(F32))
        small_o[3:4, :] = row_sum(g[0].astype(F32))

    grad_resid, grad_low, small_two = run(
        residual_back_kernel, info,
        [*low_parts, resid_own, (g_slots, (1, rows, model), (0, 0, 0)), gain_two],
        [shape_of((rows, model), F32), shape_of((rows, model), BF16), shape_of((8, model), F32)],
    )
    branch = spread(grad_low)

    quarter = hidden_width // 4
    assert quarter == width

    def chunks_out(acc, info_ref, outs):
        def chunk(r):
            start = pl.multiple_of(((info_ref[2] + r) & 3) * quarter, quarter)
            return acc[pl.ds(start, quarter), :].astype(BF16)

        m0, m1, m2t, m2b, m3 = outs
        m0[...] = chunk(0)
        m1[...] = chunk(1)
        m2 = chunk(2)
        m2t[...] = m2[: quarter // 2]
        m2b[...] = m2[quarter // 2 :]
        m3[...] = chunk(3)

    chunk_shapes = [
        shape_of((quarter, model), BF16),
        shape_of((quarter, model), BF16),
        shape_of((quarter // 2, model), BF16),
        shape_of((quarter // 2, model), BF16),
        shape_of((quarter, model), BF16),
    ]

    def fc_out_kernel(info_ref, ha, hb, g, *outs):
        acc = outs[-1]
        pair_rows = 2 * rows
        acc[...] = tn(ha[...].reshape(pair_rows, hidden_width), g[0:2].reshape(pair_rows, model))
        acc[...] += tn(hb[...].reshape(pair_rows, hidden_width), g[2:4].reshape(pair_rows, model))
        chunks_out(acc, info_ref, outs[:-1])

    fc_out_chunks = run(
        fc_out_kernel, info, [hid01, hid23, g_slots], chunk_shapes,
        [pltpu.VMEM((hidden_width, model), F32)],
        flops=2 * half * rows * model * hidden_width,
    )

    def fc_in_kernel(info_ref, pa, pb, l0, l1, l2, l3, m0, m1, m2t, m2b, m3, bias_o, acc):
        acc[...] = tn(pa[0], l0[...])
        acc[...] += tn(pa[1], l1[...])
        acc[...] += tn(pb[0], l2[...])
        acc[...] += tn(pb[1], l3[...])
        chunks_out(acc, info_ref, (m0, m1, m2t, m2b, m3))
        total = row_sum(pa[0].astype(F32)) + row_sum(pa[1].astype(F32))
        bias_o[...] = total + row_sum(pb[0].astype(F32)) + row_sum(pb[1].astype(F32))

    def fc_in_natural_kernel(info_ref, pa, pb, l0, l1, l2, l3, m0, m1, m2t, m2b, m3, bias_o, acc):
        acc[...] = tn(l0[...], pa[0])
        acc[...] += tn(l1[...], pa[1])
        acc[...] += tn(l2[...], pb[0])
        acc[...] += tn(l3[...], pb[1])
        chunks_out(acc, info_ref, (m0, m1, m2t, m2b, m3))
        total = row_sum(pa[0].astype(F32)) + row_sum(pa[1].astype(F32))
        bias_o[...] = total + row_sum(pb[0].astype(F32)) + row_sum(pb[1].astype(F32))

    *fc_in_chunks, fc_in_bias_part = run(
        fc_in_natural_kernel, info, [pre01, pre23, *low_two],
        [*chunk_shapes, shape_of((1, hidden_width), F32)],
        [pltpu.VMEM((model, hidden_width), F32)],
        flops=2 * half * rows * model * hidden_width,
    )

    def column_out(values_in, slot, info_ref, keep_o, send_o):
        ten = info_ref[1]
        place = (ten ^ slot) & 1
        for i in range(4):
            block = values_in[:, i * width : (i + 1) * width]
            apart = ten ^ i

            @pl.when((apart & 1) == 0)
            def _():
                keep_o[apart >> 1, place] = block

            @pl.when((apart & 1) == 1)
            def _():
                send_o[apart >> 1, place] = block

    column_shapes = [shape_of((2, 2, rows, width), BF16)] * 2

    def mlp_kernel(info_ref, ha, hb, w, resid, bias, keep01, send01, keep23, send23):
        for s in range(half):
            out = nn((ha, hb)[s // 2][s % 2], w[...])
            if s == 0:
                out = out + resid[...] + bias[...]
            keep_o, send_o = ((keep01, send01), (keep23, send23))[s // 2]
            column_out(out.astype(BF16), s, info_ref, keep_o, send_o)

    block_columns = run(
        mlp_kernel, info, [hid01, hid23, fc_out, resid_own, fc_out_bias_row], column_shapes * 2,
        flops=2 * half * rows * model * hidden_width,
    )

    def column_sum(keep01, send01, keep23, send23):
        got01 = core_swap(send01)
        got23 = core_swap(send23)
        far23 = x_swap(keep01[1] + got01[1])
        far01 = x_swap(keep23[1] + got23[1])
        return keep01, got01, far01, keep23, got23, far23

    def frames_of(refs, info_ref):
        keep01, got01, far01, keep23, got23, far23 = refs
        low_pair = info_ref[1] >> 1
        for i in range(2):
            for pair, keep, got, far in (
                (low_pair, keep01, got01, far01),
                (low_pair ^ 1, keep23, got23, far23),
            ):
                total = keep[0, i].astype(F32) + got[0, i].astype(F32) + far[i].astype(F32)
                yield pair * 2 + i, total[:patch]

    def column_ins(arrays):
        keep01, got01, far01, keep23, got23, far23 = arrays
        first_of = (1, 2, rows, width), (0, 0, 0, 0)
        return [
            (keep01, *first_of), (got01, *first_of), far01,
            (keep23, *first_of), (got23, *first_of), far23,
        ]

    def block_out_kernel(info_ref, *refs):
        out = refs[-1]
        for place, total in frames_of(refs[:-1], info_ref):
            out[place] = total.astype(BF16)

    (block_out,) = run(
        block_out_kernel, info, column_ins(column_sum(*block_columns)),
        [shape_of((half, patch, width), BF16)],
    )

    def attend_back_kernel(
        base, info_ref, ba, bb, q, k, v, probs, x, msg, w, vrow, wo, extra,
        keep_o, send_o, grads_o, low_o, small_o,
    ):
        ten = info_ref[1]
        masks = head_masks(rows)
        here = lax.broadcasted_iota(jnp.int32, (rows, model), 0) == patch
        gain, shift = vrow[0:1], vrow[1:2]
        small_o[...] = jnp.zeros_like(small_o)
        for j in range(2):
            grad_mixed = nt((ba, bb)[j][...], wo[...]).astype(BF16)
            dq = jnp.zeros((rows, width), F32)
            dk = jnp.zeros((rows, width), F32)
            dv = jnp.zeros((rows, width), F32)
            for h in range(heads):
                grad_head = only(masks[h], grad_mixed)
                low_probs = probs[j, h]
                wide = low_probs.astype(F32)
                dv = dv + tn(low_probs, grad_head)
                grad_probs = nt(grad_head, v[j])
                inner = jnp.sum(wide * grad_probs, axis=-1, keepdims=True)
                grad_scores = (wide * (grad_probs - inner)).astype(BF16)
                dq = dq + only(masks[h], nn(grad_scores, k[j]))
                dk = dk + tn(grad_scores, only(masks[h], q[j]))
            dq = (dq * scale).astype(BF16)
            dk = (dk * scale).astype(BF16)
            dv = dv.astype(BF16)
            grads_o[0, j] = dq
            grads_o[1, j] = dk
            grads_o[2, j] = dv
            grad_low = nn(dq, w[0]) + nn(dk, w[1]) + nn(dv, w[2])
            token = jnp.where(here, msg[j : j + 1], x[j].astype(F32))
            normed, inverse = norm_parts(token)
            low_o[j] = (normed * gain + shift).astype(BF16)
            back = norm_back(grad_low, normed, inverse, gain)
            small_o[pl.ds(ten ^ (base + j), 1), :] = row_sum(only(here, back))
            small_o[4:5, :] += row_sum(grad_low * normed)
            small_o[5:6, :] += row_sum(grad_low)
            small_o[6:7, 0:width] += row_sum(dq.astype(F32))
            small_o[6:7, 256 : 256 + width] += row_sum(dv.astype(F32))
            if base + j == 0:
                back = back + extra[...]
            column_out(back.astype(BF16), base + j, info_ref, keep_o, send_o)

    def attend_back(pair, k, v, probs, msg):
        return run(
            functools.partial(attend_back_kernel, 2 * pair),
            info,
            [
                branch[2 * pair], branch[2 * pair + 1],
                (q_one, (2, rows, width), (pair, 0, 0)),
                k, v, probs,
                (x_slots, (2, rows, model), (pair, 0, 0)),
                msg, w_in, vec, w_out, grad_resid,
            ],
            [
                *column_shapes,
                shape_of((3, 2, rows, width), BF16),
                shape_of((2, rows, model), BF16),
                shape_of((8, model), F32),
            ],
            flops=2 * 2 * rows * (4 * width * model + 4 * heads * rows * HEAD_DIM),
        )

    keep01, send01, grads01, low01, small01 = attend_back(0, k01, v01, probs01, msg01)
    keep23, send23, grads23, low23, small23 = attend_back(1, k23, v23, probs23, msg23)
    grad_columns = column_sum(keep01, send01, keep23, send23)

    def attend_weight_kernel(info_ref, ga, gb, la, lb, ma, mb, b0, b1, b2, b3, *outs):
        acc = outs[-1]
        pair_rows = 2 * rows
        low_a = la[...].reshape(pair_rows, model)
        low_b = lb[...].reshape(pair_rows, model)
        for c in range(3):
            acc[c * width : (c + 1) * width, :] = tn(
                ga[c].reshape(pair_rows, width), low_a
            ) + tn(gb[c].reshape(pair_rows, width), low_b)
        acc[3 * width :, :] = (
            tn(ma[0], b0[...]) + tn(ma[1], b1[...]) + tn(mb[0], b2[...]) + tn(mb[1], b3[...])
        )
        chunks_out(acc, info_ref, outs[:-1])

    attend_chunks = run(
        attend_weight_kernel, info,
        [grads01, grads23, low01, low23, mixed01, mixed23, *branch], chunk_shapes,
        [pltpu.VMEM((4 * width, model), F32)],
        flops=2 * half * rows * model * 4 * width,
    )

    def add(*terms):
        return sum(term.astype(F32) for term in terms).astype(BF16)

    def reduce_chunks(m0, m1, m2t, m2b, m3):
        if not ring:
            sizes = [m.shape[0] for m in (m0, m1, m2t, m2b, m3)]
            total = lax.psum(jnp.concatenate([m0, m1, m2t, m2b, m3]), ("pipe", "dp"))
            places = [sum(sizes[:i]) for i in range(6)]
            return [total[a:b] for a, b in zip(places[:-1], places[1:])]
        part = quarter // 2
        up, down = z_up(m2t), z_down(m2b)
        m1 = jnp.concatenate([add(m1[:part], up), m1[part:]])
        m3 = jnp.concatenate([m3[:part], add(m3[part:], down)])
        mine = add(m0, z_up(m1), z_down(m3))
        total = add(mine, y_swap(mine))
        before, after = z_up(total), z_down(total)
        return [total, after, z_up(before[:part]), z_down(after[part:]), before]

    def whole_kernel(info_ref, c0, c1, c2t, c2b, c3, out):
        def put(r, block, shift=0):
            start = pl.multiple_of(((info_ref[2] + r) & 3) * quarter + shift, quarter // 2)
            out[pl.ds(start, block.shape[0]), :] = block.astype(F32)

        put(0, c0[...])
        put(1, c1[...])
        put(2, c2t[...])
        put(2, c2b[...], quarter // 2)
        put(3, c3[...])

    def whole(chunks):
        return run(whole_kernel, info, chunks, [shape_of((4 * quarter, model), F32)])[0]

    fc_out_grad = whole(reduce_chunks(*fc_out_chunks))
    fc_in_grad = whole(reduce_chunks(*fc_in_chunks))
    attend_grad = reduce_chunks(*attend_chunks)

    def spot(row, at, size):
        return jnp.where(jnp.arange(size)[:, None] == at, row, 0.0)

    small = small01 + small23
    pack = jnp.concatenate(
        [
            small[:6],
            small_two[:4],
            spot(fc_in_bias_part, tensor, 4),
            spot(small[6:7], tensor, 4),
            jnp.zeros((6, model), F32),
        ]
    ).astype(BF16)
    pack = add(pack, core_swap(pack))
    pack = add(pack, x_swap(pack))
    other = y_swap(pack)
    early = jnp.where(first_section, pack[:half], other[:half])
    later = jnp.where(first_section, other[:half], pack[:half])
    pack = jnp.concatenate([early, later, add(pack[half:], other[half:])])
    packs = gather_clips(pack)

    pack_rows = pack.shape[0]

    def gather_sent(packs_ref):
        return jnp.concatenate(
            [packs_ref[c, 0:frame_count, :].astype(F32) for c in range(clips)], axis=0
        )

    def message_back(
        info_ref, packs_ref, first, q, k, v, probs, w, wo, gain,
        sent_o, grads_o, back_o,
    ):
        sent = gather_sent(packs_ref)
        low = sent.astype(BF16)
        sent_o[...] = sent
        grad_mixed = nt(low, wo[...]).astype(BF16)
        dq = jnp.zeros((all_rows, width), F32)
        dk = jnp.zeros((all_rows, width), F32)
        dv = jnp.zeros((all_rows, width), F32)
        for h, mask in enumerate(head_masks(all_rows)):
            grad_head = only(mask, grad_mixed)
            wide = probs[h]
            dv = dv + tn(wide.astype(BF16), grad_head)
            grad_probs = nt(grad_head, v[...])
            inner = jnp.sum(wide * grad_probs, axis=-1, keepdims=True)
            grad_scores = (wide * (grad_probs - inner)).astype(BF16)
            dq = dq + only(mask, nn(grad_scores, k[...]))
            dk = dk + tn(grad_scores, only(mask, q[...]))
        dq = (dq * scale).astype(BF16)
        dk = (dk * scale).astype(BF16)
        dv = dv.astype(BF16)
        grads_o[0] = dq
        grads_o[1] = dk
        grads_o[2] = dv
        grad_low = nn(dq, w[0]) + nn(dk, w[1]) + nn(dv, w[2])
        normed, inverse = norm_parts(first[...])
        back = norm_back(grad_low, normed, inverse, gain[...])
        back_o[0:all_rows, :] = back.astype(BF16)
        tail = jnp.concatenate(
            [
                row_sum(grad_low * normed),
                row_sum(grad_low),
                jnp.zeros((14, model), F32),
            ],
            axis=0,
        )
        back_o[all_rows:, :] = tail.astype(BF16)

    sent_all, grads_zero, back_zero = run(
        message_back, info,
        [packs, first_msg, q_zero, k_zero, v_zero, probs_zero, own_in, own_out, norm_gain],
        [
            shape_of((all_rows, model), F32),
            shape_of((3, all_rows, width), BF16),
            shape_of((all_rows + 16, model), BF16),
        ],
    )
    back_zero = add(back_zero, core_swap(back_zero))
    back_zero = add(back_zero, x_swap(back_zero))
    back_late = y_late(back_zero)

    def message_weight(info_ref, sent, grads, low, mixed, in_o, out_o, qv_o, bias_o):
        for c in range(3):
            in_o[c] = tn(grads[c], low[...])
        out_o[...] = tn(mixed[...], sent[...].astype(BF16))
        qv_o[0:1, :] = row_sum(grads[0].astype(F32))
        qv_o[1:2, :] = row_sum(grads[2].astype(F32))
        bias_o[...] = row_sum(sent[...])

    in_zero, out_zero, qv_zero, bias_zero = run(
        message_weight, info, [sent_all, grads_zero, low_zero, mixed_zero],
        [
            shape_of((3, width, model), F32),
            shape_of((width, model), F32),
            shape_of((2, width), F32),
            shape_of((1, model), F32),
        ],
    )

    def attend_whole_kernel(info_ref, c0, c1, c2t, c2b, c3, in_zero, out_zero, in_o, out_o, acc):
        @pl.when(info_ref[0] == 0)
        def _():
            in_o[...] = in_zero[...]
            out_o[...] = out_zero[...]

        @pl.when(info_ref[0] == 1)
        def _():
            whole_kernel(info_ref, c0, c1, c2t, c2b, c3, acc)
            for c in range(3):
                in_o[c] = acc[c * width : (c + 1) * width, :]
            out_o[...] = acc[3 * width :, :]

    attn_in_grad, attn_out_grad = run(
        attend_whole_kernel, info, [*attend_grad, in_zero, out_zero],
        [shape_of((3, width, model), F32), shape_of((width, model), F32)],
        [pltpu.VMEM((4 * width, model), F32)],
    )

    def message_end(
        info_ref, sent, own, late, cls, mw, packs_ref, qv_in, bias_in,
        w_o, cls_o, vec_o, qv_o, acc, sums,
    ):
        sec, ten = info_ref[0], info_ref[1]
        total = jnp.where(sec == 0, own[...].astype(F32), late[...].astype(F32))
        grad_first = sent[...] + total[:all_rows]
        high = grad_first.astype(BF16)
        rest = (grad_first - high.astype(F32)).astype(BF16)
        at = pl.multiple_of(ten * width, width)
        acc[...] = tn(high, cls[...]) + tn(rest, cls[...])
        w_o[...] = acc[pl.ds(at, width), :]
        mw_rows = mw[pl.ds(at, width), :]
        cls_o[...] = nt(high[:16], mw_rows) + nt(rest[:16], mw_rows)
        small = packs_ref[0, frame_count:, :].astype(F32)
        for c in range(1, clips):
            small = small + packs_ref[c, frame_count:, :].astype(F32)
        sums[...] = small
        first_one = sec == 0
        vec_o[...] = jnp.zeros_like(vec_o)
        vec_o[0:1, :] = jnp.where(first_one, total[all_rows : all_rows + 1], sums[0:1])
        vec_o[1:2, :] = jnp.where(first_one, total[all_rows + 1 : all_rows + 2], sums[1:2])
        vec_o[2:3, :] = jnp.where(first_one, bias_in[...], sums[4:5])
        vec_o[3:4, :] = sums[2:3]
        vec_o[4:5, :] = sums[3:4]
        vec_o[5:6, :] = sums[5:6]
        vec_o[6:7, :] = sums[pl.ds(6 + ten, 1), :]
        vec_o[7:8, :] = row_sum(grad_first)
        qv_row = sums[pl.ds(10 + ten, 1), :]
        qv_o[0:1, :] = jnp.where(first_one, qv_in[0:1], qv_row[:, :width])
        qv_o[1:2, :] = jnp.where(first_one, qv_in[1:2], qv_row[:, 256 : 256 + width])

    small_rows = pack_rows - frame_count
    msg_w_grad, cls_part, vec_grads, qv_grad = run(
        message_end, info,
        [sent_all, back_zero, back_late, cls_all, msg_w, packs, qv_zero, bias_zero],
        [
            shape_of((width, model), F32),
            shape_of((16, width), F32),
            shape_of((8, model), F32),
            shape_of((2, width), F32),
        ],
        [pltpu.VMEM((model, model), F32), pltpu.VMEM((small_rows, model), F32)],
    )

    def frames_grad_kernel(info_ref, *refs):
        cls, out = refs[-2:]
        top = lax.broadcasted_iota(jnp.int32, (patch, width), 0) == 0
        for place, total in frames_of(refs[:-2], info_ref):
            row = cls[pl.ds(info_ref[0] * half + place, 1), :]
            out[place] = (total + jnp.where(top, row, 0.0)).astype(BF16)

    (frames_grad,) = run(
        frames_grad_kernel, info, [*column_ins(grad_columns), cls_part],
        [shape_of((half, patch, width), BF16)],
    )

    return (
        block_out[None],
        frames_grad[None],
        msg_w_grad.T,
        vec_grads[7],
        vec_grads[0:1],
        vec_grads[1:2],
        jnp.transpose(attn_in_grad, (2, 0, 1))[None],
        qv_grad[None],
        attn_out_grad[None],
        vec_grads[2:3],
        vec_grads[3],
        vec_grads[4],
        fc_in_grad,
        vec_grads[6],
        fc_out_grad,
        vec_grads[5],
    )


def solution(mesh):
    return jax.shard_map(
        body,
        mesh=mesh,
        in_specs=(
            P("dp", None, None, None),
            P(),
            P(),
            P(),
            P("pipe", None),
            P("pipe", None),
            P("pipe", None, None, "tensor"),
            P("pipe", None, "tensor"),
            P("pipe", "tensor", None),
            P("pipe", None),
            P(),
            P(),
            P(None, "tensor"),
            P("tensor"),
            P("tensor", None),
            P(),
            P("dp", None, None, None),
        ),
        out_specs=(
            P("dp", "pipe", None, "tensor"),
            P("dp", "pipe", None, "tensor"),
            P(None, "tensor"),
            P(),
            P("pipe", None),
            P("pipe", None),
            P("pipe", None, None, "tensor"),
            P("pipe", None, "tensor"),
            P("pipe", "tensor", None),
            P("pipe", None),
            P(),
            P(),
            P(None, "tensor"),
            P("tensor"),
            P("tensor", None),
            P(),
        ),
        check_vma=False,
    )
```

time: 909 us -> 304 us (0.33)
  waiting for transfers between devices: 623 us -> 55.6 us
  Pallas kernels: 0 us -> 111 us
  blocking collectives: 95.6 us -> 0 us
  starting transfers between devices: 11 us -> 81.4 us
  local copies, waits for them, and re-layouts: 100 us -> 34.9 us
  matrix products: 18.4 us -> 0 us
  other arithmetic: 31.5 us -> 13.9 us
  between operations: 15 us -> 2.03 us
    psum x3 -> x0, waiting for transfers between devices: 531 us -> none  [the longest x1 296 us: body(): lax.psum((jnp.stack([gain_early, gain_late]), jnp.stack([shift_early, shi...]
    pallas_call x0 -> x23, Pallas kernels: none -> 111 us  [run(): pl.pallas_call(kernel, out_shape=outs, grid_spec=pltpu.PrefetchScalarGrid...]
    ppermute x5 -> x65, starting transfers between devices: 10.4 us -> 81.4 us  [the longest x14 34.8 us: z_down(): return lax.ppermute(v, 'dp', [(i, (i - 1) % clips) for i in range(clips)])]
    psum x4 -> x0, blocking collectives: 66.5 us -> none  [the longest x1 34.3 us: body(): lax.psum((jnp.stack([gain_early, gain_late]), jnp.stack([shift_early, shi...]
    another operation x37 -> x3, local copies, waits for them, and re-layouts: 38 us -> 1.99 us  [the longest x1 0.71 us: gather_clips(): return jnp.stack([v, z_down(v), z_up(v, 2), z_up(v)])]
    all_gather x2 -> x0, blocking collectives: 29.1 us -> none  [the longest x1 15.5 us: body(): lax.all_gather(key_zero, 'dp', axis=0, tiled=True)]
    reduce_scatter x4 -> x0, waiting for transfers between devices: 26.9 us -> none  [the longest x1 19.2 us: body(): lax.psum_scatter(value_grad_all.astype(jnp.bfloat16), 'dp', scatter_dimen...]
    dot_general x14 -> x0, matrix products: 18.1 us -> none  [the longest x1 3.05 us: message_input_back(): jnp.einsum('mk,dk->md', grad_first, msg_w.astype(jnp.float32), precision=...]
  transfers between devices with their start and end apart: 12 -> 65, of which waited for: 7 -> 19; matrix products, arithmetic and copies ran while one was open for 6% -> 14% of each run, Pallas kernels for 0% -> 33%
where the time goes in v1:
time: 304 us; the launch traced here: 299 us
  Pallas kernels  111 us (37%)
  starting transfers between devices  81.4 us (27%)
  waiting for transfers between devices  55.6 us (18%)
  local copies, waits for them, and re-layouts  34.9 us (11%)
  other arithmetic  13.9 us (5%)
    pallas_call x23, Pallas kernels, run(): pl.pallas_call(kernel, out_shape=outs, grid_spec=pltpu.PrefetchScalarGrid...  111 us
    ppermute x14, starting transfers between devices, z_down(): return lax.ppermute(v, 'dp', [(i, (i - 1) % clips) for i in range(clips)])  34.8 us
    ppermute x11, waiting for transfers between devices, x_swap(): return lax.ppermute(v, 'tensor', [(i, i ^ 2) for i in range(4)])  22.7 us
    ppermute x16, waiting for transfers between devices, z_up(): lax.ppermute(v, 'dp', [(i, (i + distance) % clips) for i in range(clips)])  15.6 us
    ppermute x11, starting transfers between devices, x_swap(): return lax.ppermute(v, 'tensor', [(i, i ^ 2) for i in range(4)])  15 us
    ppermute x14, waiting for transfers between devices, z_down(): return lax.ppermute(v, 'dp', [(i, (i - 1) % clips) for i in range(clips)])  14.3 us
    ppermute x16, starting transfers between devices, z_up(): lax.ppermute(v, 'dp', [(i, (i + distance) % clips) for i in range(clips)])  13.9 us
    unnamed x150, local copies, waits for them, and re-layouts  10.6 us
  transfers between devices with their start and end apart: 65, of which 19 were waited for; matrix products, arithmetic and copies ran while one was open for 14% of the time, Pallas kernels for 33%

profile of v1, /device:TPU:0, one launch (start us, length us, event | category | flops | bytes accessed | tf_op | source)
XLA Modules:
  0.0 299.0 jit_solution(14551626198050742128)
XLA Ops:
  1.4 3.0 %collective-permute-start.4 = (bf16[8,768]{1,0:T(8,128)(2,1)S(1)}, bf16[8,768]{1,0:T(8,128)(2,1)S(1)}, u32[]{:S(2)}, u32[]{:S(2)}) collective-permute-start(bf16[8,768]{1,0:T(8,128)(2,1)S(1)} %get-tuple-element.220), channel_id=1, source_target_pairs={{0,1},{1,2},{2,3},{3,0},{4,5},{5,6},{6,7},{7,4},{8,9},{9,10},{10,1... | collective-permute-start | bytes 36872 | tf_op jit(solution)/shard_map/ppermute | solution.py:134
  4.4 2.6 collective-permute-start.3
  11.8 6.9 %constant_dynamic-slice_fusion.7 = (bf16[1,1,197,768]{3,1,2,0:T(2,128)(2,1)S(1)}, bf16[1,1,197,768]{3,1,2,0:T(2,128)(2,1)S(1)}, bf16[1,1,197,768]{3,1,2,0:T(2,128)(2,1)S(1)}, bf16[1,1,197,768]{3,1,2,0:T(2,128)(2,1)S(1)}) fusion(bf16[1,8,197,768]{3,1,2,0:T(8,128)(2,1)} %param.17, s32[]{:T(128)S(6)} %select_n.84, s32[]{:T(128)S(6)} %select_n.86, ...), kind=kLoop, calls=%fused_computation.88 | loop fusion | bytes 2420752 | tf_op jit(solution)/shard_map/jit(dynamic_index_in_dim)/dynamic_slice | solution.py:223
  23.9 4.9 %shard_map.289 = (f32[32,768]{1,0:T(8,128)}, bf16[32,768]{1,0:T(8,128)(2,1)}, bf16[32,192]{1,0:T(8,128)(2,1)}, bf16[32,192]{1,0:T(8,128)(2,1)}, bf16[32,192]{1,0...) custom-call(s32[3]{0:T(128)} %pad_add_fusion.info_ref, ...), custom_call_target="tpu_custom_call" | custom-call | bytes 2422528 | tf_op jit(solution)/shard_map/pallas_call | solution.py:64
  34.2 4.8 %collective-permute-start.7 = (f32[8,768]{1,0:T(8,128)S(1)}, f32[8,768]{1,0:T(8,128)S(1)}, u32[]{:S(2)}, u32[]{:S(2)}) collective-permute-start(f32[8,768]{1,0:T(8,128)S(1)} %add.187.part), channel_id=1, source_target_pairs={{0,16},{1,17},{2,18},{3,19},{4,20},{5,21},{6,22},{7,23},{8,24},{9,... | collective-permute-start | bytes 73736 | tf_op jit(solution)/shard_map/ppermute | solution.py:128
  42.3 4.6 %shard_map.288 = (bf16[4,208,192]{2,1,0:T(8,128)(2,1)}, bf16[4,208,192]{2,1,0:T(8,128)(2,1)}, bf16[4,208,192]{2,1,0:T(8,128)(2,1)}) custom-call(s32[3]{0:T(128)} %pad_add_fusion.info_ref, bf16[4,208,768]{2,1,0:T(8,128)(2,1)} %fusion.10.x, bf16[3,192,768]{2,1,0:T(8,128)(2,1)} %broadcast_select_fusion.w, f32[5,768]{1,0:T(8,128)} %broadcast_select_fusion.2.v.vrow), custom_call_target="tpu_custom_call" | custom-call | flops 736100352 | bytes 2178048 | tf_op jit(solution)/shard_map/pallas_call | solution.py:64
  47.6 5.3 %shard_map.291 = (bf16[208,768]{1,0:T(8,128)(2,1)}, bf16[208,768]{1,0:T(8,128)(2,1)}, bf16[2,208,192]{2,1,0:T(8,128)(2,1)}, bf16[2,3,208,208]{3,2,1,0:T(8,128)(2...) custom-call(s32[3]{0:T(128)} %pad_add_fusion.info_ref, ...), custom_call_target="tpu_custom_call" | custom-call | flops 189136896 | bytes 1821696 | tf_op jit(solution)/shard_map/pallas_call | solution.py:64
  53.0 5.5 %shard_map.290 = (bf16[208,768]{1,0:T(8,128)(2,1)}, bf16[208,768]{1,0:T(8,128)(2,1)}, bf16[2,208,192]{2,1,0:T(8,128)(2,1)}, bf16[2,3,208,208]{3,2,1,0:T(8,128)(2...) custom-call(s32[3]{0:T(128)} %pad_add_fusion.info_ref, ...), custom_call_target="tpu_custom_call" | custom-call | flops 189136896 | bytes 1821696 | tf_op jit(solution)/shard_map/pallas_call | solution.py:64
  61.7 2.5 constant_dynamic-slice_fusion.3
  64.2 4.4 %collective-permute-done.11.c = bf16[208,768]{1,0:T(8,128)(2,1)S(1)} collective-permute-done((bf16[208,768]{1,0:T(8,128)(2,1)S(1)}, bf16[208,768]{1,0:T(8,128)(2,1)S(1)}, u32[]{:S(2)}, u32[]{:S(2)}) %collective-permute-start.11) | collective-permute-done | bytes 319520 | tf_op jit(solution)/shard_map/ppermute | solution.py:122
  69.4 3.1 %shard_map.292 = (f32[208,768]{1,0:T(8,128)}, bf16[208,768]{1,0:T(8,128)(2,1)}) custom-call(s32[3]{0:T(128)} %pad_add_fusion.info_ref, bf16[208,768]{1,0:T(8,128)(2,1)} %get-tuple-element.102.a, bf16[208,768]{1,0:T(8,128)(2,1)} %copy-done.29, bf16[208,768]{1,0:T(8,128)(2,1)} %copy-done.30, bf16[4,208,768]{2,1,0:T(8,128)(2,1)} %fusion.10.x, ...), custom_call_target="tpu_custom_call" | custom-call | bytes 1299456 | tf_op jit(solution)/shard_map/pallas_call | solution.py:64
  75.0 6.5 %collective-permute-done.13.low_a.l2 = bf16[208,768]{1,0:T(8,128)(2,1)S(1)} collective-permute-done((bf16[208,768]{1,0:T(8,128)(2,1)}, bf16[208,768]{1,0:T(8,128)(2,1)S(1)}, u32[]{:S(2)}, u32[]{:S(2)}) %collective-permute-start.13) | collective-permute-done | bytes 319520 | tf_op jit(solution)/shard_map/ppermute | solution.py:122
  83.8 5.0 %shard_map.293.gh = bf16[4,208,768]{2,1,0:T(8,128)(2,1)} custom-call(s32[3]{0:T(128)} %pad_add_fusion.info_ref, bf16[4,208,768]{2,1,0:T(8,128)(2,1)} %fusion.13.g, bf16[768,768]{1,0:T(8,128)(2,1)} %w.7), custom_call_target="tpu_custom_call" | custom-call | flops 981467136 | bytes 2457600 | tf_op jit(solution)/shard_map/pallas_call | solution.py:64
  89.5 4.7 %shard_map.294 = (bf16[2,208,768]{2,1,0:T(8,128)(2,1)}, bf16[2,208,768]{2,1,0:T(8,128)(2,1)}, bf16[208,768]{1,0:T(8,128)(2,1)}, bf16[208,768]{1,0:T(8,128)(2,1)}) custom-call(s32[3]{0:T(128)} %pad_add_fusion.info_ref, bf16[208,768]{1,0:T(8,128)(2,1)} %get-tuple-element.106.low_a.l0, bf16[208,768]{1,0:T(8,128)(2,1)} %copy-done.71, ...), custom_call_target="tpu_custom_call" | custom-call | flops 981467136 | bytes 2460672 | tf_op jit(solution)/shard_map/pallas_call | solution.py:64
  95.5 5.0 %shard_map.295 = (bf16[2,208,768]{2,1,0:T(8,128)(2,1)}, bf16[2,208,768]{2,1,0:T(8,128)(2,1)}, bf16[208,768]{1,0:T(8,128)(2,1)}, bf16[208,768]{1,0:T(8,128)(2,1)}) custom-call(s32[3]{0:T(128)} %pad_add_fusion.info_ref, bf16[208,768]{1,0:T(8,128)(2,1)} %copy-done.70, bf16[208,768]{1,0:T(8,128)(2,1)} %copy-done.72, bf16[4,208,768]{2,1,0:T(8,128)(2,1)} %shard_map.293.gh, ...), custom_call_target="tpu_custom_call" | custom-call | flops 981467136 | bytes 2460672 | tf_op jit(solution)/shard_map/pallas_call | solution.py:64
  100.5 5.2 %shard_map.301 = (bf16[192,768]{1,0:T(8,128)(2,1)}, bf16[192,768]{1,0:T(8,128)(2,1)}, bf16[96,768]{1,0:T(8,128)(2,1)}, bf16[96,768]{1,0:T(8,128)(2,1)}, bf16[192,768]{1,0:T(8,128)(2,1)}, /*index=5*/f32[1,768]{1,0:T(1,128)}) custom-call(s32[3]{0:T(128)} %pad_add_fusion.info_ref, bf16[2,208,768]{2,1,0:T(8,128)(2,1)} %get-tuple-element.135.pa, ...), custom_call_target="tpu_custom_call" | custom-call | flops 981467136 | bytes 2555904 | tf_op jit(solution)/shard_map/pallas_call | solution.py:64
  108.2 3.1 %collective-permute-start.49 = (bf16[96,768]{1,0:T(8,128)(2,1)}, bf16[96,768]{1,0:T(8,128)(2,1)S(1)}, u32[]{:S(2)}, u32[]{:S(2)}) collective-permute-start(bf16[96,768]{1,0:T(8,128)(2,1)} %get-tuple-element.172), channel_id=1, source_target_pairs={{0,3},{1,0},{2,1},{3,2},{4,7},{5,4},{6,5},{7,6},{8,11},{9,8},{10,9... | collective-permute-start | bytes 442376 | tf_op jit(solution)/shard_map/ppermute | solution.py:137
  111.3 5.2 %shard_map.309 = (bf16[192,768]{1,0:T(8,128)(2,1)}, bf16[192,768]{1,0:T(8,128)(2,1)}, bf16[96,768]{1,0:T(8,128)(2,1)}, bf16[96,768]{1,0:T(8,128)(2,1)}, bf16[192,768]{1,0:T(8,128)(2,1)}) custom-call(s32[3]{0:T(128)} %pad_add_fusion.info_ref, bf16[2,208,768]{2,1,0:T(8,128)(2,1)} %get-tuple-element.107.ha, bf16[2,208,768]{2,1,0:T(8,128)(2,1)} %get-tuple-element.108.hb, ...), custom_call_target="tpu_custom_call" | custom-call | flops 981467136 | bytes 2555904 | tf_op jit(solution)/shard_map/pallas_call | solution.py:64
  118.5 6.8 %shard_map.296 = (bf16[2,2,208,192]{3,2,1,0:T(8,128)(2,1)}, bf16[2,2,208,192]{3,2,1,0:T(8,128)(2,1)}, bf16[2,2,208,192]{3,2,1,0:T(8,128)(2,1)}, bf16[2,2,208,192]{3,2,1,0:T(8,128)(2,1)}) custom-call(s32[3]{0:T(128)} %pad_add_fusion.info_ref, bf16[2,208,768]{2,1,0:T(8,128)(2,1)} %get-tuple-element.107.ha, bf16[2,208,768]{2,1,0:T(8,128)(2,1)} %get-tuple-element.108.hb, ...), custom_call_target="tpu_custom_call" | custom-call | flops 981467136 | bytes 3099648 | tf_op jit(solution)/shard_map/pallas_call | solution.py:64
  125.3 3.9 %collective-permute-start.58 = (bf16[96,768]{1,0:T(8,128)(2,1)S(1)}, bf16[96,768]{1,0:T(8,128)(2,1)S(1)}, u32[]{:S(2)}, u32[]{:S(2)}) collective-permute-start(bf16[96,768]{1,0:T(8,128)(2,1)S(1)} %copy-done.73), channel_id=1, source_target_pairs={{0,3},{1,0},{2,1},{3,2},{4,7},{5,4},{6,5},{7,6},{8,11},{9,8},{10,9... | collective-permute-start | bytes 442376 | tf_op jit(solution)/shard_map/ppermute | solution.py:137
  135.2 6.4 %collective-permute-done.21.c = bf16[208,768]{1,0:T(8,128)(2,1)S(1)} collective-permute-done((bf16[208,768]{1,0:T(8,128)(2,1)S(1)}, bf16[208,768]{1,0:T(8,128)(2,1)S(1)}, u32[]{:S(2)}, u32[]{:S(2)}) %collective-permute-start.21) | collective-permute-done | bytes 319520 | tf_op jit(solution)/shard_map/ppermute | solution.py:122
  141.6 4.3 %collective-permute-start.59 = (bf16[192,768]{1,0:T(8,128)(2,1)S(1)}, bf16[192,768]{1,0:T(8,128)(2,1)S(1)}, u32[]{:S(2)}, u32[]{:S(2)}) collective-permute-start(bf16[192,768]{1,0:T(8,128)(2,1)S(1)} %pad_maximum_fusion.5), channel_id=1, source_target_pairs={{0,3},{1,0},{2,1},{3,2},{4,7},{5,4},{6,5},{7,6},{8,11},{9,8},{10,9... | collective-permute-start | bytes 884744 | tf_op jit(solution)/shard_map/ppermute | solution.py:137
  145.9 3.9 %shard_map.298 = (f32[208,768]{1,0:T(8,128)}, bf16[208,768]{1,0:T(8,128)(2,1)}, f32[8,768]{1,0:T(8,128)}) custom-call(s32[3]{0:T(128)} %pad_add_fusion.info_ref, bf16[208,768]{1,0:T(8,128)(2,1)} %get-tuple-element.114.a, bf16[208,768]{1,0:T(8,128)(2,1)} %copy-done.25, bf16[208,768]{1,0:T(8,128)(2,1)} %copy-done.26, f32[208,768]{1,0:T(8,128)} %get-tuple-element.109.resid, ...), custom_call_target="tpu_custom_call" | custom-call | bytes 1920000 | tf_op jit(solution)/shard_map/pallas_call | solution.py:64
  153.4 3.7 %collective-permute-done.24.ba.b2 = bf16[208,768]{1,0:T(8,128)(2,1)S(1)} collective-permute-done((bf16[208,768]{1,0:T(8,128)(2,1)}, bf16[208,768]{1,0:T(8,128)(2,1)S(1)}, u32[]{:S(2)}, u32[]{:S(2)}) %collective-permute-start.24) | collective-permute-done | bytes 319520 | tf_op jit(solution)/shard_map/ppermute | solution.py:122
  163.7 8.7 %shard_map.299 = (bf16[2,2,208,192]{3,2,1,0:T(8,128)(2,1)}, bf16[2,2,208,192]{3,2,1,0:T(8,128)(2,1)}, bf16[3,2,208,192]{3,2,1,0:T(8,128)(2,1)}, bf16[2,208,768]{2,1,0:T(8,128)(2,1)}, f32[8,768]{1,0:T(8,128)}) custom-call(s32[3]{0:T(128)} %pad_add_fusion.info_ref, bf16[208,768]{1,0:T(8,128)(2,1)} %get-tuple-element.118.ba.b0, bf16[208,768]{1,0:T(8,128)(2,1)} %copy-done.6, ...), custom_call_target="tpu_custom_call" | custom-call | flops 623640576 | bytes 4159488 | tf_op jit(solution)/shard_map/pallas_call | solution.py:64
  173.2 8.5 %shard_map.300 = (bf16[2,2,208,192]{3,2,1,0:T(8,128)(2,1)}, bf16[2,2,208,192]{3,2,1,0:T(8,128)(2,1)}, bf16[3,2,208,192]{3,2,1,0:T(8,128)(2,1)}, bf16[2,208,768]{2,1,0:T(8,128)(2,1)}, f32[8,768]{1,0:T(8,128)}) custom-call(s32[3]{0:T(128)} %pad_add_fusion.info_ref, bf16[208,768]{1,0:T(8,128)(2,1)} %copy-done.5, bf16[208,768]{1,0:T(8,128)(2,1)} %copy-done.7, ...), custom_call_target="tpu_custom_call" | custom-call | flops 623640576 | bytes 4159488 | tf_op jit(solution)/shard_map/pallas_call | solution.py:64
  184.1 3.7 %collective-permute-start.61 = (bf16[192,768]{1,0:T(8,128)(2,1)S(1)}, bf16[192,768]{1,0:T(8,128)(2,1)S(1)}, u32[]{:S(2)}, u32[]{:S(2)}) collective-permute-start(bf16[192,768]{1,0:T(8,128)(2,1)S(1)} %add_convert_fusion.c0), channel_id=1, source_target_pairs={{0,3},{1,0},{2,1},{3,2},{4,7},{5,4},{6,5},{7,6},{8,11},{9,8},{10,9... | collective-permute-start | bytes 884744 | tf_op jit(solution)/shard_map/ppermute | solution.py:137
  191.7 4.0 %collective-permute-done.62.c3 = bf16[192,768]{1,0:T(8,128)(2,1)S(1)} collective-permute-done((bf16[192,768]{1,0:T(8,128)(2,1)S(1)}, bf16[192,768]{1,0:T(8,128)(2,1)S(1)}, u32[]{:S(2)}, u32[]{:S(2)}) %collective-permute-start.62) | collective-permute-done | bytes 294944 | tf_op jit(solution)/shard_map/ppermute | solution.py:134
  195.7 4.1 %collective-permute-done.61.c1 = bf16[192,768]{1,0:T(8,128)(2,1)S(1)} collective-permute-done((bf16[192,768]{1,0:T(8,128)(2,1)S(1)}, bf16[192,768]{1,0:T(8,128)(2,1)S(1)}, u32[]{:S(2)}, u32[]{:S(2)}) %collective-permute-start.61) | collective-permute-done | bytes 294944 | tf_op jit(solution)/shard_map/ppermute | solution.py:137
  199.8 2.4 collective-permute-start.55
  202.2 2.1 collective-permute-start.31
  204.3 5.6 %shard_map.306 = (bf16[192,768]{1,0:T(8,128)(2,1)}, bf16[192,768]{1,0:T(8,128)(2,1)}, bf16[96,768]{1,0:T(8,128)(2,1)}, bf16[96,768]{1,0:T(8,128)(2,1)}, bf16[192,768]{1,0:T(8,128)(2,1)}) custom-call(s32[3]{0:T(128)} %pad_add_fusion.info_ref, bf16[3,2,208,192]{3,2,1,0:T(8,128)(2,1)} %get-tuple-element.152.ga, bf16[3,2,208,192]{3,2,1,0:T(8,128)(2,1)} %get-tuple-element.153.gb, ...), custom_call_target="tpu_custom_call" | custom-call | flops 981467136 | bytes 3833856 | tf_op jit(solution)/shard_map/pallas_call | solution.py:64
  211.9 8.3 %collective-permute-done.38 = bf16[96,768]{1,0:T(8,128)(2,1)S(1)} collective-permute-done((bf16[96,768]{1,0:T(8,128)(2,1)}, bf16[96,768]{1,0:T(8,128)(2,1)S(1)}, u32[]{:S(2)}, u32[]{:S(2)}) %collective-permute-start.38) | collective-permute-done | bytes 147488 | tf_op jit(solution)/shard_map/ppermute | solution.py:134
  221.2 6.5 %collective-permute-done.40 = bf16[96,768]{1,0:T(8,128)(2,1)S(1)} collective-permute-done((bf16[96,768]{1,0:T(8,128)(2,1)}, bf16[96,768]{1,0:T(8,128)(2,1)S(1)}, u32[]{:S(2)}, u32[]{:S(2)}) %collective-permute-start.40) | collective-permute-done | bytes 147488 | tf_op jit(solution)/shard_map/ppermute | solution.py:137
  228.8 3.9 %collective-permute-start.64 = (bf16[96,768]{1,0:T(8,128)(2,1)S(1)}, bf16[96,768]{1,0:T(8,128)(2,1)S(1)}, u32[]{:S(2)}, u32[]{:S(2)}) collective-permute-start(bf16[96,768]{1,0:T(8,128)(2,1)S(1)} %slice.190), channel_id=1, source_target_pairs={{0,3},{1,0},{2,1},{3,2},{4,7},{5,4},{6,5},{7,6},{8,11},{9,8},{10,9... | collective-permute-start | bytes 442376 | tf_op jit(solution)/shard_map/ppermute | solution.py:137
  236.5 2.5 collective-permute-start.32
  240.2 3.0 shard_map.297
  245.2 3.5 %shard_map.310 = f32[768,768]{1,0:T(8,128)} custom-call(s32[3]{0:T(128)} %pad_add_fusion.info_ref, bf16[192,768]{1,0:T(8,128)(2,1)} %copy-done.9, bf16[192,768]{1,0:T(8,128)(2,1)} %copy-done.22, bf16[96,768]{1,0:T(8,128)(2,1)} %copy-done.47, bf16[96,768]{1,0:T(8,128)(2,1)} %copy-done.48, bf16[192,768]{1,0:T(8,128)(2,1)} %copy-done.21), custom_call_target="tpu_custom_call" | custom-call | bytes 1179648 | tf_op jit(solution)/shard_map/pallas_call | solution.py:64
  248.7 3.6 %shard_map.308 = f32[768,768]{1,0:T(8,128)} custom-call(s32[3]{0:T(128)} %pad_add_fusion.info_ref, bf16[192,768]{1,0:T(8,128)(2,1)} %copy-done.8, bf16[192,768]{1,0:T(8,128)(2,1)} %copy-done.20, bf16[96,768]{1,0:T(8,128)(2,1)} %copy-done.45, bf16[96,768]{1,0:T(8,128)(2,1)} %copy-done.46, bf16[192,768]{1,0:T(8,128)(2,1)} %copy-done.19), custom_call_target="tpu_custom_call" | custom-call | bytes 1179648 | tf_op jit(solution)/shard_map/pallas_call | solution.py:64
  253.1 4.4 %shard_map.302 = (f32[32,768]{1,0:T(8,128)}, bf16[3,32,192]{2,1,0:T(8,128)(2,1)}, bf16[48,768]{1,0:T(8,128)(2,1)}) custom-call(s32[3]{0:T(128)} %pad_add_fusion.info_ref, bf16[4,28,768]{2,1,0:T(8,128)(2,1)} %pad_maximum_fusion.6.packs_ref, f32[32,768]{1,0:T(8,128)} %get-tuple-element.100.first, bf16[32,192]{1,0:T(8,128)(2,1)} %get-tuple-element.138.q, ...), custom_call_target="tpu_custom_call" | custom-call | bytes 1502208 | tf_op jit(solution)/shard_map/pallas_call | solution.py:64
  261.3 3.4 %shard_map.303 = (f32[3,192,768]{2,1,0:T(8,128)}, f32[192,768]{1,0:T(8,128)}, f32[2,192]{1,0:T(2,128)}, f32[1,768]{1,0:T(1,128)}) custom-call(s32[3]{0:T(128)} %pad_add_fusion.info_ref, f32[32,768]{1,0:T(8,128)} %get-tuple-element.142.sent, bf16[3,32,192]{2,1,0:T(8,128)(2,1)} %get-tuple-element.144.grads, bf16[32,768]{1,0:T(8,128)(2,1)} %get-tuple-element.145.low, ...), custom_call_target="tpu_custom_call" | custom-call | bytes 196608 | tf_op jit(solution)/shard_map/pallas_call | solution.py:64
  267.7 3.6 %collective-permute-start.43 = (bf16[192,768]{1,0:T(8,128)(2,1)S(1)}, bf16[192,768]{1,0:T(8,128)(2,1)S(1)}, u32[]{:S(2)}, u32[]{:S(2)}) collective-permute-start(bf16[192,768]{1,0:T(8,128)(2,1)S(1)} %add_convert_fusion.4.c0), channel_id=1, source_target_pairs={{0,3},{1,0},{2,1},{3,2},{4,7},{5,4},{6,5},{7,6},{8,11},{9,8},{10,9... | collective-permute-start | bytes 884744 | tf_op jit(solution)/shard_map/ppermute | solution.py:137
  271.3 3.5 %collective-permute-start.37 = (bf16[48,768]{1,0:T(8,128)(2,1)S(1)}, bf16[48,768]{1,0:T(8,128)(2,1)S(1)}, u32[]{:S(2)}, u32[]{:S(2)}) collective-permute-start(bf16[48,768]{1,0:T(8,128)(2,1)S(1)} %add_convert_fusion.12.own), channel_id=1, source_target_pairs={{0,16},{1,17},{2,18},{3,19},{4,20},{5,21},{6,22},{7,23},{8,24},{9,... | collective-permute-start | bytes 221192 | tf_op jit(solution)/shard_map/ppermute | solution.py:128
  277.4 4.0 %shard_map.304 = (f32[192,768]{1,0:T(8,128)}, f32[16,192]{1,0:T(8,128)}, f32[8,768]{1,0:T(8,128)}, f32[2,192]{1,0:T(2,128)}) custom-call(s32[3]{0:T(128)} %pad_add_fusion.info_ref, f32[32,768]{1,0:T(8,128)} %get-tuple-element.142.sent, bf16[48,768]{1,0:T(8,128)(2,1)} %copy-done.38, bf16[48,768]{1,0:T(8,128)(2,1)} %copy-done.53, ...), custom_call_target="tpu_custom_call" | custom-call | bytes 1651200 | tf_op jit(solution)/shard_map/pallas_call | solution.py:64
  282.0 3.8 %collective-permute-start.46 = (bf16[96,768]{1,0:T(8,128)(2,1)S(1)}, bf16[96,768]{1,0:T(8,128)(2,1)S(1)}, u32[]{:S(2)}, u32[]{:S(2)}) collective-permute-start(bf16[96,768]{1,0:T(8,128)(2,1)S(1)} %slice.186), channel_id=1, source_target_pairs={{0,3},{1,0},{2,1},{3,2},{4,7},{5,4},{6,5},{7,6},{8,11},{9,8},{10,9... | collective-permute-start | bytes 442376 | tf_op jit(solution)/shard_map/ppermute | solution.py:137
  285.8 2.4 fusion.21
  288.9 3.0 %shard_map.305 = bf16[4,197,192]{2,1,0:T(8,128)(2,1)} custom-call(s32[3]{0:T(128)} %pad_add_fusion.info_ref, bf16[2,2,208,192]{3,2,1,0:T(8,128)(2,1)} %get-tuple-element.124.refs_0_, bf16[2,2,208,192]{3,2,1,0:T(8,128)(2,1)} %copy-done.17, bf16[2,208,192]{2,1,0:T(8,128)(2,1)} %copy-done.44, bf16[2,2,208,192]{3,2,1,0:T(8,128)(2,1)} %get-tuple-element.130.refs_3_, ...), custom_call_target="tpu_custom_call" | custom-call | bytes 970752 | tf_op jit(solution)/shard_map/pallas_call | solution.py:64
  294.6 4.2 %shard_map.307 = (f32[3,192,768]{2,1,0:T(8,128)}, f32[192,768]{1,0:T(8,128)}) custom-call(s32[3]{0:T(128)} %pad_add_fusion.info_ref, bf16[192,768]{1,0:T(8,128)(2,1)} %copy-done.10, bf16[192,768]{1,0:T(8,128)(2,1)} %copy-done.24, bf16[96,768]{1,0:T(8,128)(2,1)} %copy-done.49, bf16[96,768]{1,0:T(8,128)(2,1)} %copy-done.50, bf16[192,768]{1,0:T(8,128)(2,1)} %copy-done.23, ...), custom_call_target="tpu_custom_call" | custom-call | bytes 3538944 | tf_op jit(solution)/shard_map/pallas_call | solution.py:64
  (337 shorter events, 83.1 us)
Async XLA Ops:
  1.4 20.6 %collective-permute-start.4 = (bf16[8,768]{1,0:T(8,128)(2,1)S(1)}, bf16[8,768]{1,0:T(8,128)(2,1)S(1)}, u32[]{:S(2)}, u32[]{:S(2)}) collective-permute-start(bf16[8,768]{1,0:T(8,128)(2,1)S(1)} %get-tuple-element.220), channel_id=1, source_target_pairs={{0,1},{1,2},{2,3},{3,0},{4,5},{5,6},{6,7},{7,4},{8,9},{9,10},{10,1... | collective-permute-start | bytes 36872 | tf_op jit(solution)/shard_map/ppermute | solution.py:134
  4.4 18.8 %collective-permute-start.3 = (bf16[8,768]{1,0:T(8,128)(2,1)S(1)}, bf16[8,768]{1,0:T(8,128)(2,1)S(1)}, u32[]{:S(2)}, u32[]{:S(2)}) collective-permute-start(bf16[8,768]{1,0:T(8,128)(2,1)S(1)} %get-tuple-element.220), channel_id=1, source_target_pairs={{0,2},{1,3},{2,0},{3,1},{4,6},{5,7},{6,4},{7,5},{8,10},{9,11},{10,... | collective-permute-start | bytes 36872 | tf_op jit(solution)/shard_map/ppermute | solution.py:134
  7.0 16.2 %collective-permute-start.2 = (bf16[8,768]{1,0:T(8,128)(2,1)S(1)}, bf16[8,768]{1,0:T(8,128)(2,1)S(1)}, u32[]{:S(2)}, u32[]{:S(2)}) collective-permute-start(bf16[8,768]{1,0:T(8,128)(2,1)S(1)} %get-tuple-element.220), channel_id=1, source_target_pairs={{0,3},{1,0},{2,1},{3,2},{4,7},{5,4},{6,5},{7,6},{8,11},{9,8},{10,9... | collective-permute-start | bytes 36872 | tf_op jit(solution)/shard_map/ppermute | solution.py:137
  9.1 22.7 %collective-permute-start.1 = (f32[5,768]{1,0:T(8,128)S(1)}, f32[5,768]{1,0:T(8,128)S(1)}, u32[]{:S(2)}, u32[]{:S(2)}) collective-permute-start(f32[5,768]{1,0:T(8,128)S(1)} %select_maximum_fusion), channel_id=1, source_target_pairs={{16,0},{17,1},{18,2},{19,3},{20,4},{21,5},{22,6},{23,7},{24,8},{25... | collective-permute-start | bytes 46088 | tf_op jit(solution)/shard_map/ppermute | solution.py:131
  10.4 30.9 %collective-permute-start = (bf16[3,192,768]{2,1,0:T(8,128)(2,1)}, bf16[3,192,768]{2,1,0:T(8,128)(2,1)S(1)}, u32[]{:S(2)}, u32[]{:S(2)}) collective-permute-start(bf16[3,192,768]{2,1,0:T(8,128)(2,1)} %bitcast.58), channel_id=1, source_target_pairs={{16,0},{17,1},{18,2},{19,3},{20,4},{21,5},{22,6},{23,7},{24,8},{25... | collective-permute-start | bytes 2654216 | tf_op jit(solution)/shard_map/ppermute | solution.py:131
  21.9 17.7 %collective-permute-start.8 = (bf16[192,768]{1,0:T(8,128)(2,1)}, bf16[192,768]{1,0:T(8,128)(2,1)S(1)}, u32[]{:S(2)}, u32[]{:S(2)}) collective-permute-start(bf16[192,768]{1,0:T(8,128)(2,1)} %bitcast.17.wo), channel_id=1, source_target_pairs={{16,0},{17,1},{18,2},{19,3},{20,4},{21,5},{22,6},{23,7},{24,8},{25... | collective-permute-start | bytes 884744 | tf_op jit(solution)/shard_map/ppermute | solution.py:131
  34.2 12.8 %collective-permute-start.7 = (f32[8,768]{1,0:T(8,128)S(1)}, f32[8,768]{1,0:T(8,128)S(1)}, u32[]{:S(2)}, u32[]{:S(2)}) collective-permute-start(f32[8,768]{1,0:T(8,128)S(1)} %add.187.part), channel_id=1, source_target_pairs={{0,16},{1,17},{2,18},{3,19},{4,20},{5,21},{6,22},{7,23},{8,24},{9,... | collective-permute-start | bytes 73736 | tf_op jit(solution)/shard_map/ppermute | solution.py:128
  59.0 9.7 %collective-permute-start.11 = (bf16[208,768]{1,0:T(8,128)(2,1)S(1)}, bf16[208,768]{1,0:T(8,128)(2,1)S(1)}, u32[]{:S(2)}, u32[]{:S(2)}) collective-permute-start(bf16[208,768]{1,0:T(8,128)(2,1)S(1)} %add.188), channel_id=1, source_target_pairs={{0,8},{4,12},{8,0},{12,4},{1,9},{5,13},{9,1},{13,5},{2,10},{6,14},... | collective-permute-start | bytes 958472 | tf_op jit(solution)/shard_map/ppermute | solution.py:122
  72.5 9.0 %collective-permute-start.13 = (bf16[208,768]{1,0:T(8,128)(2,1)}, bf16[208,768]{1,0:T(8,128)(2,1)S(1)}, u32[]{:S(2)}, u32[]{:S(2)}) collective-permute-start(bf16[208,768]{1,0:T(8,128)(2,1)} %get-tuple-element.106.low_a.l0), channel_id=1, source_target_pairs={{0,8},{4,12},{8,0},{12,4},{1,9},{5,13},{9,1},{13,5},{2,10},{6,14},... | collective-permute-start | bytes 958472 | tf_op jit(solution)/shard_map/ppermute | solution.py:122
  75.0 13.8 %collective-permute-start.12 = (bf16[208,768]{1,0:T(8,128)(2,1)S(1)}, bf16[208,768]{1,0:T(8,128)(2,1)S(1)}, u32[]{:S(2)}, u32[]{:S(2)}) collective-permute-start(bf16[208,768]{1,0:T(8,128)(2,1)S(1)} %copy-done.69), channel_id=1, source_target_pairs={{0,4},{4,0},{8,12},{12,8},{1,5},{5,1},{9,13},{13,9},{2,6},{6,2},{1... | collective-permute-start | bytes 958472 | tf_op jit(solution)/shard_map/ppermute | solution.py:119
  81.5 13.2 %collective-permute-start.14 = (bf16[208,768]{1,0:T(8,128)(2,1)S(1)}, bf16[208,768]{1,0:T(8,128)(2,1)S(1)}, u32[]{:S(2)}, u32[]{:S(2)}) collective-permute-start(bf16[208,768]{1,0:T(8,128)(2,1)S(1)} %collective-permute-done.13.low_a.l2), channel_id=1, source_target_pairs={{0,4},{4,0},{8,12},{12,8},{1,5},{5,1},{9,13},{13,9},{2,6},{6,2},{1... | collective-permute-start | bytes 958472 | tf_op jit(solution)/shard_map/ppermute | solution.py:119
  94.2 40.9 %collective-permute-start.19 = (bf16[208,768]{1,0:T(8,128)(2,1)}, bf16[208,768]{1,0:T(8,128)(2,1)S(1)}, u32[]{:S(2)}, u32[]{:S(2)}) collective-permute-start(bf16[208,768]{1,0:T(8,128)(2,1)} %get-tuple-element.115), channel_id=1, source_target_pairs={{0,4},{4,0},{8,12},{12,8},{1,5},{5,1},{9,13},{13,9},{2,6},{6,2},{1... | collective-permute-start | bytes 958472 | tf_op jit(solution)/shard_map/ppermute | solution.py:119
  107.5 17.9 %collective-permute-start.47 = (bf16[96,768]{1,0:T(8,128)(2,1)}, bf16[96,768]{1,0:T(8,128)(2,1)S(1)}, u32[]{:S(2)}, u32[]{:S(2)}) collective-permute-start(bf16[96,768]{1,0:T(8,128)(2,1)} %get-tuple-element.170), channel_id=1, source_target_pairs={{0,1},{1,2},{2,3},{3,0},{4,5},{5,6},{6,7},{7,4},{8,9},{9,10},{10,1... | collective-permute-start | bytes 442376 | tf_op jit(solution)/shard_map/ppermute | solution.py:134
  108.2 21.1 %collective-permute-start.49 = (bf16[96,768]{1,0:T(8,128)(2,1)}, bf16[96,768]{1,0:T(8,128)(2,1)S(1)}, u32[]{:S(2)}, u32[]{:S(2)}) collective-permute-start(bf16[96,768]{1,0:T(8,128)(2,1)} %get-tuple-element.172), channel_id=1, source_target_pairs={{0,3},{1,0},{2,1},{3,2},{4,7},{5,4},{6,5},{7,6},{8,11},{9,8},{10,9... | collective-permute-start | bytes 442376 | tf_op jit(solution)/shard_map/ppermute | solution.py:137
  111.3 18.4 %collective-permute-start.20 = (bf16[208,768]{1,0:T(8,128)(2,1)S(1)}, bf16[208,768]{1,0:T(8,128)(2,1)S(1)}, u32[]{:S(2)}, u32[]{:S(2)}) collective-permute-start(bf16[208,768]{1,0:T(8,128)(2,1)S(1)} %copy-done.68), channel_id=1, source_target_pairs={{0,4},{4,0},{8,12},{12,8},{1,5},{5,1},{9,13},{13,9},{2,6},{6,2},{1... | collective-permute-start | bytes 958472 | tf_op jit(solution)/shard_map/ppermute | solution.py:119
  118.4 11.0 %collective-permute-start.56 = (bf16[96,768]{1,0:T(8,128)(2,1)}, bf16[96,768]{1,0:T(8,128)(2,1)S(1)}, u32[]{:S(2)}, u32[]{:S(2)}) collective-permute-start(bf16[96,768]{1,0:T(8,128)(2,1)} %get-tuple-element.175), channel_id=1, source_target_pairs={{0,1},{1,2},{2,3},{3,0},{4,5},{5,6},{6,7},{7,4},{8,9},{9,10},{10,1... | collective-permute-start | bytes 442376 | tf_op jit(solution)/shard_map/ppermute | solution.py:134
  129.3 22.3 %collective-permute-start.15 = (bf16[2,2,208,192]{3,2,1,0:T(8,128)(2,1)}, bf16[2,2,208,192]{3,2,1,0:T(8,128)(2,1)S(1)}, u32[]{:S(2)}, u32[]{:S(2)}) collective-permute-start(bf16[2,2,208,192]{3,2,1,0:T(8,128)(2,1)} %get-tuple-element.111), channel_id=1, source_target_pairs={{0,4},{4,0},{8,12},{12,8},{1,5},{5,1},{9,13},{13,9},{2,6},{6,2},{1... | collective-permute-start | bytes 958472 | tf_op jit(solution)/shard_map/ppermute | solution.py:119
  129.4 20.4 %collective-permute-start.50 = (bf16[192,768]{1,0:T(8,128)(2,1)S(1)}, bf16[192,768]{1,0:T(8,128)(2,1)S(1)}, u32[]{:S(2)}, u32[]{:S(2)}) collective-permute-start(bf16[192,768]{1,0:T(8,128)(2,1)S(1)} %pad_maximum_fusion.3), channel_id=1, source_target_pairs={{0,3},{1,0},{2,1},{3,2},{4,7},{5,4},{6,5},{7,6},{8,11},{9,8},{10,9... | collective-permute-start | bytes 884744 | tf_op jit(solution)/shard_map/ppermute | solution.py:137
  129.8 20.1 %collective-permute-start.48 = (bf16[192,768]{1,0:T(8,128)(2,1)S(1)}, bf16[192,768]{1,0:T(8,128)(2,1)S(1)}, u32[]{:S(2)}, u32[]{:S(2)}) collective-permute-start(bf16[192,768]{1,0:T(8,128)(2,1)S(1)} %pad_maximum_fusion.2), channel_id=1, source_target_pairs={{0,1},{1,2},{2,3},{3,0},{4,5},{5,6},{6,7},{7,4},{8,9},{9,10},{10,1... | collective-permute-start | bytes 884744 | tf_op jit(solution)/shard_map/ppermute | solution.py:134
  135.1 52.8 %collective-permute-start.16 = (bf16[2,2,208,192]{3,2,1,0:T(8,128)(2,1)}, bf16[2,2,208,192]{3,2,1,0:T(8,128)(2,1)S(1)}, u32[]{:S(2)}, u32[]{:S(2)}) collective-permute-start(bf16[2,2,208,192]{3,2,1,0:T(8,128)(2,1)} %get-tuple-element.113), channel_id=1, source_target_pairs={{0,4},{4,0},{8,12},{12,8},{1,5},{5,1},{9,13},{13,9},{2,6},{6,2},{1... | collective-permute-start | bytes 958472 | tf_op jit(solution)/shard_map/ppermute | solution.py:119
  141.6 11.8 %collective-permute-start.59 = (bf16[192,768]{1,0:T(8,128)(2,1)S(1)}, bf16[192,768]{1,0:T(8,128)(2,1)S(1)}, u32[]{:S(2)}, u32[]{:S(2)}) collective-permute-start(bf16[192,768]{1,0:T(8,128)(2,1)S(1)} %pad_maximum_fusion.5), channel_id=1, source_target_pairs={{0,3},{1,0},{2,1},{3,2},{4,7},{5,4},{6,5},{7,6},{8,11},{9,8},{10,9... | collective-permute-start | bytes 884744 | tf_op jit(solution)/shard_map/ppermute | solution.py:137
  149.8 9.0 %collective-permute-start.57 = (bf16[192,768]{1,0:T(8,128)(2,1)S(1)}, bf16[192,768]{1,0:T(8,128)(2,1)S(1)}, u32[]{:S(2)}, u32[]{:S(2)}) collective-permute-start(bf16[192,768]{1,0:T(8,128)(2,1)S(1)} %pad_maximum_fusion.4), channel_id=1, source_target_pairs={{0,1},{1,2},{2,3},{3,0},{4,5},{5,6},{6,7},{7,4},{8,9},{9,10},{10,1... | collective-permute-start | bytes 884744 | tf_op jit(solution)/shard_map/ppermute | solution.py:134
  157.1 15.3 %collective-permute-start.25 = (bf16[208,768]{1,0:T(8,128)(2,1)S(1)}, bf16[208,768]{1,0:T(8,128)(2,1)S(1)}, u32[]{:S(2)}, u32[]{:S(2)}) collective-permute-start(bf16[208,768]{1,0:T(8,128)(2,1)S(1)} %collective-permute-done.24.ba.b2), channel_id=1, source_target_pairs={{0,4},{4,0},{8,12},{12,8},{1,5},{5,1},{9,13},{13,9},{2,6},{6,2},{1... | collective-permute-start | bytes 958472 | tf_op jit(solution)/shard_map/ppermute | solution.py:119
  158.9 24.0 %collective-permute-start.60 = (bf16[192,768]{1,0:T(8,128)(2,1)S(1)}, bf16[192,768]{1,0:T(8,128)(2,1)}, u32[]{:S(2)}, u32[]{:S(2)}) collective-permute-start(bf16[192,768]{1,0:T(8,128)(2,1)S(1)} %add_convert_fusion.1), channel_id=1, source_target_pairs={{0,16},{16,0},{1,17},{17,1},{2,18},{18,2},{3,19},{19,3},{4,20},{20... | collective-permute-start | bytes 884744 | tf_op jit(solution)/shard_map/ppermute | solution.py:125
  159.8 29.7 %collective-permute-start.53 = (bf16[192,768]{1,0:T(8,128)(2,1)S(1)}, bf16[192,768]{1,0:T(8,128)(2,1)S(1)}, u32[]{:S(2)}, u32[]{:S(2)}) collective-permute-start(bf16[192,768]{1,0:T(8,128)(2,1)S(1)} %add_convert_fusion.2.c0), channel_id=1, source_target_pairs={{0,1},{1,2},{2,3},{3,0},{4,5},{5,6},{6,7},{7,4},{8,9},{9,10},{10,1... | collective-permute-start | bytes 884744 | tf_op jit(solution)/shard_map/ppermute | solution.py:134
  161.7 28.4 %collective-permute-start.52 = (bf16[192,768]{1,0:T(8,128)(2,1)S(1)}, bf16[192,768]{1,0:T(8,128)(2,1)S(1)}, u32[]{:S(2)}, u32[]{:S(2)}) collective-permute-start(bf16[192,768]{1,0:T(8,128)(2,1)S(1)} %add_convert_fusion.2.c0), channel_id=1, source_target_pairs={{0,3},{1,0},{2,1},{3,2},{4,7},{5,4},{6,5},{7,6},{8,11},{9,8},{10,9... | collective-permute-start | bytes 884744 | tf_op jit(solution)/shard_map/ppermute | solution.py:137
  184.0 11.7 %collective-permute-start.62 = (bf16[192,768]{1,0:T(8,128)(2,1)S(1)}, bf16[192,768]{1,0:T(8,128)(2,1)S(1)}, u32[]{:S(2)}, u32[]{:S(2)}) collective-permute-start(bf16[192,768]{1,0:T(8,128)(2,1)S(1)} %add_convert_fusion.c0), channel_id=1, source_target_pairs={{0,1},{1,2},{2,3},{3,0},{4,5},{5,6},{6,7},{7,4},{8,9},{9,10},{10,1... | collective-permute-start | bytes 884744 | tf_op jit(solution)/shard_map/ppermute | solution.py:134
  184.1 15.7 %collective-permute-start.61 = (bf16[192,768]{1,0:T(8,128)(2,1)S(1)}, bf16[192,768]{1,0:T(8,128)(2,1)S(1)}, u32[]{:S(2)}, u32[]{:S(2)}) collective-permute-start(bf16[192,768]{1,0:T(8,128)(2,1)S(1)} %add_convert_fusion.c0), channel_id=1, source_target_pairs={{0,3},{1,0},{2,1},{3,2},{4,7},{5,4},{6,5},{7,6},{8,11},{9,8},{10,9... | collective-permute-start | bytes 884744 | tf_op jit(solution)/shard_map/ppermute | solution.py:137
  187.9 14.3 %collective-permute-start.30 = (bf16[24,768]{1,0:T(8,128)(2,1)S(1)}, bf16[24,768]{1,0:T(8,128)(2,1)S(1)}, u32[]{:S(2)}, u32[]{:S(2)}) collective-permute-start(bf16[24,768]{1,0:T(8,128)(2,1)S(1)} %add_convert_fusion.16), channel_id=1, source_target_pairs={{0,8},{4,12},{8,0},{12,4},{1,9},{5,13},{9,1},{13,5},{2,10},{6,14},... | collective-permute-start | bytes 110600 | tf_op jit(solution)/shard_map/ppermute | solution.py:122
  189.5 39.2 %collective-permute-start.18 = (bf16[2,208,192]{2,1,0:T(8,128)(2,1)S(1)}, bf16[2,208,192]{2,1,0:T(8,128)(2,1)S(1)}, u32[]{:S(2)}, u32[]{:S(2)}) collective-permute-start(bf16[2,208,192]{2,1,0:T(8,128)(2,1)S(1)} %copy-done.40), channel_id=1, source_target_pairs={{0,8},{4,12},{8,0},{12,4},{1,9},{5,13},{9,1},{13,5},{2,10},{6,14},... | collective-permute-start | bytes 479240 | tf_op jit(solution)/shard_map/ppermute | solution.py:122
  190.1 42.5 %collective-permute-start.17 = (bf16[2,208,192]{2,1,0:T(8,128)(2,1)S(1)}, bf16[2,208,192]{2,1,0:T(8,128)(2,1)S(1)}, u32[]{:S(2)}, u32[]{:S(2)}) collective-permute-start(bf16[2,208,192]{2,1,0:T(8,128)(2,1)S(1)} %fusion.17), channel_id=1, source_target_pairs={{0,8},{4,12},{8,0},{12,4},{1,9},{5,13},{9,1},{13,5},{2,10},{6,14},... | collective-permute-start | bytes 479240 | tf_op jit(solution)/shard_map/ppermute | solution.py:122
  195.7 37.0 %collective-permute-start.54 = (bf16[96,768]{1,0:T(8,128)(2,1)S(1)}, bf16[96,768]{1,0:T(8,128)(2,1)S(1)}, u32[]{:S(2)}, u32[]{:S(2)}) collective-permute-start(bf16[96,768]{1,0:T(8,128)(2,1)S(1)} %slice.187), channel_id=1, source_target_pairs={{0,1},{1,2},{2,3},{3,0},{4,5},{5,6},{6,7},{7,4},{8,9},{9,10},{10,1... | collective-permute-start | bytes 442376 | tf_op jit(solution)/shard_map/ppermute | solution.py:134
  199.8 34.9 %collective-permute-start.55 = (bf16[96,768]{1,0:T(8,128)(2,1)S(1)}, bf16[96,768]{1,0:T(8,128)(2,1)S(1)}, u32[]{:S(2)}, u32[]{:S(2)}) collective-permute-start(bf16[96,768]{1,0:T(8,128)(2,1)S(1)} %slice.188), channel_id=1, source_target_pairs={{0,3},{1,0},{2,1},{3,2},{4,7},{5,4},{6,5},{7,6},{8,11},{9,8},{10,9... | collective-permute-start | bytes 442376 | tf_op jit(solution)/shard_map/ppermute | solution.py:137
  202.2 9.6 %collective-permute-start.31 = (bf16[24,768]{1,0:T(8,128)(2,1)S(1)}, bf16[24,768]{1,0:T(8,128)(2,1)S(1)}, u32[]{:S(2)}, u32[]{:S(2)}) collective-permute-start(bf16[24,768]{1,0:T(8,128)(2,1)S(1)} %add_convert_fusion.15), channel_id=1, source_target_pairs={{0,16},{16,0},{1,17},{17,1},{2,18},{18,2},{3,19},{19,3},{4,20},{20... | collective-permute-start | bytes 110600 | tf_op jit(solution)/shard_map/ppermute | solution.py:125
  228.8 10.5 %collective-permute-start.64 = (bf16[96,768]{1,0:T(8,128)(2,1)S(1)}, bf16[96,768]{1,0:T(8,128)(2,1)S(1)}, u32[]{:S(2)}, u32[]{:S(2)}) collective-permute-start(bf16[96,768]{1,0:T(8,128)(2,1)S(1)} %slice.190), channel_id=1, source_target_pairs={{0,3},{1,0},{2,1},{3,2},{4,7},{5,4},{6,5},{7,6},{8,11},{9,8},{10,9... | collective-permute-start | bytes 442376 | tf_op jit(solution)/shard_map/ppermute | solution.py:137
  232.6 25.4 %collective-permute-start.41 = (bf16[192,768]{1,0:T(8,128)(2,1)S(1)}, bf16[192,768]{1,0:T(8,128)(2,1)S(1)}, u32[]{:S(2)}, u32[]{:S(2)}) collective-permute-start(bf16[192,768]{1,0:T(8,128)(2,1)S(1)} %pad_maximum_fusion.1), channel_id=1, source_target_pairs={{0,3},{1,0},{2,1},{3,2},{4,7},{5,4},{6,5},{7,6},{8,11},{9,8},{10,9... | collective-permute-start | bytes 884744 | tf_op jit(solution)/shard_map/ppermute | solution.py:137
  232.7 25.3 %collective-permute-start.39 = (bf16[192,768]{1,0:T(8,128)(2,1)S(1)}, bf16[192,768]{1,0:T(8,128)(2,1)S(1)}, u32[]{:S(2)}, u32[]{:S(2)}) collective-permute-start(bf16[192,768]{1,0:T(8,128)(2,1)S(1)} %pad_maximum_fusion), channel_id=1, source_target_pairs={{0,1},{1,2},{2,3},{3,0},{4,5},{5,6},{6,7},{7,4},{8,9},{9,10},{10,1... | collective-permute-start | bytes 884744 | tf_op jit(solution)/shard_map/ppermute | solution.py:134
  234.7 17.5 %collective-permute-start.33 = (bf16[28,768]{1,0:T(8,128)(2,1)S(1)}, bf16[28,768]{1,0:T(8,128)(2,1)S(1)}, u32[]{:S(2)}, u32[]{:S(2)}) collective-permute-start(bf16[28,768]{1,0:T(8,128)(2,1)S(1)} %get-tuple-element.228), channel_id=1, source_target_pairs={{0,2},{1,3},{2,0},{3,1},{4,6},{5,7},{6,4},{7,5},{8,10},{9,11},{10,... | collective-permute-start | bytes 129032 | tf_op jit(solution)/shard_map/ppermute | solution.py:134
  236.5 15.9 %collective-permute-start.32 = (bf16[28,768]{1,0:T(8,128)(2,1)S(1)}, bf16[28,768]{1,0:T(8,128)(2,1)S(1)}, u32[]{:S(2)}, u32[]{:S(2)}) collective-permute-start(bf16[28,768]{1,0:T(8,128)(2,1)S(1)} %get-tuple-element.228), channel_id=1, source_target_pairs={{0,3},{1,0},{2,1},{3,2},{4,7},{5,4},{6,5},{7,6},{8,11},{9,8},{10,9... | collective-permute-start | bytes 129032 | tf_op jit(solution)/shard_map/ppermute | solution.py:137
  239.3 13.1 %collective-permute-start.34 = (bf16[28,768]{1,0:T(8,128)(2,1)S(1)}, bf16[28,768]{1,0:T(8,128)(2,1)S(1)}, u32[]{:S(2)}, u32[]{:S(2)}) collective-permute-start(bf16[28,768]{1,0:T(8,128)(2,1)S(1)} %get-tuple-element.228), channel_id=1, source_target_pairs={{0,1},{1,2},{2,3},{3,0},{4,5},{5,6},{6,7},{7,4},{8,9},{9,10},{10,1... | collective-permute-start | bytes 129032 | tf_op jit(solution)/shard_map/ppermute | solution.py:134
  258.1 9.0 %collective-permute-start.42 = (bf16[192,768]{1,0:T(8,128)(2,1)S(1)}, bf16[192,768]{1,0:T(8,128)(2,1)S(1)}, u32[]{:S(2)}, u32[]{:S(2)}) collective-permute-start(bf16[192,768]{1,0:T(8,128)(2,1)S(1)} %add_convert_fusion.5), channel_id=1, source_target_pairs={{0,16},{16,0},{1,17},{17,1},{2,18},{18,2},{3,19},{19,3},{4,20},{20... | collective-permute-start | bytes 884744 | tf_op jit(solution)/shard_map/ppermute | solution.py:125
  259.8 28.4 %collective-permute-start.28 = (bf16[2,208,192]{2,1,0:T(8,128)(2,1)S(1)}, bf16[2,208,192]{2,1,0:T(8,128)(2,1)S(1)}, u32[]{:S(2)}, u32[]{:S(2)}) collective-permute-start(bf16[2,208,192]{2,1,0:T(8,128)(2,1)S(1)} %fusion.14), channel_id=1, source_target_pairs={{0,8},{4,12},{8,0},{12,4},{1,9},{5,13},{9,1},{13,5},{2,10},{6,14},... | collective-permute-start | bytes 479240 | tf_op jit(solution)/shard_map/ppermute | solution.py:122
  261.3 13.5 %collective-permute-start.26 = (bf16[2,2,208,192]{3,2,1,0:T(8,128)(2,1)S(1)}, bf16[2,2,208,192]{3,2,1,0:T(8,128)(2,1)S(1)}, u32[]{:S(2)}, u32[]{:S(2)}) collective-permute-start(bf16[2,2,208,192]{3,2,1,0:T(8,128)(2,1)S(1)} %copy-done.66), channel_id=1, source_target_pairs={{0,4},{4,0},{8,12},{12,8},{1,5},{5,1},{9,13},{13,9},{2,6},{6,2},{1... | collective-permute-start | bytes 958472 | tf_op jit(solution)/shard_map/ppermute | solution.py:119
  267.2 14.2 %collective-permute-start.44 = (bf16[192,768]{1,0:T(8,128)(2,1)S(1)}, bf16[192,768]{1,0:T(8,128)(2,1)S(1)}, u32[]{:S(2)}, u32[]{:S(2)}) collective-permute-start(bf16[192,768]{1,0:T(8,128)(2,1)S(1)} %add_convert_fusion.4.c0), channel_id=1, source_target_pairs={{0,1},{1,2},{2,3},{3,0},{4,5},{5,6},{6,7},{7,4},{8,9},{9,10},{10,1... | collective-permute-start | bytes 884744 | tf_op jit(solution)/shard_map/ppermute | solution.py:134
  267.7 14.3 %collective-permute-start.43 = (bf16[192,768]{1,0:T(8,128)(2,1)S(1)}, bf16[192,768]{1,0:T(8,128)(2,1)S(1)}, u32[]{:S(2)}, u32[]{:S(2)}) collective-permute-start(bf16[192,768]{1,0:T(8,128)(2,1)S(1)} %add_convert_fusion.4.c0), channel_id=1, source_target_pairs={{0,3},{1,0},{2,1},{3,2},{4,7},{5,4},{6,5},{7,6},{8,11},{9,8},{10,9... | collective-permute-start | bytes 884744 | tf_op jit(solution)/shard_map/ppermute | solution.py:137
  274.9 13.3 %collective-permute-start.27 = (bf16[2,208,192]{2,1,0:T(8,128)(2,1)S(1)}, bf16[2,208,192]{2,1,0:T(8,128)(2,1)S(1)}, u32[]{:S(2)}, u32[]{:S(2)}) collective-permute-start(bf16[2,208,192]{2,1,0:T(8,128)(2,1)S(1)} %fusion.15), channel_id=1, source_target_pairs={{0,8},{4,12},{8,0},{12,4},{1,9},{5,13},{9,1},{13,5},{2,10},{6,14},... | collective-permute-start | bytes 479240 | tf_op jit(solution)/shard_map/ppermute | solution.py:122
  281.5 12.4 %collective-permute-start.45 = (bf16[96,768]{1,0:T(8,128)(2,1)S(1)}, bf16[96,768]{1,0:T(8,128)(2,1)S(1)}, u32[]{:S(2)}, u32[]{:S(2)}) collective-permute-start(bf16[96,768]{1,0:T(8,128)(2,1)S(1)} %slice.185), channel_id=1, source_target_pairs={{0,1},{1,2},{2,3},{3,0},{4,5},{5,6},{6,7},{7,4},{8,9},{9,10},{10,1... | collective-permute-start | bytes 442376 | tf_op jit(solution)/shard_map/ppermute | solution.py:134
  282.0 11.9 %collective-permute-start.46 = (bf16[96,768]{1,0:T(8,128)(2,1)S(1)}, bf16[96,768]{1,0:T(8,128)(2,1)S(1)}, u32[]{:S(2)}, u32[]{:S(2)}) collective-permute-start(bf16[96,768]{1,0:T(8,128)(2,1)S(1)} %slice.186), channel_id=1, source_target_pairs={{0,3},{1,0},{2,1},{3,2},{4,7},{5,4},{6,5},{7,6},{8,11},{9,8},{10,9... | collective-permute-start | bytes 442376 | tf_op jit(solution)/shard_map/ppermute | solution.py:137
  (91 other events, 762.6 us)

commit v2 on v1

v2 whole, which is shorter than its diff:
```python
import functools

import jax
import jax.numpy as jnp
from jax import lax
from jax.experimental import pallas as pl
from jax.experimental.pallas import tpu as pltpu
from jax.sharding import PartitionSpec as P

HEAD_DIM = 64
EPSILON = 1e-05
QUICK_GELU = 1.702
F32 = jnp.float32
BF16 = jnp.bfloat16
VMEM_BYTES = 16 * 1024 * 1024


def nn(left, right):
    return lax.dot_general(left, right, (((1,), (0,)), ((), ())), preferred_element_type=F32)


def nt(left, right):
    return lax.dot_general(left, right, (((1,), (1,)), ((), ())), preferred_element_type=F32)


def tn(left, right):
    return lax.dot_general(left, right, (((0,), (0,)), ((), ())), preferred_element_type=F32)


def norm_parts(values_in):
    centred = values_in - jnp.mean(values_in, axis=-1, keepdims=True)
    inverse = lax.rsqrt(jnp.mean(centred * centred, axis=-1, keepdims=True) + EPSILON)
    return centred * inverse, inverse


def norm_back(incoming, normed, inverse, gain):
    weighted = incoming * gain
    centred = weighted - jnp.mean(weighted, axis=-1, keepdims=True)
    return inverse * (centred - normed * jnp.mean(weighted * normed, axis=-1, keepdims=True))


def row_sum(values_in):
    return jnp.sum(values_in, axis=0, keepdims=True)


def shape_of(shape, kind):
    return jax.ShapeDtypeStruct(shape, kind)


def near(shape, kind):
    return pltpu.VMEM(shape, kind)


class Chain:
    def __init__(self):
        self.token = None
        self.near, self.kept = set(), []

    def __call__(self, kernel, ins, outs, scratch=(), flops=0, scalars=()):
        lead, tokens = len(scalars), 0 if self.token is None else 1
        count, given = len(ins), len(outs)

        def stage(*refs):
            rest = refs[lead + tokens :]
            kernel(*refs[:lead], *rest[:count], *rest[count : count + given], *rest[count + given + 1 :])

        vmem = pl.BlockSpec(memory_space=pltpu.VMEM)
        moved = sum(a.size * a.dtype.itemsize for a in ins)
        held = [] if self.token is None else [self.token]
        ins = [
            pltpu.with_memory_space_constraint(a, pltpu.VMEM) if id(a) in self.near else a for a in ins
        ]
        results = pl.pallas_call(
            stage,
            out_shape=[*outs, near((8, 128), F32)],
            in_specs=[pl.BlockSpec(memory_space=pltpu.SMEM)] * lead
            + [pl.BlockSpec(memory_space=pl.ANY)] * tokens
            + [vmem] * count,
            out_specs=[vmem] * (given + 1),
            scratch_shapes=list(scratch),
            compiler_params=pltpu.CompilerParams(vmem_limit_bytes=VMEM_BYTES),
            cost_estimate=pl.CostEstimate(flops=flops, bytes_accessed=moved, transcendentals=0),
        )(*scalars, *held, *ins)
        self.token = results[-1]
        self.kept += results
        for out, result in zip(outs, results):
            if not isinstance(out, jax.ShapeDtypeStruct):
                self.near.add(id(result))
        return results[:-1]


def body(
    frames,
    video_group,
    msg_w,
    msg_bias,
    norm_gain,
    norm_shift,
    attn_in,
    qv_bias,
    attn_out,
    out_bias,
    norm2_gain,
    norm2_shift,
    fc_in,
    fc_in_bias,
    fc_out,
    fc_out_bias,
    cotangent,
):
    _, frame_count, patch, model = frames.shape
    width = attn_in.shape[-1]
    hidden_width = fc_in.shape[-1]
    heads = width // HEAD_DIM
    clips = lax.axis_size("dp")
    half = frame_count // 2
    rows = -(-(patch + 1) // 16) * 16
    all_rows = clips * frame_count
    scale = HEAD_DIM ** (-0.5)
    pipe = lax.axis_index("pipe")
    tensor = lax.axis_index("tensor")
    clip = lax.axis_index("dp")
    ring = clips == 4
    stage = Chain()
    quarter = hidden_width // 4
    assert quarter == width and hidden_width == model and half == 4

    def tensor_swap(v, bit):
        return lax.ppermute(v, "tensor", [(i, i ^ bit) for i in range(4)])

    def core_swap(v):
        return tensor_swap(v, 1)

    def x_swap(v):
        return tensor_swap(v, 2)

    def y_swap(v):
        return lax.ppermute(v, "pipe", [(0, 1), (1, 0)])

    def y_late(v):
        return lax.ppermute(v, "pipe", [(0, 1)])

    def y_early(v):
        return lax.ppermute(v, "pipe", [(1, 0)])

    def z_swap(v, bit):
        return lax.ppermute(v, "dp", [(i, i ^ bit) for i in range(clips)])

    def gather_clips(v):
        if ring:
            return [v] + [z_swap(v, apart) for apart in range(1, clips)]
        every = lax.all_gather(v, "dp")
        every = lax.dynamic_slice_in_dim(jnp.concatenate([every, every]), clip, clips, 0)
        return [every.reshape(clips * v.shape[0], v.shape[1])]

    def clip_block(refs, c, size):
        if len(refs) == clips:
            return refs[c][...]
        return refs[0][c * size : (c + 1) * size, :]

    blocks = clips if ring else 1

    def head_masks(n):
        lane = lax.broadcasted_iota(jnp.int32, (n, width), 1)
        return [(lane >= h * HEAD_DIM) & (lane < (h + 1) * HEAD_DIM) for h in range(heads)]

    def only(mask, v):
        return jnp.where(mask, v, jnp.zeros_like(v))

    def add(*terms):
        total = terms[0].astype(F32)
        for term in terms[1:]:
            total = total + term.astype(F32)
        return total

    def adds(*groups):
        sizes = [len(group) for group in groups]

        def kernel(*refs):
            at = 0
            for size, out in zip(sizes, refs[sum(sizes) :]):
                out[...] = add(*[ref[...] for ref in refs[at : at + size]]).astype(out.dtype)
                at += size

        return stage(
            kernel,
            [array for group in groups for array in group],
            [near(group[0].shape, group[0].dtype) for group in groups],
        )

    own_in = jnp.transpose(attn_in[0], (1, 2, 0))
    own_out = attn_out[0]
    sent_in = y_early(own_in)
    cls_rows = frames[0, :, 0, :]
    cls_all = gather_clips(cls_rows)

    def vector_kernel(mb, g2, s2, fi, fo, gain, shift, ob, qv, vecs_o, own_o):
        for i, ref in enumerate((mb, g2, s2, fi, fo)):
            vecs_o[i : i + 1, :] = ref[...].reshape(1, model)
        for i, ref in enumerate((gain, shift, ob)):
            own_o[i : i + 1, :] = ref[...]
        own_o[3:8, :] = jnp.zeros((5, model), F32)
        own_o[3:5, 0:width] = qv[...]

    vectors, own_vec = stage(
        vector_kernel,
        [
            msg_bias, norm2_gain, norm2_shift, fc_in_bias, fc_out_bias,
            norm_gain, norm_shift, out_bias, qv_bias[0],
        ],
        [near((8, model), F32)] * 2,
    )
    sent_vec = y_early(own_vec)
    sent_out = y_early(own_out)

    tokens_all = rows * frame_count
    lanes = 128

    def slot_kernel(v, *refs):
        wide = refs[-1]
        flat = v[...].astype(F32).reshape(patch * frame_count, model)
        for c in range(model // lanes):
            at = c * tokens_all
            wide[at : at + patch * frame_count, :] = flat[:, c * lanes : (c + 1) * lanes]
            wide[at + patch * frame_count : at + tokens_all, :] = jnp.zeros(
                ((rows - patch) * frame_count, lanes), F32
            )
            for s in range(half):
                frame = at + lax.axis_index("pipe") * half + (lax.axis_index("tensor") ^ s)
                refs[s][:, c * lanes : (c + 1) * lanes] = wide[
                    pl.ds(frame, rows, stride=frame_count), :
                ].astype(BF16)

    def slots(v):
        return stage(
            slot_kernel,
            [jnp.transpose(v[0], (1, 0, 2))],
            [near((rows, model), BF16)] * half,
            [pltpu.VMEM((model // lanes * tokens_all, lanes), F32)],
        )

    x_slots = slots(frames)

    def message_forward(ids, *refs):
        cls_refs, refs = refs[:blocks], refs[blocks:]
        (mw, vecs, vrow, w, wo, first_o, low_o, q_o, k_o, v_o, probs_o, mixed_o, part_o) = refs
        cls = jnp.concatenate([clip_block(cls_refs, c, frame_count).astype(F32) for c in range(clips)])
        first = nn(cls.astype(BF16), mw[...]) + vecs[0:1]
        first_o[...] = first
        normed, _ = norm_parts(first)
        low = (normed * vrow[0:1] + vrow[1:2]).astype(BF16)
        low_o[...] = low
        q = (nt(low, w[0]) + vrow[3:4, :width]).astype(BF16)
        k = nt(low, w[1]).astype(BF16)
        v = (nt(low, w[2]) + vrow[4:5, :width]).astype(BF16)
        q_o[...] = q
        k_o[...] = k
        v_o[...] = v
        of_row = lax.broadcasted_iota(jnp.int32, (all_rows, all_rows), 0) // frame_count
        of_col = lax.broadcasted_iota(jnp.int32, (all_rows, all_rows), 1) // frame_count
        mine = lax.axis_index("dp")
        row_id = jnp.zeros((all_rows, all_rows), jnp.int32)
        col_id = jnp.zeros((all_rows, all_rows), jnp.int32)
        for c in range(clips):
            mark = ids[mine ^ c if ring else lax.rem(mine + c, clips)]
            row_id = jnp.where(of_row == c, mark, row_id)
            col_id = jnp.where(of_col == c, mark, col_id)
        allowed = row_id == col_id
        mixed = jnp.zeros((all_rows, width), F32)
        for h, mask in enumerate(head_masks(all_rows)):
            scores = jnp.where(allowed, nt(only(mask, q), k) * scale, -jnp.inf)
            exponent = jnp.exp(scores - jnp.max(scores, axis=-1, keepdims=True))
            probs = exponent / jnp.sum(exponent, axis=-1, keepdims=True)
            probs_o[h] = probs
            mixed = mixed + only(mask, nn(probs.astype(BF16), v))
        mixed = mixed.astype(BF16)
        mixed_o[...] = mixed
        part = nn(mixed, wo[...]) + jnp.where(lax.axis_index("tensor") == 0, vrow[2:3], 0.0)
        part_o[...] = part[:frame_count]

    (first_msg, low_zero, q_zero, k_zero, v_zero, probs_zero, mixed_zero, part_zero) = stage(
        message_forward,
        [*cls_all, msg_w, vectors, own_vec, own_in, own_out],
        [
            near((all_rows, model), F32),
            near((all_rows, model), BF16),
            near((all_rows, width), BF16),
            near((all_rows, width), BF16),
            near((all_rows, width), BF16),
            near((heads, all_rows, all_rows), F32),
            near((all_rows, width), BF16),
            near((frame_count, model), F32),
        ],
        scalars=[video_group],
    )
    (part_zero,) = adds((part_zero, core_swap(part_zero)))
    from_x = x_swap(part_zero)

    def project_kernel(x0, x1, x2, x3, wa, wb, va, vb, w, vrow, *outs):
        early = lax.axis_index("pipe") == 0
        for c in range(3):
            w[c] = jnp.where(early, wb[c], wa[c])
        vrow[...] = jnp.where(early, vb[...], va[...])
        gain, shift = vrow[0:1], vrow[1:2]
        for s, x in enumerate((x0, x1, x2, x3)):
            normed, _ = norm_parts(x[...].astype(F32))
            low = (normed * gain + shift).astype(BF16)
            outs[s][...] = (nt(low, w[0]) + vrow[3:4, :width]).astype(BF16)
            outs[half + s][...] = nt(low, w[1]).astype(BF16)
            outs[2 * half + s][...] = (nt(low, w[2]) + vrow[4:5, :width]).astype(BF16)

    w_in, vec, *projected = stage(
        project_kernel, [*x_slots, own_in, sent_in, own_vec, sent_vec],
        [near(own_in.shape, BF16), near(own_vec.shape, F32)] + [near((rows, width), BF16)] * 12,
        flops=2 * half * rows * model * 3 * width,
    )
    q_one, k_patch, v_patch = projected[:4], projected[4:8], projected[8:]
    (part_zero,) = adds((part_zero, from_x))
    part_late = y_late(part_zero)

    def message_rows_kernel(first, part, late, w, vrow, wa, wb, msg_o, k_o, v_o, w_o):
        sec, ten = lax.axis_index("pipe"), lax.axis_index("tensor")
        w_o[...] = jnp.where(sec == 0, wb[...], wa[...])
        msg_o[...] = jnp.zeros_like(msg_o)
        for s in range(half):
            at = pl.ds(sec * half + (ten ^ s), 1)
            summed = jnp.where(sec == 0, part[at, :], late[at, :])
            msg_o[s : s + 1, :] = (first[at, :] + summed).astype(BF16).astype(F32)
        normed, _ = norm_parts(msg_o[...])
        low = (normed * vrow[0:1] + vrow[1:2]).astype(BF16)
        k_o[...] = nt(low, w[1])
        v_o[...] = nt(low, w[2]) + vrow[4:5, :width]

    msg_rows, k_msg, v_msg, w_out = stage(
        message_rows_kernel,
        [first_msg, part_zero, part_late, w_in, vec, own_out, sent_out],
        [
            near((16, model), F32), near((16, width), F32), near((16, width), F32),
            near(own_out.shape, BF16),
        ],
    )

    def attend_kernel(
        s, q, k, v, km, vm, wo, part_o, mixed_o, probs_o, k_o, v_o,
    ):
        here = lax.broadcasted_iota(jnp.int32, (rows, width), 0) == patch
        key_here = lax.broadcasted_iota(jnp.int32, (rows, rows), 1) <= patch
        kk = jnp.where(here, km[s : s + 1], k[...].astype(F32)).astype(BF16)
        vv = jnp.where(here, vm[s : s + 1], v[...].astype(F32)).astype(BF16)
        k_o[...] = kk
        v_o[...] = vv
        mixed = jnp.zeros((rows, width), F32)
        for h, mask in enumerate(head_masks(rows)):
            scores = nt(only(mask, q[...]), kk) * scale
            scores = jnp.where(key_here, scores, -jnp.inf)
            exponent = jnp.exp(scores - jnp.max(scores, axis=-1, keepdims=True))
            probs = exponent * (1.0 / jnp.sum(exponent, axis=-1, keepdims=True))
            probs = probs.astype(BF16)
            probs_o[h] = probs
            mixed = mixed + only(mask, nn(probs, vv))
        mixed = mixed.astype(BF16)
        mixed_o[...] = mixed
        part_o[...] = nn(mixed, wo[...]).astype(BF16)

    def attend(s):
        return stage(
            functools.partial(attend_kernel, s),
            [q_one[s], k_patch[s], v_patch[s], k_msg, v_msg, w_out],
            [
                near((rows, model), BF16),
                near((rows, width), BF16),
                near((heads, rows, rows), BF16),
                near((rows, width), BF16),
                near((rows, width), BF16),
            ],
            flops=2 * rows * (width * model + 2 * heads * rows * HEAD_DIM),
        )

    attended = [None] * half
    attended[3] = attend(3)
    from_core = core_swap(attended[3][0])
    attended[2] = attend(2)
    (two,) = adds((attended[2][0], from_core))
    from_x = x_swap(two)
    attended[1] = attend(1)
    from_core = core_swap(attended[1][0])
    attended[0] = attend(0)
    g_slots = slots(cotangent)

    def residual_kernel(a, b, c, x, vrow, vecs, resid_o, low_o):
        resid = x[...].astype(F32) + add(a[...], b[...], c[...]) + vrow[2:3]
        resid_o[...] = resid
        normed, _ = norm_parts(resid)
        low_o[...] = (normed * vecs[1:2] + vecs[2:3]).astype(BF16)

    resid_own, low_own = stage(
        residual_kernel, [attended[0][0], from_core, from_x, x_slots[0], vec, vectors],
        [near((rows, model), F32), near((rows, model), BF16)],
    )

    def relay_kernel(v, out):
        out[...] = v[...]

    def relay(v):
        return stage(relay_kernel, [v], [near(v.shape, v.dtype)])[0]

    from_x = x_swap(low_own)
    low_two = [low_own, core_swap(low_own)]

    def grad_hidden_kernel(g0, g1, g2, g3, w, *outs):
        for g, out in zip((g0, g1, g2, g3), outs):
            out[...] = nt(g[...], w[...]).astype(BF16)

    g_hidden = stage(
        grad_hidden_kernel, [*g_slots, fc_out], [near((rows, hidden_width), BF16)] * half,
        flops=2 * half * rows * model * hidden_width,
    )
    def feed_kernel(low, gh, w, vecs, hid_o, pre_o, grad_o, bias_o):
        hidden_in = nn(low[...], w[...]) + vecs[3:4]
        sig = 1.0 / (1.0 + jnp.exp(-QUICK_GELU * hidden_in))
        hid_o[...] = (hidden_in * sig).astype(BF16)
        slope = sig + QUICK_GELU * hidden_in * sig * (1.0 - sig)
        pre = (gh[...].astype(F32) * slope).astype(BF16)
        pre_o[...] = pre
        grad_o[...] = nt(pre, w[...]).astype(BF16)
        bias_o[...] = row_sum(pre.astype(F32))

    def feed(s):
        return stage(
            feed_kernel, [low_two[s], g_hidden[s], fc_in, vectors],
            [
                near((rows, hidden_width), BF16),
                near((rows, hidden_width), BF16),
                near((rows, model), BF16),
                near((1, hidden_width), F32),
            ],
            flops=2 * 2 * rows * model * hidden_width,
        )

    half_rows, eighth = model // 2, model // 8

    def halves_of(acc, keep, send):
        sec = lax.axis_index("pipe")
        for out, at in ((keep, sec), (send, 1 - sec)):
            start = pl.multiple_of(at * half_rows, half_rows)
            out[...] = acc[pl.ds(start, half_rows), :].astype(BF16)

    half_shapes = [near((half_rows, model), BF16)] * 2

    def weight_half_kernel(a0, a1, b0, b1, out):
        out[...] = tn(a0[...], b0[...])
        out[...] += tn(a1[...], b1[...])

    def weight_half(a0, a1, b0, b1):
        return stage(
            weight_half_kernel, [a0, a1, b0, b1], [near((a0.shape[1], b0.shape[1]), F32)],
            flops=4 * rows * model * hidden_width,
        )[0]

    def weight_kernel(half_sum, a0, a1, b0, b1, keep, send, acc):
        acc[...] = half_sum[...] + tn(a0[...], b0[...])
        acc[...] += tn(a1[...], b1[...])
        halves_of(acc, keep, send)

    def weight(half_sum, a0, a1, b0, b1):
        return stage(
            weight_kernel, [half_sum, a0, a1, b0, b1], half_shapes,
            [pltpu.VMEM((model, model), F32)], flops=4 * rows * model * hidden_width,
        )

    def over_sections(keep, send):
        return keep, y_swap(send) if ring else send

    def over_clips(keep, got):
        if not ring:
            return keep, got

        def kernel(a, b, *refs):
            acc = refs[-1]
            acc[...] = add(a[...], b[...])
            for apart in range(clips):
                start = pl.multiple_of((lax.axis_index("dp") ^ apart) * eighth, eighth)
                refs[apart][...] = acc[pl.ds(start, eighth), :].astype(BF16)

        parts = stage(
            kernel, [keep, got], [near((eighth, model), BF16)] * clips,
            [pltpu.VMEM((half_rows, model), F32)],
        )
        return [parts[0]] + [z_swap(parts[apart], apart) for apart in range(1, clips)]

    def to_clips(parts):
        if not ring:
            return parts
        (own,) = adds(parts)
        return [own] + [z_swap(own, apart) for apart in range(1, clips)]

    def to_sections(parts):
        if not ring:
            keep, send = parts
            sec = lax.axis_index("pipe")
            early = jnp.where(sec == 0, keep, send)
            later = jnp.where(sec == 0, send, keep)
            early, later = lax.psum((early, later), ("pipe", "dp"))
            return jnp.where(sec == 0, early, later), jnp.where(sec == 0, later, early)

        def kernel(*refs):
            for apart in range(clips):
                start = pl.multiple_of((lax.axis_index("dp") ^ apart) * eighth, eighth)
                refs[-1][pl.ds(start, eighth), :] = refs[apart][...]

        (summed,) = stage(kernel, parts, [near((half_rows, model), BF16)])
        return summed, y_swap(summed)

    def put_halves(keep, other, out):
        sec = lax.axis_index("pipe")
        for ref, at in ((keep, sec), (other, 1 - sec)):
            start = pl.multiple_of(at * half_rows, half_rows)
            out[pl.ds(start, half_rows), :] = ref[...].astype(F32)

    def whole(keep, other):
        return stage(put_halves, [keep, other], [shape_of((model, model), F32)])[0]

    hid, pre, grad_parts, bias_rows = [None] * half, [None] * half, [None] * half, [None] * half
    hid[0], pre[0], grad_parts[0], bias_rows[0] = feed(0)
    hid[1], pre[1], grad_parts[1], bias_rows[1] = feed(1)
    from_core1 = core_swap(grad_parts[1])
    fc_out_half = weight_half(hid[0], hid[1], g_slots[0], g_slots[1])
    low_two.append(relay(from_x))
    low_two.append(core_swap(low_two[2]))
    hid[2], pre[2], grad_parts[2], bias_rows[2] = feed(2)
    hid[3], pre[3], grad_parts[3], bias_rows[3] = feed(3)
    from_core3 = core_swap(grad_parts[3])
    fc_out_pair = over_sections(*weight(fc_out_half, hid[2], hid[3], g_slots[2], g_slots[3]))
    (two,) = adds((grad_parts[2], from_core3))
    from_x = x_swap(two)
    fc_in_half = weight_half(low_two[0], low_two[1], pre[0], pre[1])
    fc_in_pair = over_sections(*weight(fc_in_half, low_two[2], low_two[3], pre[2], pre[3]))

    def residual_back_kernel(a, b, c, resid, g, vecs, grad_o, low_o, small_o):
        incoming = add(a[...], b[...], c[...])
        normed, inverse = norm_parts(resid[...])
        real = lax.broadcasted_iota(jnp.int32, (rows, model), 0) < patch
        incoming = jnp.where(real, incoming, 0.0)
        grad = g[...].astype(F32) + norm_back(incoming, normed, inverse, vecs[1:2])
        grad = jnp.where(real, grad, 0.0)
        grad_o[...] = grad
        low = grad.astype(BF16)
        low_o[...] = low
        small_o[...] = jnp.zeros_like(small_o)
        small_o[0:1, :] = row_sum(incoming * normed)
        small_o[1:2, :] = row_sum(incoming)
        small_o[2:3, :] = row_sum(low.astype(F32))
        small_o[3:4, :] = row_sum(g[...].astype(F32))

    grad_resid, grad_low, small_two = stage(
        residual_back_kernel,
        [grad_parts[0], from_core1, from_x, resid_own, g_slots[0], vectors],
        [near((rows, model), F32), near((rows, model), BF16), near((8, model), F32)],
    )
    from_x = x_swap(grad_low)
    branch = [grad_low, core_swap(grad_low)]

    def column_out(values_in, slot, keep_o, send_o):
        ten = lax.axis_index("tensor")
        spot = (ten ^ slot) & 1
        for i in range(4):
            block = values_in[:, i * width : (i + 1) * width]
            apart = ten ^ i

            @pl.when((apart & 1) == 0)
            def _():
                keep_o[apart >> 1, spot] = block

            @pl.when((apart & 1) == 1)
            def _():
                send_o[apart >> 1, spot] = block

    def attend_back_kernel(
        s, branch_in, q, k, v, probs, x, msg, w, vrow, wo, *refs
    ):
        extra = refs[0] if s == 0 else None
        back_o, grads_o, low_o, small_o = refs[-4:]
        gain, shift = vrow[0:1], vrow[1:2]
        here = lax.broadcasted_iota(jnp.int32, (rows, model), 0) == patch
        grad_mixed = nt(branch_in[...], wo[...]).astype(BF16)
        dq = jnp.zeros((rows, width), F32)
        dk = jnp.zeros((rows, width), F32)
        dv = jnp.zeros((rows, width), F32)
        for h, mask in enumerate(head_masks(rows)):
            grad_head = only(mask, grad_mixed)
            low_probs = probs[h]
            wide = low_probs.astype(F32)
            dv = dv + tn(low_probs, grad_head)
            grad_probs = nt(grad_head, v[...])
            inner = jnp.sum(wide * grad_probs, axis=-1, keepdims=True)
            grad_scores = (wide * (grad_probs - inner)).astype(BF16)
            dq = dq + only(mask, nn(grad_scores, k[...]))
            dk = dk + tn(grad_scores, only(mask, q[...]))
        dq = (dq * scale).astype(BF16)
        dk = (dk * scale).astype(BF16)
        dv = dv.astype(BF16)
        grads_o[0] = dq
        grads_o[1] = dk
        grads_o[2] = dv
        grad_low = nn(dq, w[0]) + nn(dk, w[1]) + nn(dv, w[2])
        token = jnp.where(here, msg[s : s + 1], x[...].astype(F32))
        normed, inverse = norm_parts(token)
        low_o[...] = (normed * gain + shift).astype(BF16)
        back = norm_back(grad_low, normed, inverse, gain)
        small_o[...] = jnp.zeros_like(small_o)
        small_o[0:1, :] = row_sum(only(here, back))
        small_o[1:2, :] = row_sum(grad_low * normed)
        small_o[2:3, :] = row_sum(grad_low)
        small_o[3:4, 0:width] = row_sum(dq.astype(F32))
        small_o[3:4, 256 : 256 + width] = row_sum(dv.astype(F32))
        if s == 0:
            back = back + extra[...]
        back_o[...] = back.astype(BF16)

    def attend_back(s):
        _, _, probs, k, v = attended[s]
        ins = [branch[s], q_one[s], k, v, probs, x_slots[s], msg_rows, w_in, vec, w_out]
        return stage(
            functools.partial(attend_back_kernel, s),
            ins + ([grad_resid] if s == 0 else []),
            [
                near((rows, model), BF16),
                near((3, rows, width), BF16),
                near((rows, model), BF16),
                near((8, model), F32),
            ],
            flops=2 * rows * (4 * width * model + 4 * heads * rows * HEAD_DIM),
        )

    column_shapes = [near((2, 2, rows, width), BF16)] * 2

    def column_kernel(*refs):
        for s in range(half):
            keep_o, send_o = refs[half + 2 * (s // 2) : half + 2 * (s // 2) + 2]
            column_out(refs[s][...], s, keep_o, send_o)

    def mlp_kernel(h0, h1, h2, h3, w, resid, vecs, *outs):
        for s, h in enumerate((h0, h1, h2, h3)):
            out = nn(h[...], w[...])
            if s == 0:
                out = out + resid[...] + vecs[4:5]
            keep_o, send_o = outs[2 * (s // 2) : 2 * (s // 2) + 2]
            column_out(out.astype(BF16), s, keep_o, send_o)

    def far_adds(keep01, got01, keep23, got23):
        def kernel(ka, ga, kb, gb, out):
            out[0] = add(kb[1], gb[1]).astype(BF16)
            out[1] = add(ka[1], ga[1]).astype(BF16)

        return x_swap(
            stage(kernel, [keep01, got01, keep23, got23], [near((2, 2, rows, width), BF16)])[0]
        )

    def frames_of(refs):
        keep01, got01, keep23, got23, far = refs
        low_pair = lax.axis_index("tensor") >> 1
        for i in range(2):
            for pair, keep, got, n in (
                (low_pair, keep01, got01, 0),
                (low_pair ^ 1, keep23, got23, 1),
            ):
                yield pair * 2 + i, add(keep[0, i], got[0, i], far[n, i])

    back, grads, low_one, small = [None] * half, [None] * half, [None] * half, [None] * half
    back[0], grads[0], low_one[0], small[0] = attend_back(0)
    back[1], grads[1], low_one[1], small[1] = attend_back(1)
    fc_out_parts = over_clips(*fc_out_pair)

    def attend_weight_half_kernel(ga, gb, la, lb, ma, mb, ba, bb, out):
        for c in range(3):
            at = slice(c * width, (c + 1) * width)
            out[at, :] = tn(ga[c], la[...])
            out[at, :] += tn(gb[c], lb[...])
        out[3 * width :, :] = tn(ma[...], ba[...])
        out[3 * width :, :] += tn(mb[...], bb[...])

    def weight_ins(*picked):
        return [
            array
            for arrays in (grads, low_one, [one[1] for one in attended], branch)
            for array in [arrays[s] for s in picked]
        ]

    (attend_half,) = stage(
        attend_weight_half_kernel, weight_ins(0, 1), [near((4 * width, model), F32)],
        flops=4 * rows * model * 4 * width,
    )
    branch.append(relay(from_x))
    branch.append(core_swap(branch[2]))
    back[2], grads[2], low_one[2], small[2] = attend_back(2)
    fc_in_parts = over_clips(*fc_in_pair)
    back[3], grads[3], low_one[3], small[3] = attend_back(3)

    def pack_kernel(s0, s1, s2, s3, two, p0, p1, p2, p3, out, acc):
        ten = lax.axis_index("tensor")
        acc[...] = jnp.zeros_like(acc)
        for s, ref in enumerate((s0, s1, s2, s3)):
            acc[pl.ds(ten ^ s, 1), :] = ref[0:1, :]
        acc[4:6, :] = s0[1:3, :] + s1[1:3, :] + s2[1:3, :] + s3[1:3, :]
        acc[6:10, :] = two[0:4, :]
        acc[pl.ds(10 + ten, 1), :] = p0[...] + p1[...] + p2[...] + p3[...]
        acc[pl.ds(14 + ten, 1), :] = s0[3:4, :] + s1[3:4, :] + s2[3:4, :] + s3[3:4, :]
        out[...] = acc[...].astype(BF16)

    (pack,) = stage(
        pack_kernel, [*small, small_two, *bias_rows], [near((32, model), BF16)],
        [pltpu.VMEM((32, model), F32)],
    )
    from_core = core_swap(pack)

    def attend_weight_kernel(so_far, ga, gb, la, lb, ma, mb, ba, bb, keep, send, acc):
        for c in range(3):
            at = slice(c * width, (c + 1) * width)
            acc[at, :] = so_far[at, :] + tn(ga[c], la[...])
            acc[at, :] += tn(gb[c], lb[...])
        acc[3 * width :, :] = so_far[3 * width :, :] + tn(ma[...], ba[...])
        acc[3 * width :, :] += tn(mb[...], bb[...])
        halves_of(acc, keep, send)

    attend_pair = over_sections(
        *stage(
            attend_weight_kernel, [attend_half, *weight_ins(2, 3)], half_shapes,
            [pltpu.VMEM((4 * width, model), F32)], flops=4 * rows * model * 4 * width,
        )
    )
    (pack,) = adds((pack, from_core))
    from_x = x_swap(pack)
    keep01, send01, keep23, send23 = stage(column_kernel, back, column_shapes * 2)
    got01, got23 = core_swap(send01), core_swap(send23)
    (pack,) = adds((pack, from_x))
    other_pack = y_swap(pack)
    fc_out_parts = to_clips(fc_out_parts)
    far = far_adds(keep01, got01, keep23, got23)

    def merge_kernel(mine, other, out):
        a, b = mine[...].astype(F32), other[...].astype(F32)
        early = lax.axis_index("pipe") == 0
        out[...] = jnp.concatenate(
            [
                jnp.where(early, a[:half], b[:half]),
                jnp.where(early, b[:half], a[:half]),
                a[half : half + 24] + b[half : half + 24],
            ],
            axis=0,
        ).astype(BF16)

    (pack,) = stage(merge_kernel, [pack, other_pack], [near((32, model), BF16)])
    packs = gather_clips(pack)
    pack_rows = pack.shape[0]
    fc_in_parts = to_clips(fc_in_parts)
    attend_parts = over_clips(*attend_pair)
    block_keep01, block_send01, block_keep23, block_send23 = stage(
        mlp_kernel, [*hid, fc_out, resid_own, vectors], column_shapes * 2,
        flops=2 * half * rows * model * hidden_width,
    )
    block_got01, block_got23 = core_swap(block_send01), core_swap(block_send23)

    def message_back(*refs):
        pack_refs, refs = refs[:blocks], refs[blocks:]
        (first, q, k, v, probs, w, wo, vrow, sent_o, grads_o, back_o) = refs
        sent = jnp.concatenate(
            [clip_block(pack_refs, c, pack_rows).astype(F32)[:frame_count] for c in range(clips)],
            axis=0,
        )
        low = sent.astype(BF16)
        sent_o[...] = sent
        grad_mixed = nt(low, wo[...]).astype(BF16)
        dq = jnp.zeros((all_rows, width), F32)
        dk = jnp.zeros((all_rows, width), F32)
        dv = jnp.zeros((all_rows, width), F32)
        for h, mask in enumerate(head_masks(all_rows)):
            grad_head = only(mask, grad_mixed)
            wide = probs[h]
            dv = dv + tn(wide.astype(BF16), grad_head)
            grad_probs = nt(grad_head, v[...])
            inner = jnp.sum(wide * grad_probs, axis=-1, keepdims=True)
            grad_scores = (wide * (grad_probs - inner)).astype(BF16)
            dq = dq + only(mask, nn(grad_scores, k[...]))
            dk = dk + tn(grad_scores, only(mask, q[...]))
        dq = (dq * scale).astype(BF16)
        dk = (dk * scale).astype(BF16)
        dv = dv.astype(BF16)
        grads_o[0] = dq
        grads_o[1] = dk
        grads_o[2] = dv
        grad_low = nn(dq, w[0]) + nn(dk, w[1]) + nn(dv, w[2])
        normed, inverse = norm_parts(first[...])
        back_msg = norm_back(grad_low, normed, inverse, vrow[0:1])
        back_o[0:all_rows, :] = back_msg.astype(BF16)
        tail = jnp.concatenate(
            [row_sum(grad_low * normed), row_sum(grad_low), jnp.zeros((14, model), F32)], axis=0
        )
        back_o[all_rows:, :] = tail.astype(BF16)

    sent_all, grads_zero, back_zero = stage(
        message_back,
        [*packs, first_msg, q_zero, k_zero, v_zero, probs_zero, own_in, own_out, own_vec],
        [
            near((all_rows, model), F32),
            near((3, all_rows, width), BF16),
            near((all_rows + 16, model), BF16),
        ],
    )
    from_core = core_swap(back_zero)
    fc_out_halves = to_sections(fc_out_parts)
    (back_zero,) = adds((back_zero, from_core))
    from_x = x_swap(back_zero)
    block_far = far_adds(block_keep01, block_got01, block_keep23, block_got23)

    def message_weight(sent, grads_in, low, mixed, in_o, out_o, qv_o, bias_o):
        for c in range(3):
            in_o[c] = tn(grads_in[c], low[...])
        out_o[...] = tn(mixed[...], sent[...].astype(BF16))
        qv_o[0:1, :] = row_sum(grads_in[0].astype(F32))
        qv_o[1:2, :] = row_sum(grads_in[2].astype(F32))
        bias_o[...] = row_sum(sent[...])

    in_zero, out_zero, qv_zero, bias_zero = stage(
        message_weight, [sent_all, grads_zero, low_zero, mixed_zero],
        [
            near((3, width, model), F32),
            near((width, model), F32),
            near((2, width), F32),
            near((1, model), F32),
        ],
    )
    attend_parts = to_clips(attend_parts)
    (back_zero,) = adds((back_zero, from_x))
    back_late = y_late(back_zero)

    def block_out_kernel(*refs):
        for at, total in frames_of(refs[:-1]):
            refs[-1][at] = total.T[:, :patch].astype(BF16)

    (block_out,) = stage(
        block_out_kernel, [block_keep01, block_got01, block_keep23, block_got23, block_far],
        [shape_of((half, width, patch), BF16)],
    )
    fc_in_halves = to_sections(fc_in_parts)
    fc_out_grad = whole(*fc_out_halves)

    def message_end(*refs):
        pack_refs, refs = refs[:blocks], refs[blocks:]
        cls_refs, refs = refs[:blocks], refs[blocks:]
        (sent, own, late, mw, qv_in, bias_in, w_o, cls_o, vec_o, qv_o, turned, sums) = refs
        sec, ten = lax.axis_index("pipe"), lax.axis_index("tensor")
        total = jnp.where(sec == 0, own[...].astype(F32), late[...].astype(F32))
        grad_first = sent[...] + total[:all_rows]
        at = pl.ds(pl.multiple_of(ten * width, width), width)
        mine = grad_first[:16]
        high = mine.astype(BF16)
        rest = (mine - high.astype(F32)).astype(BF16)
        mw_rows = mw[at, :]
        cls_o[...] = nt(high, mw_rows) + nt(rest, mw_rows)
        turned[...] = grad_first.T
        mine = turned[at, :]
        high = mine.astype(BF16)
        rest = (mine - high.astype(F32)).astype(BF16)
        cls = jnp.concatenate([clip_block(cls_refs, c, frame_count).astype(F32) for c in range(clips)])
        cls = cls.astype(BF16)
        w_o[...] = nn(high, cls) + nn(rest, cls)
        summed = clip_block(pack_refs, 0, pack_rows).astype(F32)
        for c in range(1, clips):
            summed = summed + clip_block(pack_refs, c, pack_rows).astype(F32)
        sums[...] = summed[frame_count:]
        first_one = sec == 0
        vec_o[0:1, :] = jnp.where(first_one, total[all_rows : all_rows + 1], sums[0:1])
        vec_o[1:2, :] = jnp.where(first_one, total[all_rows + 1 : all_rows + 2], sums[1:2])
        vec_o[2:3, :] = jnp.where(first_one, bias_in[...], sums[4:5])
        vec_o[3:4, :] = sums[2:3]
        vec_o[4:5, :] = sums[3:4]
        vec_o[5:6, :] = sums[5:6]
        vec_o[6:7, :] = sums[pl.ds(6 + ten, 1), :]
        vec_o[7:8, :] = row_sum(grad_first)
        qv_row = sums[pl.ds(10 + ten, 1), :]
        qv_o[0:1, :] = jnp.where(first_one, qv_in[0:1], qv_row[:, :width])
        qv_o[1:2, :] = jnp.where(first_one, qv_in[1:2], qv_row[:, 256 : 256 + width])

    msg_w_grad, cls_part, vec_grads, qv_grad = stage(
        message_end,
        [*packs, *cls_all, sent_all, back_zero, back_late, msg_w, qv_zero, bias_zero],
        [
            shape_of((width, model), F32),
            near((16, width), F32),
            near((8, model), F32),
            near((2, width), F32),
        ],
        [pltpu.VMEM((model, all_rows), F32), pltpu.VMEM((24, model), F32)],
    )

    def frames_grad_kernel(*refs):
        cls, out = refs[-2:]
        top = lax.broadcasted_iota(jnp.int32, (rows, width), 0) == 0
        for at, total in frames_of(refs[:-2]):
            row = cls[pl.ds(lax.axis_index("pipe") * half + at, 1), :]
            out[at] = (total + jnp.where(top, row, 0.0)).T[:, :patch].astype(BF16)

    (frames_grad,) = stage(
        frames_grad_kernel, [keep01, got01, keep23, got23, far, cls_part],
        [shape_of((half, width, patch), BF16)],
    )
    attend_halves = to_sections(attend_parts)
    fc_in_grad = whole(*fc_in_halves)

    def attend_whole_kernel(keep, other, in_zero_ref, out_zero_ref, in_o, out_o, acc):
        @pl.when(lax.axis_index("pipe") == 0)
        def _():
            in_o[...] = in_zero_ref[...]
            out_o[...] = out_zero_ref[...]

        @pl.when(lax.axis_index("pipe") == 1)
        def _():
            put_halves(keep, other, acc)
            for c in range(3):
                in_o[c] = acc[c * width : (c + 1) * width, :]
            out_o[...] = acc[3 * width :, :]

    attn_in_grad, attn_out_grad = stage(
        attend_whole_kernel, [*attend_halves, in_zero, out_zero],
        [shape_of((3, width, model), F32), shape_of((width, model), F32)],
        [pltpu.VMEM((4 * width, model), F32)],
    )

    return (
        jnp.swapaxes(block_out, 1, 2)[None],
        jnp.swapaxes(frames_grad, 1, 2)[None],
        msg_w_grad.T,
        vec_grads[7],
        vec_grads[0:1],
        vec_grads[1:2],
        jnp.transpose(attn_in_grad, (2, 0, 1))[None],
        qv_grad[None],
        attn_out_grad[None],
        vec_grads[2:3],
        vec_grads[3],
        vec_grads[4],
        fc_in_grad,
        vec_grads[6],
        fc_out_grad,
        vec_grads[5],
    )


def solution(mesh):
    return jax.shard_map(
        body,
        mesh=mesh,
        in_specs=(
            P("dp", None, None, None),
            P(),
            P(),
            P(),
            P("pipe", None),
            P("pipe", None),
            P("pipe", None, None, "tensor"),
            P("pipe", None, "tensor"),
            P("pipe", "tensor", None),
            P("pipe", None),
            P(),
            P(),
            P(None, "tensor"),
            P("tensor"),
            P("tensor", None),
            P(),
            P("dp", None, None, None),
        ),
        out_specs=(
            P("dp", "pipe", None, "tensor"),
            P("dp", "pipe", None, "tensor"),
            P(None, "tensor"),
            P(),
            P("pipe", None),
            P("pipe", None),
            P("pipe", None, None, "tensor"),
            P("pipe", None, "tensor"),
            P("pipe", "tensor", None),
            P("pipe", None),
            P(),
            P(),
            P(None, "tensor"),
            P("tensor"),
            P("tensor", None),
            P(),
        ),
        check_vma=False,
    )
```

time: 304 us -> 228 us (0.75)
  Pallas kernels: 111 us -> 47.2 us
  waiting for transfers between devices: 55.6 us -> 87.5 us
  local copies, waits for them, and re-layouts: 34.9 us -> 10.4 us
  other arithmetic: 13.9 us -> 0 us
  starting transfers between devices: 81.4 us -> 77.3 us
    pallas_call x23 -> x60, Pallas kernels: 111 us -> 47.2 us  [__call__(): pl.pallas_call(stage, out_shape=[*outs, near((8, 128), F32)], in_specs=[p...]
    ppermute x4 -> x7, waiting for transfers between devices: 1.73 us -> 28.1 us  [y_swap(): return lax.ppermute(v, 'pipe', [(0, 1), (1, 0)])]
    dynamic_slice x6 -> x0, local copies, waits for them, and re-layouts: 9.64 us -> none  [slots(): lax.dynamic_index_in_dim(v[0], pipe * half + (tensor ^ s), 0, keepdims=Fa...]
    ppermute x56 -> x48, starting transfers between devices: 65.5 us -> 57.3 us  [the longest x24 42.2 us: z_swap(): return lax.ppermute(v, 'dp', [(i, i ^ bit) for i in range(clips)])]
    ppermute x4 -> x7, starting transfers between devices: 3.82 us -> 10.7 us  [y_swap(): return lax.ppermute(v, 'pipe', [(0, 1), (1, 0)])]
    ppermute x3, waiting for transfers between devices: 0.67 us -> 7.28 us  [y_early(): return lax.ppermute(v, 'pipe', [(1, 0)])]
    slice x15 -> x0, local copies, waits for them, and re-layouts: 6.36 us -> none  [the longest x3 2.76 us: reduce_chunks(): m3 = jnp.concatenate([m3[:part], add(m3[part:], down)])]
    another operation x6 -> x0, other arithmetic: 3.65 us -> none  [the longest x2 2.28 us: slots(): return jnp.pad(jnp.stack(picked), ((0, 0), (0, rows - patch), (0, 0)))]
  transfers between devices with their start and end apart: 65 -> 60, of which waited for: 19 -> 24; matrix products, arithmetic and copies ran while one was open for 14% -> 1% of each run, Pallas kernels for 33% -> 18%
where the time goes in v2:
time: 228 us; the launch traced here: 224 us
  waiting for transfers between devices  87.5 us (38%)
  starting transfers between devices  77.3 us (34%)
  Pallas kernels  47.2 us (21%)
  local copies, waits for them, and re-layouts  10.4 us (5%)
    pallas_call x60, Pallas kernels, __call__(): pl.pallas_call(stage, out_shape=[*outs, near((8, 128), F32)], in_specs=[p...  47.2 us
    ppermute x24, starting transfers between devices, z_swap(): return lax.ppermute(v, 'dp', [(i, i ^ bit) for i in range(clips)])  42.2 us
    ppermute x24, waiting for transfers between devices, z_swap(): return lax.ppermute(v, 'dp', [(i, i ^ bit) for i in range(clips)])  36.2 us
    ppermute x7, waiting for transfers between devices, y_swap(): return lax.ppermute(v, 'pipe', [(0, 1), (1, 0)])  28.1 us
    ppermute x24, starting transfers between devices, tensor_swap(): return lax.ppermute(v, 'tensor', [(i, i ^ bit) for i in range(4)])  15.1 us
    ppermute x24, waiting for transfers between devices, tensor_swap(): return lax.ppermute(v, 'tensor', [(i, i ^ bit) for i in range(4)])  14.5 us
    ppermute x7, starting transfers between devices, y_swap(): return lax.ppermute(v, 'pipe', [(0, 1), (1, 0)])  10.7 us
    unnamed x35, local copies, waits for them, and re-layouts  8.45 us
  transfers between devices with their start and end apart: 60, of which 24 were waited for; matrix products, arithmetic and copies ran while one was open for 1% of the time, Pallas kernels for 18%

profile of v2, /device:TPU:0, one launch (start us, length us, event | category | flops | bytes accessed | tf_op | source)
XLA Modules:
  0.0 224.1 jit_solution(8703857103716080983)
XLA Ops:
  4.1 5.0 %collective-permute-start.2 = (bf16[8,768]{1,0:T(8,128)(2,1)S(1)}, bf16[8,768]{1,0:T(8,128)(2,1)S(1)}, u32[]{:S(2)}, u32[]{:S(2)}) collective-permute-start(bf16[8,768]{1,0:T(8,128)(2,1)S(1)} %slice_bitcast_fusion.refs_2_.refs_5_), channel_id=1, source_target_pairs={{0,3},{1,2},{2,1},{3,0},{4,7},{5,6},{6,5},{7,4},{8,11},{9,10},{10,... | collective-permute-start | bytes 36872 | tf_op jit(solution)/shard_map/ppermute | solution.py:147
  15.9 1.7 copy-done.4
  18.8 2.5 %shard_map.290 = (f32[32,768]{1,0:T(8,128)S(1)}, bf16[32,768]{1,0:T(8,128)(2,1)S(1)}, bf16[32,192]{1,0:T(8,128)(2,1)S(1)}, bf16[32,192]{1,0:T(8,128)(2,1)S(1)}, ...) custom-call(s32[4]{0:T(128)S(1)} %copy-done.15, ...), custom_call_target="tpu_custom_call" | custom-call | bytes 2457600 | tf_op jit(solution)/shard_map/pallas_call | solution.py:73
  22.7 1.8 collective-permute-start.6
  24.5 7.3 %collective-permute-done.5.refs_8_ = f32[8,768]{1,0:T(8,128)S(1)} collective-permute-done((f32[8,768]{1,0:T(8,128)S(1)}, f32[8,768]{1,0:T(8,128)S(1)}, u32[]{:S(2)}, u32[]{:S(2)}) %collective-permute-start.5) | collective-permute-done | bytes 24608 | tf_op jit(solution)/shard_map/ppermute | solution.py:144
  33.4 1.6 collective-permute-start.7
  39.8 2.4 %collective-permute-start.11 = (bf16[208,768]{1,0:T(8,128)(2,1)S(1)}, bf16[208,768]{1,0:T(8,128)(2,1)S(1)}, u32[]{:S(2)}, u32[]{:S(2)}) collective-permute-start(bf16[208,768]{1,0:T(8,128)(2,1)S(1)} %get-tuple-element.282), channel_id=1, source_target_pairs={{0,8},{4,12},{8,0},{12,4},{1,9},{5,13},{9,1},{13,5},{2,10},{6,14},... | collective-permute-start | bytes 958472 | tf_op jit(solution)/shard_map/ppermute | solution.py:129
  45.8 4.2 %collective-permute-done.11.refs_3_ = bf16[208,768]{1,0:T(8,128)(2,1)S(1)} collective-permute-done((bf16[208,768]{1,0:T(8,128)(2,1)S(1)}, bf16[208,768]{1,0:T(8,128)(2,1)S(1)}, u32[]{:S(2)}, u32[]{:S(2)}) %collective-permute-start.11) | collective-permute-done | bytes 319520 | tf_op jit(solution)/shard_map/ppermute | solution.py:129
  50.4 1.8 collective-permute-start.13
  56.7 3.7 %collective-permute-done.13.refs_1_ = bf16[208,768]{1,0:T(8,128)(2,1)S(1)} collective-permute-done((bf16[208,768]{1,0:T(8,128)(2,1)S(1)}, bf16[208,768]{1,0:T(8,128)(2,1)S(1)}, u32[]{:S(2)}, u32[]{:S(2)}) %collective-permute-start.13) | collective-permute-done | bytes 319520 | tf_op jit(solution)/shard_map/ppermute | solution.py:129
  64.9 1.8 collective-permute-start.17
  66.7 2.3 %collective-permute-start.19 = (bf16[384,768]{1,0:T(8,128)(2,1)S(1)}, bf16[384,768]{1,0:T(8,128)(2,1)S(1)}, u32[]{:S(2)}, u32[]{:S(2)}) collective-permute-start(bf16[384,768]{1,0:T(8,128)(2,1)S(1)} %get-tuple-element.334), channel_id=1, source_target_pairs={{0,16},{16,0},{1,17},{17,1},{2,18},{18,2},{3,19},{19,3},{4,20},{20... | collective-permute-start | bytes 1769480 | tf_op jit(solution)/shard_map/ppermute | solution.py:138
  71.2 3.4 %collective-permute-done.17.refs_3_ = bf16[208,768]{1,0:T(8,128)(2,1)S(1)} collective-permute-done((bf16[208,768]{1,0:T(8,128)(2,1)S(1)}, bf16[208,768]{1,0:T(8,128)(2,1)S(1)}, u32[]{:S(2)}, u32[]{:S(2)}) %collective-permute-start.17) | collective-permute-done | bytes 319520 | tf_op jit(solution)/shard_map/ppermute | solution.py:129
  75.4 1.8 collective-permute-start.20
  77.2 2.3 %collective-permute-start.21 = (bf16[384,768]{1,0:T(8,128)(2,1)S(1)}, bf16[384,768]{1,0:T(8,128)(2,1)S(1)}, u32[]{:S(2)}, u32[]{:S(2)}) collective-permute-start(bf16[384,768]{1,0:T(8,128)(2,1)S(1)} %get-tuple-element.350), channel_id=1, source_target_pairs={{0,16},{16,0},{1,17},{17,1},{2,18},{18,2},{3,19},{19,3},{4,20},{20... | collective-permute-start | bytes 1769480 | tf_op jit(solution)/shard_map/ppermute | solution.py:138
  79.5 1.7 shard_map.314
  81.2 1.7 shard_map.315
  85.5 1.7 shard_map.319
  87.2 7.9 %collective-permute-done.21.refs_2_ = bf16[384,768]{1,0:T(8,128)(2,1)S(1)} collective-permute-done((bf16[384,768]{1,0:T(8,128)(2,1)S(1)}, bf16[384,768]{1,0:T(8,128)(2,1)S(1)}, u32[]{:S(2)}, u32[]{:S(2)}) %collective-permute-start.21) | collective-permute-done | bytes 589856 | tf_op jit(solution)/shard_map/ppermute | solution.py:138
  95.3 1.7 shard_map.321
  98.3 1.8 collective-permute-start.34
  102.9 1.6 collective-permute-start.25
  104.5 2.6 %collective-permute-start.26 = (bf16[96,768]{1,0:T(8,128)(2,1)S(1)}, bf16[96,768]{1,0:T(8,128)(2,1)S(1)}, u32[]{:S(2)}, u32[]{:S(2)}) collective-permute-start(bf16[96,768]{1,0:T(8,128)(2,1)S(1)} %get-tuple-element.385), channel_id=1, source_target_pairs={{0,2},{1,3},{2,0},{3,1},{4,6},{5,7},{6,4},{7,5},{8,10},{9,11},{10,... | collective-permute-start | bytes 442376 | tf_op jit(solution)/shard_map/ppermute | solution.py:147
  107.1 4.3 %collective-permute-done.25.refs_2_ = bf16[96,768]{1,0:T(8,128)(2,1)S(1)} collective-permute-done((bf16[96,768]{1,0:T(8,128)(2,1)S(1)}, bf16[96,768]{1,0:T(8,128)(2,1)S(1)}, u32[]{:S(2)}, u32[]{:S(2)}) %collective-permute-start.25) | collective-permute-done | bytes 147488 | tf_op jit(solution)/shard_map/ppermute | solution.py:147
  111.4 2.7 %collective-permute-start.27 = (bf16[96,768]{1,0:T(8,128)(2,1)S(1)}, bf16[96,768]{1,0:T(8,128)(2,1)S(1)}, u32[]{:S(2)}, u32[]{:S(2)}) collective-permute-start(bf16[96,768]{1,0:T(8,128)(2,1)S(1)} %get-tuple-element.386), channel_id=1, source_target_pairs={{0,3},{1,2},{2,1},{3,0},{4,7},{5,6},{6,5},{7,4},{8,11},{9,10},{10,... | collective-permute-start | bytes 442376 | tf_op jit(solution)/shard_map/ppermute | solution.py:147
  114.1 2.8 %collective-permute-done.26.refs_3_ = bf16[96,768]{1,0:T(8,128)(2,1)S(1)} collective-permute-done((bf16[96,768]{1,0:T(8,128)(2,1)S(1)}, bf16[96,768]{1,0:T(8,128)(2,1)S(1)}, u32[]{:S(2)}, u32[]{:S(2)}) %collective-permute-start.26) | collective-permute-done | bytes 147488 | tf_op jit(solution)/shard_map/ppermute | solution.py:147
  116.9 2.1 collective-permute-start.24
  119.0 2.7 %collective-permute-start.31 = (bf16[96,768]{1,0:T(8,128)(2,1)S(1)}, bf16[96,768]{1,0:T(8,128)(2,1)S(1)}, u32[]{:S(2)}, u32[]{:S(2)}) collective-permute-start(bf16[96,768]{1,0:T(8,128)(2,1)S(1)} %get-tuple-element.396), channel_id=1, source_target_pairs={{0,1},{1,0},{2,3},{3,2},{4,5},{5,4},{6,7},{7,6},{8,9},{9,8},{10,11... | collective-permute-start | bytes 442376 | tf_op jit(solution)/shard_map/ppermute | solution.py:147
  124.8 3.6 %collective-permute-done.30.refs_2_ = bf16[32,768]{1,0:T(8,128)(2,1)S(1)} collective-permute-done((bf16[32,768]{1,0:T(8,128)(2,1)S(1)}, bf16[32,768]{1,0:T(8,128)(2,1)S(1)}, u32[]{:S(2)}, u32[]{:S(2)}) %collective-permute-start.30) | collective-permute-done | bytes 49184 | tf_op jit(solution)/shard_map/ppermute | solution.py:138
  128.5 2.4 %collective-permute-start.37 = (bf16[32,768]{1,0:T(8,128)(2,1)S(1)}, bf16[32,768]{1,0:T(8,128)(2,1)S(1)}, u32[]{:S(2)}, u32[]{:S(2)}) collective-permute-start(bf16[32,768]{1,0:T(8,128)(2,1)S(1)} %get-tuple-element.404.refs_1_), channel_id=1, source_target_pairs={{0,3},{1,2},{2,1},{3,0},{4,7},{5,6},{6,5},{7,4},{8,11},{9,10},{10,... | collective-permute-start | bytes 147464 | tf_op jit(solution)/shard_map/ppermute | solution.py:147
  132.4 7.6 %collective-permute-done.32.refs_3_ = bf16[96,768]{1,0:T(8,128)(2,1)S(1)} collective-permute-done((bf16[96,768]{1,0:T(8,128)(2,1)S(1)}, bf16[96,768]{1,0:T(8,128)(2,1)S(1)}, u32[]{:S(2)}, u32[]{:S(2)}) %collective-permute-start.32) | collective-permute-done | bytes 147488 | tf_op jit(solution)/shard_map/ppermute | solution.py:147
  139.9 5.3 %collective-permute-start.38 = (bf16[96,768]{1,0:T(8,128)(2,1)S(1)}, bf16[96,768]{1,0:T(8,128)(2,1)S(1)}, u32[]{:S(2)}, u32[]{:S(2)}) collective-permute-start(bf16[96,768]{1,0:T(8,128)(2,1)S(1)} %get-tuple-element.410.refs_1_), channel_id=1, source_target_pairs={{0,1},{1,0},{2,3},{3,2},{4,5},{5,4},{6,7},{7,6},{8,9},{9,8},{10,11... | collective-permute-start | bytes 442376 | tf_op jit(solution)/shard_map/ppermute | solution.py:147
  145.3 2.1 collective-permute-start.36
  147.7 2.1 collective-permute-start.35
  149.8 2.9 %shard_map.332 = (bf16[2,2,208,192]{3,2,1,0:T(8,128)(2,1)S(1)}, bf16[2,2,208,192]{3,2,1,0:T(8,128)(2,1)S(1)}, bf16[2,2,208,192]{3,2,1,0:T(8,128)(2,1)S(1)}, bf16...) custom-call(f32[8,128]{1,0:T(8,128)S(1)} %get-tuple-element.402.refs_0_, bf16[208,768]{1,0:T(8,128)(2,1)S(1)} %get-tuple-element.294.refs_1_, ...), custom_call_target="tpu_custom_call" | custom-call | flops 981467136 | bytes 3121152 | tf_op jit(solution)/shard_map/pallas_call | solution.py:73
  156.6 2.5 %collective-permute-start.51 = (bf16[96,768]{1,0:T(8,128)(2,1)S(1)}, bf16[96,768]{1,0:T(8,128)(2,1)S(1)}, u32[]{:S(2)}, u32[]{:S(2)}) collective-permute-start(bf16[96,768]{1,0:T(8,128)(2,1)S(1)} %get-tuple-element.434.refs_1_), channel_id=1, source_target_pairs={{0,3},{1,2},{2,1},{3,0},{4,7},{5,6},{6,5},{7,4},{8,11},{9,10},{10,... | collective-permute-start | bytes 442376 | tf_op jit(solution)/shard_map/ppermute | solution.py:147
  159.1 1.9 collective-permute-start.44
  162.2 3.0 %collective-permute-done.51.refs_4_ = bf16[96,768]{1,0:T(8,128)(2,1)S(1)} collective-permute-done((bf16[96,768]{1,0:T(8,128)(2,1)S(1)}, bf16[96,768]{1,0:T(8,128)(2,1)S(1)}, u32[]{:S(2)}, u32[]{:S(2)}) %collective-permute-start.51) | collective-permute-done | bytes 147488 | tf_op jit(solution)/shard_map/ppermute | solution.py:147
  165.7 9.1 %collective-permute-done.50.refs_3_ = bf16[96,768]{1,0:T(8,128)(2,1)S(1)} collective-permute-done((bf16[96,768]{1,0:T(8,128)(2,1)S(1)}, bf16[96,768]{1,0:T(8,128)(2,1)S(1)}, u32[]{:S(2)}, u32[]{:S(2)}) %collective-permute-start.50) | collective-permute-done | bytes 147488 | tf_op jit(solution)/shard_map/ppermute | solution.py:147
  175.3 4.2 %collective-permute-done.45.refs_3_ = bf16[96,768]{1,0:T(8,128)(2,1)S(1)} collective-permute-done((bf16[96,768]{1,0:T(8,128)(2,1)S(1)}, bf16[96,768]{1,0:T(8,128)(2,1)S(1)}, u32[]{:S(2)}, u32[]{:S(2)}) %collective-permute-start.45) | collective-permute-done | bytes 147488 | tf_op jit(solution)/shard_map/ppermute | solution.py:147
  180.2 1.6 collective-permute-done.46.refs_4_
  182.9 2.0 collective-permute-done.49.refs_2_
  185.0 3.8 %collective-permute-start.57 = (bf16[96,768]{1,0:T(8,128)(2,1)S(1)}, bf16[96,768]{1,0:T(8,128)(2,1)S(1)}, u32[]{:S(2)}, u32[]{:S(2)}) collective-permute-start(bf16[96,768]{1,0:T(8,128)(2,1)S(1)} %get-tuple-element.448.refs_1_), channel_id=1, source_target_pairs={{0,3},{1,2},{2,1},{3,0},{4,7},{5,6},{6,5},{7,4},{8,11},{9,10},{10,... | collective-permute-start | bytes 442376 | tf_op jit(solution)/shard_map/ppermute | solution.py:147
  189.9 3.7 %collective-permute-start.53 = (bf16[48,768]{1,0:T(8,128)(2,1)S(1)}, bf16[48,768]{1,0:T(8,128)(2,1)S(1)}, u32[]{:S(2)}, u32[]{:S(2)}) collective-permute-start(bf16[48,768]{1,0:T(8,128)(2,1)S(1)} %get-tuple-element.438.refs_10_), channel_id=1, source_target_pairs={{0,16},{1,17},{2,18},{3,19},{4,20},{5,21},{6,22},{7,23},{8,24},{9,... | collective-permute-start | bytes 221192 | tf_op jit(solution)/shard_map/ppermute | solution.py:141
  196.2 1.7 collective-permute-start.58
  200.6 1.8 collective-permute-start.59
  204.2 8.3 %collective-permute-done.58.refs_2_ = bf16[384,768]{1,0:T(8,128)(2,1)S(1)} collective-permute-done((bf16[384,768]{1,0:T(8,128)(2,1)S(1)}, bf16[384,768]{1,0:T(8,128)(2,1)S(1)}, u32[]{:S(2)}, u32[]{:S(2)}) %collective-permute-start.58) | collective-permute-done | bytes 589856 | tf_op jit(solution)/shard_map/ppermute | solution.py:138
  214.1 8.1 %collective-permute-done.59.refs_2_ = bf16[384,768]{1,0:T(8,128)(2,1)S(1)} collective-permute-done((bf16[384,768]{1,0:T(8,128)(2,1)S(1)}, bf16[384,768]{1,0:T(8,128)(2,1)S(1)}, u32[]{:S(2)}, u32[]{:S(2)}) %collective-permute-start.59) | collective-permute-done | bytes 589856 | tf_op jit(solution)/shard_map/ppermute | solution.py:138
  (169 shorter events, 66.1 us)
Async XLA Ops:
  0.7 31.1 %collective-permute-start.4 = (bf16[3,192,768]{2,1,0:T(8,128)(2,1)}, bf16[3,192,768]{2,1,0:T(8,128)(2,1)S(1)}, u32[]{:S(2)}, u32[]{:S(2)}) collective-permute-start(bf16[3,192,768]{2,1,0:T(8,128)(2,1)} %bitcast.26), channel_id=1, source_target_pairs={{16,0},{17,1},{18,2},{19,3},{20,4},{21,5},{22,6},{23,7},{24,8},{25... | collective-permute-start | bytes 2654216 | tf_op jit(solution)/shard_map/ppermute | solution.py:144
  2.1 32.9 %collective-permute-start.8 = (bf16[192,768]{1,0:T(8,128)(2,1)}, bf16[192,768]{1,0:T(8,128)(2,1)S(1)}, u32[]{:S(2)}, u32[]{:S(2)}) collective-permute-start(bf16[192,768]{1,0:T(8,128)(2,1)} %bitcast.30), channel_id=1, source_target_pairs={{16,0},{17,1},{18,2},{19,3},{20,4},{21,5},{22,6},{23,7},{24,8},{25... | collective-permute-start | bytes 884744 | tf_op jit(solution)/shard_map/ppermute | solution.py:144
  4.1 14.7 %collective-permute-start.2 = (bf16[8,768]{1,0:T(8,128)(2,1)S(1)}, bf16[8,768]{1,0:T(8,128)(2,1)S(1)}, u32[]{:S(2)}, u32[]{:S(2)}) collective-permute-start(bf16[8,768]{1,0:T(8,128)(2,1)S(1)} %slice_bitcast_fusion.refs_2_.refs_5_), channel_id=1, source_target_pairs={{0,3},{1,2},{2,1},{3,0},{4,7},{5,6},{6,5},{7,4},{8,11},{9,10},{10,... | collective-permute-start | bytes 36872 | tf_op jit(solution)/shard_map/ppermute | solution.py:147
  9.2 9.6 %collective-permute-start.1 = (bf16[8,768]{1,0:T(8,128)(2,1)S(1)}, bf16[8,768]{1,0:T(8,128)(2,1)S(1)}, u32[]{:S(2)}, u32[]{:S(2)}) collective-permute-start(bf16[8,768]{1,0:T(8,128)(2,1)S(1)} %slice_bitcast_fusion.refs_2_.refs_5_), channel_id=1, source_target_pairs={{0,2},{1,3},{2,0},{3,1},{4,6},{5,7},{6,4},{7,5},{8,10},{9,11},{10,... | collective-permute-start | bytes 36872 | tf_op jit(solution)/shard_map/ppermute | solution.py:147
  9.2 9.6 %collective-permute-start = (bf16[8,768]{1,0:T(8,128)(2,1)S(1)}, bf16[8,768]{1,0:T(8,128)(2,1)S(1)}, u32[]{:S(2)}, u32[]{:S(2)}) collective-permute-start(bf16[8,768]{1,0:T(8,128)(2,1)S(1)} %slice_bitcast_fusion.refs_2_.refs_5_), channel_id=1, source_target_pairs={{0,1},{1,0},{2,3},{3,2},{4,5},{5,4},{6,7},{7,6},{8,9},{9,8},{10,11... | collective-permute-start | bytes 36872 | tf_op jit(solution)/shard_map/ppermute | solution.py:147
  21.4 10.4 %collective-permute-start.5 = (f32[8,768]{1,0:T(8,128)S(1)}, f32[8,768]{1,0:T(8,128)S(1)}, u32[]{:S(2)}, u32[]{:S(2)}) collective-permute-start(f32[8,768]{1,0:T(8,128)S(1)} %get-tuple-element.241.refs_8_.refs_7_.refs_12_), channel_id=1, source_target_pairs={{16,0},{17,1},{18,2},{19,3},{20,4},{21,5},{22,6},{23,7},{24,8},{25... | collective-permute-start | bytes 73736 | tf_op jit(solution)/shard_map/ppermute | solution.py:144
  22.7 10.6 %collective-permute-start.6 = (f32[8,768]{1,0:T(8,128)S(1)}, f32[8,768]{1,0:T(8,128)S(1)}, u32[]{:S(2)}, u32[]{:S(2)}) collective-permute-start(f32[8,768]{1,0:T(8,128)S(1)} %get-tuple-element.250.refs_1_), channel_id=1, source_target_pairs={{0,8},{4,12},{8,0},{12,4},{1,9},{5,13},{9,1},{13,5},{2,10},{6,14},... | collective-permute-start | bytes 73736 | tf_op jit(solution)/shard_map/ppermute | solution.py:129
  39.8 10.2 %collective-permute-start.11 = (bf16[208,768]{1,0:T(8,128)(2,1)S(1)}, bf16[208,768]{1,0:T(8,128)(2,1)S(1)}, u32[]{:S(2)}, u32[]{:S(2)}) collective-permute-start(bf16[208,768]{1,0:T(8,128)(2,1)S(1)} %get-tuple-element.282), channel_id=1, source_target_pairs={{0,8},{4,12},{8,0},{12,4},{1,9},{5,13},{9,1},{13,5},{2,10},{6,14},... | collective-permute-start | bytes 958472 | tf_op jit(solution)/shard_map/ppermute | solution.py:129
  43.3 6.6 %collective-permute-start.10 = (bf16[208,768]{1,0:T(8,128)(2,1)S(1)}, bf16[208,768]{1,0:T(8,128)(2,1)S(1)}, u32[]{:S(2)}, u32[]{:S(2)}) collective-permute-start(bf16[208,768]{1,0:T(8,128)(2,1)S(1)} %get-tuple-element.281), channel_id=1, source_target_pairs={{0,4},{4,0},{8,12},{12,8},{1,5},{5,1},{9,13},{13,9},{2,6},{6,2},{1... | collective-permute-start | bytes 958472 | tf_op jit(solution)/shard_map/ppermute | solution.py:129
  50.4 10.0 %collective-permute-start.13 = (bf16[208,768]{1,0:T(8,128)(2,1)S(1)}, bf16[208,768]{1,0:T(8,128)(2,1)S(1)}, u32[]{:S(2)}, u32[]{:S(2)}) collective-permute-start(bf16[208,768]{1,0:T(8,128)(2,1)S(1)} %get-tuple-element.289.refs_1_), channel_id=1, source_target_pairs={{0,8},{4,12},{8,0},{12,4},{1,9},{5,13},{9,1},{13,5},{2,10},{6,14},... | collective-permute-start | bytes 958472 | tf_op jit(solution)/shard_map/ppermute | solution.py:129
  63.3 7.9 %collective-permute-start.16 = (bf16[208,768]{1,0:T(8,128)(2,1)S(1)}, bf16[208,768]{1,0:T(8,128)(2,1)S(1)}, u32[]{:S(2)}, u32[]{:S(2)}) collective-permute-start(bf16[208,768]{1,0:T(8,128)(2,1)S(1)} %get-tuple-element.318), channel_id=1, source_target_pairs={{0,4},{4,0},{8,12},{12,8},{1,5},{5,1},{9,13},{13,9},{2,6},{6,2},{1... | collective-permute-start | bytes 958472 | tf_op jit(solution)/shard_map/ppermute | solution.py:129
  64.9 9.6 %collective-permute-start.17 = (bf16[208,768]{1,0:T(8,128)(2,1)S(1)}, bf16[208,768]{1,0:T(8,128)(2,1)S(1)}, u32[]{:S(2)}, u32[]{:S(2)}) collective-permute-start(bf16[208,768]{1,0:T(8,128)(2,1)S(1)} %get-tuple-element.319), channel_id=1, source_target_pairs={{0,8},{4,12},{8,0},{12,4},{1,9},{5,13},{9,1},{13,5},{2,10},{6,14},... | collective-permute-start | bytes 958472 | tf_op jit(solution)/shard_map/ppermute | solution.py:129
  66.7 16.5 %collective-permute-start.19 = (bf16[384,768]{1,0:T(8,128)(2,1)S(1)}, bf16[384,768]{1,0:T(8,128)(2,1)S(1)}, u32[]{:S(2)}, u32[]{:S(2)}) collective-permute-start(bf16[384,768]{1,0:T(8,128)(2,1)S(1)} %get-tuple-element.334), channel_id=1, source_target_pairs={{0,16},{16,0},{1,17},{17,1},{2,18},{18,2},{3,19},{19,3},{4,20},{20... | collective-permute-start | bytes 1769480 | tf_op jit(solution)/shard_map/ppermute | solution.py:138
  75.3 5.9 %collective-permute-start.18 = (bf16[208,768]{1,0:T(8,128)(2,1)S(1)}, bf16[208,768]{1,0:T(8,128)(2,1)S(1)}, u32[]{:S(2)}, u32[]{:S(2)}) collective-permute-start(bf16[208,768]{1,0:T(8,128)(2,1)S(1)} %get-tuple-element.322.refs_1_.refs_7_), channel_id=1, source_target_pairs={{0,4},{4,0},{8,12},{12,8},{1,5},{5,1},{9,13},{13,9},{2,6},{6,2},{1... | collective-permute-start | bytes 958472 | tf_op jit(solution)/shard_map/ppermute | solution.py:129
  75.4 10.0 %collective-permute-start.20 = (bf16[208,768]{1,0:T(8,128)(2,1)S(1)}, bf16[208,768]{1,0:T(8,128)(2,1)S(1)}, u32[]{:S(2)}, u32[]{:S(2)}) collective-permute-start(bf16[208,768]{1,0:T(8,128)(2,1)S(1)} %get-tuple-element.322.refs_1_.refs_7_), channel_id=1, source_target_pairs={{0,8},{4,12},{8,0},{12,4},{1,9},{5,13},{9,1},{13,5},{2,10},{6,14},... | collective-permute-start | bytes 958472 | tf_op jit(solution)/shard_map/ppermute | solution.py:129
  77.2 17.8 %collective-permute-start.21 = (bf16[384,768]{1,0:T(8,128)(2,1)S(1)}, bf16[384,768]{1,0:T(8,128)(2,1)S(1)}, u32[]{:S(2)}, u32[]{:S(2)}) collective-permute-start(bf16[384,768]{1,0:T(8,128)(2,1)S(1)} %get-tuple-element.350), channel_id=1, source_target_pairs={{0,16},{16,0},{1,17},{17,1},{2,18},{18,2},{3,19},{19,3},{4,20},{20... | collective-permute-start | bytes 1769480 | tf_op jit(solution)/shard_map/ppermute | solution.py:138
  85.4 9.9 %collective-permute-start.22 = (bf16[208,768]{1,0:T(8,128)(2,1)S(1)}, bf16[208,768]{1,0:T(8,128)(2,1)S(1)}, u32[]{:S(2)}, u32[]{:S(2)}) collective-permute-start(bf16[208,768]{1,0:T(8,128)(2,1)S(1)} %get-tuple-element.344.refs_1_.refs_8_), channel_id=1, source_target_pairs={{0,4},{4,0},{8,12},{12,8},{1,5},{5,1},{9,13},{13,9},{2,6},{6,2},{1... | collective-permute-start | bytes 958472 | tf_op jit(solution)/shard_map/ppermute | solution.py:129
  98.3 47.0 %collective-permute-start.34 = (bf16[384,768]{1,0:T(8,128)(2,1)S(1)}, bf16[384,768]{1,0:T(8,128)(2,1)S(1)}, u32[]{:S(2)}, u32[]{:S(2)}) collective-permute-start(bf16[384,768]{1,0:T(8,128)(2,1)S(1)} %get-tuple-element.401), channel_id=1, source_target_pairs={{0,16},{16,0},{1,17},{17,1},{2,18},{18,2},{3,19},{19,3},{4,20},{20... | collective-permute-start | bytes 1769480 | tf_op jit(solution)/shard_map/ppermute | solution.py:138
  102.7 20.1 %collective-permute-start.28 = (bf16[2,2,208,192]{3,2,1,0:T(8,128)(2,1)S(1)}, bf16[2,2,208,192]{3,2,1,0:T(8,128)(2,1)S(1)}, u32[]{:S(2)}, u32[]{:S(2)}) collective-permute-start(bf16[2,2,208,192]{3,2,1,0:T(8,128)(2,1)S(1)} %get-tuple-element.389), channel_id=1, source_target_pairs={{0,4},{4,0},{8,12},{12,8},{1,5},{5,1},{9,13},{13,9},{2,6},{6,2},{1... | collective-permute-start | bytes 958472 | tf_op jit(solution)/shard_map/ppermute | solution.py:129
  102.9 8.6 %collective-permute-start.25 = (bf16[96,768]{1,0:T(8,128)(2,1)S(1)}, bf16[96,768]{1,0:T(8,128)(2,1)S(1)}, u32[]{:S(2)}, u32[]{:S(2)}) collective-permute-start(bf16[96,768]{1,0:T(8,128)(2,1)S(1)} %get-tuple-element.384), channel_id=1, source_target_pairs={{0,1},{1,0},{2,3},{3,2},{4,5},{5,4},{6,7},{7,6},{8,9},{9,8},{10,11... | collective-permute-start | bytes 442376 | tf_op jit(solution)/shard_map/ppermute | solution.py:147
  104.5 19.8 %collective-permute-start.29 = (bf16[2,2,208,192]{3,2,1,0:T(8,128)(2,1)S(1)}, bf16[2,2,208,192]{3,2,1,0:T(8,128)(2,1)S(1)}, u32[]{:S(2)}, u32[]{:S(2)}) collective-permute-start(bf16[2,2,208,192]{3,2,1,0:T(8,128)(2,1)S(1)} %get-tuple-element.391), channel_id=1, source_target_pairs={{0,4},{4,0},{8,12},{12,8},{1,5},{5,1},{9,13},{13,9},{2,6},{6,2},{1... | collective-permute-start | bytes 958472 | tf_op jit(solution)/shard_map/ppermute | solution.py:129
  104.5 12.3 %collective-permute-start.26 = (bf16[96,768]{1,0:T(8,128)(2,1)S(1)}, bf16[96,768]{1,0:T(8,128)(2,1)S(1)}, u32[]{:S(2)}, u32[]{:S(2)}) collective-permute-start(bf16[96,768]{1,0:T(8,128)(2,1)S(1)} %get-tuple-element.385), channel_id=1, source_target_pairs={{0,2},{1,3},{2,0},{3,1},{4,6},{5,7},{6,4},{7,5},{8,10},{9,11},{10,... | collective-permute-start | bytes 442376 | tf_op jit(solution)/shard_map/ppermute | solution.py:147
  111.4 7.6 %collective-permute-start.27 = (bf16[96,768]{1,0:T(8,128)(2,1)S(1)}, bf16[96,768]{1,0:T(8,128)(2,1)S(1)}, u32[]{:S(2)}, u32[]{:S(2)}) collective-permute-start(bf16[96,768]{1,0:T(8,128)(2,1)S(1)} %get-tuple-element.386), channel_id=1, source_target_pairs={{0,3},{1,2},{2,1},{3,0},{4,7},{5,6},{6,5},{7,4},{8,11},{9,10},{10,... | collective-permute-start | bytes 442376 | tf_op jit(solution)/shard_map/ppermute | solution.py:147
  119.0 11.9 %collective-permute-start.31 = (bf16[96,768]{1,0:T(8,128)(2,1)S(1)}, bf16[96,768]{1,0:T(8,128)(2,1)S(1)}, u32[]{:S(2)}, u32[]{:S(2)}) collective-permute-start(bf16[96,768]{1,0:T(8,128)(2,1)S(1)} %get-tuple-element.396), channel_id=1, source_target_pairs={{0,1},{1,0},{2,3},{3,2},{4,5},{5,4},{6,7},{7,6},{8,9},{9,8},{10,11... | collective-permute-start | bytes 442376 | tf_op jit(solution)/shard_map/ppermute | solution.py:147
  121.7 18.2 %collective-permute-start.32 = (bf16[96,768]{1,0:T(8,128)(2,1)S(1)}, bf16[96,768]{1,0:T(8,128)(2,1)S(1)}, u32[]{:S(2)}, u32[]{:S(2)}) collective-permute-start(bf16[96,768]{1,0:T(8,128)(2,1)S(1)} %get-tuple-element.397), channel_id=1, source_target_pairs={{0,2},{1,3},{2,0},{3,1},{4,6},{5,7},{6,4},{7,5},{8,10},{9,11},{10,... | collective-permute-start | bytes 442376 | tf_op jit(solution)/shard_map/ppermute | solution.py:147
  122.7 17.2 %collective-permute-start.33 = (bf16[96,768]{1,0:T(8,128)(2,1)S(1)}, bf16[96,768]{1,0:T(8,128)(2,1)S(1)}, u32[]{:S(2)}, u32[]{:S(2)}) collective-permute-start(bf16[96,768]{1,0:T(8,128)(2,1)S(1)} %get-tuple-element.398), channel_id=1, source_target_pairs={{0,3},{1,2},{2,1},{3,0},{4,7},{5,6},{6,5},{7,4},{8,11},{9,10},{10,... | collective-permute-start | bytes 442376 | tf_op jit(solution)/shard_map/ppermute | solution.py:147
  128.5 19.2 %collective-permute-start.37 = (bf16[32,768]{1,0:T(8,128)(2,1)S(1)}, bf16[32,768]{1,0:T(8,128)(2,1)S(1)}, u32[]{:S(2)}, u32[]{:S(2)}) collective-permute-start(bf16[32,768]{1,0:T(8,128)(2,1)S(1)} %get-tuple-element.404.refs_1_), channel_id=1, source_target_pairs={{0,3},{1,2},{2,1},{3,0},{4,7},{5,6},{6,5},{7,4},{8,11},{9,10},{10,... | collective-permute-start | bytes 147464 | tf_op jit(solution)/shard_map/ppermute | solution.py:147
  130.8 25.3 %collective-permute-start.40 = (bf16[96,768]{1,0:T(8,128)(2,1)S(1)}, bf16[96,768]{1,0:T(8,128)(2,1)S(1)}, u32[]{:S(2)}, u32[]{:S(2)}) collective-permute-start(bf16[96,768]{1,0:T(8,128)(2,1)S(1)} %get-tuple-element.410.refs_1_), channel_id=1, source_target_pairs={{0,3},{1,2},{2,1},{3,0},{4,7},{5,6},{6,5},{7,4},{8,11},{9,10},{10,... | collective-permute-start | bytes 442376 | tf_op jit(solution)/shard_map/ppermute | solution.py:147
  139.9 16.2 %collective-permute-start.39 = (bf16[96,768]{1,0:T(8,128)(2,1)S(1)}, bf16[96,768]{1,0:T(8,128)(2,1)S(1)}, u32[]{:S(2)}, u32[]{:S(2)}) collective-permute-start(bf16[96,768]{1,0:T(8,128)(2,1)S(1)} %get-tuple-element.410.refs_1_), channel_id=1, source_target_pairs={{0,2},{1,3},{2,0},{3,1},{4,6},{5,7},{6,4},{7,5},{8,10},{9,11},{10,... | collective-permute-start | bytes 442376 | tf_op jit(solution)/shard_map/ppermute | solution.py:147
  139.9 16.2 %collective-permute-start.38 = (bf16[96,768]{1,0:T(8,128)(2,1)S(1)}, bf16[96,768]{1,0:T(8,128)(2,1)S(1)}, u32[]{:S(2)}, u32[]{:S(2)}) collective-permute-start(bf16[96,768]{1,0:T(8,128)(2,1)S(1)} %get-tuple-element.410.refs_1_), channel_id=1, source_target_pairs={{0,1},{1,0},{2,3},{3,2},{4,5},{5,4},{6,7},{7,6},{8,9},{9,8},{10,11... | collective-permute-start | bytes 442376 | tf_op jit(solution)/shard_map/ppermute | solution.py:147
  145.3 8.8 %collective-permute-start.36 = (bf16[32,768]{1,0:T(8,128)(2,1)S(1)}, bf16[32,768]{1,0:T(8,128)(2,1)S(1)}, u32[]{:S(2)}, u32[]{:S(2)}) collective-permute-start(bf16[32,768]{1,0:T(8,128)(2,1)S(1)} %get-tuple-element.404.refs_1_), channel_id=1, source_target_pairs={{0,2},{1,3},{2,0},{3,1},{4,6},{5,7},{6,4},{7,5},{8,10},{9,11},{10,... | collective-permute-start | bytes 147464 | tf_op jit(solution)/shard_map/ppermute | solution.py:147
  147.7 6.4 %collective-permute-start.35 = (bf16[32,768]{1,0:T(8,128)(2,1)S(1)}, bf16[32,768]{1,0:T(8,128)(2,1)S(1)}, u32[]{:S(2)}, u32[]{:S(2)}) collective-permute-start(bf16[32,768]{1,0:T(8,128)(2,1)S(1)} %get-tuple-element.404.refs_1_), channel_id=1, source_target_pairs={{0,1},{1,0},{2,3},{3,2},{4,5},{5,4},{6,7},{7,6},{8,9},{9,8},{10,11... | collective-permute-start | bytes 147464 | tf_op jit(solution)/shard_map/ppermute | solution.py:147
  154.1 6.9 %collective-permute-start.43 = (bf16[2,2,208,192]{3,2,1,0:T(8,128)(2,1)S(1)}, bf16[2,2,208,192]{3,2,1,0:T(8,128)(2,1)S(1)}, u32[]{:S(2)}, u32[]{:S(2)}) collective-permute-start(bf16[2,2,208,192]{3,2,1,0:T(8,128)(2,1)S(1)} %get-tuple-element.417), channel_id=1, source_target_pairs={{0,4},{4,0},{8,12},{12,8},{1,5},{5,1},{9,13},{13,9},{2,6},{6,2},{1... | collective-permute-start | bytes 958472 | tf_op jit(solution)/shard_map/ppermute | solution.py:129
  156.2 33.3 %collective-permute-start.52 = (bf16[384,768]{1,0:T(8,128)(2,1)S(1)}, bf16[384,768]{1,0:T(8,128)(2,1)S(1)}, u32[]{:S(2)}, u32[]{:S(2)}) collective-permute-start(bf16[384,768]{1,0:T(8,128)(2,1)S(1)} %get-tuple-element.436.refs_1_), channel_id=1, source_target_pairs={{0,16},{16,0},{1,17},{17,1},{2,18},{18,2},{3,19},{19,3},{4,20},{20... | collective-permute-start | bytes 1769480 | tf_op jit(solution)/shard_map/ppermute | solution.py:138
  156.6 8.6 %collective-permute-start.51 = (bf16[96,768]{1,0:T(8,128)(2,1)S(1)}, bf16[96,768]{1,0:T(8,128)(2,1)S(1)}, u32[]{:S(2)}, u32[]{:S(2)}) collective-permute-start(bf16[96,768]{1,0:T(8,128)(2,1)S(1)} %get-tuple-element.434.refs_1_), channel_id=1, source_target_pairs={{0,3},{1,2},{2,1},{3,0},{4,7},{5,6},{6,5},{7,4},{8,11},{9,10},{10,... | collective-permute-start | bytes 442376 | tf_op jit(solution)/shard_map/ppermute | solution.py:147
  159.1 15.7 %collective-permute-start.50 = (bf16[96,768]{1,0:T(8,128)(2,1)S(1)}, bf16[96,768]{1,0:T(8,128)(2,1)S(1)}, u32[]{:S(2)}, u32[]{:S(2)}) collective-permute-start(bf16[96,768]{1,0:T(8,128)(2,1)S(1)} %get-tuple-element.434.refs_1_), channel_id=1, source_target_pairs={{0,2},{1,3},{2,0},{3,1},{4,6},{5,7},{6,4},{7,5},{8,10},{9,11},{10,... | collective-permute-start | bytes 442376 | tf_op jit(solution)/shard_map/ppermute | solution.py:147
  159.1 15.7 %collective-permute-start.44 = (bf16[96,768]{1,0:T(8,128)(2,1)S(1)}, bf16[96,768]{1,0:T(8,128)(2,1)S(1)}, u32[]{:S(2)}, u32[]{:S(2)}) collective-permute-start(bf16[96,768]{1,0:T(8,128)(2,1)S(1)} %get-tuple-element.425), channel_id=1, source_target_pairs={{0,1},{1,0},{2,3},{3,2},{4,5},{5,4},{6,7},{7,6},{8,9},{9,8},{10,11... | collective-permute-start | bytes 442376 | tf_op jit(solution)/shard_map/ppermute | solution.py:147
  161.0 18.5 %collective-permute-start.45 = (bf16[96,768]{1,0:T(8,128)(2,1)S(1)}, bf16[96,768]{1,0:T(8,128)(2,1)S(1)}, u32[]{:S(2)}, u32[]{:S(2)}) collective-permute-start(bf16[96,768]{1,0:T(8,128)(2,1)S(1)} %get-tuple-element.426), channel_id=1, source_target_pairs={{0,2},{1,3},{2,0},{3,1},{4,6},{5,7},{6,4},{7,5},{8,10},{9,11},{10,... | collective-permute-start | bytes 442376 | tf_op jit(solution)/shard_map/ppermute | solution.py:147
  165.2 24.8 %collective-permute-start.48 = (bf16[2,2,208,192]{3,2,1,0:T(8,128)(2,1)S(1)}, bf16[2,2,208,192]{3,2,1,0:T(8,128)(2,1)S(1)}, u32[]{:S(2)}, u32[]{:S(2)}) collective-permute-start(bf16[2,2,208,192]{3,2,1,0:T(8,128)(2,1)S(1)} %get-tuple-element.431), channel_id=1, source_target_pairs={{0,8},{4,12},{8,0},{12,4},{1,9},{5,13},{9,1},{13,5},{2,10},{6,14},... | collective-permute-start | bytes 958472 | tf_op jit(solution)/shard_map/ppermute | solution.py:129
  174.8 7.0 %collective-permute-start.46 = (bf16[96,768]{1,0:T(8,128)(2,1)S(1)}, bf16[96,768]{1,0:T(8,128)(2,1)S(1)}, u32[]{:S(2)}, u32[]{:S(2)}) collective-permute-start(bf16[96,768]{1,0:T(8,128)(2,1)S(1)} %get-tuple-element.427), channel_id=1, source_target_pairs={{0,3},{1,2},{2,1},{3,0},{4,7},{5,6},{6,5},{7,4},{8,11},{9,10},{10,... | collective-permute-start | bytes 442376 | tf_op jit(solution)/shard_map/ppermute | solution.py:147
  174.8 24.6 %collective-permute-start.54 = (bf16[2,2,208,192]{3,2,1,0:T(8,128)(2,1)S(1)}, bf16[2,2,208,192]{3,2,1,0:T(8,128)(2,1)S(1)}, u32[]{:S(2)}, u32[]{:S(2)}) collective-permute-start(bf16[2,2,208,192]{3,2,1,0:T(8,128)(2,1)S(1)} %get-tuple-element.442), channel_id=1, source_target_pairs={{0,8},{4,12},{8,0},{12,4},{1,9},{5,13},{9,1},{13,5},{2,10},{6,14},... | collective-permute-start | bytes 958472 | tf_op jit(solution)/shard_map/ppermute | solution.py:129
  181.8 6.9 %collective-permute-start.47 = (bf16[48,768]{1,0:T(8,128)(2,1)S(1)}, bf16[48,768]{1,0:T(8,128)(2,1)S(1)}, u32[]{:S(2)}, u32[]{:S(2)}) collective-permute-start(bf16[48,768]{1,0:T(8,128)(2,1)S(1)} %get-tuple-element.429.refs_1_), channel_id=1, source_target_pairs={{0,8},{4,12},{8,0},{12,4},{1,9},{5,13},{9,1},{13,5},{2,10},{6,14},... | collective-permute-start | bytes 221192 | tf_op jit(solution)/shard_map/ppermute | solution.py:129
  185.0 15.4 %collective-permute-start.57 = (bf16[96,768]{1,0:T(8,128)(2,1)S(1)}, bf16[96,768]{1,0:T(8,128)(2,1)S(1)}, u32[]{:S(2)}, u32[]{:S(2)}) collective-permute-start(bf16[96,768]{1,0:T(8,128)(2,1)S(1)} %get-tuple-element.448.refs_1_), channel_id=1, source_target_pairs={{0,3},{1,2},{2,1},{3,0},{4,7},{5,6},{6,5},{7,4},{8,11},{9,10},{10,... | collective-permute-start | bytes 442376 | tf_op jit(solution)/shard_map/ppermute | solution.py:147
  188.8 11.8 %collective-permute-start.56 = (bf16[96,768]{1,0:T(8,128)(2,1)S(1)}, bf16[96,768]{1,0:T(8,128)(2,1)S(1)}, u32[]{:S(2)}, u32[]{:S(2)}) collective-permute-start(bf16[96,768]{1,0:T(8,128)(2,1)S(1)} %get-tuple-element.448.refs_1_), channel_id=1, source_target_pairs={{0,2},{1,3},{2,0},{3,1},{4,6},{5,7},{6,4},{7,5},{8,10},{9,11},{10,... | collective-permute-start | bytes 442376 | tf_op jit(solution)/shard_map/ppermute | solution.py:147
  189.6 10.9 %collective-permute-start.55 = (bf16[96,768]{1,0:T(8,128)(2,1)S(1)}, bf16[96,768]{1,0:T(8,128)(2,1)S(1)}, u32[]{:S(2)}, u32[]{:S(2)}) collective-permute-start(bf16[96,768]{1,0:T(8,128)(2,1)S(1)} %get-tuple-element.448.refs_1_), channel_id=1, source_target_pairs={{0,1},{1,0},{2,3},{3,2},{4,5},{5,4},{6,7},{7,6},{8,9},{9,8},{10,11... | collective-permute-start | bytes 442376 | tf_op jit(solution)/shard_map/ppermute | solution.py:147
  189.9 6.3 %collective-permute-start.53 = (bf16[48,768]{1,0:T(8,128)(2,1)S(1)}, bf16[48,768]{1,0:T(8,128)(2,1)S(1)}, u32[]{:S(2)}, u32[]{:S(2)}) collective-permute-start(bf16[48,768]{1,0:T(8,128)(2,1)S(1)} %get-tuple-element.438.refs_10_), channel_id=1, source_target_pairs={{0,16},{1,17},{2,18},{3,19},{4,20},{5,21},{6,22},{7,23},{8,24},{9,... | collective-permute-start | bytes 221192 | tf_op jit(solution)/shard_map/ppermute | solution.py:141
  196.2 16.3 %collective-permute-start.58 = (bf16[384,768]{1,0:T(8,128)(2,1)S(1)}, bf16[384,768]{1,0:T(8,128)(2,1)S(1)}, u32[]{:S(2)}, u32[]{:S(2)}) collective-permute-start(bf16[384,768]{1,0:T(8,128)(2,1)S(1)} %get-tuple-element.450.refs_1_), channel_id=1, source_target_pairs={{0,16},{16,0},{1,17},{17,1},{2,18},{18,2},{3,19},{19,3},{4,20},{20... | collective-permute-start | bytes 1769480 | tf_op jit(solution)/shard_map/ppermute | solution.py:138
  200.6 21.5 %collective-permute-start.59 = (bf16[384,768]{1,0:T(8,128)(2,1)S(1)}, bf16[384,768]{1,0:T(8,128)(2,1)S(1)}, u32[]{:S(2)}, u32[]{:S(2)}) collective-permute-start(bf16[384,768]{1,0:T(8,128)(2,1)S(1)} %get-tuple-element.452.refs_1_), channel_id=1, source_target_pairs={{0,16},{16,0},{1,17},{17,1},{2,18},{18,2},{3,19},{19,3},{4,20},{20... | collective-permute-start | bytes 1769480 | tf_op jit(solution)/shard_map/ppermute | solution.py:138
  (29 other events, 121.7 us)

commit v3 on v2

v3 whole, which is shorter than its diff:
```python
import functools

import jax
import jax.numpy as jnp
from jax import lax
from jax.experimental import pallas as pl
from jax.experimental.pallas import tpu as pltpu
from jax.sharding import PartitionSpec as P

HEAD_DIM = 64
EPSILON = 1e-05
QUICK_GELU = 1.702
F32 = jnp.float32
BF16 = jnp.bfloat16
VMEM_BYTES = 16 * 1024 * 1024


def nn(left, right):
    return lax.dot_general(left, right, (((1,), (0,)), ((), ())), preferred_element_type=F32)


def nt(left, right):
    return lax.dot_general(left, right, (((1,), (1,)), ((), ())), preferred_element_type=F32)


def tn(left, right):
    return lax.dot_general(left, right, (((0,), (0,)), ((), ())), preferred_element_type=F32)


def norm_parts(values_in):
    centred = values_in - jnp.mean(values_in, axis=-1, keepdims=True)
    inverse = lax.rsqrt(jnp.mean(centred * centred, axis=-1, keepdims=True) + EPSILON)
    return centred * inverse, inverse


def norm_back(incoming, normed, inverse, gain):
    weighted = incoming * gain
    centred = weighted - jnp.mean(weighted, axis=-1, keepdims=True)
    return inverse * (centred - normed * jnp.mean(weighted * normed, axis=-1, keepdims=True))


def row_sum(values_in):
    return jnp.sum(values_in, axis=0, keepdims=True)


def shape_of(shape, kind):
    return jax.ShapeDtypeStruct(shape, kind)


def near(shape, kind):
    return pltpu.VMEM(shape, kind)


class Chain:
    def __init__(self):
        self.token = None
        self.near, self.kept = set(), []
        self.cost = 4 * 10**9

    def __call__(self, kernel, ins, outs, scratch=(), flops=0, far=0):
        tokens = 0 if self.token is None else 1
        count, given = len(ins), len(outs)

        def stage(*refs):
            rest = refs[tokens:]
            kernel(*rest[:count], *rest[count : count + given], *rest[count + given + 1 :])

        vmem = pl.BlockSpec(memory_space=pltpu.VMEM)
        held = [] if self.token is None else [self.token]
        ins = [
            pltpu.with_memory_space_constraint(a, pltpu.HBM)
            if i < far
            else pltpu.with_memory_space_constraint(a, pltpu.VMEM)
            if id(a) in self.near
            else a
            for i, a in enumerate(ins)
        ]
        results = pl.pallas_call(
            stage,
            out_shape=[*outs, near((8, 128), F32)],
            in_specs=[pl.BlockSpec(memory_space=pl.ANY)] * tokens
            + [pl.BlockSpec(memory_space=pltpu.HBM)] * far
            + [vmem] * (count - far),
            out_specs=[vmem] * (given + 1),
            scratch_shapes=list(scratch),
            compiler_params=pltpu.CompilerParams(vmem_limit_bytes=VMEM_BYTES),
            cost_estimate=pl.CostEstimate(flops=self.cost, bytes_accessed=0, transcendentals=0),
        )(*held, *ins)
        self.token = results[-1]
        self.kept += results
        for out, result in zip(outs, results):
            if not isinstance(out, jax.ShapeDtypeStruct):
                self.near.add(id(result))
        return results[:-1]


def body(
    frames,
    video_group,
    msg_w,
    msg_bias,
    norm_gain,
    norm_shift,
    attn_in,
    qv_bias,
    attn_out,
    out_bias,
    norm2_gain,
    norm2_shift,
    fc_in,
    fc_in_bias,
    fc_out,
    fc_out_bias,
    cotangent,
):
    _, frame_count, patch, model = frames.shape

    width = attn_in.shape[-1]

    hidden_width = fc_in.shape[-1]

    heads = width // HEAD_DIM

    clips = lax.axis_size("dp")

    half = frame_count // 2

    rows = -(-(patch + 1) // 16) * 16

    all_rows = clips * frame_count

    scale = HEAD_DIM ** (-0.5)

    pipe = lax.axis_index("pipe")

    tensor = lax.axis_index("tensor")

    clip = lax.axis_index("dp")

    ring = clips == 4

    stage = Chain()

    quarter = hidden_width // 4

    assert quarter == width and hidden_width == model and half == 4

    def tensor_swap(v, bit):
        return lax.ppermute(v, "tensor", [(i, i ^ bit) for i in range(4)])

    def core_swap(v):
        return tensor_swap(v, 1)

    def x_swap(v):
        return tensor_swap(v, 2)

    def y_swap(v):
        return lax.ppermute(v, "pipe", [(0, 1), (1, 0)])

    def y_late(v):
        return lax.ppermute(v, "pipe", [(0, 1)])

    def y_early(v):
        return lax.ppermute(v, "pipe", [(1, 0)])

    def z_swap(v, bit):
        return lax.ppermute(v, "dp", [(i, i ^ bit) for i in range(clips)])

    def gather_clips(v):
        if ring:
            return [v] + [z_swap(v, apart) for apart in range(1, clips)]
        every = lax.all_gather(v, "dp")
        every = lax.dynamic_slice_in_dim(jnp.concatenate([every, every]), clip, clips, 0)
        return [every.reshape(clips * v.shape[0], v.shape[1])]

    def clip_block(refs, c, size):
        each = clips // len(refs)
        at = c % each * size
        return refs[c // each][at : at + size, :]

    blocks = clips if ring else 1

    pack_blocks = 2 if ring else 1

    def head_masks(n):
        lane = lax.broadcasted_iota(jnp.int32, (n, width), 1)
        return [(lane >= h * HEAD_DIM) & (lane < (h + 1) * HEAD_DIM) for h in range(heads)]

    def only(mask, v):
        return jnp.where(mask, v, jnp.zeros_like(v))

    def add(*terms):
        total = terms[0].astype(F32)
        for term in terms[1:]:
            total = total + term.astype(F32)
        return total

    def adds(*groups):
        sizes = [len(group) for group in groups]

        def kernel(*refs):
            at = 0
            for size, out in zip(sizes, refs[sum(sizes) :]):
                out[...] = add(*[ref[...] for ref in refs[at : at + size]]).astype(out.dtype)
                at += size

        return stage(
            kernel,
            [array for group in groups for array in group],
            [near(group[0].shape, group[0].dtype) for group in groups],
        )

    own_in = jnp.transpose(attn_in[0], (1, 2, 0))

    own_out = attn_out[0]

    tokens = jnp.transpose(frames[0], (1, 0, 2))

    grads_in = jnp.transpose(cotangent[0], (1, 0, 2))

    def small_kernel(*refs):
        ins, vecs_o, own_o, in_o, both_o = refs[:10], *refs[10:14]
        lines, rest, sem = refs[14:19], refs[19:23], refs[23]
        pairs = [(ins[0], in_o)] + list(zip(ins[1:], (*lines, *rest)))
        pairs += [(ins[0].at[c], both_o.at[c * width : (c + 1) * width]) for c in range(3)]
        copies = [pltpu.make_async_copy(a, b, sem.at[i]) for i, (a, b) in enumerate(pairs)]
        for copy in copies:
            copy.start()
        for copy in copies:
            copy.wait()
        for i, line in enumerate(lines):
            vecs_o[i : i + 1, :] = line[...].reshape(1, model)
        for i, line in enumerate(rest[:3]):
            own_o[i : i + 1, :] = line[...]
        own_o[3:8, :] = jnp.zeros((5, model), F32)
        own_o[3:5, 0:width] = rest[3][0]
        high = own_o[...].astype(BF16).astype(F32)
        both_o[3 * width :, :] = jnp.concatenate([high, own_o[...] - high], axis=0).astype(BF16)

    def load_kernel(*refs):
        sem = refs[4]
        copies = [
            pltpu.make_async_copy(a, b, sem.at[i]) for i, (a, b) in enumerate(zip(refs[:2], refs[2:4]))
        ]
        for copy in copies:
            copy.start()
        for copy in copies:
            copy.wait()

    tokens_all = rows * frame_count

    lanes = 128

    def slot_kernel(v, *refs):
        outs, (wide, held, sem) = refs[:-3], refs[-3:]
        copy = pltpu.make_async_copy(v, held, sem)
        copy.start()
        copy.wait()
        flat = held[...].astype(F32).reshape(patch * frame_count, model)
        sec, ten = lax.axis_index("pipe"), lax.axis_index("tensor")
        for c in range(model // lanes):
            at = c * tokens_all
            wide[at : at + patch * frame_count, :] = flat[:, c * lanes : (c + 1) * lanes]
            wide[at + patch * frame_count : at + tokens_all, :] = jnp.zeros(
                ((rows - patch) * frame_count, lanes), F32
            )
            for s, out in enumerate(outs):
                frame = at + (sec if s < half else 1 - sec) * half + (ten ^ (s % half))
                out[:, c * lanes : (c + 1) * lanes] = wide[
                    pl.ds(frame, rows, stride=frame_count), :
                ].astype(BF16)

    def slots(v, count):
        return stage(
            slot_kernel,
            [v],
            [near((rows, model), BF16)] * count,
            [
                pltpu.VMEM((model // lanes * tokens_all, lanes), F32),
                pltpu.VMEM((patch, frame_count, model), BF16),
                pltpu.SemaphoreType.DMA,
            ],
            far=1,
        )

    def message_forward(groups, *refs):
        cls_refs, refs = refs[:blocks], refs[blocks:]
        (mw, vecs, vrow, w, wo, first_o, low_o, q_o, k_o, v_o, probs_o, mixed_o, part_o, ids, sem) = refs
        copy = pltpu.make_async_copy(groups, ids, sem)
        copy.start()
        cls = jnp.concatenate([clip_block(cls_refs, c, frame_count).astype(F32) for c in range(clips)])
        first = nn(cls.astype(BF16), mw[...]) + vecs[0:1]
        first_o[...] = first
        normed, _ = norm_parts(first)
        low = (normed * vrow[0:1] + vrow[1:2]).astype(BF16)
        low_o[...] = low
        q = (nt(low, w[0]) + vrow[3:4, :width]).astype(BF16)
        k = nt(low, w[1]).astype(BF16)
        v = (nt(low, w[2]) + vrow[4:5, :width]).astype(BF16)
        q_o[...] = q
        k_o[...] = k
        v_o[...] = v
        of_row = lax.broadcasted_iota(jnp.int32, (all_rows, all_rows), 0) // frame_count
        of_col = lax.broadcasted_iota(jnp.int32, (all_rows, all_rows), 1) // frame_count
        mine = lax.axis_index("dp")
        copy.wait()
        row_id = jnp.zeros((all_rows, all_rows), jnp.int32)
        col_id = jnp.zeros((all_rows, all_rows), jnp.int32)
        for c in range(clips):
            mark = ids[mine ^ c if ring else lax.rem(mine + c, clips)]
            row_id = jnp.where(of_row == c, mark, row_id)
            col_id = jnp.where(of_col == c, mark, col_id)
        allowed = row_id == col_id
        mixed = jnp.zeros((all_rows, width), F32)
        for h, mask in enumerate(head_masks(all_rows)):
            scores = jnp.where(allowed, nt(only(mask, q), k) * scale, -jnp.inf)
            exponent = jnp.exp(scores - jnp.max(scores, axis=-1, keepdims=True))
            probs = exponent / jnp.sum(exponent, axis=-1, keepdims=True)
            probs_o[h] = probs
            mixed = mixed + only(mask, nn(probs.astype(BF16), v))
        mixed = mixed.astype(BF16)
        mixed_o[...] = mixed
        part = nn(mixed, wo[...]) + jnp.where(lax.axis_index("tensor") == 0, vrow[2:3], 0.0)
        part_o[...] = part[:frame_count]

    def project_kernel(x0, x1, x2, x3, wa, wb, va, w, vrow, *outs):
        early = lax.axis_index("pipe") == 0
        for c in range(3):
            w[c] = jnp.where(early, wb[c * width : (c + 1) * width, :], wa[c])
        sent = wb[3 * width :, :].astype(F32)
        vrow[...] = jnp.where(early, sent[0:8] + sent[8:16], va[...])
        gain, shift = vrow[0:1], vrow[1:2]
        for s, x in enumerate((x0, x1, x2, x3)):
            normed, _ = norm_parts(x[...].astype(F32))
            low = (normed * gain + shift).astype(BF16)
            outs[s][...] = (nt(low, w[0]) + vrow[3:4, :width]).astype(BF16)
            outs[half + s][...] = nt(low, w[1]).astype(BF16)
            outs[2 * half + s][...] = (nt(low, w[2]) + vrow[4:5, :width]).astype(BF16)

    def message_rows_kernel(first, part, late, w, vrow, wa, wb, msg_o, k_o, v_o, w_o):
        sec, ten = lax.axis_index("pipe"), lax.axis_index("tensor")
        w_o[...] = jnp.where(sec == 0, wb[...], wa[...])
        msg_o[...] = jnp.zeros_like(msg_o)
        for s in range(half):
            at = pl.ds(sec * half + (ten ^ s), 1)
            summed = jnp.where(sec == 0, part[at, :], late[at, :])
            msg_o[s : s + 1, :] = (first[at, :] + summed).astype(BF16).astype(F32)
        normed, _ = norm_parts(msg_o[...])
        low = (normed * vrow[0:1] + vrow[1:2]).astype(BF16)
        k_o[...] = nt(low, w[1])
        v_o[...] = nt(low, w[2]) + vrow[4:5, :width]

    def attend_kernel(
        s, q, k, v, km, vm, wo, part_o, mixed_o, probs_o, k_o, v_o,
    ):
        here = lax.broadcasted_iota(jnp.int32, (rows, width), 0) == patch
        key_here = lax.broadcasted_iota(jnp.int32, (rows, rows), 1) <= patch
        kk = jnp.where(here, km[s : s + 1], k[...].astype(F32)).astype(BF16)
        vv = jnp.where(here, vm[s : s + 1], v[...].astype(F32)).astype(BF16)
        k_o[...] = kk
        v_o[...] = vv
        mixed = jnp.zeros((rows, width), F32)
        for h, mask in enumerate(head_masks(rows)):
            scores = nt(only(mask, q[...]), kk) * scale
            scores = jnp.where(key_here, scores, -jnp.inf)
            exponent = jnp.exp(scores - jnp.max(scores, axis=-1, keepdims=True))
            probs = exponent * (1.0 / jnp.sum(exponent, axis=-1, keepdims=True))
            probs = probs.astype(BF16)
            probs_o[h] = probs
            mixed = mixed + only(mask, nn(probs, vv))
        mixed = mixed.astype(BF16)
        mixed_o[...] = mixed
        part_o[...] = nn(mixed, wo[...]).astype(BF16)

    def attend(s):
        return stage(
            functools.partial(attend_kernel, s),
            [q_one[s], k_patch[s], v_patch[s], k_msg, v_msg, w_out],
            [
                near((rows, model), BF16),
                near((rows, width), BF16),
                near((heads, rows, rows), BF16),
                near((rows, width), BF16),
                near((rows, width), BF16),
            ],
            flops=2 * rows * (width * model + 2 * heads * rows * HEAD_DIM),
        )

    def residual_kernel(a, b, x, vrow, vecs, resid_o, low_o):
        resid = x[...].astype(F32) + add(a[...], b[...]) + vrow[2:3]
        resid_o[...] = resid
        normed, _ = norm_parts(resid)
        low_o[...] = (normed * vecs[1:2] + vecs[2:3]).astype(BF16)

    def relay_kernel(v, out):
        out[...] = v[...]

    def relay(v):
        return stage(relay_kernel, [v], [near(v.shape, v.dtype)])[0]

    def grad_hidden_kernel(g0, g1, g2, g3, w, *outs):
        for g, out in zip((g0, g1, g2, g3), outs):
            out[...] = nt(g[...], w[...]).astype(BF16)

    def feed_kernel(low, gh, w, vecs, hid_o, pre_o, grad_o, bias_o):
        hidden_in = nn(low[...], w[...]) + vecs[3:4]
        sig = 1.0 / (1.0 + jnp.exp(-QUICK_GELU * hidden_in))
        hid_o[...] = (hidden_in * sig).astype(BF16)
        slope = sig + QUICK_GELU * hidden_in * sig * (1.0 - sig)
        pre = (gh[...].astype(F32) * slope).astype(BF16)
        pre_o[...] = pre
        grad_o[...] = nt(pre, w[...]).astype(BF16)
        bias_o[...] = row_sum(pre.astype(F32))

    def feed(low, gh):
        return stage(
            feed_kernel, [low, gh, fc_in, vectors],
            [
                near((rows, hidden_width), BF16),
                near((rows, hidden_width), BF16),
                near((rows, model), BF16),
                near((1, hidden_width), F32),
            ],
            flops=2 * 2 * rows * model * hidden_width,
        )

    half_rows, eighth = model // 2, model // 8

    def halves_of(acc, keep, send):
        sec = lax.axis_index("pipe")
        for out, at in ((keep, sec), (send, 1 - sec)):
            start = pl.multiple_of(at * half_rows, half_rows)
            out[...] = acc[pl.ds(start, half_rows), :].astype(BF16)

    half_shapes = [near((half_rows, model), BF16)] * 2

    def section_columns():
        return pl.ds(pl.multiple_of(lax.axis_index("pipe") * half_rows, half_rows), half_rows)

    def feed_other_kernel(low, g, w, w_out, vecs, hid_o, pre_o):
        columns = section_columns()
        hidden_in = nn(low[...], w[:, columns]) + vecs[3:4, columns]
        sig = 1.0 / (1.0 + jnp.exp(-QUICK_GELU * hidden_in))
        hid_o[...] = (hidden_in * sig).astype(BF16)
        slope = sig + QUICK_GELU * hidden_in * sig * (1.0 - sig)
        pre_o[...] = (nt(g[...], w_out[columns, :]).astype(BF16).astype(F32) * slope).astype(BF16)

    def feed_other(low, g):
        return stage(
            feed_other_kernel, [low, g, fc_in, fc_out, vectors],
            [near((rows, half_rows), BF16)] * 2,
        )

    def own_out_kernel(h0, h1, g0, g1, out):
        out[...] = tn(h0[:, section_columns()], g0[...])
        out[...] += tn(h1[:, section_columns()], g1[...])

    def own_in_kernel(l0, l1, p0, p1, out):
        out[...] = tn(l0[...], p0[:, section_columns()])
        out[...] += tn(l1[...], p1[:, section_columns()])

    def own_part(kernel, shape, *ins):
        return stage(kernel, list(ins), [near(shape, F32)])[0]

    def clip_parts(acc, mine, send):
        size = mine.shape[0] // 2
        for out, first in ((mine, 0), (send, 1)):
            for at, apart in ((0, first), (size, first ^ 2)):
                out[at : at + size, :] = acc[clip_rows(apart, size), :].astype(BF16)

    def sum_out_kernel(part, h2, h3, g2, g3, o0, o1, o2, o3, q0, q1, q2, q3, mine, send, acc):
        acc[...] = part[...] + tn(h2[:, section_columns()], g2[...])
        acc[...] += tn(h3[:, section_columns()], g3[...])
        for o, q in ((o0, q0), (o1, q1), (o2, q2), (o3, q3)):
            acc[...] += tn(o[...], q[...])
        clip_parts(acc, mine, send)

    def sum_in_kernel(part, l2, l3, p2, p3, m0, m1, m2, m3, q0, q1, q2, q3, mine, send, acc):
        acc[...] = part[...] + tn(l2[...], p2[:, section_columns()])
        acc[...] += tn(l3[...], p3[:, section_columns()])
        for m, q in ((m0, q0), (m1, q1), (m2, q2), (m3, q3)):
            acc[...] += tn(m[...], q[...])
        clip_parts(acc, mine, send)

    def whole_part(kernel, part, *ins):
        rows_in, columns = part.shape
        mine, send = stage(
            kernel, [part, *ins], [near((rows_in // 2, columns), BF16)] * 2,
            [pltpu.VMEM((rows_in, columns), F32)],
        )
        return mine, z_swap(send, 1) if ring else send

    def over_sections(keep, send):
        return keep, y_swap(send) if ring else send

    def clip_rows(apart, size=eighth):
        here = lax.axis_index("dp") if ring else 0
        return pl.ds(pl.multiple_of((here ^ apart) * size, size), size)

    def over_near_clip(keep, got):
        if not ring:
            return keep, got

        def kernel(a, b, mine, send, acc):
            acc[...] = add(a[...], b[...])
            for out, first in ((mine, 0), (send, 1)):
                out[0:eighth, :] = acc[clip_rows(first), :].astype(BF16)
                out[eighth:, :] = acc[clip_rows(first ^ 2), :].astype(BF16)

        mine, send = stage(
            kernel, [keep, got], [near((2 * eighth, model), BF16)] * 2,
            [pltpu.VMEM((half_rows, model), F32)],
        )
        return mine, z_swap(send, 1)

    def over_far_clip(mine, got):
        if not ring:
            return mine, got
        size = mine.shape[0] // 2

        def kernel(a, b, own, send):
            own[...] = add(a[0:size, :], b[0:size, :]).astype(BF16)
            send[...] = add(a[size:, :], b[size:, :]).astype(BF16)

        own, send = stage(kernel, [mine, got], [near((size, mine.shape[1]), BF16)] * 2)
        return own, z_swap(send, 2)

    def to_far_clip(own, got):
        if not ring:
            return own, got
        (own,) = adds((own, got))
        return own, z_swap(own, 2)

    def to_near_clip(own, got):
        if not ring:
            return own, got

        size = own.shape[0]

        def kernel(a, b, out):
            out[0:size, :] = a[...]
            out[size:, :] = b[...]

        (both,) = stage(kernel, [own, got], [near((2 * size, own.shape[1]), BF16)])
        return both, z_swap(both, 1)

    def join_kernel(a, b, out):
        size = a.shape[0] // 2
        for apart, ref, at in ((0, a, 0), (2, a, size), (1, b, 0), (3, b, size)):
            out[clip_rows(apart, size), :] = ref[at : at + size, :]

    def to_sections(both, got, move=y_swap):
        if not ring:
            sec = lax.axis_index("pipe")
            early = jnp.where(sec == 0, both, got)
            later = jnp.where(sec == 0, got, both)
            early, later = lax.psum((early, later), ("pipe", "dp"))
            return jnp.where(sec == 0, early, later), jnp.where(sec == 0, later, early)
        (summed,) = stage(join_kernel, [both, got], [near((half_rows, model), BF16)])
        return summed, move(summed)

    def to_other_section(both, got):
        if not ring:
            both, got = lax.psum((both, got), "dp")
        (summed,) = stage(join_kernel, [both, got], [near((2 * both.shape[0], both.shape[1]), BF16)])
        return summed, y_swap(summed)

    def put_halves(keep, other, out):
        sec = lax.axis_index("pipe")
        for ref, at in ((keep, sec), (other, 1 - sec)):
            start = pl.multiple_of(at * half_rows, half_rows)
            out[pl.ds(start, half_rows), :] = ref[...].astype(F32)

    def whole(keep, other):
        return stage(put_halves, [keep, other], [shape_of((model, model), F32)])[0]

    def put_columns(keep, other, out):
        sec = lax.axis_index("pipe")
        for ref, at in ((keep, sec), (other, 1 - sec)):
            start = pl.multiple_of(at * half_rows, half_rows)
            out[:, pl.ds(start, half_rows)] = ref[...].astype(F32)

    def whole_of_columns(keep, other):
        return stage(put_columns, [keep, other], [shape_of((model, model), F32)])[0]

    def residual_back_kernel(a, b, resid, g, vecs, grad_o, low_o, small_o):
        incoming = add(a[...], b[...])
        normed, inverse = norm_parts(resid[...])
        real = lax.broadcasted_iota(jnp.int32, (rows, model), 0) < patch
        incoming = jnp.where(real, incoming, 0.0)
        grad = g[...].astype(F32) + norm_back(incoming, normed, inverse, vecs[1:2])
        grad = jnp.where(real, grad, 0.0)
        grad_o[...] = grad
        low = grad.astype(BF16)
        low_o[...] = low
        small_o[...] = jnp.zeros_like(small_o)
        small_o[0:1, :] = row_sum(incoming * normed)
        small_o[1:2, :] = row_sum(incoming)
        small_o[2:3, :] = row_sum(low.astype(F32))
        small_o[3:4, :] = row_sum(g[...].astype(F32))

    def column_out(values_in, slot, keep_o, send_o):
        ten = lax.axis_index("tensor")
        spot = (ten ^ slot) & 1
        for i in range(4):
            block = values_in[:, i * width : (i + 1) * width]
            apart = ten ^ i
            for out, odd in ((keep_o, 0), (send_o, 1)):
                for side in range(2):

                    @pl.when(((apart & 1) == odd) & (spot == side))
                    def _():
                        out[apart >> 1, slot >> 1, :, side * width : (side + 1) * width] = block

    def attend_back_kernel(
        s, branch_in, q, k, v, probs, x, msg, w, vrow, wo, *refs
    ):
        extra = refs[0] if s == 0 else None
        back_o, grads_o, low_o, small_o = refs[-4:]
        gain, shift = vrow[0:1], vrow[1:2]
        here = lax.broadcasted_iota(jnp.int32, (rows, model), 0) == patch
        grad_mixed = nt(branch_in[...], wo[...]).astype(BF16)
        dq = jnp.zeros((rows, width), F32)
        dk = jnp.zeros((rows, width), F32)
        dv = jnp.zeros((rows, width), F32)
        for h, mask in enumerate(head_masks(rows)):
            grad_head = only(mask, grad_mixed)
            low_probs = probs[h]
            wide = low_probs.astype(F32)
            dv = dv + tn(low_probs, grad_head)
            grad_probs = nt(grad_head, v[...])
            inner = jnp.sum(wide * grad_probs, axis=-1, keepdims=True)
            grad_scores = (wide * (grad_probs - inner)).astype(BF16)
            dq = dq + only(mask, nn(grad_scores, k[...]))
            dk = dk + tn(grad_scores, only(mask, q[...]))
        dq = (dq * scale).astype(BF16)
        dk = (dk * scale).astype(BF16)
        dv = dv.astype(BF16)
        grads_o[0] = dq
        grads_o[1] = dk
        grads_o[2] = dv
        grad_low = nn(dq, w[0]) + nn(dk, w[1]) + nn(dv, w[2])
        token = jnp.where(here, msg[s : s + 1], x[...].astype(F32))
        normed, inverse = norm_parts(token)
        low_o[...] = (normed * gain + shift).astype(BF16)
        back = norm_back(grad_low, normed, inverse, gain)
        small_o[...] = jnp.zeros_like(small_o)
        small_o[0:1, :] = row_sum(only(here, back))
        small_o[1:2, :] = row_sum(grad_low * normed)
        small_o[2:3, :] = row_sum(grad_low)
        small_o[3:4, 0:width] = row_sum(dq.astype(F32))
        small_o[3:4, 256 : 256 + width] = row_sum(dv.astype(F32))
        if s == 0:
            back = back + extra[...]
        back_o[...] = back.astype(BF16)

    def attend_back(s, low_grad, kept):
        _, mixed, probs, k, v = kept
        ins = [low_grad, q_one[s], k, v, probs, x_slots[s], msg_rows, w_in, vec, w_out]
        return stage(
            functools.partial(attend_back_kernel, s),
            ins + ([grad_resid] if s == 0 else []),
            [
                near((rows, model), BF16),
                near((3, rows, width), BF16),
                near((rows, model), BF16),
                near((8, model), F32),
            ],
            flops=2 * rows * (4 * width * model + 4 * heads * rows * HEAD_DIM),
        )

    column_shapes = [near((2, 2, rows, 2 * width), BF16)] * 2

    def column_kernel(b0, b1, b2, b3, keep_o, send_o):
        for s, ref in enumerate((b0, b1, b2, b3)):
            column_out(ref[...], s, keep_o, send_o)

    def mlp_kernel(h0, h1, h2, h3, w, resid, vecs, *outs):
        for s, h in enumerate((h0, h1, h2, h3)):
            out = nn(h[...], w[...])
            if s == 0:
                out = out + resid[...] + vecs[4:5]
            outs[s][...] = out.astype(BF16)

    def far_columns(keep, got):
        def kernel(a, b, near_o, far_o):
            for i in range(2):
                near_o[i] = add(a[0, i], b[0, i]).astype(BF16)
                far_o[i ^ 1] = add(a[1, i], b[1, i]).astype(BF16)

        kept, send = stage(kernel, [keep, got], [near((2, rows, 2 * width), BF16)] * 2)
        return kept, x_swap(send)

    def frames_of(kept, far):
        low_pair = lax.axis_index("tensor") >> 1
        for i in range(2):
            total = add(kept[i], far[i])
            for side in range(2):
                yield (low_pair ^ i) * 2 + side, total[:, side * width : (side + 1) * width]

    def attend_weight_half_kernel(ga, gb, la, lb, ma, mb, ba, bb, out):
        for c in range(3):
            at = slice(c * width, (c + 1) * width)
            out[at, :] = tn(ga[c], la[...])
            out[at, :] += tn(gb[c], lb[...])
        out[3 * width :, :] = tn(ma[...], ba[...])
        out[3 * width :, :] += tn(mb[...], bb[...])

    def pack_kernel(s0, s1, s2, s3, two, p0, p1, p2, p3, out, acc):
        ten = lax.axis_index("tensor")
        acc[...] = jnp.zeros_like(acc)
        for s, ref in enumerate((s0, s1, s2, s3)):
            acc[pl.ds(ten ^ s, 1), :] = ref[0:1, :]
        acc[4:6, :] = s0[1:3, :] + s1[1:3, :] + s2[1:3, :] + s3[1:3, :]
        acc[6:10, :] = two[0:4, :]
        acc[pl.ds(10 + ten, 1), :] = p0[...] + p1[...] + p2[...] + p3[...]
        acc[pl.ds(14 + ten, 1), :] = s0[3:4, :] + s1[3:4, :] + s2[3:4, :] + s3[3:4, :]
        out[...] = acc[...].astype(BF16)

    def attend_weight_kernel(so_far, ga, gb, la, lb, ma, mb, ba, bb, keep, send, acc):
        for c in range(3):
            at = slice(c * width, (c + 1) * width)
            acc[at, :] = so_far[at, :] + tn(ga[c], la[...])
            acc[at, :] += tn(gb[c], lb[...])
        acc[3 * width :, :] = so_far[3 * width :, :] + tn(ma[...], ba[...])
        acc[3 * width :, :] += tn(mb[...], bb[...])
        halves_of(acc, keep, send)

    def merge_kernel(mine, other, out):
        a, b = mine[...].astype(F32), other[...].astype(F32)
        early = lax.axis_index("pipe") == 0
        out[...] = jnp.concatenate(
            [
                jnp.where(early, a[:half], b[:half]),
                jnp.where(early, b[:half], a[:half]),
                a[half : half + 24] + b[half : half + 24],
            ],
            axis=0,
        ).astype(BF16)

    def message_back(*refs):
        pack_refs, refs = refs[:pack_blocks], refs[pack_blocks:]
        (first, q, k, v, probs, w, wo, vrow, sent_o, grads_o, back_o) = refs
        sent = jnp.concatenate(
            [clip_block(pack_refs, c, pack_rows).astype(F32)[:frame_count] for c in range(clips)],
            axis=0,
        )
        low = sent.astype(BF16)
        sent_o[...] = sent
        grad_mixed = nt(low, wo[...]).astype(BF16)
        dq = jnp.zeros((all_rows, width), F32)
        dk = jnp.zeros((all_rows, width), F32)
        dv = jnp.zeros((all_rows, width), F32)
        for h, mask in enumerate(head_masks(all_rows)):
            grad_head = only(mask, grad_mixed)
            wide = probs[h]
            dv = dv + tn(wide.astype(BF16), grad_head)
            grad_probs = nt(grad_head, v[...])
            inner = jnp.sum(wide * grad_probs, axis=-1, keepdims=True)
            grad_scores = (wide * (grad_probs - inner)).astype(BF16)
            dq = dq + only(mask, nn(grad_scores, k[...]))
            dk = dk + tn(grad_scores, only(mask, q[...]))
        dq = (dq * scale).astype(BF16)
        dk = (dk * scale).astype(BF16)
        dv = dv.astype(BF16)
        grads_o[0] = dq
        grads_o[1] = dk
        grads_o[2] = dv
        grad_low = nn(dq, w[0]) + nn(dk, w[1]) + nn(dv, w[2])
        normed, inverse = norm_parts(first[...])
        back_msg = norm_back(grad_low, normed, inverse, vrow[0:1])
        back_o[0:all_rows, :] = back_msg.astype(BF16)
        tail = jnp.concatenate(
            [row_sum(grad_low * normed), row_sum(grad_low), jnp.zeros((14, model), F32)], axis=0
        )
        back_o[all_rows:, :] = tail.astype(BF16)

    def message_weight(sent, grads_in, low, mixed, in_o, out_o, qv_o, bias_o):
        for c in range(3):
            in_o[c] = tn(grads_in[c], low[...])
        out_o[...] = tn(mixed[...], sent[...].astype(BF16))
        qv_o[0:1, :] = row_sum(grads_in[0].astype(F32))
        qv_o[1:2, :] = row_sum(grads_in[2].astype(F32))
        bias_o[...] = row_sum(sent[...])

    def block_out_kernel(*refs):
        for at, total in frames_of(*refs[:-1]):
            refs[-1][at] = total.T[:, :patch].astype(BF16)

    def message_end(*refs):
        pack_refs, refs = refs[:pack_blocks], refs[pack_blocks:]
        cls_refs, refs = refs[:blocks], refs[blocks:]
        (sent, own, late, mw, qv_in, bias_in, w_o, cls_o, vec_o, qv_o, turned, sums) = refs
        sec, ten = lax.axis_index("pipe"), lax.axis_index("tensor")
        total = jnp.where(sec == 0, own[...].astype(F32), late[...].astype(F32))
        grad_first = sent[...] + total[:all_rows]
        at = pl.ds(pl.multiple_of(ten * width, width), width)
        mine = grad_first[:16]
        high = mine.astype(BF16)
        rest = (mine - high.astype(F32)).astype(BF16)
        mw_rows = mw[at, :]
        cls_o[...] = nt(high, mw_rows) + nt(rest, mw_rows)
        turned[...] = grad_first.T
        mine = turned[at, :]
        high = mine.astype(BF16)
        rest = (mine - high.astype(F32)).astype(BF16)
        cls = jnp.concatenate([clip_block(cls_refs, c, frame_count).astype(F32) for c in range(clips)])
        cls = cls.astype(BF16)
        w_o[...] = nn(high, cls) + nn(rest, cls)
        summed = clip_block(pack_refs, 0, pack_rows).astype(F32)
        for c in range(1, clips):
            summed = summed + clip_block(pack_refs, c, pack_rows).astype(F32)
        sums[...] = summed[frame_count:]
        first_one = sec == 0
        vec_o[0:1, :] = jnp.where(first_one, total[all_rows : all_rows + 1], sums[0:1])
        vec_o[1:2, :] = jnp.where(first_one, total[all_rows + 1 : all_rows + 2], sums[1:2])
        vec_o[2:3, :] = jnp.where(first_one, bias_in[...], sums[4:5])
        vec_o[3:4, :] = sums[2:3]
        vec_o[4:5, :] = sums[3:4]
        vec_o[5:6, :] = sums[5:6]
        vec_o[6:7, :] = sums[pl.ds(6 + ten, 1), :]
        vec_o[7:8, :] = row_sum(grad_first)
        qv_row = sums[pl.ds(10 + ten, 1), :]
        qv_o[0:1, :] = jnp.where(first_one, qv_in[0:1], qv_row[:, :width])
        qv_o[1:2, :] = jnp.where(first_one, qv_in[1:2], qv_row[:, 256 : 256 + width])

    def frames_grad_kernel(*refs):
        cls, out = refs[-2:]
        top = lax.broadcasted_iota(jnp.int32, (rows, width), 0) == 0
        for at, total in frames_of(*refs[:-2]):
            row = cls[pl.ds(lax.axis_index("pipe") * half + at, 1), :]
            out[at] = (total + jnp.where(top, row, 0.0)).T[:, :patch].astype(BF16)

    def attend_whole_kernel(keep, other, in_zero_ref, out_zero_ref, in_o, out_o, acc):
        @pl.when(lax.axis_index("pipe") == 0)
        def _():
            in_o[...] = in_zero_ref[...]
            out_o[...] = out_zero_ref[...]

        @pl.when(lax.axis_index("pipe") == 1)
        def _():
            put_halves(keep, other, acc)
            for c in range(3):
                in_o[c] = acc[c * width : (c + 1) * width, :]
            out_o[...] = acc[3 * width :, :]

    def pack_join_kernel(a, b, out):
        size = a.shape[0]
        out[0:size, :] = a[...]
        out[size:, :] = b[...]

    stage.cost = 0
    cls_all = gather_clips(frames[0, :, 0, :])
    vectors, own_vec, near_in, in_and_vec = stage(
        small_kernel,
        [
            own_in, msg_bias, norm2_gain, norm2_shift, fc_in_bias, fc_out_bias,
            norm_gain, norm_shift, out_bias, qv_bias,
        ],
        [near((8, model), F32)] * 2 + [near(own_in.shape, BF16), near((3 * width + 16, model), BF16)],
        [pltpu.VMEM((model,), F32)] * 5
        + [pltpu.VMEM((1, model), F32)] * 3
        + [pltpu.VMEM((1, 2, width), F32), pltpu.SemaphoreType.DMA((13,))],
        far=10,
    )
    sent_in = y_early(in_and_vec)
    near_msg_w, near_out = stage(
        load_kernel, [msg_w, own_out], [near(msg_w.shape, BF16), near(own_out.shape, BF16)],
        [pltpu.SemaphoreType.DMA((2,))],
        far=2,
    )
    x_slots = slots(tokens, half)
    (first_msg, low_zero, q_zero, k_zero, v_zero, probs_zero, mixed_zero, part_zero) = stage(
        message_forward,
        [video_group, *cls_all, near_msg_w, vectors, own_vec, near_in, near_out],
        [
            near((all_rows, model), F32),
            near((all_rows, model), BF16),
            near((all_rows, width), BF16),
            near((all_rows, width), BF16),
            near((all_rows, width), BF16),
            near((heads, all_rows, all_rows), F32),
            near((all_rows, width), BF16),
            near((frame_count, model), F32),
        ],
        [pltpu.SMEM(video_group.shape, jnp.int32), pltpu.SemaphoreType.DMA],
        far=1,
    )
    from_core = core_swap(part_zero)
    sent_out = y_early(relay(near_out))
    (part_zero,) = adds((part_zero, from_core))
    from_x = x_swap(part_zero)
    (part_zero,) = adds((part_zero, from_x))
    part_late = y_late(part_zero)
    w_in, vec, *projected = stage(
        project_kernel, [*x_slots, near_in, sent_in, own_vec],
        [near(own_in.shape, BF16), near(own_vec.shape, F32)] + [near((rows, width), BF16)] * 12,
    )
    stage.cost = 4 * 10**9
    q_one, k_patch, v_patch = projected[:4], projected[4:8], projected[8:]
    msg_rows, k_msg, v_msg, w_out = stage(
        message_rows_kernel,
        [first_msg, part_zero, part_late, w_in, vec, near_out, sent_out],
        [
            near((16, model), F32), near((16, width), F32), near((16, width), F32),
            near(own_out.shape, BF16),
        ],
    )

    at3 = attend(3)
    ac3 = core_swap(at3[0])
    at2 = attend(2)
    (two,) = adds((at2[0], ac3))
    ax = x_swap(two)
    at1 = attend(1)
    ac1 = core_swap(at1[0])
    at0 = attend(0)
    g_slots = slots(grads_in, 2 * half)
    (aown,) = adds((at0[0], ac1))
    resid_own, low_own = stage(
        residual_kernel, [aown, ax, x_slots[0], vec, vectors],
        [near((rows, model), F32), near((rows, model), BF16)],
    )
    lx = x_swap(low_own)
    l1 = core_swap(low_own)
    ly = y_swap(low_own)
    g_hidden = stage(
        grad_hidden_kernel, [*g_slots[:half], fc_out], [near((rows, hidden_width), BF16)] * half,
    )
    hid0, pre0, gp0, bs0 = feed(low_own, g_hidden[0])
    hid1, pre1, gp1, bs1 = feed(l1, g_hidden[1])
    fc1 = core_swap(gp1)
    fc_out_half = own_part(own_out_kernel, (half_rows, model), hid0, hid1, g_slots[0], g_slots[1])
    (fown,) = adds((gp0, fc1))
    l2 = relay(lx)
    l3 = core_swap(l2)
    ly2 = y_swap(l2)
    hid2, pre2, gp2, bs2 = feed(l2, g_hidden[2])
    hid3, pre3, gp3, bs3 = feed(l3, g_hidden[3])
    fc3 = core_swap(gp3)
    m0 = relay(ly)
    m1 = core_swap(m0)
    (two,) = adds((gp2, fc3))
    fx = x_swap(two)
    ho0, po0 = feed_other(m0, g_slots[4])
    ho1, po1 = feed_other(m1, g_slots[5])
    fc_in_half = own_part(own_in_kernel, (model, half_rows), low_own, l1, pre0, pre1)
    block_parts = stage(
        mlp_kernel, [hid0, hid1, hid2, hid3, fc_out, resid_own, vectors],
        [near((rows, model), BF16)] * half,
    )
    grad_resid, grad_low, small_two = stage(
        residual_back_kernel, [fown, fx, resid_own, g_slots[0], vectors],
        [near((rows, model), F32), near((rows, model), BF16), near((8, model), F32)],
    )
    bx = x_swap(grad_low)
    b1 = core_swap(grad_low)
    m2 = relay(ly2)
    m3 = core_swap(m2)
    ho2, po2 = feed_other(m2, g_slots[6])
    ho3, po3 = feed_other(m3, g_slots[7])
    p0 = whole_part(
        sum_out_kernel, fc_out_half, hid2, hid3, g_slots[2], g_slots[3], ho0, ho1, ho2, ho3, *g_slots[half:],
    )
    q0 = whole_part(
        sum_in_kernel, fc_in_half, l2, l3, pre2, pre3, m0, m1, m2, m3, po0, po1, po2, po3,
    )
    ba0, gr0, lo0, sm0 = attend_back(0, grad_low, at0)
    ba1, gr1, lo1, sm1 = attend_back(1, b1, at1)
    (attend_half,) = stage(
        attend_weight_half_kernel, [gr0, gr1, lo0, lo1, at0[1], at1[1], grad_low, b1],
        [near((4 * width, model), F32)],
    )
    b2 = relay(bx)
    b3 = core_swap(b2)
    ba2, gr2, lo2, sm2 = attend_back(2, b2, at2)
    p1 = over_far_clip(*p0)
    ba3, gr3, lo3, sm3 = attend_back(3, b3, at3)
    (pk0,) = stage(
        pack_kernel, [sm0, sm1, sm2, sm3, small_two, bs0, bs1, bs2, bs3], [near((32, model), BF16)],
        [pltpu.VMEM((32, model), F32)],
    )
    pkc = core_swap(pk0)
    r0 = over_sections(
        *stage(
            attend_weight_kernel,
            [attend_half, gr2, gr3, lo2, lo3, at2[1], at3[1], b2, b3],
            half_shapes,
            [pltpu.VMEM((4 * width, model), F32)],
        )
    )
    (pk1,) = adds((pk0, pkc))
    pkx = x_swap(pk1)
    q1 = over_far_clip(*q0)
    p2 = to_far_clip(*p1)
    (pk2,) = adds((pk1, pkx))
    pky = y_swap(pk2)
    r1 = over_near_clip(*r0)
    q2 = to_far_clip(*q1)
    (pk3,) = stage(merge_kernel, [pk2, pky], [near((32, model), BF16)])
    pack_rows = pk3.shape[0]
    pkz = z_swap(pk3, 1) if ring else None
    p3 = to_near_clip(*p2)
    r2 = over_far_clip(*r1)
    if ring:
        (pk4,) = stage(pack_join_kernel, [pk3, pkz], [near((2 * pack_rows, model), BF16)])
        packs = [pk4, z_swap(pk4, 2)]
    else:
        packs = gather_clips(pk3)
    q3 = to_near_clip(*q2)
    p4 = to_other_section(*p3)
    sent_all, grads_zero, bz0 = stage(
        message_back,
        [*packs, first_msg, q_zero, k_zero, v_zero, probs_zero, near_in, near_out, own_vec],
        [
            near((all_rows, model), F32),
            near((3, all_rows, width), BF16),
            near((all_rows + 16, model), BF16),
        ],
    )
    bzc = core_swap(bz0)
    in_zero, out_zero, qv_zero, bias_zero = stage(
        message_weight, [sent_all, grads_zero, low_zero, mixed_zero],
        [
            near((3, width, model), F32),
            near((width, model), F32),
            near((2, width), F32),
            near((1, model), F32),
        ],
    )
    (bz1,) = adds((bz0, bzc))
    bzx = x_swap(bz1)
    r3 = to_far_clip(*r2)
    q4 = to_other_section(*q3)
    (bz2,) = adds((bz1, bzx))
    bzy = y_late(bz2)
    ck, send = stage(column_kernel, [ba0, ba1, ba2, ba3], column_shapes)
    cs = core_swap(send)
    fc_out_grad = whole(*p4)
    msg_w_grad, cls_part, vec_grads, qv_grad = stage(
        message_end,
        [*packs, *cls_all, sent_all, bz2, bzy, near_msg_w, qv_zero, bias_zero],
        [
            shape_of((width, model), F32),
            near((16, width), F32),
            near((8, model), F32),
            near((2, width), F32),
        ],
        [pltpu.VMEM((model, all_rows), F32), pltpu.VMEM((24, model), F32)],
    )
    kept, far = far_columns(ck, cs)
    r4 = to_near_clip(*r3)
    (frames_grad,) = stage(
        frames_grad_kernel, [kept, far, cls_part], [shape_of((half, width, patch), BF16)],
    )
    bk, send = stage(column_kernel, block_parts, column_shapes)
    bcs = core_swap(send)
    r5 = to_sections(*r4, move=y_late)
    fc_in_grad = whole_of_columns(*q4)
    bkept, bfar = far_columns(bk, bcs)
    (block_out,) = stage(
        block_out_kernel, [bkept, bfar], [shape_of((half, width, patch), BF16)],
    )
    attn_in_grad, attn_out_grad = stage(
        attend_whole_kernel, [*r5, in_zero, out_zero],
        [shape_of((3, width, model), F32), shape_of((width, model), F32)],
        [pltpu.VMEM((4 * width, model), F32)],
    )

    return (
        jnp.swapaxes(block_out, 1, 2)[None],
        jnp.swapaxes(frames_grad, 1, 2)[None],
        msg_w_grad.T,
        vec_grads[7],
        vec_grads[0:1],
        vec_grads[1:2],
        jnp.transpose(attn_in_grad, (2, 0, 1))[None],
        qv_grad[None],
        attn_out_grad[None],
        vec_grads[2:3],
        vec_grads[3],
        vec_grads[4],
        fc_in_grad,
        vec_grads[6],
        fc_out_grad,
        vec_grads[5],
    )


def solution(mesh):
    return jax.shard_map(
        body,
        mesh=mesh,
        in_specs=(
            P("dp", None, None, None),
            P(),
            P(),
            P(),
            P("pipe", None),
            P("pipe", None),
            P("pipe", None, None, "tensor"),
            P("pipe", None, "tensor"),
            P("pipe", "tensor", None),
            P("pipe", None),
            P(),
            P(),
            P(None, "tensor"),
            P("tensor"),
            P("tensor", None),
            P(),
            P("dp", None, None, None),
        ),
        out_specs=(
            P("dp", "pipe", None, "tensor"),
            P("dp", "pipe", None, "tensor"),
            P(None, "tensor"),
            P(),
            P("pipe", None),
            P("pipe", None),
            P("pipe", None, None, "tensor"),
            P("pipe", None, "tensor"),
            P("pipe", "tensor", None),
            P("pipe", None),
            P(),
            P(),
            P(None, "tensor"),
            P("tensor"),
            P("tensor", None),
            P(),
        ),
        check_vma=False,
    )
```

time: 228 us -> 189 us (0.83)
  starting transfers between devices: 77.3 us -> 52.9 us
  waiting for transfers between devices: 87.5 us -> 71.8 us
  Pallas kernels: 47.2 us -> 57.2 us
  local copies, waits for them, and re-layouts: 10.4 us -> 2.58 us
    ppermute x24 -> x17, starting transfers between devices: 42.2 us -> 20.4 us  [z_swap(): return lax.ppermute(v, 'dp', [(i, i ^ bit) for i in range(clips)])]
    ppermute x7 -> x6, waiting for transfers between devices: 28.1 us -> 7.03 us  [y_swap(): return lax.ppermute(v, 'pipe', [(0, 1), (1, 0)])]
    ppermute x24, waiting for transfers between devices: 14.5 us -> 34.2 us  [tensor_swap(): return lax.ppermute(v, 'tensor', [(i, i ^ bit) for i in range(4)])]
    ppermute x24 -> x17, waiting for transfers between devices: 36.2 us -> 21.3 us  [z_swap(): return lax.ppermute(v, 'dp', [(i, i ^ bit) for i in range(clips)])]
    pallas_call x60 -> x76, Pallas kernels: 47.2 us -> 57.2 us  [__call__(): pl.pallas_call(stage, out_shape=[*outs, near((8, 128), F32)], in_specs=[p...]
    unnamed x35 -> x37, local copies, waits for them, and re-layouts: 8.45 us -> 0.67 us
    ppermute x7 -> x6, starting transfers between devices: 10.7 us -> 4.4 us  [y_swap(): return lax.ppermute(v, 'pipe', [(0, 1), (1, 0)])]
    ppermute x2 -> x3, starting transfers between devices: 5.28 us -> 11.5 us  [y_late(): return lax.ppermute(v, 'pipe', [(0, 1)])]
  transfers between devices with their start and end apart: 60 -> 52, of which waited for: 24 -> 26; matrix products, arithmetic and copies ran while one was open for 1% -> 1% of each run, Pallas kernels for 18% -> 27%
where the time goes in v3:
time: 189 us; the launch traced here: 186 us
  waiting for transfers between devices  71.8 us (38%)
  Pallas kernels  57.2 us (30%)
  starting transfers between devices  52.9 us (28%)
  local copies, waits for them, and re-layouts  2.58 us (1%)
    pallas_call x76, Pallas kernels, __call__(): pl.pallas_call(stage, out_shape=[*outs, near((8, 128), F32)], in_specs=[p...  57.2 us
    ppermute x24, waiting for transfers between devices, tensor_swap(): return lax.ppermute(v, 'tensor', [(i, i ^ bit) for i in range(4)])  34.2 us
    ppermute x17, waiting for transfers between devices, z_swap(): return lax.ppermute(v, 'dp', [(i, i ^ bit) for i in range(clips)])  21.3 us
    ppermute x17, starting transfers between devices, z_swap(): return lax.ppermute(v, 'dp', [(i, i ^ bit) for i in range(clips)])  20.4 us
    ppermute x24, starting transfers between devices, tensor_swap(): return lax.ppermute(v, 'tensor', [(i, i ^ bit) for i in range(4)])  14 us
    ppermute x3, starting transfers between devices, y_late(): return lax.ppermute(v, 'pipe', [(0, 1)])  11.5 us
    ppermute x6, waiting for transfers between devices, y_swap(): return lax.ppermute(v, 'pipe', [(0, 1), (1, 0)])  7.03 us
    ppermute x3, waiting for transfers between devices, y_late(): return lax.ppermute(v, 'pipe', [(0, 1)])  6.7 us
  transfers between devices with their start and end apart: 52, of which 26 were waited for; matrix products, arithmetic and copies ran while one was open for 1% of the time, Pallas kernels for 27%

profile of v3, /device:TPU:0, one launch (start us, length us, event | category | flops | bytes accessed | tf_op | source)
XLA Modules:
  0.0 186.2 jit_solution(8931366616624223959)
XLA Ops:
  0.6 1.7 shard_map.288
  4.4 3.0 %collective-permute-start = (bf16[8,768]{1,0:T(8,128)(2,1)S(1)}, bf16[8,768]{1,0:T(8,128)(2,1)S(1)}, u32[]{:S(2)}, u32[]{:S(2)}) collective-permute-start(bf16[8,768]{1,0:T(8,128)(2,1)S(1)} %slice_bitcast_fusion.refs_2_.refs_3_), channel_id=1, source_target_pairs={{0,1},{1,0},{2,3},{3,2},{4,5},{5,4},{6,7},{7,6},{8,9},{9,8},{10,11... | collective-permute-start | bytes 36872 | tf_op jit(solution)/shard_map/ppermute | solution.py:167
  7.4 2.6 %collective-permute-start.1 = (bf16[8,768]{1,0:T(8,128)(2,1)S(1)}, bf16[8,768]{1,0:T(8,128)(2,1)S(1)}, u32[]{:S(2)}, u32[]{:S(2)}) collective-permute-start(bf16[8,768]{1,0:T(8,128)(2,1)S(1)} %slice_bitcast_fusion.refs_2_.refs_3_), channel_id=1, source_target_pairs={{0,2},{1,3},{2,0},{3,1},{4,6},{5,7},{6,4},{7,5},{8,10},{9,11},{10,... | collective-permute-start | bytes 36872 | tf_op jit(solution)/shard_map/ppermute | solution.py:167
  11.3 3.3 %shard_map.290 = (bf16[208,768]{1,0:T(8,128)(2,1)S(1)}, bf16[208,768]{1,0:T(8,128)(2,1)S(1)}, bf16[208,768]{1,0:T(8,128)(2,1)S(1)}, bf16[208,768]{1,0:T(8,128)(2,1)S(1)}, f32[8,128]{1,0:T(8,128)S(1)}) custom-call(f32[8,128]{1,0:T(8,128)S(1)} %get-tuple-element.278.refs_0_, bf16[197,8,768]{2,1,0:T(8,128)(2,1)} %bitcast.25), custom_call_target="tpu_custom_call" | custom-call | tf_op jit(solution)/shard_map/pallas_call | solution.py:78
  15.5 2.1 %shard_map.291 = (f32[32,768]{1,0:T(8,128)S(1)}, bf16[32,768]{1,0:T(8,128)(2,1)S(1)}, bf16[32,192]{1,0:T(8,128)(2,1)S(1)}, bf16[32,192]{1,0:T(8,128)(2,1)S(1)}, ...) custom-call(f32[8,128]{1,0:T(8,128)S(1)} %get-tuple-element.279.refs, ...), custom_call_target="tpu_custom_call" | custom-call | tf_op jit(solution)/shard_map/pallas_call | solution.py:78
  20.2 1.5 collective-permute-start.4
  21.7 2.3 %collective-permute-done.4.refs_2_ = f32[8,768]{1,0:T(8,128)S(1)} collective-permute-done((f32[8,768]{1,0:T(8,128)S(1)}, f32[8,768]{1,0:T(8,128)S(1)}, u32[]{:S(2)}, u32[]{:S(2)}) %collective-permute-start.4) | collective-permute-done | bytes 24608 | tf_op jit(solution)/shard_map/ppermute | solution.py:149
  24.0 4.8 %collective-permute-start.6 = (f32[8,768]{1,0:T(8,128)S(1)}, f32[8,768]{1,0:T(8,128)S(1)}, u32[]{:S(2)}, u32[]{:S(2)}) collective-permute-start(f32[8,768]{1,0:T(8,128)S(1)} %get-tuple-element.298.refs_2_), channel_id=1, source_target_pairs={{0,16},{1,17},{2,18},{3,19},{4,20},{5,21},{6,22},{7,23},{8,24},{9,... | collective-permute-start | bytes 73736 | tf_op jit(solution)/shard_map/ppermute | solution.py:161
  28.8 1.6 shard_map.295
  30.5 2.6 %collective-permute-done.7.refs_7_ = bf16[192,768]{1,0:T(8,128)(2,1)S(1)} collective-permute-done((bf16[192,768]{1,0:T(8,128)(2,1)S(1)}, bf16[192,768]{1,0:T(8,128)(2,1)S(1)}, u32[]{:S(2)}, u32[]{:S(2)}) %collective-permute-start.7) | collective-permute-done | bytes 294944 | tf_op jit(solution)/shard_map/ppermute | solution.py:164
  37.9 2.3 %collective-permute-start.10 = (bf16[208,768]{1,0:T(8,128)(2,1)S(1)}, bf16[208,768]{1,0:T(8,128)(2,1)S(1)}, u32[]{:S(2)}, u32[]{:S(2)}) collective-permute-start(bf16[208,768]{1,0:T(8,128)(2,1)S(1)} %get-tuple-element.330), channel_id=1, source_target_pairs={{0,8},{4,12},{8,0},{12,4},{1,9},{5,13},{9,1},{13,5},{2,10},{6,14},... | collective-permute-start | bytes 958472 | tf_op jit(solution)/shard_map/ppermute | solution.py:149
  41.4 3.6 %shard_map.302 = (bf16[208,768]{1,0:T(8,128)(2,1)S(1)}, bf16[208,768]{1,0:T(8,128)(2,1)S(1)}, bf16[208,768]{1,0:T(8,128)(2,1)S(1)}, bf16[208,768]{1,0:T(8,128)(2...) custom-call(f32[8,128]{1,0:T(8,128)S(1)} %get-tuple-element.324.refs, ...), custom_call_target="tpu_custom_call" | custom-call | flops 4000000000 | tf_op jit(solution)/shard_map/pallas_call | solution.py:78
  45.1 3.2 %collective-permute-done.10.refs_2_ = bf16[208,768]{1,0:T(8,128)(2,1)S(1)} collective-permute-done((bf16[208,768]{1,0:T(8,128)(2,1)S(1)}, bf16[208,768]{1,0:T(8,128)(2,1)S(1)}, u32[]{:S(2)}, u32[]{:S(2)}) %collective-permute-start.10) | collective-permute-done | bytes 319520 | tf_op jit(solution)/shard_map/ppermute | solution.py:149
  48.7 1.8 collective-permute-start.13
  50.5 1.6 shard_map.305
  55.9 2.7 %collective-permute-done.13.refs_1_ = bf16[208,768]{1,0:T(8,128)(2,1)S(1)} collective-permute-done((bf16[208,768]{1,0:T(8,128)(2,1)S(1)}, bf16[208,768]{1,0:T(8,128)(2,1)S(1)}, u32[]{:S(2)}, u32[]{:S(2)}) %collective-permute-start.13) | collective-permute-done | bytes 319520 | tf_op jit(solution)/shard_map/ppermute | solution.py:149
  60.4 1.4 shard_map.312
  63.6 1.8 collective-permute-start.18
  68.3 4.9 %collective-permute-done.18.refs_2_ = bf16[208,768]{1,0:T(8,128)(2,1)S(1)} collective-permute-done((bf16[208,768]{1,0:T(8,128)(2,1)S(1)}, bf16[208,768]{1,0:T(8,128)(2,1)S(1)}, u32[]{:S(2)}, u32[]{:S(2)}) %collective-permute-start.18) | collective-permute-done | bytes 319520 | tf_op jit(solution)/shard_map/ppermute | solution.py:149
  74.0 1.8 collective-permute-start.22
  79.3 1.6 collective-permute-start.23
  80.9 1.6 shard_map.324
  82.5 1.7 shard_map.325
  84.2 1.7 shard_map.326
  87.4 1.7 shard_map.329
  89.4 2.7 %collective-permute-start.27 = (bf16[96,768]{1,0:T(8,128)(2,1)S(1)}, bf16[96,768]{1,0:T(8,128)(2,1)S(1)}, u32[]{:S(2)}, u32[]{:S(2)}) collective-permute-start(bf16[96,768]{1,0:T(8,128)(2,1)S(1)} %get-tuple-element.448), channel_id=1, source_target_pairs={{0,2},{1,3},{2,0},{3,1},{4,6},{5,7},{6,4},{7,5},{8,10},{9,11},{10,... | collective-permute-start | bytes 442376 | tf_op jit(solution)/shard_map/ppermute | solution.py:167
  92.0 1.7 shard_map.331
  95.0 1.6 collective-permute-start.29
  97.3 2.2 %collective-permute-done.26.refs_2_ = bf16[384,384]{1,0:T(8,128)(2,1)S(1)} collective-permute-done((bf16[384,384]{1,0:T(8,128)(2,1)S(1)}, bf16[384,384]{1,0:T(8,128)(2,1)S(1)}, u32[]{:S(2)}, u32[]{:S(2)}) %collective-permute-start.26) | collective-permute-done | bytes 294944 | tf_op jit(solution)/shard_map/ppermute | solution.py:167
  101.4 2.8 %collective-permute-start.32 = (bf16[96,768]{1,0:T(8,128)(2,1)S(1)}, bf16[96,768]{1,0:T(8,128)(2,1)S(1)}, u32[]{:S(2)}, u32[]{:S(2)}) collective-permute-start(bf16[96,768]{1,0:T(8,128)(2,1)S(1)} %get-tuple-element.460.refs_1_), channel_id=1, source_target_pairs={{0,2},{1,3},{2,0},{3,1},{4,6},{5,7},{6,4},{7,5},{8,10},{9,11},{10,... | collective-permute-start | bytes 442376 | tf_op jit(solution)/shard_map/ppermute | solution.py:167
  104.2 7.0 %collective-permute-done.29.refs_2_ = bf16[384,768]{1,0:T(8,128)(2,1)S(1)} collective-permute-done((bf16[384,768]{1,0:T(8,128)(2,1)S(1)}, bf16[384,768]{1,0:T(8,128)(2,1)S(1)}, u32[]{:S(2)}, u32[]{:S(2)}) %collective-permute-start.29) | collective-permute-done | bytes 589856 | tf_op jit(solution)/shard_map/ppermute | solution.py:158
  111.5 1.6 collective-permute-start.33
  115.7 8.9 %collective-permute-done.33.refs_2_ = bf16[192,768]{1,0:T(8,128)(2,1)S(1)} collective-permute-done((bf16[192,768]{1,0:T(8,128)(2,1)S(1)}, bf16[192,768]{1,0:T(8,128)(2,1)S(1)}, u32[]{:S(2)}, u32[]{:S(2)}) %collective-permute-start.33) | collective-permute-done | bytes 294944 | tf_op jit(solution)/shard_map/ppermute | solution.py:167
  125.8 2.9 %collective-permute-start.39 = (bf16[96,768]{1,0:T(8,128)(2,1)S(1)}, bf16[96,768]{1,0:T(8,128)(2,1)S(1)}, u32[]{:S(2)}, u32[]{:S(2)}) collective-permute-start(bf16[96,768]{1,0:T(8,128)(2,1)S(1)} %get-tuple-element.485), channel_id=1, source_target_pairs={{0,2},{1,3},{2,0},{3,1},{4,6},{5,7},{6,4},{7,5},{8,10},{9,11},{10,... | collective-permute-start | bytes 442376 | tf_op jit(solution)/shard_map/ppermute | solution.py:167
  128.8 5.7 %collective-permute-done.36.refs_2_ = bf16[192,768]{1,0:T(8,128)(2,1)S(1)} collective-permute-done((bf16[192,768]{1,0:T(8,128)(2,1)S(1)}, bf16[192,768]{1,0:T(8,128)(2,1)S(1)}, u32[]{:S(2)}, u32[]{:S(2)}) %collective-permute-start.36) | collective-permute-done | bytes 294944 | tf_op jit(solution)/shard_map/ppermute | solution.py:167
  134.6 2.1 %collective-permute-start.42 = (bf16[384,768]{1,0:T(8,128)(2,1)S(1)}, bf16[384,768]{1,0:T(8,128)(2,1)S(1)}, u32[]{:S(2)}, u32[]{:S(2)}) collective-permute-start(bf16[384,768]{1,0:T(8,128)(2,1)S(1)} %get-tuple-element.496.refs_1_), channel_id=1, source_target_pairs={{0,16},{16,0},{1,17},{17,1},{2,18},{18,2},{3,19},{19,3},{4,20},{20... | collective-permute-start | bytes 1769480 | tf_op jit(solution)/shard_map/ppermute | solution.py:158
  136.7 1.5 shard_map.346
  140.6 2.3 %collective-permute-done.40.refs_2_ = bf16[384,384]{1,0:T(8,128)(2,1)S(1)} collective-permute-done((bf16[384,384]{1,0:T(8,128)(2,1)S(1)}, bf16[384,384]{1,0:T(8,128)(2,1)S(1)}, u32[]{:S(2)}, u32[]{:S(2)}) %collective-permute-start.40) | collective-permute-done | bytes 294944 | tf_op jit(solution)/shard_map/ppermute | solution.py:167
  144.1 3.1 %collective-permute-start.43 = (bf16[48,768]{1,0:T(8,128)(2,1)S(1)}, bf16[48,768]{1,0:T(8,128)(2,1)S(1)}, u32[]{:S(2)}, u32[]{:S(2)}) collective-permute-start(bf16[48,768]{1,0:T(8,128)(2,1)S(1)} %get-tuple-element.498.refs_8_), channel_id=1, source_target_pairs={{0,16},{1,17},{2,18},{3,19},{4,20},{5,21},{6,22},{7,23},{8,24},{9,... | collective-permute-start | bytes 221192 | tf_op jit(solution)/shard_map/ppermute | solution.py:161
  147.2 1.5 shard_map.352
  148.9 1.6 shard_map.353
  152.9 9.1 %collective-permute-done.46.refs_2_ = bf16[2,208,384]{2,1,0:T(8,128)(2,1)S(1)} collective-permute-done((bf16[2,208,384]{2,1,0:T(8,128)(2,1)S(1)}, bf16[2,208,384]{2,1,0:T(8,128)(2,1)S(1)}, u32[]{:S(2)}, u32[]{:S(2)}) %collective-permute-start.46) | collective-permute-done | bytes 319520 | tf_op jit(solution)/shard_map/ppermute | solution.py:149
  163.3 1.5 shard_map.358
  164.9 1.6 shard_map.360
  168.3 3.6 %collective-permute-start.51 = (bf16[384,768]{1,0:T(8,128)(2,1)S(1)}, bf16[384,768]{1,0:T(8,128)(2,1)S(1)}, u32[]{:S(2)}, u32[]{:S(2)}) collective-permute-start(bf16[384,768]{1,0:T(8,128)(2,1)S(1)} %get-tuple-element.530.refs_1_), channel_id=1, source_target_pairs={{0,16},{1,17},{2,18},{3,19},{4,20},{5,21},{6,22},{7,23},{8,24},{9,... | collective-permute-start | bytes 1769480 | tf_op jit(solution)/shard_map/ppermute | solution.py:161
  173.2 3.6 %collective-permute-done.50.refs_2_ = bf16[2,208,384]{2,1,0:T(8,128)(2,1)S(1)} collective-permute-done((bf16[2,208,384]{2,1,0:T(8,128)(2,1)S(1)}, bf16[2,208,384]{2,1,0:T(8,128)(2,1)S(1)}, u32[]{:S(2)}, u32[]{:S(2)}) %collective-permute-start.50) | collective-permute-done | bytes 319520 | tf_op jit(solution)/shard_map/ppermute | solution.py:149
  177.8 6.7 %collective-permute-done.51.refs_2_ = bf16[384,768]{1,0:T(8,128)(2,1)S(1)} collective-permute-done((bf16[384,768]{1,0:T(8,128)(2,1)S(1)}, bf16[384,768]{1,0:T(8,128)(2,1)S(1)}, u32[]{:S(2)}, u32[]{:S(2)}) %collective-permute-start.51) | collective-permute-done | bytes 589856 | tf_op jit(solution)/shard_map/ppermute | solution.py:161
  184.5 1.6 shard_map.363
  (171 shorter events, 48.6 us)
Async XLA Ops:
  2.3 26.5 %collective-permute-start.5 = (bf16[592,768]{1,0:T(8,128)(2,1)S(1)}, bf16[592,768]{1,0:T(8,128)(2,1)S(1)}, u32[]{:S(2)}, u32[]{:S(2)}) collective-permute-start(bf16[592,768]{1,0:T(8,128)(2,1)S(1)} %get-tuple-element.295), channel_id=1, source_target_pairs={{16,0},{17,1},{18,2},{19,3},{20,4},{21,5},{22,6},{23,7},{24,8},{25... | collective-permute-start | bytes 2727944 | tf_op jit(solution)/shard_map/ppermute | solution.py:164
  4.4 10.3 %collective-permute-start = (bf16[8,768]{1,0:T(8,128)(2,1)S(1)}, bf16[8,768]{1,0:T(8,128)(2,1)S(1)}, u32[]{:S(2)}, u32[]{:S(2)}) collective-permute-start(bf16[8,768]{1,0:T(8,128)(2,1)S(1)} %slice_bitcast_fusion.refs_2_.refs_3_), channel_id=1, source_target_pairs={{0,1},{1,0},{2,3},{3,2},{4,5},{5,4},{6,7},{7,6},{8,9},{9,8},{10,11... | collective-permute-start | bytes 36872 | tf_op jit(solution)/shard_map/ppermute | solution.py:167
  7.4 7.3 %collective-permute-start.1 = (bf16[8,768]{1,0:T(8,128)(2,1)S(1)}, bf16[8,768]{1,0:T(8,128)(2,1)S(1)}, u32[]{:S(2)}, u32[]{:S(2)}) collective-permute-start(bf16[8,768]{1,0:T(8,128)(2,1)S(1)} %slice_bitcast_fusion.refs_2_.refs_3_), channel_id=1, source_target_pairs={{0,2},{1,3},{2,0},{3,1},{4,6},{5,7},{6,4},{7,5},{8,10},{9,11},{10,... | collective-permute-start | bytes 36872 | tf_op jit(solution)/shard_map/ppermute | solution.py:167
  10.0 5.5 %collective-permute-start.2 = (bf16[8,768]{1,0:T(8,128)(2,1)S(1)}, bf16[8,768]{1,0:T(8,128)(2,1)S(1)}, u32[]{:S(2)}, u32[]{:S(2)}) collective-permute-start(bf16[8,768]{1,0:T(8,128)(2,1)S(1)} %slice_bitcast_fusion.refs_2_.refs_3_), channel_id=1, source_target_pairs={{0,3},{1,2},{2,1},{3,0},{4,7},{5,6},{6,5},{7,4},{8,11},{9,10},{10,... | collective-permute-start | bytes 36872 | tf_op jit(solution)/shard_map/ppermute | solution.py:167
  17.6 15.5 %collective-permute-start.7 = (bf16[192,768]{1,0:T(8,128)(2,1)S(1)}, bf16[192,768]{1,0:T(8,128)(2,1)S(1)}, u32[]{:S(2)}, u32[]{:S(2)}) collective-permute-start(bf16[192,768]{1,0:T(8,128)(2,1)S(1)} %get-tuple-element.301), channel_id=1, source_target_pairs={{16,0},{17,1},{18,2},{19,3},{20,4},{21,5},{22,6},{23,7},{24,8},{25... | collective-permute-start | bytes 884744 | tf_op jit(solution)/shard_map/ppermute | solution.py:164
  20.2 3.8 %collective-permute-start.4 = (f32[8,768]{1,0:T(8,128)S(1)}, f32[8,768]{1,0:T(8,128)S(1)}, u32[]{:S(2)}, u32[]{:S(2)}) collective-permute-start(f32[8,768]{1,0:T(8,128)S(1)} %get-tuple-element.289.refs_1_), channel_id=1, source_target_pairs={{0,8},{4,12},{8,0},{12,4},{1,9},{5,13},{9,1},{13,5},{2,10},{6,14},... | collective-permute-start | bytes 73736 | tf_op jit(solution)/shard_map/ppermute | solution.py:149
  24.0 6.5 %collective-permute-start.6 = (f32[8,768]{1,0:T(8,128)S(1)}, f32[8,768]{1,0:T(8,128)S(1)}, u32[]{:S(2)}, u32[]{:S(2)}) collective-permute-start(f32[8,768]{1,0:T(8,128)S(1)} %get-tuple-element.298.refs_2_), channel_id=1, source_target_pairs={{0,16},{1,17},{2,18},{3,19},{4,20},{5,21},{6,22},{7,23},{8,24},{9,... | collective-permute-start | bytes 73736 | tf_op jit(solution)/shard_map/ppermute | solution.py:161
  34.7 1.7 collective-permute-start.8
  37.7 7.3 %collective-permute-start.9 = (bf16[208,768]{1,0:T(8,128)(2,1)S(1)}, bf16[208,768]{1,0:T(8,128)(2,1)S(1)}, u32[]{:S(2)}, u32[]{:S(2)}) collective-permute-start(bf16[208,768]{1,0:T(8,128)(2,1)S(1)} %get-tuple-element.327), channel_id=1, source_target_pairs={{0,4},{4,0},{8,12},{12,8},{1,5},{5,1},{9,13},{13,9},{2,6},{6,2},{1... | collective-permute-start | bytes 958472 | tf_op jit(solution)/shard_map/ppermute | solution.py:149
  37.9 10.4 %collective-permute-start.10 = (bf16[208,768]{1,0:T(8,128)(2,1)S(1)}, bf16[208,768]{1,0:T(8,128)(2,1)S(1)}, u32[]{:S(2)}, u32[]{:S(2)}) collective-permute-start(bf16[208,768]{1,0:T(8,128)(2,1)S(1)} %get-tuple-element.330), channel_id=1, source_target_pairs={{0,8},{4,12},{8,0},{12,4},{1,9},{5,13},{9,1},{13,5},{2,10},{6,14},... | collective-permute-start | bytes 958472 | tf_op jit(solution)/shard_map/ppermute | solution.py:149
  48.6 4.5 %collective-permute-start.11 = (bf16[208,768]{1,0:T(8,128)(2,1)S(1)}, bf16[208,768]{1,0:T(8,128)(2,1)S(1)}, u32[]{:S(2)}, u32[]{:S(2)}) collective-permute-start(bf16[208,768]{1,0:T(8,128)(2,1)S(1)} %get-tuple-element.337.refs_1_), channel_id=1, source_target_pairs={{0,4},{4,0},{8,12},{12,8},{1,5},{5,1},{9,13},{13,9},{2,6},{6,2},{1... | collective-permute-start | bytes 958472 | tf_op jit(solution)/shard_map/ppermute | solution.py:149
  48.7 10.0 %collective-permute-start.13 = (bf16[208,768]{1,0:T(8,128)(2,1)S(1)}, bf16[208,768]{1,0:T(8,128)(2,1)S(1)}, u32[]{:S(2)}, u32[]{:S(2)}) collective-permute-start(bf16[208,768]{1,0:T(8,128)(2,1)S(1)} %get-tuple-element.337.refs_1_), channel_id=1, source_target_pairs={{0,8},{4,12},{8,0},{12,4},{1,9},{5,13},{9,1},{13,5},{2,10},{6,14},... | collective-permute-start | bytes 958472 | tf_op jit(solution)/shard_map/ppermute | solution.py:149
  50.5 11.5 %collective-permute-start.15 = (bf16[208,768]{1,0:T(8,128)(2,1)S(1)}, bf16[208,768]{1,0:T(8,128)(2,1)S(1)}, u32[]{:S(2)}, u32[]{:S(2)}) collective-permute-start(bf16[208,768]{1,0:T(8,128)(2,1)S(1)} %get-tuple-element.337.refs_1_), channel_id=1, source_target_pairs={{0,16},{16,0},{1,17},{17,1},{2,18},{18,2},{3,19},{19,3},{4,20},{20... | collective-permute-start | bytes 958472 | tf_op jit(solution)/shard_map/ppermute | solution.py:158
  54.2 1.7 collective-permute-start.12
  58.7 1.7 collective-permute-start.14
  58.8 17.0 %collective-permute-start.19 = (bf16[208,768]{1,0:T(8,128)(2,1)S(1)}, bf16[208,768]{1,0:T(8,128)(2,1)S(1)}, u32[]{:S(2)}, u32[]{:S(2)}) collective-permute-start(bf16[208,768]{1,0:T(8,128)(2,1)S(1)} %get-tuple-element.349.refs_1_.refs_2_), channel_id=1, source_target_pairs={{0,16},{16,0},{1,17},{17,1},{2,18},{18,2},{3,19},{19,3},{4,20},{20... | collective-permute-start | bytes 958472 | tf_op jit(solution)/shard_map/ppermute | solution.py:158
  62.0 3.9 %collective-permute-start.17 = (bf16[208,768]{1,0:T(8,128)(2,1)S(1)}, bf16[208,768]{1,0:T(8,128)(2,1)S(1)}, u32[]{:S(2)}, u32[]{:S(2)}) collective-permute-start(bf16[208,768]{1,0:T(8,128)(2,1)S(1)} %get-tuple-element.358.refs_1_.refs_6_), channel_id=1, source_target_pairs={{0,4},{4,0},{8,12},{12,8},{1,5},{5,1},{9,13},{13,9},{2,6},{6,2},{1... | collective-permute-start | bytes 958472 | tf_op jit(solution)/shard_map/ppermute | solution.py:149
  63.6 9.6 %collective-permute-start.18 = (bf16[208,768]{1,0:T(8,128)(2,1)S(1)}, bf16[208,768]{1,0:T(8,128)(2,1)S(1)}, u32[]{:S(2)}, u32[]{:S(2)}) collective-permute-start(bf16[208,768]{1,0:T(8,128)(2,1)S(1)} %get-tuple-element.371), channel_id=1, source_target_pairs={{0,8},{4,12},{8,0},{12,4},{1,9},{5,13},{9,1},{13,5},{2,10},{6,14},... | collective-permute-start | bytes 958472 | tf_op jit(solution)/shard_map/ppermute | solution.py:149
  73.9 10.3 %collective-permute-start.21 = (bf16[208,768]{1,0:T(8,128)(2,1)S(1)}, bf16[208,768]{1,0:T(8,128)(2,1)S(1)}, u32[]{:S(2)}, u32[]{:S(2)}) collective-permute-start(bf16[208,768]{1,0:T(8,128)(2,1)S(1)} %get-tuple-element.393.refs_1_.refs_7_), channel_id=1, source_target_pairs={{0,4},{4,0},{8,12},{12,8},{1,5},{5,1},{9,13},{13,9},{2,6},{6,2},{1... | collective-permute-start | bytes 958472 | tf_op jit(solution)/shard_map/ppermute | solution.py:149
  74.0 12.8 %collective-permute-start.22 = (bf16[208,768]{1,0:T(8,128)(2,1)S(1)}, bf16[208,768]{1,0:T(8,128)(2,1)S(1)}, u32[]{:S(2)}, u32[]{:S(2)}) collective-permute-start(bf16[208,768]{1,0:T(8,128)(2,1)S(1)} %get-tuple-element.393.refs_1_.refs_7_), channel_id=1, source_target_pairs={{0,8},{4,12},{8,0},{12,4},{1,9},{5,13},{9,1},{13,5},{2,10},{6,14},... | collective-permute-start | bytes 958472 | tf_op jit(solution)/shard_map/ppermute | solution.py:149
  79.3 9.8 %collective-permute-start.23 = (bf16[192,768]{1,0:T(8,128)(2,1)S(1)}, bf16[192,768]{1,0:T(8,128)(2,1)S(1)}, u32[]{:S(2)}, u32[]{:S(2)}) collective-permute-start(bf16[192,768]{1,0:T(8,128)(2,1)S(1)} %get-tuple-element.418), channel_id=1, source_target_pairs={{0,1},{1,0},{2,3},{3,2},{4,5},{5,4},{6,7},{7,6},{8,9},{9,8},{10,11... | collective-permute-start | bytes 884744 | tf_op jit(solution)/shard_map/ppermute | solution.py:167
  86.8 5.2 %collective-permute-start.24 = (bf16[208,768]{1,0:T(8,128)(2,1)S(1)}, bf16[208,768]{1,0:T(8,128)(2,1)S(1)}, u32[]{:S(2)}, u32[]{:S(2)}) collective-permute-start(bf16[208,768]{1,0:T(8,128)(2,1)S(1)} %get-tuple-element.412.refs_1_.refs_8_), channel_id=1, source_target_pairs={{0,4},{4,0},{8,12},{12,8},{1,5},{5,1},{9,13},{13,9},{2,6},{6,2},{1... | collective-permute-start | bytes 958472 | tf_op jit(solution)/shard_map/ppermute | solution.py:149
  86.9 12.6 %collective-permute-start.26 = (bf16[384,384]{1,0:T(8,128)(2,1)S(1)}, bf16[384,384]{1,0:T(8,128)(2,1)S(1)}, u32[]{:S(2)}, u32[]{:S(2)}) collective-permute-start(bf16[384,384]{1,0:T(8,128)(2,1)S(1)} %get-tuple-element.445), channel_id=1, source_target_pairs={{0,1},{1,0},{2,3},{3,2},{4,5},{5,4},{6,7},{7,6},{8,9},{9,8},{10,11... | collective-permute-start | bytes 884744 | tf_op jit(solution)/shard_map/ppermute | solution.py:167
  89.4 10.3 %collective-permute-start.27 = (bf16[96,768]{1,0:T(8,128)(2,1)S(1)}, bf16[96,768]{1,0:T(8,128)(2,1)S(1)}, u32[]{:S(2)}, u32[]{:S(2)}) collective-permute-start(bf16[96,768]{1,0:T(8,128)(2,1)S(1)} %get-tuple-element.448), channel_id=1, source_target_pairs={{0,2},{1,3},{2,0},{3,1},{4,6},{5,7},{6,4},{7,5},{8,10},{9,11},{10,... | collective-permute-start | bytes 442376 | tf_op jit(solution)/shard_map/ppermute | solution.py:167
  93.8 2.9 %collective-permute-start.25 = (bf16[32,768]{1,0:T(8,128)(2,1)S(1)}, bf16[32,768]{1,0:T(8,128)(2,1)S(1)}, u32[]{:S(2)}, u32[]{:S(2)}) collective-permute-start(bf16[32,768]{1,0:T(8,128)(2,1)S(1)} %get-tuple-element.442.refs_1_), channel_id=1, source_target_pairs={{0,4},{4,0},{8,12},{12,8},{1,5},{5,1},{9,13},{13,9},{2,6},{6,2},{1... | collective-permute-start | bytes 147464 | tf_op jit(solution)/shard_map/ppermute | solution.py:149
  95.0 16.2 %collective-permute-start.29 = (bf16[384,768]{1,0:T(8,128)(2,1)S(1)}, bf16[384,768]{1,0:T(8,128)(2,1)S(1)}, u32[]{:S(2)}, u32[]{:S(2)}) collective-permute-start(bf16[384,768]{1,0:T(8,128)(2,1)S(1)} %get-tuple-element.453), channel_id=1, source_target_pairs={{0,16},{16,0},{1,17},{17,1},{2,18},{18,2},{3,19},{19,3},{4,20},{20... | collective-permute-start | bytes 1769480 | tf_op jit(solution)/shard_map/ppermute | solution.py:158
  96.7 4.2 %collective-permute-start.28 = (bf16[32,768]{1,0:T(8,128)(2,1)S(1)}, bf16[32,768]{1,0:T(8,128)(2,1)S(1)}, u32[]{:S(2)}, u32[]{:S(2)}) collective-permute-start(bf16[32,768]{1,0:T(8,128)(2,1)S(1)} %get-tuple-element.450.refs_1_), channel_id=1, source_target_pairs={{0,8},{4,12},{8,0},{12,4},{1,9},{5,13},{9,1},{13,5},{2,10},{6,14},... | collective-permute-start | bytes 147464 | tf_op jit(solution)/shard_map/ppermute | solution.py:149
  99.6 13.6 %collective-permute-start.30 = (bf16[192,384]{1,0:T(8,128)(2,1)S(1)}, bf16[192,384]{1,0:T(8,128)(2,1)S(1)}, u32[]{:S(2)}, u32[]{:S(2)}) collective-permute-start(bf16[192,384]{1,0:T(8,128)(2,1)S(1)} %get-tuple-element.456), channel_id=1, source_target_pairs={{0,2},{1,3},{2,0},{3,1},{4,6},{5,7},{6,4},{7,5},{8,10},{9,11},{10,... | collective-permute-start | bytes 442376 | tf_op jit(solution)/shard_map/ppermute | solution.py:167
  100.9 12.3 %collective-permute-start.31 = (bf16[32,768]{1,0:T(8,128)(2,1)S(1)}, bf16[32,768]{1,0:T(8,128)(2,1)S(1)}, u32[]{:S(2)}, u32[]{:S(2)}) collective-permute-start(bf16[32,768]{1,0:T(8,128)(2,1)S(1)} %get-tuple-element.458.refs_1_), channel_id=1, source_target_pairs={{0,16},{16,0},{1,17},{17,1},{2,18},{18,2},{3,19},{19,3},{4,20},{20... | collective-permute-start | bytes 147464 | tf_op jit(solution)/shard_map/ppermute | solution.py:158
  101.4 13.2 %collective-permute-start.32 = (bf16[96,768]{1,0:T(8,128)(2,1)S(1)}, bf16[96,768]{1,0:T(8,128)(2,1)S(1)}, u32[]{:S(2)}, u32[]{:S(2)}) collective-permute-start(bf16[96,768]{1,0:T(8,128)(2,1)S(1)} %get-tuple-element.460.refs_1_), channel_id=1, source_target_pairs={{0,2},{1,3},{2,0},{3,1},{4,6},{5,7},{6,4},{7,5},{8,10},{9,11},{10,... | collective-permute-start | bytes 442376 | tf_op jit(solution)/shard_map/ppermute | solution.py:167
  111.5 13.2 %collective-permute-start.33 = (bf16[192,768]{1,0:T(8,128)(2,1)S(1)}, bf16[192,768]{1,0:T(8,128)(2,1)S(1)}, u32[]{:S(2)}, u32[]{:S(2)}) collective-permute-start(bf16[192,768]{1,0:T(8,128)(2,1)S(1)} %get-tuple-element.463), channel_id=1, source_target_pairs={{0,1},{1,0},{2,3},{3,2},{4,5},{5,4},{6,7},{7,6},{8,9},{9,8},{10,11... | collective-permute-start | bytes 884744 | tf_op jit(solution)/shard_map/ppermute | solution.py:167
  113.2 12.5 %collective-permute-start.34 = (bf16[32,768]{1,0:T(8,128)(2,1)S(1)}, bf16[32,768]{1,0:T(8,128)(2,1)S(1)}, u32[]{:S(2)}, u32[]{:S(2)}) collective-permute-start(bf16[32,768]{1,0:T(8,128)(2,1)S(1)} %get-tuple-element.465.refs_1_), channel_id=1, source_target_pairs={{0,1},{1,0},{2,3},{3,2},{4,5},{5,4},{6,7},{7,6},{8,9},{9,8},{10,11... | collective-permute-start | bytes 147464 | tf_op jit(solution)/shard_map/ppermute | solution.py:167
  113.7 15.0 %collective-permute-start.35 = (bf16[192,384]{1,0:T(8,128)(2,1)S(1)}, bf16[192,384]{1,0:T(8,128)(2,1)S(1)}, u32[]{:S(2)}, u32[]{:S(2)}) collective-permute-start(bf16[192,384]{1,0:T(8,128)(2,1)S(1)} %get-tuple-element.467.refs_1_), channel_id=1, source_target_pairs={{0,2},{1,3},{2,0},{3,1},{4,6},{5,7},{6,4},{7,5},{8,10},{9,11},{10,... | collective-permute-start | bytes 442376 | tf_op jit(solution)/shard_map/ppermute | solution.py:167
  114.6 19.9 %collective-permute-start.36 = (bf16[192,768]{1,0:T(8,128)(2,1)S(1)}, bf16[192,768]{1,0:T(8,128)(2,1)S(1)}, u32[]{:S(2)}, u32[]{:S(2)}) collective-permute-start(bf16[192,768]{1,0:T(8,128)(2,1)S(1)} %get-tuple-element.469.refs_1_), channel_id=1, source_target_pairs={{0,1},{1,0},{2,3},{3,2},{4,5},{5,4},{6,7},{7,6},{8,9},{9,8},{10,11... | collective-permute-start | bytes 884744 | tf_op jit(solution)/shard_map/ppermute | solution.py:167
  125.7 11.0 %collective-permute-start.37 = (bf16[64,768]{1,0:T(8,128)(2,1)S(1)}, bf16[64,768]{1,0:T(8,128)(2,1)S(1)}, u32[]{:S(2)}, u32[]{:S(2)}) collective-permute-start(bf16[64,768]{1,0:T(8,128)(2,1)S(1)} %get-tuple-element.471.refs_1_), channel_id=1, source_target_pairs={{0,2},{1,3},{2,0},{3,1},{4,6},{5,7},{6,4},{7,5},{8,10},{9,11},{10,... | collective-permute-start | bytes 294920 | tf_op jit(solution)/shard_map/ppermute | solution.py:167
  125.8 14.7 %collective-permute-start.39 = (bf16[96,768]{1,0:T(8,128)(2,1)S(1)}, bf16[96,768]{1,0:T(8,128)(2,1)S(1)}, u32[]{:S(2)}, u32[]{:S(2)}) collective-permute-start(bf16[96,768]{1,0:T(8,128)(2,1)S(1)} %get-tuple-element.485), channel_id=1, source_target_pairs={{0,2},{1,3},{2,0},{3,1},{4,6},{5,7},{6,4},{7,5},{8,10},{9,11},{10,... | collective-permute-start | bytes 442376 | tf_op jit(solution)/shard_map/ppermute | solution.py:167
  128.8 14.2 %collective-permute-start.40 = (bf16[384,384]{1,0:T(8,128)(2,1)S(1)}, bf16[384,384]{1,0:T(8,128)(2,1)S(1)}, u32[]{:S(2)}, u32[]{:S(2)}) collective-permute-start(bf16[384,384]{1,0:T(8,128)(2,1)S(1)} %get-tuple-element.487.refs_1_), channel_id=1, source_target_pairs={{0,1},{1,0},{2,3},{3,2},{4,5},{5,4},{6,7},{7,6},{8,9},{9,8},{10,11... | collective-permute-start | bytes 884744 | tf_op jit(solution)/shard_map/ppermute | solution.py:167
  134.6 14.2 %collective-permute-start.42 = (bf16[384,768]{1,0:T(8,128)(2,1)S(1)}, bf16[384,768]{1,0:T(8,128)(2,1)S(1)}, u32[]{:S(2)}, u32[]{:S(2)}) collective-permute-start(bf16[384,768]{1,0:T(8,128)(2,1)S(1)} %get-tuple-element.496.refs_1_), channel_id=1, source_target_pairs={{0,16},{16,0},{1,17},{17,1},{2,18},{18,2},{3,19},{19,3},{4,20},{20... | collective-permute-start | bytes 1769480 | tf_op jit(solution)/shard_map/ppermute | solution.py:158
  139.6 4.4 %collective-permute-start.41 = (bf16[48,768]{1,0:T(8,128)(2,1)S(1)}, bf16[48,768]{1,0:T(8,128)(2,1)S(1)}, u32[]{:S(2)}, u32[]{:S(2)}) collective-permute-start(bf16[48,768]{1,0:T(8,128)(2,1)S(1)} %get-tuple-element.489.refs_1_), channel_id=1, source_target_pairs={{0,8},{4,12},{8,0},{12,4},{1,9},{5,13},{9,1},{13,5},{2,10},{6,14},... | collective-permute-start | bytes 221192 | tf_op jit(solution)/shard_map/ppermute | solution.py:149
  140.6 12.2 %collective-permute-start.45 = (bf16[96,768]{1,0:T(8,128)(2,1)S(1)}, bf16[96,768]{1,0:T(8,128)(2,1)S(1)}, u32[]{:S(2)}, u32[]{:S(2)}) collective-permute-start(bf16[96,768]{1,0:T(8,128)(2,1)S(1)} %get-tuple-element.505.refs_1_), channel_id=1, source_target_pairs={{0,2},{1,3},{2,0},{3,1},{4,6},{5,7},{6,4},{7,5},{8,10},{9,11},{10,... | collective-permute-start | bytes 442376 | tf_op jit(solution)/shard_map/ppermute | solution.py:167
  144.1 6.4 %collective-permute-start.43 = (bf16[48,768]{1,0:T(8,128)(2,1)S(1)}, bf16[48,768]{1,0:T(8,128)(2,1)S(1)}, u32[]{:S(2)}, u32[]{:S(2)}) collective-permute-start(bf16[48,768]{1,0:T(8,128)(2,1)S(1)} %get-tuple-element.498.refs_8_), channel_id=1, source_target_pairs={{0,16},{1,17},{2,18},{3,19},{4,20},{5,21},{6,22},{7,23},{8,24},{9,... | collective-permute-start | bytes 221192 | tf_op jit(solution)/shard_map/ppermute | solution.py:161
  148.7 3.2 %collective-permute-start.44 = (bf16[2,2,208,384]{3,2,1,0:T(8,128)(2,1)S(1)}, bf16[2,2,208,384]{3,2,1,0:T(8,128)(2,1)S(1)}, u32[]{:S(2)}, u32[]{:S(2)}) collective-permute-start(bf16[2,2,208,384]{3,2,1,0:T(8,128)(2,1)S(1)} %get-tuple-element.503), channel_id=1, source_target_pairs={{0,4},{4,0},{8,12},{12,8},{1,5},{5,1},{9,13},{13,9},{2,6},{6,2},{1... | collective-permute-start | bytes 1916936 | tf_op jit(solution)/shard_map/ppermute | solution.py:149
  148.7 16.2 %collective-permute-start.48 = (bf16[768,384]{1,0:T(8,128)(2,1)S(1)}, bf16[768,384]{1,0:T(8,128)(2,1)S(1)}, u32[]{:S(2)}, u32[]{:S(2)}) collective-permute-start(bf16[768,384]{1,0:T(8,128)(2,1)S(1)} %get-tuple-element.518.refs_1_), channel_id=1, source_target_pairs={{0,16},{16,0},{1,17},{17,1},{2,18},{18,2},{3,19},{19,3},{4,20},{20... | collective-permute-start | bytes 1769480 | tf_op jit(solution)/shard_map/ppermute | solution.py:158
  152.1 9.9 %collective-permute-start.46 = (bf16[2,208,384]{2,1,0:T(8,128)(2,1)S(1)}, bf16[2,208,384]{2,1,0:T(8,128)(2,1)S(1)}, u32[]{:S(2)}, u32[]{:S(2)}) collective-permute-start(bf16[2,208,384]{2,1,0:T(8,128)(2,1)S(1)} %get-tuple-element.508), channel_id=1, source_target_pairs={{0,8},{4,12},{8,0},{12,4},{1,9},{5,13},{9,1},{13,5},{2,10},{6,14},... | collective-permute-start | bytes 958472 | tf_op jit(solution)/shard_map/ppermute | solution.py:149
  152.7 12.1 %collective-permute-start.47 = (bf16[192,768]{1,0:T(8,128)(2,1)S(1)}, bf16[192,768]{1,0:T(8,128)(2,1)S(1)}, u32[]{:S(2)}, u32[]{:S(2)}) collective-permute-start(bf16[192,768]{1,0:T(8,128)(2,1)S(1)} %get-tuple-element.516.refs_1_), channel_id=1, source_target_pairs={{0,1},{1,0},{2,3},{3,2},{4,5},{5,4},{6,7},{7,6},{8,9},{9,8},{10,11... | collective-permute-start | bytes 884744 | tf_op jit(solution)/shard_map/ppermute | solution.py:167
  164.8 2.1 %collective-permute-start.49 = (bf16[2,2,208,384]{3,2,1,0:T(8,128)(2,1)S(1)}, bf16[2,2,208,384]{3,2,1,0:T(8,128)(2,1)S(1)}, u32[]{:S(2)}, u32[]{:S(2)}) collective-permute-start(bf16[2,2,208,384]{3,2,1,0:T(8,128)(2,1)S(1)} %get-tuple-element.521), channel_id=1, source_target_pairs={{0,4},{4,0},{8,12},{12,8},{1,5},{5,1},{9,13},{13,9},{2,6},{6,2},{1... | collective-permute-start | bytes 1916936 | tf_op jit(solution)/shard_map/ppermute | solution.py:149
  167.1 9.6 %collective-permute-start.50 = (bf16[2,208,384]{2,1,0:T(8,128)(2,1)S(1)}, bf16[2,208,384]{2,1,0:T(8,128)(2,1)S(1)}, u32[]{:S(2)}, u32[]{:S(2)}) collective-permute-start(bf16[2,208,384]{2,1,0:T(8,128)(2,1)S(1)} %get-tuple-element.524), channel_id=1, source_target_pairs={{0,8},{4,12},{8,0},{12,4},{1,9},{5,13},{9,1},{13,5},{2,10},{6,14},... | collective-permute-start | bytes 958472 | tf_op jit(solution)/shard_map/ppermute | solution.py:149
  168.3 16.2 %collective-permute-start.51 = (bf16[384,768]{1,0:T(8,128)(2,1)S(1)}, bf16[384,768]{1,0:T(8,128)(2,1)S(1)}, u32[]{:S(2)}, u32[]{:S(2)}) collective-permute-start(bf16[384,768]{1,0:T(8,128)(2,1)S(1)} %get-tuple-element.530.refs_1_), channel_id=1, source_target_pairs={{0,16},{1,17},{2,18},{3,19},{4,20},{5,21},{6,22},{7,23},{8,24},{9,... | collective-permute-start | bytes 1769480 | tf_op jit(solution)/shard_map/ppermute | solution.py:161
  (22 other events, 157.2 us)

commit v4 on v3

--- a/solution.py
+++ b/solution.py
@@ -386,11 +386,40 @@
             flops=2 * rows * (width * model + 2 * heads * rows * HEAD_DIM),
         )
 
-    def residual_kernel(a, b, x, vrow, vecs, resid_o, low_o):
-        resid = x[...].astype(F32) + add(a[...], b[...]) + vrow[2:3]
-        resid_o[...] = resid
+    first_rows = rows // 32 * 16 + 16
+
+    row_parts = (slice(0, first_rows), slice(first_rows, rows))
+
+    def add_parts(a, b):
+        def kernel(a_ref, b_ref, *outs):
+            for at, out in zip(row_parts, outs):
+                out[...] = add(a_ref[at, :], b_ref[at, :]).astype(BF16)
+
+        return stage(
+            kernel, [a, b], [near((at.stop - at.start, model), BF16) for at in row_parts]
+        )
+
+    def join_parts(a, b):
+        def kernel(a_ref, b_ref, out):
+            for at, ref in zip(row_parts, (a_ref, b_ref)):
+                out[at, :] = ref[...]
+
+        return stage(kernel, [a, b], [near((rows, model), a.dtype)])[0]
+
+    def residual_of(at, a, b, x, vrow, vecs):
+        resid = x[at, :].astype(F32) + add(a[at, :], b[...]) + vrow[2:3]
         normed, _ = norm_parts(resid)
-        low_o[...] = (normed * vecs[1:2] + vecs[2:3]).astype(BF16)
+        return resid, (normed * vecs[1:2] + vecs[2:3]).astype(BF16)
+
+    def residual_first_kernel(a, b, x, vrow, vecs, resid_o, low_o):
+        resid_o[...], low_o[...] = residual_of(row_parts[0], a, b, x, vrow, vecs)
+
+    def residual_last_kernel(a, b, x, vrow, vecs, resid_in, low_in, resid_o, low_o, part_o):
+        resid, low = residual_of(row_parts[1], a, b, x, vrow, vecs)
+        for at, one, two in zip(row_parts, (resid_in[...], resid), (low_in[...], low)):
+            resid_o[at, :] = one
+            low_o[at, :] = two
+        part_o[...] = low
 
     def relay_kernel(v, out):
         out[...] = v[...]
@@ -583,21 +612,30 @@
     def whole_of_columns(keep, other):
         return stage(put_columns, [keep, other], [shape_of((model, model), F32)])[0]
 
-    def residual_back_kernel(a, b, resid, g, vecs, grad_o, low_o, small_o):
-        incoming = add(a[...], b[...])
-        normed, inverse = norm_parts(resid[...])
-        real = lax.broadcasted_iota(jnp.int32, (rows, model), 0) < patch
+    def residual_back_of(at, a, b, resid, g, vecs):
+        incoming = add(a[at, :], b[...])
+        normed, inverse = norm_parts(resid[at, :])
+        real = lax.broadcasted_iota(jnp.int32, incoming.shape, 0) < patch - at.start
         incoming = jnp.where(real, incoming, 0.0)
-        grad = g[...].astype(F32) + norm_back(incoming, normed, inverse, vecs[1:2])
+        from_out = g[at, :].astype(F32)
+        grad = from_out + norm_back(incoming, normed, inverse, vecs[1:2])
         grad = jnp.where(real, grad, 0.0)
-        grad_o[...] = grad
         low = grad.astype(BF16)
-        low_o[...] = low
-        small_o[...] = jnp.zeros_like(small_o)
-        small_o[0:1, :] = row_sum(incoming * normed)
-        small_o[1:2, :] = row_sum(incoming)
-        small_o[2:3, :] = row_sum(low.astype(F32))
-        small_o[3:4, :] = row_sum(g[...].astype(F32))
+        sums = [row_sum(incoming * normed), row_sum(incoming), row_sum(low.astype(F32)), row_sum(from_out)]
+        return grad, low, jnp.concatenate(sums + [jnp.zeros((4, model), F32)], axis=0)
+
+    def residual_back_first_kernel(a, b, resid, g, vecs, grad_o, low_o, small_o):
+        grad_o[...], low_o[...], small_o[...] = residual_back_of(row_parts[0], a, b, resid, g, vecs)
+
+    def residual_back_last_kernel(
+        a, b, resid, g, vecs, grad_in, low_in, small_in, grad_o, low_o, part_o, small_o
+    ):
+        grad, low, small = residual_back_of(row_parts[1], a, b, resid, g, vecs)
+        for at, one, two in zip(row_parts, (grad_in[...], grad), (low_in[...], low)):
+            grad_o[at, :] = one
+            low_o[at, :] = two
+        part_o[...] = low
+        small_o[...] = small_in[...] + small
 
     def column_out(values_in, slot, keep_o, send_o):
         ten = lax.axis_index("tensor")
@@ -850,6 +888,7 @@
         out[size:, :] = b[...]
 
     stage.cost = 0
+    sent_out = y_early(own_out)
     cls_all = gather_clips(frames[0, :, 0, :])
     vectors, own_vec, near_in, in_and_vec = stage(
         small_kernel,
@@ -887,7 +926,6 @@
         far=1,
     )
     from_core = core_swap(part_zero)
-    sent_out = y_early(relay(near_out))
     (part_zero,) = adds((part_zero, from_core))
     from_x = x_swap(part_zero)
     (part_zero,) = adds((part_zero, from_x))
@@ -910,18 +948,24 @@
     at3 = attend(3)
     ac3 = core_swap(at3[0])
     at2 = attend(2)
-    (two,) = adds((at2[0], ac3))
-    ax = x_swap(two)
+    two0, two1 = add_parts(at2[0], ac3)
+    ax0 = x_swap(two0)
+    ax1 = x_swap(two1)
     at1 = attend(1)
     ac1 = core_swap(at1[0])
     at0 = attend(0)
     g_slots = slots(grads_in, 2 * half)
     (aown,) = adds((at0[0], ac1))
-    resid_own, low_own = stage(
-        residual_kernel, [aown, ax, x_slots[0], vec, vectors],
-        [near((rows, model), F32), near((rows, model), BF16)],
-    )
-    lx = x_swap(low_own)
+    resid0, low0 = stage(
+        residual_first_kernel, [aown, ax0, x_slots[0], vec, vectors],
+        [near((first_rows, model), F32), near((first_rows, model), BF16)],
+    )
+    lx0 = x_swap(low0)
+    resid_own, low_own, low1 = stage(
+        residual_last_kernel, [aown, ax1, x_slots[0], vec, vectors, resid0, low0],
+        [near((rows, model), F32), near((rows, model), BF16), near((rows - first_rows, model), BF16)],
+    )
+    lx1 = x_swap(low1)
     l1 = core_swap(low_own)
     ly = y_swap(low_own)
     g_hidden = stage(
@@ -932,7 +976,7 @@
     fc1 = core_swap(gp1)
     fc_out_half = own_part(own_out_kernel, (half_rows, model), hid0, hid1, g_slots[0], g_slots[1])
     (fown,) = adds((gp0, fc1))
-    l2 = relay(lx)
+    l2 = join_parts(lx0, lx1)
     l3 = core_swap(l2)
     ly2 = y_swap(l2)
     hid2, pre2, gp2, bs2 = feed(l2, g_hidden[2])
@@ -940,23 +984,33 @@
     fc3 = core_swap(gp3)
     m0 = relay(ly)
     m1 = core_swap(m0)
-    (two,) = adds((gp2, fc3))
-    fx = x_swap(two)
+    two0, two1 = add_parts(gp2, fc3)
+    fx0 = x_swap(two0)
+    fx1 = x_swap(two1)
     ho0, po0 = feed_other(m0, g_slots[4])
     ho1, po1 = feed_other(m1, g_slots[5])
-    fc_in_half = own_part(own_in_kernel, (model, half_rows), low_own, l1, pre0, pre1)
     block_parts = stage(
         mlp_kernel, [hid0, hid1, hid2, hid3, fc_out, resid_own, vectors],
         [near((rows, model), BF16)] * half,
     )
-    grad_resid, grad_low, small_two = stage(
-        residual_back_kernel, [fown, fx, resid_own, g_slots[0], vectors],
-        [near((rows, model), F32), near((rows, model), BF16), near((8, model), F32)],
-    )
-    bx = x_swap(grad_low)
-    b1 = core_swap(grad_low)
+    fc_in_half = own_part(own_in_kernel, (model, half_rows), low_own, l1, pre0, pre1)
+    grad0, glow0, small0 = stage(
+        residual_back_first_kernel, [fown, fx0, resid_own, g_slots[0], vectors],
+        [near((first_rows, model), F32), near((first_rows, model), BF16), near((8, model), F32)],
+    )
+    bx0 = x_swap(glow0)
     m2 = relay(ly2)
     m3 = core_swap(m2)
+    grad_resid, grad_low, glow1, small_two = stage(
+        residual_back_last_kernel,
+        [fown, fx1, resid_own, g_slots[0], vectors, grad0, glow0, small0],
+        [
+            near((rows, model), F32), near((rows, model), BF16),
+            near((rows - first_rows, model), BF16), near((8, model), F32),
+        ],
+    )
+    bx1 = x_swap(glow1)
+    b1 = core_swap(grad_low)
     ho2, po2 = feed_other(m2, g_slots[6])
     ho3, po3 = feed_other(m3, g_slots[7])
     p0 = whole_part(
@@ -971,7 +1025,7 @@
         attend_weight_half_kernel, [gr0, gr1, lo0, lo1, at0[1], at1[1], grad_low, b1],
         [near((4 * width, model), F32)],
     )
-    b2 = relay(bx)
+    b2 = join_parts(bx0, bx1)
     b3 = core_swap(b2)
     ba2, gr2, lo2, sm2 = attend_back(2, b2, at2)
     p1 = over_far_clip(*p0)
@@ -1036,7 +1090,6 @@
     bzy = y_late(bz2)
     ck, send = stage(column_kernel, [ba0, ba1, ba2, ba3], column_shapes)
     cs = core_swap(send)
-    fc_out_grad = whole(*p4)
     msg_w_grad, cls_part, vec_grads, qv_grad = stage(
         message_end,
         [*packs, *cls_all, sent_all, bz2, bzy, near_msg_w, qv_zero, bias_zero],
@@ -1048,16 +1101,17 @@
         ],
         [pltpu.VMEM((model, all_rows), F32), pltpu.VMEM((24, model), F32)],
     )
+    fc_out_grad = whole(*p4)
     kept, far = far_columns(ck, cs)
+    bk, send = stage(column_kernel, block_parts, column_shapes)
+    bcs = core_swap(send)
     r4 = to_near_clip(*r3)
     (frames_grad,) = stage(
         frames_grad_kernel, [kept, far, cls_part], [shape_of((half, width, patch), BF16)],
     )
-    bk, send = stage(column_kernel, block_parts, column_shapes)
-    bcs = core_swap(send)
+    bkept, bfar = far_columns(bk, bcs)
+    fc_in_grad = whole_of_columns(*q4)
     r5 = to_sections(*r4, move=y_late)
-    fc_in_grad = whole_of_columns(*q4)
-    bkept, bfar = far_columns(bk, bcs)
     (block_out,) = stage(
         block_out_kernel, [bkept, bfar], [shape_of((half, width, patch), BF16)],
     )

time: 189 us -> 183 us (0.968)
  waiting for transfers between devices: 71.8 us -> 61.3 us
  starting transfers between devices: 52.9 us -> 56.6 us
    ppermute x24 -> x28, waiting for transfers between devices: 34.2 us -> 19.8 us  [tensor_swap(): return lax.ppermute(v, 'tensor', [(i, i ^ bit) for i in range(4)])]
    ppermute x24 -> x28, starting transfers between devices: 14 us -> 18.5 us  [tensor_swap(): return lax.ppermute(v, 'tensor', [(i, i ^ bit) for i in range(4)])]
    pallas_call x76 -> x77, Pallas kernels: 57.2 us -> 57.5 us  [__call__(): pl.pallas_call(stage, out_shape=[*outs, near((8, 128), F32)], in_specs=[p...]
  transfers between devices with their start and end apart: 52 -> 56, of which waited for: 26 -> 26; matrix products, arithmetic and copies ran while one was open for 1% -> 1% of each run, Pallas kernels for 27% -> 29%
where the time goes in v4:
time: 183 us; the launch traced here: 180 us
  waiting for transfers between devices  61.3 us (33%)
  Pallas kernels  57.5 us (31%)
  starting transfers between devices  56.6 us (31%)
  local copies, waits for them, and re-layouts  2.59 us (1%)
    pallas_call x77, Pallas kernels, __call__(): pl.pallas_call(stage, out_shape=[*outs, near((8, 128), F32)], in_specs=[p...  57.5 us
    ppermute x17, waiting for transfers between devices, z_swap(): return lax.ppermute(v, 'dp', [(i, i ^ bit) for i in range(clips)])  22.3 us
    ppermute x28, waiting for transfers between devices, tensor_swap(): return lax.ppermute(v, 'tensor', [(i, i ^ bit) for i in range(4)])  19.8 us
    ppermute x17, starting transfers between devices, z_swap(): return lax.ppermute(v, 'dp', [(i, i ^ bit) for i in range(clips)])  19.7 us
    ppermute x28, starting transfers between devices, tensor_swap(): return lax.ppermute(v, 'tensor', [(i, i ^ bit) for i in range(4)])  18.5 us
    ppermute x3, starting transfers between devices, y_late(): return lax.ppermute(v, 'pipe', [(0, 1)])  11.4 us
    ppermute x3, waiting for transfers between devices, y_late(): return lax.ppermute(v, 'pipe', [(0, 1)])  8.38 us
    ppermute x6, waiting for transfers between devices, y_swap(): return lax.ppermute(v, 'pipe', [(0, 1), (1, 0)])  8.12 us
  transfers between devices with their start and end apart: 56, of which 26 were waited for; matrix products, arithmetic and copies ran while one was open for 1% of the time, Pallas kernels for 29%

profile of v4, /device:TPU:0, one launch (start us, length us, event | category | flops | bytes accessed | tf_op | source)
XLA Modules:
  0.0 179.7 jit_solution(11606963893563509222)
XLA Ops:
  0.6 1.7 shard_map.288
  5.7 3.0 %collective-permute-start = (bf16[8,768]{1,0:T(8,128)(2,1)S(1)}, bf16[8,768]{1,0:T(8,128)(2,1)S(1)}, u32[]{:S(2)}, u32[]{:S(2)}) collective-permute-start(bf16[8,768]{1,0:T(8,128)(2,1)S(1)} %slice_bitcast_fusion.refs_2_.refs_3_), channel_id=1, source_target_pairs={{0,1},{1,0},{2,3},{3,2},{4,5},{5,4},{6,7},{7,6},{8,9},{9,8},{10,11... | collective-permute-start | bytes 36872 | tf_op jit(solution)/shard_map/ppermute | solution.py:167
  8.7 2.6 %collective-permute-start.1 = (bf16[8,768]{1,0:T(8,128)(2,1)S(1)}, bf16[8,768]{1,0:T(8,128)(2,1)S(1)}, u32[]{:S(2)}, u32[]{:S(2)}) collective-permute-start(bf16[8,768]{1,0:T(8,128)(2,1)S(1)} %slice_bitcast_fusion.refs_2_.refs_3_), channel_id=1, source_target_pairs={{0,2},{1,3},{2,0},{3,1},{4,6},{5,7},{6,4},{7,5},{8,10},{9,11},{10,... | collective-permute-start | bytes 36872 | tf_op jit(solution)/shard_map/ppermute | solution.py:167
  12.6 3.3 %shard_map.290 = (bf16[208,768]{1,0:T(8,128)(2,1)S(1)}, bf16[208,768]{1,0:T(8,128)(2,1)S(1)}, bf16[208,768]{1,0:T(8,128)(2,1)S(1)}, bf16[208,768]{1,0:T(8,128)(2,1)S(1)}, f32[8,128]{1,0:T(8,128)S(1)}) custom-call(f32[8,128]{1,0:T(8,128)S(1)} %get-tuple-element.287.refs_0_, bf16[197,8,768]{2,1,0:T(8,128)(2,1)} %bitcast.25), custom_call_target="tpu_custom_call" | custom-call | tf_op jit(solution)/shard_map/pallas_call | solution.py:78
  16.8 2.1 %shard_map.291 = (f32[32,768]{1,0:T(8,128)S(1)}, bf16[32,768]{1,0:T(8,128)(2,1)S(1)}, bf16[32,192]{1,0:T(8,128)(2,1)S(1)}, bf16[32,192]{1,0:T(8,128)(2,1)S(1)}, ...) custom-call(f32[8,128]{1,0:T(8,128)S(1)} %get-tuple-element.288.refs, ...), custom_call_target="tpu_custom_call" | custom-call | tf_op jit(solution)/shard_map/pallas_call | solution.py:78
  20.2 1.5 collective-permute-start.4
  21.6 2.3 %collective-permute-done.4.refs_2_ = f32[8,768]{1,0:T(8,128)S(1)} collective-permute-done((f32[8,768]{1,0:T(8,128)S(1)}, f32[8,768]{1,0:T(8,128)S(1)}, u32[]{:S(2)}, u32[]{:S(2)}) %collective-permute-start.4) | collective-permute-done | bytes 24608 | tf_op jit(solution)/shard_map/ppermute | solution.py:149
  24.0 4.8 %collective-permute-start.6 = (f32[8,768]{1,0:T(8,128)S(1)}, f32[8,768]{1,0:T(8,128)S(1)}, u32[]{:S(2)}, u32[]{:S(2)}) collective-permute-start(f32[8,768]{1,0:T(8,128)S(1)} %get-tuple-element.306.refs_2_), channel_id=1, source_target_pairs={{0,16},{1,17},{2,18},{3,19},{4,20},{5,21},{6,22},{7,23},{8,24},{9,... | collective-permute-start | bytes 73736 | tf_op jit(solution)/shard_map/ppermute | solution.py:161
  28.8 1.6 shard_map.294
  30.4 2.6 %collective-permute-done.7.refs_7_ = bf16[192,768]{1,0:T(8,128)(2,1)S(1)} collective-permute-done((bf16[192,768]{1,0:T(8,128)(2,1)}, bf16[192,768]{1,0:T(8,128)(2,1)S(1)}, u32[]{:S(2)}, u32[]{:S(2)}) %collective-permute-start.7) | collective-permute-done | bytes 294944 | tf_op jit(solution)/shard_map/ppermute | solution.py:164
  37.9 2.4 %collective-permute-start.10 = (bf16[112,768]{1,0:T(8,128)(2,1)S(1)}, bf16[112,768]{1,0:T(8,128)(2,1)S(1)}, u32[]{:S(2)}, u32[]{:S(2)}) collective-permute-start(bf16[112,768]{1,0:T(8,128)(2,1)S(1)} %get-tuple-element.337), channel_id=1, source_target_pairs={{0,8},{4,12},{8,0},{12,4},{1,9},{5,13},{9,1},{13,5},{2,10},{6,14},... | collective-permute-start | bytes 516104 | tf_op jit(solution)/shard_map/ppermute | solution.py:149
  41.5 3.6 %shard_map.301 = (bf16[208,768]{1,0:T(8,128)(2,1)S(1)}, bf16[208,768]{1,0:T(8,128)(2,1)S(1)}, bf16[208,768]{1,0:T(8,128)(2,1)S(1)}, bf16[208,768]{1,0:T(8,128)(2...) custom-call(f32[8,128]{1,0:T(8,128)S(1)} %get-tuple-element.331.refs, ...), custom_call_target="tpu_custom_call" | custom-call | flops 4000000000 | tf_op jit(solution)/shard_map/pallas_call | solution.py:78
  45.7 2.1 %collective-permute-start.14 = (bf16[112,768]{1,0:T(8,128)(2,1)S(1)}, bf16[112,768]{1,0:T(8,128)(2,1)S(1)}, u32[]{:S(2)}, u32[]{:S(2)}) collective-permute-start(bf16[112,768]{1,0:T(8,128)(2,1)S(1)} %get-tuple-element.341.refs_7_), channel_id=1, source_target_pairs={{0,8},{4,12},{8,0},{12,4},{1,9},{5,13},{9,1},{13,5},{2,10},{6,14},... | collective-permute-start | bytes 516104 | tf_op jit(solution)/shard_map/ppermute | solution.py:149
  48.8 1.8 %collective-permute-start.15 = (bf16[96,768]{1,0:T(8,128)(2,1)S(1)}, bf16[96,768]{1,0:T(8,128)(2,1)S(1)}, u32[]{:S(2)}, u32[]{:S(2)}) collective-permute-start(bf16[96,768]{1,0:T(8,128)(2,1)S(1)} %get-tuple-element.359), channel_id=1, source_target_pairs={{0,8},{4,12},{8,0},{12,4},{1,9},{5,13},{9,1},{13,5},{2,10},{6,14},... | collective-permute-start | bytes 442376 | tf_op jit(solution)/shard_map/ppermute | solution.py:149
  50.6 1.6 shard_map.305
  56.3 2.0 %collective-permute-start.21 = (bf16[208,768]{1,0:T(8,128)(2,1)S(1)}, bf16[208,768]{1,0:T(8,128)(2,1)S(1)}, u32[]{:S(2)}, u32[]{:S(2)}) collective-permute-start(bf16[208,768]{1,0:T(8,128)(2,1)S(1)} %get-tuple-element.361.refs_1_.refs_2_), channel_id=1, source_target_pairs={{0,16},{16,0},{1,17},{17,1},{2,18},{18,2},{3,19},{19,3},{4,20},{20... | collective-permute-start | bytes 958472 | tf_op jit(solution)/shard_map/ppermute | solution.py:158
  62.9 1.6 collective-permute-start.22
  67.4 2.3 %collective-permute-done.20.refs_2_ = bf16[112,768]{1,0:T(8,128)(2,1)S(1)} collective-permute-done((bf16[112,768]{1,0:T(8,128)(2,1)S(1)}, bf16[112,768]{1,0:T(8,128)(2,1)S(1)}, u32[]{:S(2)}, u32[]{:S(2)}) %collective-permute-start.20) | collective-permute-done | bytes 172064 | tf_op jit(solution)/shard_map/ppermute | solution.py:149
  75.4 1.7 collective-permute-start.27
  77.2 1.6 shard_map.325
  78.7 1.7 shard_map.326
  80.5 1.7 shard_map.327
  83.5 1.8 %shard_map.330 = (bf16[208,768]{1,0:T(8,128)(2,1)S(1)}, bf16[3,208,192]{2,1,0:T(8,128)(2,1)S(1)}, bf16[208,768]{1,0:T(8,128)(2,1)S(1)}, f32[8,768]{1,0:T(8,128)S(1)}, f32[8,128]{1,0:T(8,128)S(1)}) custom-call(f32[8,128]{1,0:T(8,128)S(1)} %get-tuple-element.429.refs_0_, bf16[208,768]{1,0:T(8,128)(2,1)S(1)} %get-tuple-element.430.refs_1_.refs_8_, ...), custom_call_target="tpu_custom_call" | custom-call | flops 4000000000 | tf_op jit(solution)/shard_map/pallas_call | solution.py:78
  85.5 2.8 %collective-permute-start.31 = (bf16[96,768]{1,0:T(8,128)(2,1)S(1)}, bf16[96,768]{1,0:T(8,128)(2,1)S(1)}, u32[]{:S(2)}, u32[]{:S(2)}) collective-permute-start(bf16[96,768]{1,0:T(8,128)(2,1)S(1)} %get-tuple-element.466), channel_id=1, source_target_pairs={{0,2},{1,3},{2,0},{3,1},{4,6},{5,7},{6,4},{7,5},{8,10},{9,11},{10,... | collective-permute-start | bytes 442376 | tf_op jit(solution)/shard_map/ppermute | solution.py:167
  88.2 1.7 shard_map.332
  91.8 1.6 collective-permute-start.32
  93.4 2.3 %collective-permute-done.30.refs_2_ = bf16[384,384]{1,0:T(8,128)(2,1)S(1)} collective-permute-done((bf16[384,384]{1,0:T(8,128)(2,1)S(1)}, bf16[384,384]{1,0:T(8,128)(2,1)S(1)}, u32[]{:S(2)}, u32[]{:S(2)}) %collective-permute-start.30) | collective-permute-done | bytes 294944 | tf_op jit(solution)/shard_map/ppermute | solution.py:167
  96.0 1.6 collective-permute-start.35
  97.6 1.7 collective-permute-start.36
  99.4 8.1 %collective-permute-done.33.refs_2_ = bf16[384,768]{1,0:T(8,128)(2,1)S(1)} collective-permute-done((bf16[384,768]{1,0:T(8,128)(2,1)S(1)}, bf16[384,768]{1,0:T(8,128)(2,1)S(1)}, u32[]{:S(2)}, u32[]{:S(2)}) %collective-permute-start.33) | collective-permute-done | bytes 589856 | tf_op jit(solution)/shard_map/ppermute | solution.py:158
  107.7 1.6 collective-permute-start.37
  112.0 8.9 %collective-permute-done.37.refs_2_ = bf16[192,768]{1,0:T(8,128)(2,1)S(1)} collective-permute-done((bf16[192,768]{1,0:T(8,128)(2,1)S(1)}, bf16[192,768]{1,0:T(8,128)(2,1)S(1)}, u32[]{:S(2)}, u32[]{:S(2)}) %collective-permute-start.37) | collective-permute-done | bytes 294944 | tf_op jit(solution)/shard_map/ppermute | solution.py:167
  122.0 2.9 %collective-permute-start.43 = (bf16[96,768]{1,0:T(8,128)(2,1)S(1)}, bf16[96,768]{1,0:T(8,128)(2,1)S(1)}, u32[]{:S(2)}, u32[]{:S(2)}) collective-permute-start(bf16[96,768]{1,0:T(8,128)(2,1)S(1)} %get-tuple-element.503), channel_id=1, source_target_pairs={{0,2},{1,3},{2,0},{3,1},{4,6},{5,7},{6,4},{7,5},{8,10},{9,11},{10,... | collective-permute-start | bytes 442376 | tf_op jit(solution)/shard_map/ppermute | solution.py:167
  125.1 6.0 %collective-permute-done.40.refs_2_ = bf16[192,768]{1,0:T(8,128)(2,1)S(1)} collective-permute-done((bf16[192,768]{1,0:T(8,128)(2,1)S(1)}, bf16[192,768]{1,0:T(8,128)(2,1)S(1)}, u32[]{:S(2)}, u32[]{:S(2)}) %collective-permute-start.40) | collective-permute-done | bytes 294944 | tf_op jit(solution)/shard_map/ppermute | solution.py:167
  131.2 1.5 collective-permute-done.41.refs_2_
  132.7 1.5 shard_map.347
  135.6 1.4 collective-permute-start.45
  137.5 1.6 collective-permute-done.44.refs_2_
  140.0 2.9 %collective-permute-start.46 = (bf16[48,768]{1,0:T(8,128)(2,1)S(1)}, bf16[48,768]{1,0:T(8,128)(2,1)S(1)}, u32[]{:S(2)}, u32[]{:S(2)}) collective-permute-start(bf16[48,768]{1,0:T(8,128)(2,1)S(1)} %get-tuple-element.514.refs_8_), channel_id=1, source_target_pairs={{0,16},{1,17},{2,18},{3,19},{4,20},{5,21},{6,22},{7,23},{8,24},{9,... | collective-permute-start | bytes 221192 | tf_op jit(solution)/shard_map/ppermute | solution.py:161
  143.0 1.5 shard_map.353
  146.9 1.6 shard_map.355
  148.7 1.4 collective-permute-start.50
  150.1 1.5 shard_map.357
  151.8 6.6 %collective-permute-done.50.refs_2_ = bf16[2,208,384]{2,1,0:T(8,128)(2,1)S(1)} collective-permute-done((bf16[2,208,384]{2,1,0:T(8,128)(2,1)S(1)}, bf16[2,208,384]{2,1,0:T(8,128)(2,1)S(1)}, u32[]{:S(2)}, u32[]{:S(2)}) %collective-permute-start.50) | collective-permute-done | bytes 319520 | tf_op jit(solution)/shard_map/ppermute | solution.py:149
  161.2 1.6 shard_map.361
  162.9 3.7 %collective-permute-start.55 = (bf16[384,768]{1,0:T(8,128)(2,1)S(1)}, bf16[384,768]{1,0:T(8,128)(2,1)S(1)}, u32[]{:S(2)}, u32[]{:S(2)}) collective-permute-start(bf16[384,768]{1,0:T(8,128)(2,1)S(1)} %get-tuple-element.548.refs_1_), channel_id=1, source_target_pairs={{0,16},{1,17},{2,18},{3,19},{4,20},{5,21},{6,22},{7,23},{8,24},{9,... | collective-permute-start | bytes 1769480 | tf_op jit(solution)/shard_map/ppermute | solution.py:161
  169.8 8.1 %collective-permute-done.55.refs_2_ = bf16[384,768]{1,0:T(8,128)(2,1)S(1)} collective-permute-done((bf16[384,768]{1,0:T(8,128)(2,1)S(1)}, bf16[384,768]{1,0:T(8,128)(2,1)S(1)}, u32[]{:S(2)}, u32[]{:S(2)}) %collective-permute-start.55) | collective-permute-done | bytes 589856 | tf_op jit(solution)/shard_map/ppermute | solution.py:161
  177.9 1.6 shard_map.364
  (180 shorter events, 50.8 us)
Async XLA Ops:
  2.3 26.4 %collective-permute-start.5 = (bf16[592,768]{1,0:T(8,128)(2,1)S(1)}, bf16[592,768]{1,0:T(8,128)(2,1)S(1)}, u32[]{:S(2)}, u32[]{:S(2)}) collective-permute-start(bf16[592,768]{1,0:T(8,128)(2,1)S(1)} %get-tuple-element.303), channel_id=1, source_target_pairs={{16,0},{17,1},{18,2},{19,3},{20,4},{21,5},{22,6},{23,7},{24,8},{25... | collective-permute-start | bytes 2727944 | tf_op jit(solution)/shard_map/ppermute | solution.py:164
  3.6 29.4 %collective-permute-start.7 = (bf16[192,768]{1,0:T(8,128)(2,1)}, bf16[192,768]{1,0:T(8,128)(2,1)S(1)}, u32[]{:S(2)}, u32[]{:S(2)}) collective-permute-start(bf16[192,768]{1,0:T(8,128)(2,1)} %bitcast.27), channel_id=1, source_target_pairs={{16,0},{17,1},{18,2},{19,3},{20,4},{21,5},{22,6},{23,7},{24,8},{25... | collective-permute-start | bytes 884744 | tf_op jit(solution)/shard_map/ppermute | solution.py:164
  5.7 10.3 %collective-permute-start = (bf16[8,768]{1,0:T(8,128)(2,1)S(1)}, bf16[8,768]{1,0:T(8,128)(2,1)S(1)}, u32[]{:S(2)}, u32[]{:S(2)}) collective-permute-start(bf16[8,768]{1,0:T(8,128)(2,1)S(1)} %slice_bitcast_fusion.refs_2_.refs_3_), channel_id=1, source_target_pairs={{0,1},{1,0},{2,3},{3,2},{4,5},{5,4},{6,7},{7,6},{8,9},{9,8},{10,11... | collective-permute-start | bytes 36872 | tf_op jit(solution)/shard_map/ppermute | solution.py:167
  8.7 7.3 %collective-permute-start.1 = (bf16[8,768]{1,0:T(8,128)(2,1)S(1)}, bf16[8,768]{1,0:T(8,128)(2,1)S(1)}, u32[]{:S(2)}, u32[]{:S(2)}) collective-permute-start(bf16[8,768]{1,0:T(8,128)(2,1)S(1)} %slice_bitcast_fusion.refs_2_.refs_3_), channel_id=1, source_target_pairs={{0,2},{1,3},{2,0},{3,1},{4,6},{5,7},{6,4},{7,5},{8,10},{9,11},{10,... | collective-permute-start | bytes 36872 | tf_op jit(solution)/shard_map/ppermute | solution.py:167
  11.3 5.5 %collective-permute-start.2 = (bf16[8,768]{1,0:T(8,128)(2,1)S(1)}, bf16[8,768]{1,0:T(8,128)(2,1)S(1)}, u32[]{:S(2)}, u32[]{:S(2)}) collective-permute-start(bf16[8,768]{1,0:T(8,128)(2,1)S(1)} %slice_bitcast_fusion.refs_2_.refs_3_), channel_id=1, source_target_pairs={{0,3},{1,2},{2,1},{3,0},{4,7},{5,6},{6,5},{7,4},{8,11},{9,10},{10,... | collective-permute-start | bytes 36872 | tf_op jit(solution)/shard_map/ppermute | solution.py:167
  20.2 3.8 %collective-permute-start.4 = (f32[8,768]{1,0:T(8,128)S(1)}, f32[8,768]{1,0:T(8,128)S(1)}, u32[]{:S(2)}, u32[]{:S(2)}) collective-permute-start(f32[8,768]{1,0:T(8,128)S(1)} %get-tuple-element.297.refs_1_), channel_id=1, source_target_pairs={{0,8},{4,12},{8,0},{12,4},{1,9},{5,13},{9,1},{13,5},{2,10},{6,14},... | collective-permute-start | bytes 73736 | tf_op jit(solution)/shard_map/ppermute | solution.py:149
  24.0 6.5 %collective-permute-start.6 = (f32[8,768]{1,0:T(8,128)S(1)}, f32[8,768]{1,0:T(8,128)S(1)}, u32[]{:S(2)}, u32[]{:S(2)}) collective-permute-start(f32[8,768]{1,0:T(8,128)S(1)} %get-tuple-element.306.refs_2_), channel_id=1, source_target_pairs={{0,16},{1,17},{2,18},{3,19},{4,20},{5,21},{6,22},{7,23},{8,24},{9,... | collective-permute-start | bytes 73736 | tf_op jit(solution)/shard_map/ppermute | solution.py:161
  37.7 7.3 %collective-permute-start.9 = (bf16[208,768]{1,0:T(8,128)(2,1)S(1)}, bf16[208,768]{1,0:T(8,128)(2,1)S(1)}, u32[]{:S(2)}, u32[]{:S(2)}) collective-permute-start(bf16[208,768]{1,0:T(8,128)(2,1)S(1)} %get-tuple-element.334), channel_id=1, source_target_pairs={{0,4},{4,0},{8,12},{12,8},{1,5},{5,1},{9,13},{13,9},{2,6},{6,2},{1... | collective-permute-start | bytes 958472 | tf_op jit(solution)/shard_map/ppermute | solution.py:149
  37.9 7.5 %collective-permute-start.10 = (bf16[112,768]{1,0:T(8,128)(2,1)S(1)}, bf16[112,768]{1,0:T(8,128)(2,1)S(1)}, u32[]{:S(2)}, u32[]{:S(2)}) collective-permute-start(bf16[112,768]{1,0:T(8,128)(2,1)S(1)} %get-tuple-element.337), channel_id=1, source_target_pairs={{0,8},{4,12},{8,0},{12,4},{1,9},{5,13},{9,1},{13,5},{2,10},{6,14},... | collective-permute-start | bytes 516104 | tf_op jit(solution)/shard_map/ppermute | solution.py:149
  40.3 8.1 %collective-permute-start.11 = (bf16[96,768]{1,0:T(8,128)(2,1)S(1)}, bf16[96,768]{1,0:T(8,128)(2,1)S(1)}, u32[]{:S(2)}, u32[]{:S(2)}) collective-permute-start(bf16[96,768]{1,0:T(8,128)(2,1)S(1)} %get-tuple-element.339), channel_id=1, source_target_pairs={{0,8},{4,12},{8,0},{12,4},{1,9},{5,13},{9,1},{13,5},{2,10},{6,14},... | collective-permute-start | bytes 442376 | tf_op jit(solution)/shard_map/ppermute | solution.py:149
  45.7 10.3 %collective-permute-start.14 = (bf16[112,768]{1,0:T(8,128)(2,1)S(1)}, bf16[112,768]{1,0:T(8,128)(2,1)S(1)}, u32[]{:S(2)}, u32[]{:S(2)}) collective-permute-start(bf16[112,768]{1,0:T(8,128)(2,1)S(1)} %get-tuple-element.341.refs_7_), channel_id=1, source_target_pairs={{0,8},{4,12},{8,0},{12,4},{1,9},{5,13},{9,1},{13,5},{2,10},{6,14},... | collective-permute-start | bytes 516104 | tf_op jit(solution)/shard_map/ppermute | solution.py:149
  48.6 4.6 %collective-permute-start.12 = (bf16[208,768]{1,0:T(8,128)(2,1)S(1)}, bf16[208,768]{1,0:T(8,128)(2,1)S(1)}, u32[]{:S(2)}, u32[]{:S(2)}) collective-permute-start(bf16[208,768]{1,0:T(8,128)(2,1)S(1)} %get-tuple-element.348.refs_1_), channel_id=1, source_target_pairs={{0,4},{4,0},{8,12},{12,8},{1,5},{5,1},{9,13},{13,9},{2,6},{6,2},{1... | collective-permute-start | bytes 958472 | tf_op jit(solution)/shard_map/ppermute | solution.py:149
  48.7 12.1 %collective-permute-start.17 = (bf16[208,768]{1,0:T(8,128)(2,1)S(1)}, bf16[208,768]{1,0:T(8,128)(2,1)S(1)}, u32[]{:S(2)}, u32[]{:S(2)}) collective-permute-start(bf16[208,768]{1,0:T(8,128)(2,1)S(1)} %get-tuple-element.348.refs_1_), channel_id=1, source_target_pairs={{0,16},{16,0},{1,17},{17,1},{2,18},{18,2},{3,19},{19,3},{4,20},{20... | collective-permute-start | bytes 958472 | tf_op jit(solution)/shard_map/ppermute | solution.py:158
  48.8 7.3 %collective-permute-start.15 = (bf16[96,768]{1,0:T(8,128)(2,1)S(1)}, bf16[96,768]{1,0:T(8,128)(2,1)S(1)}, u32[]{:S(2)}, u32[]{:S(2)}) collective-permute-start(bf16[96,768]{1,0:T(8,128)(2,1)S(1)} %get-tuple-element.359), channel_id=1, source_target_pairs={{0,8},{4,12},{8,0},{12,4},{1,9},{5,13},{9,1},{13,5},{2,10},{6,14},... | collective-permute-start | bytes 442376 | tf_op jit(solution)/shard_map/ppermute | solution.py:149
  56.3 13.9 %collective-permute-start.21 = (bf16[208,768]{1,0:T(8,128)(2,1)S(1)}, bf16[208,768]{1,0:T(8,128)(2,1)S(1)}, u32[]{:S(2)}, u32[]{:S(2)}) collective-permute-start(bf16[208,768]{1,0:T(8,128)(2,1)S(1)} %get-tuple-element.361.refs_1_.refs_2_), channel_id=1, source_target_pairs={{0,16},{16,0},{1,17},{17,1},{2,18},{18,2},{3,19},{19,3},{4,20},{20... | collective-permute-start | bytes 958472 | tf_op jit(solution)/shard_map/ppermute | solution.py:158
  60.9 4.2 %collective-permute-start.19 = (bf16[208,768]{1,0:T(8,128)(2,1)S(1)}, bf16[208,768]{1,0:T(8,128)(2,1)S(1)}, u32[]{:S(2)}, u32[]{:S(2)}) collective-permute-start(bf16[208,768]{1,0:T(8,128)(2,1)S(1)} %get-tuple-element.370.refs_1_.refs_6_), channel_id=1, source_target_pairs={{0,4},{4,0},{8,12},{12,8},{1,5},{5,1},{9,13},{13,9},{2,6},{6,2},{1... | collective-permute-start | bytes 958472 | tf_op jit(solution)/shard_map/ppermute | solution.py:149
  62.5 7.3 %collective-permute-start.20 = (bf16[112,768]{1,0:T(8,128)(2,1)S(1)}, bf16[112,768]{1,0:T(8,128)(2,1)S(1)}, u32[]{:S(2)}, u32[]{:S(2)}) collective-permute-start(bf16[112,768]{1,0:T(8,128)(2,1)S(1)} %get-tuple-element.383), channel_id=1, source_target_pairs={{0,8},{4,12},{8,0},{12,4},{1,9},{5,13},{9,1},{13,5},{2,10},{6,14},... | collective-permute-start | bytes 516104 | tf_op jit(solution)/shard_map/ppermute | solution.py:149
  62.9 9.2 %collective-permute-start.22 = (bf16[96,768]{1,0:T(8,128)(2,1)S(1)}, bf16[96,768]{1,0:T(8,128)(2,1)S(1)}, u32[]{:S(2)}, u32[]{:S(2)}) collective-permute-start(bf16[96,768]{1,0:T(8,128)(2,1)S(1)} %get-tuple-element.386), channel_id=1, source_target_pairs={{0,8},{4,12},{8,0},{12,4},{1,9},{5,13},{9,1},{13,5},{2,10},{6,14},... | collective-permute-start | bytes 442376 | tf_op jit(solution)/shard_map/ppermute | solution.py:149
  70.3 12.7 %collective-permute-start.25 = (bf16[112,768]{1,0:T(8,128)(2,1)S(1)}, bf16[112,768]{1,0:T(8,128)(2,1)S(1)}, u32[]{:S(2)}, u32[]{:S(2)}) collective-permute-start(bf16[112,768]{1,0:T(8,128)(2,1)S(1)} %get-tuple-element.388.refs_7_), channel_id=1, source_target_pairs={{0,8},{4,12},{8,0},{12,4},{1,9},{5,13},{9,1},{13,5},{2,10},{6,14},... | collective-permute-start | bytes 516104 | tf_op jit(solution)/shard_map/ppermute | solution.py:149
  72.5 8.0 %collective-permute-start.24 = (bf16[208,768]{1,0:T(8,128)(2,1)S(1)}, bf16[208,768]{1,0:T(8,128)(2,1)S(1)}, u32[]{:S(2)}, u32[]{:S(2)}) collective-permute-start(bf16[208,768]{1,0:T(8,128)(2,1)S(1)} %get-tuple-element.410.refs_1_.refs_7_), channel_id=1, source_target_pairs={{0,4},{4,0},{8,12},{12,8},{1,5},{5,1},{9,13},{13,9},{2,6},{6,2},{1... | collective-permute-start | bytes 958472 | tf_op jit(solution)/shard_map/ppermute | solution.py:149
  72.6 10.4 %collective-permute-start.26 = (bf16[96,768]{1,0:T(8,128)(2,1)S(1)}, bf16[96,768]{1,0:T(8,128)(2,1)S(1)}, u32[]{:S(2)}, u32[]{:S(2)}) collective-permute-start(bf16[96,768]{1,0:T(8,128)(2,1)S(1)} %get-tuple-element.428), channel_id=1, source_target_pairs={{0,8},{4,12},{8,0},{12,4},{1,9},{5,13},{9,1},{13,5},{2,10},{6,14},... | collective-permute-start | bytes 442376 | tf_op jit(solution)/shard_map/ppermute | solution.py:149
  75.4 10.0 %collective-permute-start.27 = (bf16[192,768]{1,0:T(8,128)(2,1)S(1)}, bf16[192,768]{1,0:T(8,128)(2,1)S(1)}, u32[]{:S(2)}, u32[]{:S(2)}) collective-permute-start(bf16[192,768]{1,0:T(8,128)(2,1)S(1)} %get-tuple-element.436), channel_id=1, source_target_pairs={{0,1},{1,0},{2,3},{3,2},{4,5},{5,4},{6,7},{7,6},{8,9},{9,8},{10,11... | collective-permute-start | bytes 884744 | tf_op jit(solution)/shard_map/ppermute | solution.py:167
  83.0 5.2 %collective-permute-start.28 = (bf16[208,768]{1,0:T(8,128)(2,1)S(1)}, bf16[208,768]{1,0:T(8,128)(2,1)S(1)}, u32[]{:S(2)}, u32[]{:S(2)}) collective-permute-start(bf16[208,768]{1,0:T(8,128)(2,1)S(1)} %get-tuple-element.430.refs_1_.refs_8_), channel_id=1, source_target_pairs={{0,4},{4,0},{8,12},{12,8},{1,5},{5,1},{9,13},{13,9},{2,6},{6,2},{1... | collective-permute-start | bytes 958472 | tf_op jit(solution)/shard_map/ppermute | solution.py:149
  83.1 12.6 %collective-permute-start.30 = (bf16[384,384]{1,0:T(8,128)(2,1)S(1)}, bf16[384,384]{1,0:T(8,128)(2,1)S(1)}, u32[]{:S(2)}, u32[]{:S(2)}) collective-permute-start(bf16[384,384]{1,0:T(8,128)(2,1)S(1)} %get-tuple-element.463), channel_id=1, source_target_pairs={{0,1},{1,0},{2,3},{3,2},{4,5},{5,4},{6,7},{7,6},{8,9},{9,8},{10,11... | collective-permute-start | bytes 884744 | tf_op jit(solution)/shard_map/ppermute | solution.py:167
  85.5 10.4 %collective-permute-start.31 = (bf16[96,768]{1,0:T(8,128)(2,1)S(1)}, bf16[96,768]{1,0:T(8,128)(2,1)S(1)}, u32[]{:S(2)}, u32[]{:S(2)}) collective-permute-start(bf16[96,768]{1,0:T(8,128)(2,1)S(1)} %get-tuple-element.466), channel_id=1, source_target_pairs={{0,2},{1,3},{2,0},{3,1},{4,6},{5,7},{6,4},{7,5},{8,10},{9,11},{10,... | collective-permute-start | bytes 442376 | tf_op jit(solution)/shard_map/ppermute | solution.py:167
  91.3 16.2 %collective-permute-start.33 = (bf16[384,768]{1,0:T(8,128)(2,1)S(1)}, bf16[384,768]{1,0:T(8,128)(2,1)S(1)}, u32[]{:S(2)}, u32[]{:S(2)}) collective-permute-start(bf16[384,768]{1,0:T(8,128)(2,1)S(1)} %get-tuple-element.471), channel_id=1, source_target_pairs={{0,16},{16,0},{1,17},{17,1},{2,18},{18,2},{3,19},{19,3},{4,20},{20... | collective-permute-start | bytes 1769480 | tf_op jit(solution)/shard_map/ppermute | solution.py:158
  91.8 4.2 %collective-permute-start.32 = (bf16[32,768]{1,0:T(8,128)(2,1)S(1)}, bf16[32,768]{1,0:T(8,128)(2,1)S(1)}, u32[]{:S(2)}, u32[]{:S(2)}) collective-permute-start(bf16[32,768]{1,0:T(8,128)(2,1)S(1)} %get-tuple-element.468.refs_1_), channel_id=1, source_target_pairs={{0,8},{4,12},{8,0},{12,4},{1,9},{5,13},{9,1},{13,5},{2,10},{6,14},... | collective-permute-start | bytes 147464 | tf_op jit(solution)/shard_map/ppermute | solution.py:149
  95.8 13.6 %collective-permute-start.34 = (bf16[192,384]{1,0:T(8,128)(2,1)S(1)}, bf16[192,384]{1,0:T(8,128)(2,1)S(1)}, u32[]{:S(2)}, u32[]{:S(2)}) collective-permute-start(bf16[192,384]{1,0:T(8,128)(2,1)S(1)} %get-tuple-element.474), channel_id=1, source_target_pairs={{0,2},{1,3},{2,0},{3,1},{4,6},{5,7},{6,4},{7,5},{8,10},{9,11},{10,... | collective-permute-start | bytes 442376 | tf_op jit(solution)/shard_map/ppermute | solution.py:167
  96.0 13.4 %collective-permute-start.35 = (bf16[32,768]{1,0:T(8,128)(2,1)S(1)}, bf16[32,768]{1,0:T(8,128)(2,1)S(1)}, u32[]{:S(2)}, u32[]{:S(2)}) collective-permute-start(bf16[32,768]{1,0:T(8,128)(2,1)S(1)} %get-tuple-element.476.refs_1_), channel_id=1, source_target_pairs={{0,16},{16,0},{1,17},{17,1},{2,18},{18,2},{3,19},{19,3},{4,20},{20... | collective-permute-start | bytes 147464 | tf_op jit(solution)/shard_map/ppermute | solution.py:158
  97.6 13.1 %collective-permute-start.36 = (bf16[96,768]{1,0:T(8,128)(2,1)S(1)}, bf16[96,768]{1,0:T(8,128)(2,1)S(1)}, u32[]{:S(2)}, u32[]{:S(2)}) collective-permute-start(bf16[96,768]{1,0:T(8,128)(2,1)S(1)} %get-tuple-element.478.refs_1_), channel_id=1, source_target_pairs={{0,2},{1,3},{2,0},{3,1},{4,6},{5,7},{6,4},{7,5},{8,10},{9,11},{10,... | collective-permute-start | bytes 442376 | tf_op jit(solution)/shard_map/ppermute | solution.py:167
  107.7 13.2 %collective-permute-start.37 = (bf16[192,768]{1,0:T(8,128)(2,1)S(1)}, bf16[192,768]{1,0:T(8,128)(2,1)S(1)}, u32[]{:S(2)}, u32[]{:S(2)}) collective-permute-start(bf16[192,768]{1,0:T(8,128)(2,1)S(1)} %get-tuple-element.481), channel_id=1, source_target_pairs={{0,1},{1,0},{2,3},{3,2},{4,5},{5,4},{6,7},{7,6},{8,9},{9,8},{10,11... | collective-permute-start | bytes 884744 | tf_op jit(solution)/shard_map/ppermute | solution.py:167
  109.5 12.5 %collective-permute-start.38 = (bf16[32,768]{1,0:T(8,128)(2,1)S(1)}, bf16[32,768]{1,0:T(8,128)(2,1)S(1)}, u32[]{:S(2)}, u32[]{:S(2)}) collective-permute-start(bf16[32,768]{1,0:T(8,128)(2,1)S(1)} %get-tuple-element.483.refs_1_), channel_id=1, source_target_pairs={{0,1},{1,0},{2,3},{3,2},{4,5},{5,4},{6,7},{7,6},{8,9},{9,8},{10,11... | collective-permute-start | bytes 147464 | tf_op jit(solution)/shard_map/ppermute | solution.py:167
  110.0 15.0 %collective-permute-start.39 = (bf16[192,384]{1,0:T(8,128)(2,1)S(1)}, bf16[192,384]{1,0:T(8,128)(2,1)S(1)}, u32[]{:S(2)}, u32[]{:S(2)}) collective-permute-start(bf16[192,384]{1,0:T(8,128)(2,1)S(1)} %get-tuple-element.485.refs_1_), channel_id=1, source_target_pairs={{0,2},{1,3},{2,0},{3,1},{4,6},{5,7},{6,4},{7,5},{8,10},{9,11},{10,... | collective-permute-start | bytes 442376 | tf_op jit(solution)/shard_map/ppermute | solution.py:167
  110.7 20.3 %collective-permute-start.40 = (bf16[192,768]{1,0:T(8,128)(2,1)S(1)}, bf16[192,768]{1,0:T(8,128)(2,1)S(1)}, u32[]{:S(2)}, u32[]{:S(2)}) collective-permute-start(bf16[192,768]{1,0:T(8,128)(2,1)S(1)} %get-tuple-element.487.refs_1_), channel_id=1, source_target_pairs={{0,1},{1,0},{2,3},{3,2},{4,5},{5,4},{6,7},{7,6},{8,9},{9,8},{10,11... | collective-permute-start | bytes 884744 | tf_op jit(solution)/shard_map/ppermute | solution.py:167
  122.0 10.7 %collective-permute-start.41 = (bf16[64,768]{1,0:T(8,128)(2,1)S(1)}, bf16[64,768]{1,0:T(8,128)(2,1)S(1)}, u32[]{:S(2)}, u32[]{:S(2)}) collective-permute-start(bf16[64,768]{1,0:T(8,128)(2,1)S(1)} %get-tuple-element.489.refs_1_), channel_id=1, source_target_pairs={{0,2},{1,3},{2,0},{3,1},{4,6},{5,7},{6,4},{7,5},{8,10},{9,11},{10,... | collective-permute-start | bytes 294920 | tf_op jit(solution)/shard_map/ppermute | solution.py:167
  122.0 15.0 %collective-permute-start.43 = (bf16[96,768]{1,0:T(8,128)(2,1)S(1)}, bf16[96,768]{1,0:T(8,128)(2,1)S(1)}, u32[]{:S(2)}, u32[]{:S(2)}) collective-permute-start(bf16[96,768]{1,0:T(8,128)(2,1)S(1)} %get-tuple-element.503), channel_id=1, source_target_pairs={{0,2},{1,3},{2,0},{3,1},{4,6},{5,7},{6,4},{7,5},{8,10},{9,11},{10,... | collective-permute-start | bytes 442376 | tf_op jit(solution)/shard_map/ppermute | solution.py:167
  125.0 14.1 %collective-permute-start.44 = (bf16[384,384]{1,0:T(8,128)(2,1)S(1)}, bf16[384,384]{1,0:T(8,128)(2,1)S(1)}, u32[]{:S(2)}, u32[]{:S(2)}) collective-permute-start(bf16[384,384]{1,0:T(8,128)(2,1)S(1)} %get-tuple-element.505.refs_1_), channel_id=1, source_target_pairs={{0,1},{1,0},{2,3},{3,2},{4,5},{5,4},{6,7},{7,6},{8,9},{9,8},{10,11... | collective-permute-start | bytes 884744 | tf_op jit(solution)/shard_map/ppermute | solution.py:167
  131.1 15.8 %collective-permute-start.47 = (bf16[384,768]{1,0:T(8,128)(2,1)S(1)}, bf16[384,768]{1,0:T(8,128)(2,1)S(1)}, u32[]{:S(2)}, u32[]{:S(2)}) collective-permute-start(bf16[384,768]{1,0:T(8,128)(2,1)S(1)} %get-tuple-element.518.refs_1_), channel_id=1, source_target_pairs={{0,16},{16,0},{1,17},{17,1},{2,18},{18,2},{3,19},{19,3},{4,20},{20... | collective-permute-start | bytes 1769480 | tf_op jit(solution)/shard_map/ppermute | solution.py:158
  135.6 4.4 %collective-permute-start.45 = (bf16[48,768]{1,0:T(8,128)(2,1)S(1)}, bf16[48,768]{1,0:T(8,128)(2,1)S(1)}, u32[]{:S(2)}, u32[]{:S(2)}) collective-permute-start(bf16[48,768]{1,0:T(8,128)(2,1)S(1)} %get-tuple-element.507.refs_1_), channel_id=1, source_target_pairs={{0,8},{4,12},{8,0},{12,4},{1,9},{5,13},{9,1},{13,5},{2,10},{6,14},... | collective-permute-start | bytes 221192 | tf_op jit(solution)/shard_map/ppermute | solution.py:149
  137.1 14.6 %collective-permute-start.49 = (bf16[96,768]{1,0:T(8,128)(2,1)S(1)}, bf16[96,768]{1,0:T(8,128)(2,1)S(1)}, u32[]{:S(2)}, u32[]{:S(2)}) collective-permute-start(bf16[96,768]{1,0:T(8,128)(2,1)S(1)} %get-tuple-element.528.refs_1_), channel_id=1, source_target_pairs={{0,2},{1,3},{2,0},{3,1},{4,6},{5,7},{6,4},{7,5},{8,10},{9,11},{10,... | collective-permute-start | bytes 442376 | tf_op jit(solution)/shard_map/ppermute | solution.py:167
  140.0 4.9 %collective-permute-start.46 = (bf16[48,768]{1,0:T(8,128)(2,1)S(1)}, bf16[48,768]{1,0:T(8,128)(2,1)S(1)}, u32[]{:S(2)}, u32[]{:S(2)}) collective-permute-start(bf16[48,768]{1,0:T(8,128)(2,1)S(1)} %get-tuple-element.514.refs_8_), channel_id=1, source_target_pairs={{0,16},{1,17},{2,18},{3,19},{4,20},{5,21},{6,22},{7,23},{8,24},{9,... | collective-permute-start | bytes 221192 | tf_op jit(solution)/shard_map/ppermute | solution.py:161
  144.5 4.0 %collective-permute-start.48 = (bf16[2,2,208,384]{3,2,1,0:T(8,128)(2,1)S(1)}, bf16[2,2,208,384]{3,2,1,0:T(8,128)(2,1)S(1)}, u32[]{:S(2)}, u32[]{:S(2)}) collective-permute-start(bf16[2,2,208,384]{3,2,1,0:T(8,128)(2,1)S(1)} %get-tuple-element.521), channel_id=1, source_target_pairs={{0,4},{4,0},{8,12},{12,8},{1,5},{5,1},{9,13},{13,9},{2,6},{6,2},{1... | collective-permute-start | bytes 1916936 | tf_op jit(solution)/shard_map/ppermute | solution.py:149
  144.6 16.6 %collective-permute-start.52 = (bf16[768,384]{1,0:T(8,128)(2,1)S(1)}, bf16[768,384]{1,0:T(8,128)(2,1)S(1)}, u32[]{:S(2)}, u32[]{:S(2)}) collective-permute-start(bf16[768,384]{1,0:T(8,128)(2,1)S(1)} %get-tuple-element.537.refs_1_), channel_id=1, source_target_pairs={{0,16},{16,0},{1,17},{17,1},{2,18},{18,2},{3,19},{19,3},{4,20},{20... | collective-permute-start | bytes 1769480 | tf_op jit(solution)/shard_map/ppermute | solution.py:158
  148.7 9.7 %collective-permute-start.50 = (bf16[2,208,384]{2,1,0:T(8,128)(2,1)S(1)}, bf16[2,208,384]{2,1,0:T(8,128)(2,1)S(1)}, u32[]{:S(2)}, u32[]{:S(2)}) collective-permute-start(bf16[2,208,384]{2,1,0:T(8,128)(2,1)S(1)} %get-tuple-element.531), channel_id=1, source_target_pairs={{0,8},{4,12},{8,0},{12,4},{1,9},{5,13},{9,1},{13,5},{2,10},{6,14},... | collective-permute-start | bytes 958472 | tf_op jit(solution)/shard_map/ppermute | solution.py:149
  151.6 8.1 %collective-permute-start.51 = (bf16[2,2,208,384]{3,2,1,0:T(8,128)(2,1)S(1)}, bf16[2,2,208,384]{3,2,1,0:T(8,128)(2,1)S(1)}, u32[]{:S(2)}, u32[]{:S(2)}) collective-permute-start(bf16[2,2,208,384]{3,2,1,0:T(8,128)(2,1)S(1)} %get-tuple-element.535), channel_id=1, source_target_pairs={{0,4},{4,0},{8,12},{12,8},{1,5},{5,1},{9,13},{13,9},{2,6},{6,2},{1... | collective-permute-start | bytes 1916936 | tf_op jit(solution)/shard_map/ppermute | solution.py:149
  151.7 11.2 %collective-permute-start.53 = (bf16[192,768]{1,0:T(8,128)(2,1)S(1)}, bf16[192,768]{1,0:T(8,128)(2,1)S(1)}, u32[]{:S(2)}, u32[]{:S(2)}) collective-permute-start(bf16[192,768]{1,0:T(8,128)(2,1)S(1)} %get-tuple-element.539.refs_1_), channel_id=1, source_target_pairs={{0,1},{1,0},{2,3},{3,2},{4,5},{5,4},{6,7},{7,6},{8,9},{9,8},{10,11... | collective-permute-start | bytes 884744 | tf_op jit(solution)/shard_map/ppermute | solution.py:167
  159.8 8.9 %collective-permute-start.54 = (bf16[2,208,384]{2,1,0:T(8,128)(2,1)S(1)}, bf16[2,208,384]{2,1,0:T(8,128)(2,1)S(1)}, u32[]{:S(2)}, u32[]{:S(2)}) collective-permute-start(bf16[2,208,384]{2,1,0:T(8,128)(2,1)S(1)} %get-tuple-element.542), channel_id=1, source_target_pairs={{0,8},{4,12},{8,0},{12,4},{1,9},{5,13},{9,1},{13,5},{2,10},{6,14},... | collective-permute-start | bytes 958472 | tf_op jit(solution)/shard_map/ppermute | solution.py:149
  162.9 15.0 %collective-permute-start.55 = (bf16[384,768]{1,0:T(8,128)(2,1)S(1)}, bf16[384,768]{1,0:T(8,128)(2,1)S(1)}, u32[]{:S(2)}, u32[]{:S(2)}) collective-permute-start(bf16[384,768]{1,0:T(8,128)(2,1)S(1)} %get-tuple-element.548.refs_1_), channel_id=1, source_target_pairs={{0,16},{1,17},{2,18},{3,19},{4,20},{5,21},{6,22},{7,23},{8,24},{9,... | collective-permute-start | bytes 1769480 | tf_op jit(solution)/shard_map/ppermute | solution.py:161
  (26 other events, 162.1 us)

commit v5 on v4

--- a/solution.py
+++ b/solution.py
@@ -337,9 +337,8 @@
             outs[half + s][...] = nt(low, w[1]).astype(BF16)
             outs[2 * half + s][...] = (nt(low, w[2]) + vrow[4:5, :width]).astype(BF16)
 
-    def message_rows_kernel(first, part, late, w, vrow, wa, wb, msg_o, k_o, v_o, w_o):
+    def message_rows_kernel(first, part, late, w, vrow, msg_o, k_o, v_o):
         sec, ten = lax.axis_index("pipe"), lax.axis_index("tensor")
-        w_o[...] = jnp.where(sec == 0, wb[...], wa[...])
         msg_o[...] = jnp.zeros_like(msg_o)
         for s in range(half):
             at = pl.ds(sec * half + (ten ^ s), 1)
@@ -351,8 +350,9 @@
         v_o[...] = nt(low, w[2]) + vrow[4:5, :width]
 
     def attend_kernel(
-        s, q, k, v, km, vm, wo, part_o, mixed_o, probs_o, k_o, v_o,
+        s, with_out, q, k, v, km, vm, *refs
     ):
+        mixed_o, probs_o, k_o, v_o = refs[-4:]
         here = lax.broadcasted_iota(jnp.int32, (rows, width), 0) == patch
         key_here = lax.broadcasted_iota(jnp.int32, (rows, rows), 1) <= patch
         kk = jnp.where(here, km[s : s + 1], k[...].astype(F32)).astype(BF16)
@@ -370,14 +370,16 @@
             mixed = mixed + only(mask, nn(probs, vv))
         mixed = mixed.astype(BF16)
         mixed_o[...] = mixed
-        part_o[...] = nn(mixed, wo[...]).astype(BF16)
-
-    def attend(s):
+        if with_out:
+            wo, part_o = refs[:2]
+            part_o[...] = nn(mixed, wo[...]).astype(BF16)
+
+    def attend(s, *out):
         return stage(
-            functools.partial(attend_kernel, s),
-            [q_one[s], k_patch[s], v_patch[s], k_msg, v_msg, w_out],
-            [
-                near((rows, model), BF16),
+            functools.partial(attend_kernel, s, bool(out)),
+            [q_one[s], k_patch[s], v_patch[s], k_msg, v_msg, *out],
+            [near((rows, model), BF16)] * len(out)
+            + [
                 near((rows, width), BF16),
                 near((heads, rows, rows), BF16),
                 near((rows, width), BF16),
@@ -385,6 +387,13 @@
             ],
             flops=2 * rows * (width * model + 2 * heads * rows * HEAD_DIM),
         )
+
+    def first_out_kernel(mixed, wa, wb, part_o, w_o):
+        w_o[...] = jnp.where(lax.axis_index("pipe") == 0, wb[...], wa[...])
+        part_o[...] = nn(mixed[...], w_o[...]).astype(BF16)
+
+    def out_kernel(mixed, w, part_o):
+        part_o[...] = nn(mixed[...], w[...]).astype(BF16)
 
     first_rows = rows // 32 * 16 + 16
 
@@ -934,26 +943,28 @@
         project_kernel, [*x_slots, near_in, sent_in, own_vec],
         [near(own_in.shape, BF16), near(own_vec.shape, F32)] + [near((rows, width), BF16)] * 12,
     )
+    stage.cost = 0
+    q_one, k_patch, v_patch = projected[:4], projected[4:8], projected[8:]
+    msg_rows, k_msg, v_msg = stage(
+        message_rows_kernel, [first_msg, part_zero, part_late, w_in, vec],
+        [near((16, model), F32), near((16, width), F32), near((16, width), F32)],
+    )
+
+    at3 = (None, *attend(3))
+    at2 = (None, *attend(2))
+    pr3, w_out = stage(
+        first_out_kernel, [at3[1], near_out, sent_out],
+        [near((rows, model), BF16), near(own_out.shape, BF16)],
+    )
+    ac3 = core_swap(pr3)
     stage.cost = 4 * 10**9
-    q_one, k_patch, v_patch = projected[:4], projected[4:8], projected[8:]
-    msg_rows, k_msg, v_msg, w_out = stage(
-        message_rows_kernel,
-        [first_msg, part_zero, part_late, w_in, vec, near_out, sent_out],
-        [
-            near((16, model), F32), near((16, width), F32), near((16, width), F32),
-            near(own_out.shape, BF16),
-        ],
-    )
-
-    at3 = attend(3)
-    ac3 = core_swap(at3[0])
-    at2 = attend(2)
-    two0, two1 = add_parts(at2[0], ac3)
+    (pr2,) = stage(out_kernel, [at2[1], w_out], [near((rows, model), BF16)])
+    two0, two1 = add_parts(pr2, ac3)
     ax0 = x_swap(two0)
     ax1 = x_swap(two1)
-    at1 = attend(1)
+    at1 = attend(1, w_out)
     ac1 = core_swap(at1[0])
-    at0 = attend(0)
+    at0 = attend(0, w_out)
     g_slots = slots(grads_in, 2 * half)
     (aown,) = adds((at0[0], ac1))
     resid0, low0 = stage(
@@ -1061,7 +1072,9 @@
         packs = [pk4, z_swap(pk4, 2)]
     else:
         packs = gather_clips(pk3)
+    stage.cost = 0
     q3 = to_near_clip(*q2)
+    stage.cost = 4 * 10**9
     p4 = to_other_section(*p3)
     sent_all, grads_zero, bz0 = stage(
         message_back,
@@ -1073,6 +1086,7 @@
         ],
     )
     bzc = core_swap(bz0)
+    stage.cost = 10**10
     in_zero, out_zero, qv_zero, bias_zero = stage(
         message_weight, [sent_all, grads_zero, low_zero, mixed_zero],
         [
@@ -1082,6 +1096,7 @@
             near((1, model), F32),
         ],
     )
+    stage.cost = 4 * 10**9
     (bz1,) = adds((bz0, bzc))
     bzx = x_swap(bz1)
     r3 = to_far_clip(*r2)
@@ -1109,9 +1124,9 @@
     (frames_grad,) = stage(
         frames_grad_kernel, [kept, far, cls_part], [shape_of((half, width, patch), BF16)],
     )
+    r5 = to_sections(*r4, move=y_late)
     bkept, bfar = far_columns(bk, bcs)
     fc_in_grad = whole_of_columns(*q4)
-    r5 = to_sections(*r4, move=y_late)
     (block_out,) = stage(
         block_out_kernel, [bkept, bfar], [shape_of((half, width, patch), BF16)],
     )

time: 183 us -> 181 us (0.989)
    ppermute x28, waiting for transfers between devices: 19.8 us -> 27.2 us  [tensor_swap(): return lax.ppermute(v, 'tensor', [(i, i ^ bit) for i in range(4)])]
    ppermute x3, waiting for transfers between devices: 8.38 us -> 2.45 us  [y_late(): return lax.ppermute(v, 'pipe', [(0, 1)])]
    ppermute x2, waiting for transfers between devices: 2.65 us -> 0.15 us  [y_early(): return lax.ppermute(v, 'pipe', [(1, 0)])]
    pallas_call x77 -> x79, Pallas kernels: 57.5 us -> 57.9 us  [__call__(): pl.pallas_call(stage, out_shape=[*outs, near((8, 128), F32)], in_specs=[p...]
  transfers between devices with their start and end apart: 56 -> 56, of which waited for: 26 -> 26; matrix products, arithmetic and copies ran while one was open for 1% -> 1% of each run, Pallas kernels for 29% -> 30%
where the time goes in v5:
time: 181 us; the launch traced here: 179 us
  waiting for transfers between devices  59.9 us (33%)
  Pallas kernels  57.9 us (32%)
  starting transfers between devices  55.1 us (30%)
  local copies, waits for them, and re-layouts  4.38 us (2%)
  between operations  1.83 us (1%)
    pallas_call x79, Pallas kernels, __call__(): pl.pallas_call(stage, out_shape=[*outs, near((8, 128), F32)], in_specs=[p...  57.9 us
    ppermute x28, waiting for transfers between devices, tensor_swap(): return lax.ppermute(v, 'tensor', [(i, i ^ bit) for i in range(4)])  27.2 us
    ppermute x17, waiting for transfers between devices, z_swap(): return lax.ppermute(v, 'dp', [(i, i ^ bit) for i in range(clips)])  21.4 us
    ppermute x17, starting transfers between devices, z_swap(): return lax.ppermute(v, 'dp', [(i, i ^ bit) for i in range(clips)])  18.4 us
    ppermute x28, starting transfers between devices, tensor_swap(): return lax.ppermute(v, 'tensor', [(i, i ^ bit) for i in range(4)])  18.1 us
    ppermute x3, starting transfers between devices, y_late(): return lax.ppermute(v, 'pipe', [(0, 1)])  11.4 us
    ppermute x6, waiting for transfers between devices, y_swap(): return lax.ppermute(v, 'pipe', [(0, 1), (1, 0)])  8.68 us
    ppermute x6, starting transfers between devices, y_swap(): return lax.ppermute(v, 'pipe', [(0, 1), (1, 0)])  4.69 us
  transfers between devices with their start and end apart: 56, of which 26 were waited for; matrix products, arithmetic and copies ran while one was open for 1% of the time, Pallas kernels for 30%

profile of v5, /device:TPU:0, one launch (start us, length us, event | category | flops | bytes accessed | tf_op | source)
XLA Modules:
  0.0 179.0 jit_solution(1764455670401061149)
XLA Ops:
  0.6 1.7 shard_map.288
  5.7 3.0 %collective-permute-start = (bf16[8,768]{1,0:T(8,128)(2,1)S(1)}, bf16[8,768]{1,0:T(8,128)(2,1)S(1)}, u32[]{:S(2)}, u32[]{:S(2)}) collective-permute-start(bf16[8,768]{1,0:T(8,128)(2,1)S(1)} %slice_bitcast_fusion.refs_2_.refs_3_), channel_id=1, source_target_pairs={{0,1},{1,0},{2,3},{3,2},{4,5},{5,4},{6,7},{7,6},{8,9},{9,8},{10,11... | collective-permute-start | bytes 36872 | tf_op jit(solution)/shard_map/ppermute | solution.py:167
  8.7 2.6 %collective-permute-start.1 = (bf16[8,768]{1,0:T(8,128)(2,1)S(1)}, bf16[8,768]{1,0:T(8,128)(2,1)S(1)}, u32[]{:S(2)}, u32[]{:S(2)}) collective-permute-start(bf16[8,768]{1,0:T(8,128)(2,1)S(1)} %slice_bitcast_fusion.refs_2_.refs_3_), channel_id=1, source_target_pairs={{0,2},{1,3},{2,0},{3,1},{4,6},{5,7},{6,4},{7,5},{8,10},{9,11},{10,... | collective-permute-start | bytes 36872 | tf_op jit(solution)/shard_map/ppermute | solution.py:167
  12.6 3.3 %shard_map.290 = (bf16[208,768]{1,0:T(8,128)(2,1)S(1)}, bf16[208,768]{1,0:T(8,128)(2,1)S(1)}, bf16[208,768]{1,0:T(8,128)(2,1)S(1)}, bf16[208,768]{1,0:T(8,128)(2,1)S(1)}, f32[8,128]{1,0:T(8,128)S(1)}) custom-call(f32[8,128]{1,0:T(8,128)S(1)} %get-tuple-element.289.refs_0_, bf16[197,8,768]{2,1,0:T(8,128)(2,1)} %bitcast.25), custom_call_target="tpu_custom_call" | custom-call | tf_op jit(solution)/shard_map/pallas_call | solution.py:78
  16.8 2.1 %shard_map.291 = (f32[32,768]{1,0:T(8,128)S(1)}, bf16[32,768]{1,0:T(8,128)(2,1)S(1)}, bf16[32,192]{1,0:T(8,128)(2,1)S(1)}, bf16[32,192]{1,0:T(8,128)(2,1)S(1)}, ...) custom-call(f32[8,128]{1,0:T(8,128)S(1)} %get-tuple-element.290.refs, ...), custom_call_target="tpu_custom_call" | custom-call | tf_op jit(solution)/shard_map/pallas_call | solution.py:78
  20.2 1.5 collective-permute-start.4
  21.6 2.3 %collective-permute-done.4.refs_2_ = f32[8,768]{1,0:T(8,128)S(1)} collective-permute-done((f32[8,768]{1,0:T(8,128)S(1)}, f32[8,768]{1,0:T(8,128)S(1)}, u32[]{:S(2)}, u32[]{:S(2)}) %collective-permute-start.4) | collective-permute-done | bytes 24608 | tf_op jit(solution)/shard_map/ppermute | solution.py:149
  24.0 4.8 %collective-permute-start.6 = (f32[8,768]{1,0:T(8,128)S(1)}, f32[8,768]{1,0:T(8,128)S(1)}, u32[]{:S(2)}, u32[]{:S(2)}) collective-permute-start(f32[8,768]{1,0:T(8,128)S(1)} %get-tuple-element.308.refs_2_), channel_id=1, source_target_pairs={{0,16},{1,17},{2,18},{3,19},{4,20},{5,21},{6,22},{7,23},{8,24},{9,... | collective-permute-start | bytes 73736 | tf_op jit(solution)/shard_map/ppermute | solution.py:161
  28.8 1.7 shard_map.294
  36.5 2.4 %collective-permute-start.10 = (bf16[112,768]{1,0:T(8,128)(2,1)S(1)}, bf16[112,768]{1,0:T(8,128)(2,1)S(1)}, u32[]{:S(2)}, u32[]{:S(2)}) collective-permute-start(bf16[112,768]{1,0:T(8,128)(2,1)S(1)} %get-tuple-element.343), channel_id=1, source_target_pairs={{0,8},{4,12},{8,0},{12,4},{1,9},{5,13},{9,1},{13,5},{2,10},{6,14},... | collective-permute-start | bytes 516104 | tf_op jit(solution)/shard_map/ppermute | solution.py:149
  40.1 3.6 %shard_map.303 = (bf16[208,768]{1,0:T(8,128)(2,1)S(1)}, bf16[208,768]{1,0:T(8,128)(2,1)S(1)}, bf16[208,768]{1,0:T(8,128)(2,1)S(1)}, bf16[208,768]{1,0:T(8,128)(2...) custom-call(f32[8,128]{1,0:T(8,128)S(1)} %get-tuple-element.337.refs, ...), custom_call_target="tpu_custom_call" | custom-call | flops 4000000000 | tf_op jit(solution)/shard_map/pallas_call | solution.py:78
  44.3 2.1 %collective-permute-start.14 = (bf16[112,768]{1,0:T(8,128)(2,1)S(1)}, bf16[112,768]{1,0:T(8,128)(2,1)S(1)}, u32[]{:S(2)}, u32[]{:S(2)}) collective-permute-start(bf16[112,768]{1,0:T(8,128)(2,1)S(1)} %get-tuple-element.347.refs_7_), channel_id=1, source_target_pairs={{0,8},{4,12},{8,0},{12,4},{1,9},{5,13},{9,1},{13,5},{2,10},{6,14},... | collective-permute-start | bytes 516104 | tf_op jit(solution)/shard_map/ppermute | solution.py:149
  48.6 1.5 collective-permute-start.15
  50.1 1.6 shard_map.307
  61.4 1.6 collective-permute-start.22
  65.9 2.3 %collective-permute-done.20.refs_2_ = bf16[112,768]{1,0:T(8,128)(2,1)S(1)} collective-permute-done((bf16[112,768]{1,0:T(8,128)(2,1)S(1)}, bf16[112,768]{1,0:T(8,128)(2,1)S(1)}, u32[]{:S(2)}, u32[]{:S(2)}) %collective-permute-start.20) | collective-permute-done | bytes 172064 | tf_op jit(solution)/shard_map/ppermute | solution.py:149
  69.2 1.4 collective-permute-done.22.refs_2_
  73.9 1.8 collective-permute-start.27
  75.6 1.6 shard_map.327
  77.2 1.7 shard_map.328
  78.9 1.7 shard_map.329
  82.0 2.1 %shard_map.332 = (bf16[208,768]{1,0:T(8,128)(2,1)S(1)}, bf16[3,208,192]{2,1,0:T(8,128)(2,1)S(1)}, bf16[208,768]{1,0:T(8,128)(2,1)S(1)}, f32[8,768]{1,0:T(8,128)S(1)}, f32[8,128]{1,0:T(8,128)S(1)}) custom-call(f32[8,128]{1,0:T(8,128)S(1)} %get-tuple-element.435.refs_0_, bf16[208,768]{1,0:T(8,128)(2,1)S(1)} %get-tuple-element.436.refs_1_.refs_8_, ...), custom_call_target="tpu_custom_call" | custom-call | flops 4000000000 | tf_op jit(solution)/shard_map/pallas_call | solution.py:78
  84.2 2.8 %collective-permute-start.31 = (bf16[96,768]{1,0:T(8,128)(2,1)S(1)}, bf16[96,768]{1,0:T(8,128)(2,1)S(1)}, u32[]{:S(2)}, u32[]{:S(2)}) collective-permute-start(bf16[96,768]{1,0:T(8,128)(2,1)S(1)} %get-tuple-element.470), channel_id=1, source_target_pairs={{0,2},{1,3},{2,0},{3,1},{4,6},{5,7},{6,4},{7,5},{8,10},{9,11},{10,... | collective-permute-start | bytes 442376 | tf_op jit(solution)/shard_map/ppermute | solution.py:167
  87.0 1.7 shard_map.334
  91.3 1.5 collective-permute-start.32
  95.5 1.7 collective-permute-start.35
  97.8 8.7 %collective-permute-done.33.refs_2_ = bf16[384,768]{1,0:T(8,128)(2,1)S(1)} collective-permute-done((bf16[384,768]{1,0:T(8,128)(2,1)S(1)}, bf16[384,768]{1,0:T(8,128)(2,1)S(1)}, u32[]{:S(2)}, u32[]{:S(2)}) %collective-permute-start.33) | collective-permute-done | bytes 589856 | tf_op jit(solution)/shard_map/ppermute | solution.py:158
  106.8 1.6 collective-permute-start.37
  109.6 1.4 collective-permute-start.40
  111.0 8.9 %collective-permute-done.37.refs_2_ = bf16[192,768]{1,0:T(8,128)(2,1)S(1)} collective-permute-done((bf16[192,768]{1,0:T(8,128)(2,1)S(1)}, bf16[192,768]{1,0:T(8,128)(2,1)S(1)}, u32[]{:S(2)}, u32[]{:S(2)}) %collective-permute-start.37) | collective-permute-done | bytes 294944 | tf_op jit(solution)/shard_map/ppermute | solution.py:167
  121.1 2.9 %collective-permute-start.43 = (bf16[96,768]{1,0:T(8,128)(2,1)S(1)}, bf16[96,768]{1,0:T(8,128)(2,1)S(1)}, u32[]{:S(2)}, u32[]{:S(2)}) collective-permute-start(bf16[96,768]{1,0:T(8,128)(2,1)S(1)} %get-tuple-element.507), channel_id=1, source_target_pairs={{0,2},{1,3},{2,0},{3,1},{4,6},{5,7},{6,4},{7,5},{8,10},{9,11},{10,... | collective-permute-start | bytes 442376 | tf_op jit(solution)/shard_map/ppermute | solution.py:167
  124.1 7.4 %collective-permute-done.40.refs_2_ = bf16[192,768]{1,0:T(8,128)(2,1)S(1)} collective-permute-done((bf16[192,768]{1,0:T(8,128)(2,1)S(1)}, bf16[192,768]{1,0:T(8,128)(2,1)S(1)}, u32[]{:S(2)}, u32[]{:S(2)}) %collective-permute-start.40) | collective-permute-done | bytes 294944 | tf_op jit(solution)/shard_map/ppermute | solution.py:167
  132.7 1.5 shard_map.349
  135.5 2.0 %collective-permute-start.45 = (bf16[48,768]{1,0:T(8,128)(2,1)S(1)}, bf16[48,768]{1,0:T(8,128)(2,1)S(1)}, u32[]{:S(2)}, u32[]{:S(2)}) collective-permute-start(bf16[48,768]{1,0:T(8,128)(2,1)S(1)} %get-tuple-element.511.refs_1_), channel_id=1, source_target_pairs={{0,8},{4,12},{8,0},{12,4},{1,9},{5,13},{9,1},{13,5},{2,10},{6,14},... | collective-permute-start | bytes 221192 | tf_op jit(solution)/shard_map/ppermute | solution.py:149
  138.0 2.2 %collective-permute-done.45.refs_2_ = bf16[48,768]{1,0:T(8,128)(2,1)S(1)} collective-permute-done((bf16[48,768]{1,0:T(8,128)(2,1)S(1)}, bf16[48,768]{1,0:T(8,128)(2,1)S(1)}, u32[]{:S(2)}, u32[]{:S(2)}) %collective-permute-start.45) | collective-permute-done | bytes 73760 | tf_op jit(solution)/shard_map/ppermute | solution.py:149
  140.2 2.9 %collective-permute-start.46 = (bf16[48,768]{1,0:T(8,128)(2,1)S(1)}, bf16[48,768]{1,0:T(8,128)(2,1)S(1)}, u32[]{:S(2)}, u32[]{:S(2)}) collective-permute-start(bf16[48,768]{1,0:T(8,128)(2,1)S(1)} %get-tuple-element.518.refs_8_), channel_id=1, source_target_pairs={{0,16},{1,17},{2,18},{3,19},{4,20},{5,21},{6,22},{7,23},{8,24},{9,... | collective-permute-start | bytes 221192 | tf_op jit(solution)/shard_map/ppermute | solution.py:161
  143.2 1.5 shard_map.355
  145.1 1.4 shard_map.356
  148.3 1.6 shard_map.357
  150.0 1.8 %collective-permute-start.50 = (bf16[2,208,384]{2,1,0:T(8,128)(2,1)S(1)}, bf16[2,208,384]{2,1,0:T(8,128)(2,1)S(1)}, u32[]{:S(2)}, u32[]{:S(2)}) collective-permute-start(bf16[2,208,384]{2,1,0:T(8,128)(2,1)S(1)} %get-tuple-element.535), channel_id=1, source_target_pairs={{0,8},{4,12},{8,0},{12,4},{1,9},{5,13},{9,1},{13,5},{2,10},{6,14},... | collective-permute-start | bytes 958472 | tf_op jit(solution)/shard_map/ppermute | solution.py:149
  151.8 1.7 shard_map.359
  153.7 6.0 %collective-permute-done.50.refs_2_ = bf16[2,208,384]{2,1,0:T(8,128)(2,1)S(1)} collective-permute-done((bf16[2,208,384]{2,1,0:T(8,128)(2,1)S(1)}, bf16[2,208,384]{2,1,0:T(8,128)(2,1)S(1)}, u32[]{:S(2)}, u32[]{:S(2)}) %collective-permute-start.50) | collective-permute-done | bytes 319520 | tf_op jit(solution)/shard_map/ppermute | solution.py:149
  161.0 1.4 collective-permute-done.51.refs_2_
  162.5 3.7 %collective-permute-start.55 = (bf16[384,768]{1,0:T(8,128)(2,1)S(1)}, bf16[384,768]{1,0:T(8,128)(2,1)S(1)}, u32[]{:S(2)}, u32[]{:S(2)}) collective-permute-start(bf16[384,768]{1,0:T(8,128)(2,1)S(1)} %get-tuple-element.552.refs_1_), channel_id=1, source_target_pairs={{0,16},{1,17},{2,18},{3,19},{4,20},{5,21},{6,22},{7,23},{8,24},{9,... | collective-permute-start | bytes 1769480 | tf_op jit(solution)/shard_map/ppermute | solution.py:161
  166.8 1.6 shard_map.364
  168.4 5.6 %collective-permute-done.54.refs_2_ = bf16[2,208,384]{2,1,0:T(8,128)(2,1)S(1)} collective-permute-done((bf16[2,208,384]{2,1,0:T(8,128)(2,1)S(1)}, bf16[2,208,384]{2,1,0:T(8,128)(2,1)S(1)}, u32[]{:S(2)}, u32[]{:S(2)}) %collective-permute-start.54) | collective-permute-done | bytes 319520 | tf_op jit(solution)/shard_map/ppermute | solution.py:149
  175.1 2.2 %collective-permute-done.55.refs_2_ = bf16[384,768]{1,0:T(8,128)(2,1)S(1)} collective-permute-done((bf16[384,768]{1,0:T(8,128)(2,1)S(1)}, bf16[384,768]{1,0:T(8,128)(2,1)S(1)}, u32[]{:S(2)}, u32[]{:S(2)}) %collective-permute-start.55) | collective-permute-done | bytes 589856 | tf_op jit(solution)/shard_map/ppermute | solution.py:161
  177.3 1.6 shard_map.366
  (186 shorter events, 51.7 us)
Async XLA Ops:
  2.3 26.4 %collective-permute-start.5 = (bf16[592,768]{1,0:T(8,128)(2,1)S(1)}, bf16[592,768]{1,0:T(8,128)(2,1)S(1)}, u32[]{:S(2)}, u32[]{:S(2)}) collective-permute-start(bf16[592,768]{1,0:T(8,128)(2,1)S(1)} %get-tuple-element.305), channel_id=1, source_target_pairs={{16,0},{17,1},{18,2},{19,3},{20,4},{21,5},{22,6},{23,7},{24,8},{25... | collective-permute-start | bytes 2727944 | tf_op jit(solution)/shard_map/ppermute | solution.py:164
  3.6 29.4 %collective-permute-start.7 = (bf16[192,768]{1,0:T(8,128)(2,1)}, bf16[192,768]{1,0:T(8,128)(2,1)S(1)}, u32[]{:S(2)}, u32[]{:S(2)}) collective-permute-start(bf16[192,768]{1,0:T(8,128)(2,1)} %bitcast.27), channel_id=1, source_target_pairs={{16,0},{17,1},{18,2},{19,3},{20,4},{21,5},{22,6},{23,7},{24,8},{25... | collective-permute-start | bytes 884744 | tf_op jit(solution)/shard_map/ppermute | solution.py:164
  5.7 10.3 %collective-permute-start = (bf16[8,768]{1,0:T(8,128)(2,1)S(1)}, bf16[8,768]{1,0:T(8,128)(2,1)S(1)}, u32[]{:S(2)}, u32[]{:S(2)}) collective-permute-start(bf16[8,768]{1,0:T(8,128)(2,1)S(1)} %slice_bitcast_fusion.refs_2_.refs_3_), channel_id=1, source_target_pairs={{0,1},{1,0},{2,3},{3,2},{4,5},{5,4},{6,7},{7,6},{8,9},{9,8},{10,11... | collective-permute-start | bytes 36872 | tf_op jit(solution)/shard_map/ppermute | solution.py:167
  8.7 7.3 %collective-permute-start.1 = (bf16[8,768]{1,0:T(8,128)(2,1)S(1)}, bf16[8,768]{1,0:T(8,128)(2,1)S(1)}, u32[]{:S(2)}, u32[]{:S(2)}) collective-permute-start(bf16[8,768]{1,0:T(8,128)(2,1)S(1)} %slice_bitcast_fusion.refs_2_.refs_3_), channel_id=1, source_target_pairs={{0,2},{1,3},{2,0},{3,1},{4,6},{5,7},{6,4},{7,5},{8,10},{9,11},{10,... | collective-permute-start | bytes 36872 | tf_op jit(solution)/shard_map/ppermute | solution.py:167
  11.3 5.5 %collective-permute-start.2 = (bf16[8,768]{1,0:T(8,128)(2,1)S(1)}, bf16[8,768]{1,0:T(8,128)(2,1)S(1)}, u32[]{:S(2)}, u32[]{:S(2)}) collective-permute-start(bf16[8,768]{1,0:T(8,128)(2,1)S(1)} %slice_bitcast_fusion.refs_2_.refs_3_), channel_id=1, source_target_pairs={{0,3},{1,2},{2,1},{3,0},{4,7},{5,6},{6,5},{7,4},{8,11},{9,10},{10,... | collective-permute-start | bytes 36872 | tf_op jit(solution)/shard_map/ppermute | solution.py:167
  20.2 3.8 %collective-permute-start.4 = (f32[8,768]{1,0:T(8,128)S(1)}, f32[8,768]{1,0:T(8,128)S(1)}, u32[]{:S(2)}, u32[]{:S(2)}) collective-permute-start(f32[8,768]{1,0:T(8,128)S(1)} %get-tuple-element.299.refs_1_), channel_id=1, source_target_pairs={{0,8},{4,12},{8,0},{12,4},{1,9},{5,13},{9,1},{13,5},{2,10},{6,14},... | collective-permute-start | bytes 73736 | tf_op jit(solution)/shard_map/ppermute | solution.py:149
  24.0 6.5 %collective-permute-start.6 = (f32[8,768]{1,0:T(8,128)S(1)}, f32[8,768]{1,0:T(8,128)S(1)}, u32[]{:S(2)}, u32[]{:S(2)}) collective-permute-start(f32[8,768]{1,0:T(8,128)S(1)} %get-tuple-element.308.refs_2_), channel_id=1, source_target_pairs={{0,16},{1,17},{2,18},{3,19},{4,20},{5,21},{6,22},{7,23},{8,24},{9,... | collective-permute-start | bytes 73736 | tf_op jit(solution)/shard_map/ppermute | solution.py:161
  36.3 7.3 %collective-permute-start.9 = (bf16[208,768]{1,0:T(8,128)(2,1)S(1)}, bf16[208,768]{1,0:T(8,128)(2,1)S(1)}, u32[]{:S(2)}, u32[]{:S(2)}) collective-permute-start(bf16[208,768]{1,0:T(8,128)(2,1)S(1)} %get-tuple-element.340), channel_id=1, source_target_pairs={{0,4},{4,0},{8,12},{12,8},{1,5},{5,1},{9,13},{13,9},{2,6},{6,2},{1... | collective-permute-start | bytes 958472 | tf_op jit(solution)/shard_map/ppermute | solution.py:149
  36.5 7.5 %collective-permute-start.10 = (bf16[112,768]{1,0:T(8,128)(2,1)S(1)}, bf16[112,768]{1,0:T(8,128)(2,1)S(1)}, u32[]{:S(2)}, u32[]{:S(2)}) collective-permute-start(bf16[112,768]{1,0:T(8,128)(2,1)S(1)} %get-tuple-element.343), channel_id=1, source_target_pairs={{0,8},{4,12},{8,0},{12,4},{1,9},{5,13},{9,1},{13,5},{2,10},{6,14},... | collective-permute-start | bytes 516104 | tf_op jit(solution)/shard_map/ppermute | solution.py:149
  38.9 8.1 %collective-permute-start.11 = (bf16[96,768]{1,0:T(8,128)(2,1)S(1)}, bf16[96,768]{1,0:T(8,128)(2,1)S(1)}, u32[]{:S(2)}, u32[]{:S(2)}) collective-permute-start(bf16[96,768]{1,0:T(8,128)(2,1)S(1)} %get-tuple-element.345), channel_id=1, source_target_pairs={{0,8},{4,12},{8,0},{12,4},{1,9},{5,13},{9,1},{13,5},{2,10},{6,14},... | collective-permute-start | bytes 442376 | tf_op jit(solution)/shard_map/ppermute | solution.py:149
  44.3 11.2 %collective-permute-start.14 = (bf16[112,768]{1,0:T(8,128)(2,1)S(1)}, bf16[112,768]{1,0:T(8,128)(2,1)S(1)}, u32[]{:S(2)}, u32[]{:S(2)}) collective-permute-start(bf16[112,768]{1,0:T(8,128)(2,1)S(1)} %get-tuple-element.347.refs_7_), channel_id=1, source_target_pairs={{0,8},{4,12},{8,0},{12,4},{1,9},{5,13},{9,1},{13,5},{2,10},{6,14},... | collective-permute-start | bytes 516104 | tf_op jit(solution)/shard_map/ppermute | solution.py:149
  47.2 5.5 %collective-permute-start.12 = (bf16[208,768]{1,0:T(8,128)(2,1)S(1)}, bf16[208,768]{1,0:T(8,128)(2,1)S(1)}, u32[]{:S(2)}, u32[]{:S(2)}) collective-permute-start(bf16[208,768]{1,0:T(8,128)(2,1)S(1)} %get-tuple-element.354.refs_1_), channel_id=1, source_target_pairs={{0,4},{4,0},{8,12},{12,8},{1,5},{5,1},{9,13},{13,9},{2,6},{6,2},{1... | collective-permute-start | bytes 958472 | tf_op jit(solution)/shard_map/ppermute | solution.py:149
  47.3 12.0 %collective-permute-start.17 = (bf16[208,768]{1,0:T(8,128)(2,1)S(1)}, bf16[208,768]{1,0:T(8,128)(2,1)S(1)}, u32[]{:S(2)}, u32[]{:S(2)}) collective-permute-start(bf16[208,768]{1,0:T(8,128)(2,1)S(1)} %get-tuple-element.354.refs_1_), channel_id=1, source_target_pairs={{0,16},{16,0},{1,17},{17,1},{2,18},{18,2},{3,19},{19,3},{4,20},{20... | collective-permute-start | bytes 958472 | tf_op jit(solution)/shard_map/ppermute | solution.py:158
  48.6 6.9 %collective-permute-start.15 = (bf16[96,768]{1,0:T(8,128)(2,1)S(1)}, bf16[96,768]{1,0:T(8,128)(2,1)S(1)}, u32[]{:S(2)}, u32[]{:S(2)}) collective-permute-start(bf16[96,768]{1,0:T(8,128)(2,1)S(1)} %get-tuple-element.365), channel_id=1, source_target_pairs={{0,8},{4,12},{8,0},{12,4},{1,9},{5,13},{9,1},{13,5},{2,10},{6,14},... | collective-permute-start | bytes 442376 | tf_op jit(solution)/shard_map/ppermute | solution.py:149
  55.8 12.9 %collective-permute-start.21 = (bf16[208,768]{1,0:T(8,128)(2,1)S(1)}, bf16[208,768]{1,0:T(8,128)(2,1)S(1)}, u32[]{:S(2)}, u32[]{:S(2)}) collective-permute-start(bf16[208,768]{1,0:T(8,128)(2,1)S(1)} %get-tuple-element.367.refs_1_.refs_2_), channel_id=1, source_target_pairs={{0,16},{16,0},{1,17},{17,1},{2,18},{18,2},{3,19},{19,3},{4,20},{20... | collective-permute-start | bytes 958472 | tf_op jit(solution)/shard_map/ppermute | solution.py:158
  59.3 4.2 %collective-permute-start.19 = (bf16[208,768]{1,0:T(8,128)(2,1)S(1)}, bf16[208,768]{1,0:T(8,128)(2,1)S(1)}, u32[]{:S(2)}, u32[]{:S(2)}) collective-permute-start(bf16[208,768]{1,0:T(8,128)(2,1)S(1)} %get-tuple-element.376.refs_1_.refs_6_), channel_id=1, source_target_pairs={{0,4},{4,0},{8,12},{12,8},{1,5},{5,1},{9,13},{13,9},{2,6},{6,2},{1... | collective-permute-start | bytes 958472 | tf_op jit(solution)/shard_map/ppermute | solution.py:149
  60.9 7.3 %collective-permute-start.20 = (bf16[112,768]{1,0:T(8,128)(2,1)S(1)}, bf16[112,768]{1,0:T(8,128)(2,1)S(1)}, u32[]{:S(2)}, u32[]{:S(2)}) collective-permute-start(bf16[112,768]{1,0:T(8,128)(2,1)S(1)} %get-tuple-element.389), channel_id=1, source_target_pairs={{0,8},{4,12},{8,0},{12,4},{1,9},{5,13},{9,1},{13,5},{2,10},{6,14},... | collective-permute-start | bytes 516104 | tf_op jit(solution)/shard_map/ppermute | solution.py:149
  61.4 9.2 %collective-permute-start.22 = (bf16[96,768]{1,0:T(8,128)(2,1)S(1)}, bf16[96,768]{1,0:T(8,128)(2,1)S(1)}, u32[]{:S(2)}, u32[]{:S(2)}) collective-permute-start(bf16[96,768]{1,0:T(8,128)(2,1)S(1)} %get-tuple-element.392), channel_id=1, source_target_pairs={{0,8},{4,12},{8,0},{12,4},{1,9},{5,13},{9,1},{13,5},{2,10},{6,14},... | collective-permute-start | bytes 442376 | tf_op jit(solution)/shard_map/ppermute | solution.py:149
  68.7 12.7 %collective-permute-start.25 = (bf16[112,768]{1,0:T(8,128)(2,1)S(1)}, bf16[112,768]{1,0:T(8,128)(2,1)S(1)}, u32[]{:S(2)}, u32[]{:S(2)}) collective-permute-start(bf16[112,768]{1,0:T(8,128)(2,1)S(1)} %get-tuple-element.394.refs_7_), channel_id=1, source_target_pairs={{0,8},{4,12},{8,0},{12,4},{1,9},{5,13},{9,1},{13,5},{2,10},{6,14},... | collective-permute-start | bytes 516104 | tf_op jit(solution)/shard_map/ppermute | solution.py:149
  71.0 8.0 %collective-permute-start.24 = (bf16[208,768]{1,0:T(8,128)(2,1)S(1)}, bf16[208,768]{1,0:T(8,128)(2,1)S(1)}, u32[]{:S(2)}, u32[]{:S(2)}) collective-permute-start(bf16[208,768]{1,0:T(8,128)(2,1)S(1)} %get-tuple-element.416.refs_1_.refs_7_), channel_id=1, source_target_pairs={{0,4},{4,0},{8,12},{12,8},{1,5},{5,1},{9,13},{13,9},{2,6},{6,2},{1... | collective-permute-start | bytes 958472 | tf_op jit(solution)/shard_map/ppermute | solution.py:149
  71.0 10.4 %collective-permute-start.26 = (bf16[96,768]{1,0:T(8,128)(2,1)S(1)}, bf16[96,768]{1,0:T(8,128)(2,1)S(1)}, u32[]{:S(2)}, u32[]{:S(2)}) collective-permute-start(bf16[96,768]{1,0:T(8,128)(2,1)S(1)} %get-tuple-element.434), channel_id=1, source_target_pairs={{0,8},{4,12},{8,0},{12,4},{1,9},{5,13},{9,1},{13,5},{2,10},{6,14},... | collective-permute-start | bytes 442376 | tf_op jit(solution)/shard_map/ppermute | solution.py:149
  73.9 10.2 %collective-permute-start.27 = (bf16[192,768]{1,0:T(8,128)(2,1)S(1)}, bf16[192,768]{1,0:T(8,128)(2,1)S(1)}, u32[]{:S(2)}, u32[]{:S(2)}) collective-permute-start(bf16[192,768]{1,0:T(8,128)(2,1)S(1)} %get-tuple-element.442), channel_id=1, source_target_pairs={{0,1},{1,0},{2,3},{3,2},{4,5},{5,4},{6,7},{7,6},{8,9},{9,8},{10,11... | collective-permute-start | bytes 884744 | tf_op jit(solution)/shard_map/ppermute | solution.py:167
  81.5 5.5 %collective-permute-start.28 = (bf16[208,768]{1,0:T(8,128)(2,1)S(1)}, bf16[208,768]{1,0:T(8,128)(2,1)S(1)}, u32[]{:S(2)}, u32[]{:S(2)}) collective-permute-start(bf16[208,768]{1,0:T(8,128)(2,1)S(1)} %get-tuple-element.436.refs_1_.refs_8_), channel_id=1, source_target_pairs={{0,4},{4,0},{8,12},{12,8},{1,5},{5,1},{9,13},{13,9},{2,6},{6,2},{1... | collective-permute-start | bytes 958472 | tf_op jit(solution)/shard_map/ppermute | solution.py:149
  81.6 12.6 %collective-permute-start.30 = (bf16[384,384]{1,0:T(8,128)(2,1)S(1)}, bf16[384,384]{1,0:T(8,128)(2,1)S(1)}, u32[]{:S(2)}, u32[]{:S(2)}) collective-permute-start(bf16[384,384]{1,0:T(8,128)(2,1)S(1)} %get-tuple-element.467), channel_id=1, source_target_pairs={{0,1},{1,0},{2,3},{3,2},{4,5},{5,4},{6,7},{7,6},{8,9},{9,8},{10,11... | collective-permute-start | bytes 884744 | tf_op jit(solution)/shard_map/ppermute | solution.py:167
  84.2 10.1 %collective-permute-start.31 = (bf16[96,768]{1,0:T(8,128)(2,1)S(1)}, bf16[96,768]{1,0:T(8,128)(2,1)S(1)}, u32[]{:S(2)}, u32[]{:S(2)}) collective-permute-start(bf16[96,768]{1,0:T(8,128)(2,1)S(1)} %get-tuple-element.470), channel_id=1, source_target_pairs={{0,2},{1,3},{2,0},{3,1},{4,6},{5,7},{6,4},{7,5},{8,10},{9,11},{10,... | collective-permute-start | bytes 442376 | tf_op jit(solution)/shard_map/ppermute | solution.py:167
  90.8 15.7 %collective-permute-start.33 = (bf16[384,768]{1,0:T(8,128)(2,1)S(1)}, bf16[384,768]{1,0:T(8,128)(2,1)S(1)}, u32[]{:S(2)}, u32[]{:S(2)}) collective-permute-start(bf16[384,768]{1,0:T(8,128)(2,1)S(1)} %get-tuple-element.475), channel_id=1, source_target_pairs={{0,16},{16,0},{1,17},{17,1},{2,18},{18,2},{3,19},{19,3},{4,20},{20... | collective-permute-start | bytes 1769480 | tf_op jit(solution)/shard_map/ppermute | solution.py:158
  91.3 4.2 %collective-permute-start.32 = (bf16[32,768]{1,0:T(8,128)(2,1)S(1)}, bf16[32,768]{1,0:T(8,128)(2,1)S(1)}, u32[]{:S(2)}, u32[]{:S(2)}) collective-permute-start(bf16[32,768]{1,0:T(8,128)(2,1)S(1)} %get-tuple-element.472.refs_1_), channel_id=1, source_target_pairs={{0,8},{4,12},{8,0},{12,4},{1,9},{5,13},{9,1},{13,5},{2,10},{6,14},... | collective-permute-start | bytes 147464 | tf_op jit(solution)/shard_map/ppermute | solution.py:149
  94.3 14.1 %collective-permute-start.34 = (bf16[192,384]{1,0:T(8,128)(2,1)S(1)}, bf16[192,384]{1,0:T(8,128)(2,1)S(1)}, u32[]{:S(2)}, u32[]{:S(2)}) collective-permute-start(bf16[192,384]{1,0:T(8,128)(2,1)S(1)} %get-tuple-element.478), channel_id=1, source_target_pairs={{0,2},{1,3},{2,0},{3,1},{4,6},{5,7},{6,4},{7,5},{8,10},{9,11},{10,... | collective-permute-start | bytes 442376 | tf_op jit(solution)/shard_map/ppermute | solution.py:167
  95.5 13.0 %collective-permute-start.35 = (bf16[32,768]{1,0:T(8,128)(2,1)S(1)}, bf16[32,768]{1,0:T(8,128)(2,1)S(1)}, u32[]{:S(2)}, u32[]{:S(2)}) collective-permute-start(bf16[32,768]{1,0:T(8,128)(2,1)S(1)} %get-tuple-element.480.refs_1_), channel_id=1, source_target_pairs={{0,16},{16,0},{1,17},{17,1},{2,18},{18,2},{3,19},{19,3},{4,20},{20... | collective-permute-start | bytes 147464 | tf_op jit(solution)/shard_map/ppermute | solution.py:158
  97.2 12.4 %collective-permute-start.36 = (bf16[96,768]{1,0:T(8,128)(2,1)S(1)}, bf16[96,768]{1,0:T(8,128)(2,1)S(1)}, u32[]{:S(2)}, u32[]{:S(2)}) collective-permute-start(bf16[96,768]{1,0:T(8,128)(2,1)S(1)} %get-tuple-element.482.refs_1_), channel_id=1, source_target_pairs={{0,2},{1,3},{2,0},{3,1},{4,6},{5,7},{6,4},{7,5},{8,10},{9,11},{10,... | collective-permute-start | bytes 442376 | tf_op jit(solution)/shard_map/ppermute | solution.py:167
  106.8 13.2 %collective-permute-start.37 = (bf16[192,768]{1,0:T(8,128)(2,1)S(1)}, bf16[192,768]{1,0:T(8,128)(2,1)S(1)}, u32[]{:S(2)}, u32[]{:S(2)}) collective-permute-start(bf16[192,768]{1,0:T(8,128)(2,1)S(1)} %get-tuple-element.485), channel_id=1, source_target_pairs={{0,1},{1,0},{2,3},{3,2},{4,5},{5,4},{6,7},{7,6},{8,9},{9,8},{10,11... | collective-permute-start | bytes 884744 | tf_op jit(solution)/shard_map/ppermute | solution.py:167
  108.5 12.5 %collective-permute-start.38 = (bf16[32,768]{1,0:T(8,128)(2,1)S(1)}, bf16[32,768]{1,0:T(8,128)(2,1)S(1)}, u32[]{:S(2)}, u32[]{:S(2)}) collective-permute-start(bf16[32,768]{1,0:T(8,128)(2,1)S(1)} %get-tuple-element.487.refs_1_), channel_id=1, source_target_pairs={{0,1},{1,0},{2,3},{3,2},{4,5},{5,4},{6,7},{7,6},{8,9},{9,8},{10,11... | collective-permute-start | bytes 147464 | tf_op jit(solution)/shard_map/ppermute | solution.py:167
  109.0 15.0 %collective-permute-start.39 = (bf16[192,384]{1,0:T(8,128)(2,1)S(1)}, bf16[192,384]{1,0:T(8,128)(2,1)S(1)}, u32[]{:S(2)}, u32[]{:S(2)}) collective-permute-start(bf16[192,384]{1,0:T(8,128)(2,1)S(1)} %get-tuple-element.489.refs_1_), channel_id=1, source_target_pairs={{0,2},{1,3},{2,0},{3,1},{4,6},{5,7},{6,4},{7,5},{8,10},{9,11},{10,... | collective-permute-start | bytes 442376 | tf_op jit(solution)/shard_map/ppermute | solution.py:167
  109.6 21.9 %collective-permute-start.40 = (bf16[192,768]{1,0:T(8,128)(2,1)S(1)}, bf16[192,768]{1,0:T(8,128)(2,1)S(1)}, u32[]{:S(2)}, u32[]{:S(2)}) collective-permute-start(bf16[192,768]{1,0:T(8,128)(2,1)S(1)} %get-tuple-element.491.refs_1_), channel_id=1, source_target_pairs={{0,1},{1,0},{2,3},{3,2},{4,5},{5,4},{6,7},{7,6},{8,9},{9,8},{10,11... | collective-permute-start | bytes 884744 | tf_op jit(solution)/shard_map/ppermute | solution.py:167
  121.0 10.6 %collective-permute-start.41 = (bf16[64,768]{1,0:T(8,128)(2,1)S(1)}, bf16[64,768]{1,0:T(8,128)(2,1)S(1)}, u32[]{:S(2)}, u32[]{:S(2)}) collective-permute-start(bf16[64,768]{1,0:T(8,128)(2,1)S(1)} %get-tuple-element.493.refs_1_), channel_id=1, source_target_pairs={{0,2},{1,3},{2,0},{3,1},{4,6},{5,7},{6,4},{7,5},{8,10},{9,11},{10,... | collective-permute-start | bytes 294920 | tf_op jit(solution)/shard_map/ppermute | solution.py:167
  121.1 16.5 %collective-permute-start.43 = (bf16[96,768]{1,0:T(8,128)(2,1)S(1)}, bf16[96,768]{1,0:T(8,128)(2,1)S(1)}, u32[]{:S(2)}, u32[]{:S(2)}) collective-permute-start(bf16[96,768]{1,0:T(8,128)(2,1)S(1)} %get-tuple-element.507), channel_id=1, source_target_pairs={{0,2},{1,3},{2,0},{3,1},{4,6},{5,7},{6,4},{7,5},{8,10},{9,11},{10,... | collective-permute-start | bytes 442376 | tf_op jit(solution)/shard_map/ppermute | solution.py:167
  124.0 13.9 %collective-permute-start.44 = (bf16[384,384]{1,0:T(8,128)(2,1)S(1)}, bf16[384,384]{1,0:T(8,128)(2,1)S(1)}, u32[]{:S(2)}, u32[]{:S(2)}) collective-permute-start(bf16[384,384]{1,0:T(8,128)(2,1)S(1)} %get-tuple-element.509.refs_1_), channel_id=1, source_target_pairs={{0,1},{1,0},{2,3},{3,2},{4,5},{5,4},{6,7},{7,6},{8,9},{9,8},{10,11... | collective-permute-start | bytes 884744 | tf_op jit(solution)/shard_map/ppermute | solution.py:167
  131.5 16.7 %collective-permute-start.47 = (bf16[384,768]{1,0:T(8,128)(2,1)S(1)}, bf16[384,768]{1,0:T(8,128)(2,1)S(1)}, u32[]{:S(2)}, u32[]{:S(2)}) collective-permute-start(bf16[384,768]{1,0:T(8,128)(2,1)S(1)} %get-tuple-element.522.refs_1_), channel_id=1, source_target_pairs={{0,16},{16,0},{1,17},{17,1},{2,18},{18,2},{3,19},{19,3},{4,20},{20... | collective-permute-start | bytes 1769480 | tf_op jit(solution)/shard_map/ppermute | solution.py:158
  135.5 4.6 %collective-permute-start.45 = (bf16[48,768]{1,0:T(8,128)(2,1)S(1)}, bf16[48,768]{1,0:T(8,128)(2,1)S(1)}, u32[]{:S(2)}, u32[]{:S(2)}) collective-permute-start(bf16[48,768]{1,0:T(8,128)(2,1)S(1)} %get-tuple-element.511.refs_1_), channel_id=1, source_target_pairs={{0,8},{4,12},{8,0},{12,4},{1,9},{5,13},{9,1},{13,5},{2,10},{6,14},... | collective-permute-start | bytes 221192 | tf_op jit(solution)/shard_map/ppermute | solution.py:149
  137.6 15.9 %collective-permute-start.49 = (bf16[96,768]{1,0:T(8,128)(2,1)S(1)}, bf16[96,768]{1,0:T(8,128)(2,1)S(1)}, u32[]{:S(2)}, u32[]{:S(2)}) collective-permute-start(bf16[96,768]{1,0:T(8,128)(2,1)S(1)} %get-tuple-element.532.refs_1_), channel_id=1, source_target_pairs={{0,2},{1,3},{2,0},{3,1},{4,6},{5,7},{6,4},{7,5},{8,10},{9,11},{10,... | collective-permute-start | bytes 442376 | tf_op jit(solution)/shard_map/ppermute | solution.py:167
  140.2 4.9 %collective-permute-start.46 = (bf16[48,768]{1,0:T(8,128)(2,1)S(1)}, bf16[48,768]{1,0:T(8,128)(2,1)S(1)}, u32[]{:S(2)}, u32[]{:S(2)}) collective-permute-start(bf16[48,768]{1,0:T(8,128)(2,1)S(1)} %get-tuple-element.518.refs_8_), channel_id=1, source_target_pairs={{0,16},{1,17},{2,18},{3,19},{4,20},{5,21},{6,22},{7,23},{8,24},{9,... | collective-permute-start | bytes 221192 | tf_op jit(solution)/shard_map/ppermute | solution.py:161
  144.7 5.2 %collective-permute-start.48 = (bf16[2,2,208,384]{3,2,1,0:T(8,128)(2,1)S(1)}, bf16[2,2,208,384]{3,2,1,0:T(8,128)(2,1)S(1)}, u32[]{:S(2)}, u32[]{:S(2)}) collective-permute-start(bf16[2,2,208,384]{3,2,1,0:T(8,128)(2,1)S(1)} %get-tuple-element.525), channel_id=1, source_target_pairs={{0,4},{4,0},{8,12},{12,8},{1,5},{5,1},{9,13},{13,9},{2,6},{6,2},{1... | collective-permute-start | bytes 1916936 | tf_op jit(solution)/shard_map/ppermute | solution.py:149
  144.7 22.0 %collective-permute-start.53 = (bf16[768,384]{1,0:T(8,128)(2,1)S(1)}, bf16[768,384]{1,0:T(8,128)(2,1)S(1)}, u32[]{:S(2)}, u32[]{:S(2)}) collective-permute-start(bf16[768,384]{1,0:T(8,128)(2,1)S(1)} %get-tuple-element.543.refs_1_), channel_id=1, source_target_pairs={{0,16},{16,0},{1,17},{17,1},{2,18},{18,2},{3,19},{19,3},{4,20},{20... | collective-permute-start | bytes 1769480 | tf_op jit(solution)/shard_map/ppermute | solution.py:158
  150.0 9.7 %collective-permute-start.50 = (bf16[2,208,384]{2,1,0:T(8,128)(2,1)S(1)}, bf16[2,208,384]{2,1,0:T(8,128)(2,1)S(1)}, u32[]{:S(2)}, u32[]{:S(2)}) collective-permute-start(bf16[2,208,384]{2,1,0:T(8,128)(2,1)S(1)} %get-tuple-element.535), channel_id=1, source_target_pairs={{0,8},{4,12},{8,0},{12,4},{1,9},{5,13},{9,1},{13,5},{2,10},{6,14},... | collective-permute-start | bytes 958472 | tf_op jit(solution)/shard_map/ppermute | solution.py:149
  153.6 8.9 %collective-permute-start.51 = (bf16[192,768]{1,0:T(8,128)(2,1)S(1)}, bf16[192,768]{1,0:T(8,128)(2,1)S(1)}, u32[]{:S(2)}, u32[]{:S(2)}) collective-permute-start(bf16[192,768]{1,0:T(8,128)(2,1)S(1)} %get-tuple-element.538.refs_1_), channel_id=1, source_target_pairs={{0,1},{1,0},{2,3},{3,2},{4,5},{5,4},{6,7},{7,6},{8,9},{9,8},{10,11... | collective-permute-start | bytes 884744 | tf_op jit(solution)/shard_map/ppermute | solution.py:167
  153.6 12.6 %collective-permute-start.52 = (bf16[2,2,208,384]{3,2,1,0:T(8,128)(2,1)S(1)}, bf16[2,2,208,384]{3,2,1,0:T(8,128)(2,1)S(1)}, u32[]{:S(2)}, u32[]{:S(2)}) collective-permute-start(bf16[2,2,208,384]{3,2,1,0:T(8,128)(2,1)S(1)} %get-tuple-element.541), channel_id=1, source_target_pairs={{0,4},{4,0},{8,12},{12,8},{1,5},{5,1},{9,13},{13,9},{2,6},{6,2},{1... | collective-permute-start | bytes 1916936 | tf_op jit(solution)/shard_map/ppermute | solution.py:149
  162.5 14.8 %collective-permute-start.55 = (bf16[384,768]{1,0:T(8,128)(2,1)S(1)}, bf16[384,768]{1,0:T(8,128)(2,1)S(1)}, u32[]{:S(2)}, u32[]{:S(2)}) collective-permute-start(bf16[384,768]{1,0:T(8,128)(2,1)S(1)} %get-tuple-element.552.refs_1_), channel_id=1, source_target_pairs={{0,16},{1,17},{2,18},{3,19},{4,20},{5,21},{6,22},{7,23},{8,24},{9,... | collective-permute-start | bytes 1769480 | tf_op jit(solution)/shard_map/ppermute | solution.py:161
  166.4 7.6 %collective-permute-start.54 = (bf16[2,208,384]{2,1,0:T(8,128)(2,1)S(1)}, bf16[2,208,384]{2,1,0:T(8,128)(2,1)S(1)}, u32[]{:S(2)}, u32[]{:S(2)}) collective-permute-start(bf16[2,208,384]{2,1,0:T(8,128)(2,1)S(1)} %get-tuple-element.546), channel_id=1, source_target_pairs={{0,8},{4,12},{8,0},{12,4},{1,9},{5,13},{9,1},{13,5},{2,10},{6,14},... | collective-permute-start | bytes 958472 | tf_op jit(solution)/shard_map/ppermute | solution.py:149
  (28 other events, 161.7 us)

commit v6 on v5

--- a/solution.py
+++ b/solution.py
@@ -1097,9 +1097,9 @@
         ],
     )
     stage.cost = 4 * 10**9
+    r3 = to_far_clip(*r2)
     (bz1,) = adds((bz0, bzc))
     bzx = x_swap(bz1)
-    r3 = to_far_clip(*r2)
     q4 = to_other_section(*q3)
     (bz2,) = adds((bz1, bzx))
     bzy = y_late(bz2)

time: 181 us -> 181 us (level)
  no operation moved by 1% of the time
where the time goes in v6:
time: 181 us; the launch traced here: 179 us
  waiting for transfers between devices  58.4 us (32%)
  Pallas kernels  57.9 us (32%)
  starting transfers between devices  56.5 us (31%)
  local copies, waits for them, and re-layouts  4.38 us (2%)
  between operations  1.82 us (1%)
    pallas_call x79, Pallas kernels, __call__(): pl.pallas_call(stage, out_shape=[*outs, near((8, 128), F32)], in_specs=[p...  57.9 us
    ppermute x28, waiting for transfers between devices, tensor_swap(): return lax.ppermute(v, 'tensor', [(i, i ^ bit) for i in range(4)])  25.6 us
    ppermute x17, waiting for transfers between devices, z_swap(): return lax.ppermute(v, 'dp', [(i, i ^ bit) for i in range(clips)])  21.5 us
    ppermute x17, starting transfers between devices, z_swap(): return lax.ppermute(v, 'dp', [(i, i ^ bit) for i in range(clips)])  19.9 us
    ppermute x28, starting transfers between devices, tensor_swap(): return lax.ppermute(v, 'tensor', [(i, i ^ bit) for i in range(4)])  18 us
    ppermute x3, starting transfers between devices, y_late(): return lax.ppermute(v, 'pipe', [(0, 1)])  11.4 us
    ppermute x6, waiting for transfers between devices, y_swap(): return lax.ppermute(v, 'pipe', [(0, 1), (1, 0)])  8.68 us
    ppermute x6, starting transfers between devices, y_swap(): return lax.ppermute(v, 'pipe', [(0, 1), (1, 0)])  4.69 us
  transfers between devices with their start and end apart: 56, of which 26 were waited for; matrix products, arithmetic and copies ran while one was open for 1% of the time, Pallas kernels for 30%

profile of v6, /device:TPU:0, one launch (start us, length us, event | category | flops | bytes accessed | tf_op | source)
XLA Modules:
  0.0 179.0 jit_solution(2807554890319851329)
XLA Ops:
  0.6 1.7 shard_map.288
  5.7 3.0 %collective-permute-start = (bf16[8,768]{1,0:T(8,128)(2,1)S(1)}, bf16[8,768]{1,0:T(8,128)(2,1)S(1)}, u32[]{:S(2)}, u32[]{:S(2)}) collective-permute-start(bf16[8,768]{1,0:T(8,128)(2,1)S(1)} %slice_bitcast_fusion.refs_2_.refs_3_), channel_id=1, source_target_pairs={{0,1},{1,0},{2,3},{3,2},{4,5},{5,4},{6,7},{7,6},{8,9},{9,8},{10,11... | collective-permute-start | bytes 36872 | tf_op jit(solution)/shard_map/ppermute | solution.py:167
  8.7 2.6 %collective-permute-start.1 = (bf16[8,768]{1,0:T(8,128)(2,1)S(1)}, bf16[8,768]{1,0:T(8,128)(2,1)S(1)}, u32[]{:S(2)}, u32[]{:S(2)}) collective-permute-start(bf16[8,768]{1,0:T(8,128)(2,1)S(1)} %slice_bitcast_fusion.refs_2_.refs_3_), channel_id=1, source_target_pairs={{0,2},{1,3},{2,0},{3,1},{4,6},{5,7},{6,4},{7,5},{8,10},{9,11},{10,... | collective-permute-start | bytes 36872 | tf_op jit(solution)/shard_map/ppermute | solution.py:167
  12.6 3.3 %shard_map.290 = (bf16[208,768]{1,0:T(8,128)(2,1)S(1)}, bf16[208,768]{1,0:T(8,128)(2,1)S(1)}, bf16[208,768]{1,0:T(8,128)(2,1)S(1)}, bf16[208,768]{1,0:T(8,128)(2,1)S(1)}, f32[8,128]{1,0:T(8,128)S(1)}) custom-call(f32[8,128]{1,0:T(8,128)S(1)} %get-tuple-element.289.refs_0_, bf16[197,8,768]{2,1,0:T(8,128)(2,1)} %bitcast.25), custom_call_target="tpu_custom_call" | custom-call | tf_op jit(solution)/shard_map/pallas_call | solution.py:78
  16.8 2.1 %shard_map.291 = (f32[32,768]{1,0:T(8,128)S(1)}, bf16[32,768]{1,0:T(8,128)(2,1)S(1)}, bf16[32,192]{1,0:T(8,128)(2,1)S(1)}, bf16[32,192]{1,0:T(8,128)(2,1)S(1)}, ...) custom-call(f32[8,128]{1,0:T(8,128)S(1)} %get-tuple-element.290.refs, ...), custom_call_target="tpu_custom_call" | custom-call | tf_op jit(solution)/shard_map/pallas_call | solution.py:78
  20.2 1.5 collective-permute-start.4
  21.6 2.3 %collective-permute-done.4.refs_2_ = f32[8,768]{1,0:T(8,128)S(1)} collective-permute-done((f32[8,768]{1,0:T(8,128)S(1)}, f32[8,768]{1,0:T(8,128)S(1)}, u32[]{:S(2)}, u32[]{:S(2)}) %collective-permute-start.4) | collective-permute-done | bytes 24608 | tf_op jit(solution)/shard_map/ppermute | solution.py:149
  24.0 4.8 %collective-permute-start.6 = (f32[8,768]{1,0:T(8,128)S(1)}, f32[8,768]{1,0:T(8,128)S(1)}, u32[]{:S(2)}, u32[]{:S(2)}) collective-permute-start(f32[8,768]{1,0:T(8,128)S(1)} %get-tuple-element.308.refs_2_), channel_id=1, source_target_pairs={{0,16},{1,17},{2,18},{3,19},{4,20},{5,21},{6,22},{7,23},{8,24},{9,... | collective-permute-start | bytes 73736 | tf_op jit(solution)/shard_map/ppermute | solution.py:161
  28.8 1.7 shard_map.294
  36.5 2.4 %collective-permute-start.10 = (bf16[112,768]{1,0:T(8,128)(2,1)S(1)}, bf16[112,768]{1,0:T(8,128)(2,1)S(1)}, u32[]{:S(2)}, u32[]{:S(2)}) collective-permute-start(bf16[112,768]{1,0:T(8,128)(2,1)S(1)} %get-tuple-element.343), channel_id=1, source_target_pairs={{0,8},{4,12},{8,0},{12,4},{1,9},{5,13},{9,1},{13,5},{2,10},{6,14},... | collective-permute-start | bytes 516104 | tf_op jit(solution)/shard_map/ppermute | solution.py:149
  40.1 3.6 %shard_map.303 = (bf16[208,768]{1,0:T(8,128)(2,1)S(1)}, bf16[208,768]{1,0:T(8,128)(2,1)S(1)}, bf16[208,768]{1,0:T(8,128)(2,1)S(1)}, bf16[208,768]{1,0:T(8,128)(2...) custom-call(f32[8,128]{1,0:T(8,128)S(1)} %get-tuple-element.337.refs, ...), custom_call_target="tpu_custom_call" | custom-call | flops 4000000000 | tf_op jit(solution)/shard_map/pallas_call | solution.py:78
  44.3 2.1 %collective-permute-start.14 = (bf16[112,768]{1,0:T(8,128)(2,1)S(1)}, bf16[112,768]{1,0:T(8,128)(2,1)S(1)}, u32[]{:S(2)}, u32[]{:S(2)}) collective-permute-start(bf16[112,768]{1,0:T(8,128)(2,1)S(1)} %get-tuple-element.347.refs_7_), channel_id=1, source_target_pairs={{0,8},{4,12},{8,0},{12,4},{1,9},{5,13},{9,1},{13,5},{2,10},{6,14},... | collective-permute-start | bytes 516104 | tf_op jit(solution)/shard_map/ppermute | solution.py:149
  48.6 1.5 collective-permute-start.15
  50.1 1.6 shard_map.307
  61.4 1.6 collective-permute-start.22
  65.9 2.3 %collective-permute-done.20.refs_2_ = bf16[112,768]{1,0:T(8,128)(2,1)S(1)} collective-permute-done((bf16[112,768]{1,0:T(8,128)(2,1)S(1)}, bf16[112,768]{1,0:T(8,128)(2,1)S(1)}, u32[]{:S(2)}, u32[]{:S(2)}) %collective-permute-start.20) | collective-permute-done | bytes 172064 | tf_op jit(solution)/shard_map/ppermute | solution.py:149
  69.2 1.4 collective-permute-done.22.refs_2_
  73.9 1.8 collective-permute-start.27
  75.6 1.6 shard_map.327
  77.2 1.7 shard_map.328
  78.9 1.7 shard_map.329
  82.0 2.1 %shard_map.332 = (bf16[208,768]{1,0:T(8,128)(2,1)S(1)}, bf16[3,208,192]{2,1,0:T(8,128)(2,1)S(1)}, bf16[208,768]{1,0:T(8,128)(2,1)S(1)}, f32[8,768]{1,0:T(8,128)S(1)}, f32[8,128]{1,0:T(8,128)S(1)}) custom-call(f32[8,128]{1,0:T(8,128)S(1)} %get-tuple-element.435.refs_0_, bf16[208,768]{1,0:T(8,128)(2,1)S(1)} %get-tuple-element.436.refs_1_.refs_8_, ...), custom_call_target="tpu_custom_call" | custom-call | flops 4000000000 | tf_op jit(solution)/shard_map/pallas_call | solution.py:78
  84.2 2.8 %collective-permute-start.31 = (bf16[96,768]{1,0:T(8,128)(2,1)S(1)}, bf16[96,768]{1,0:T(8,128)(2,1)S(1)}, u32[]{:S(2)}, u32[]{:S(2)}) collective-permute-start(bf16[96,768]{1,0:T(8,128)(2,1)S(1)} %get-tuple-element.470), channel_id=1, source_target_pairs={{0,2},{1,3},{2,0},{3,1},{4,6},{5,7},{6,4},{7,5},{8,10},{9,11},{10,... | collective-permute-start | bytes 442376 | tf_op jit(solution)/shard_map/ppermute | solution.py:167
  87.0 1.7 shard_map.334
  91.3 1.5 collective-permute-start.32
  95.5 1.7 collective-permute-start.35
  97.8 8.7 %collective-permute-done.33.refs_2_ = bf16[384,768]{1,0:T(8,128)(2,1)S(1)} collective-permute-done((bf16[384,768]{1,0:T(8,128)(2,1)S(1)}, bf16[384,768]{1,0:T(8,128)(2,1)S(1)}, u32[]{:S(2)}, u32[]{:S(2)}) %collective-permute-start.33) | collective-permute-done | bytes 589856 | tf_op jit(solution)/shard_map/ppermute | solution.py:158
  106.8 1.6 collective-permute-start.37
  109.6 1.4 collective-permute-start.40
  111.0 8.9 %collective-permute-done.37.refs_2_ = bf16[192,768]{1,0:T(8,128)(2,1)S(1)} collective-permute-done((bf16[192,768]{1,0:T(8,128)(2,1)S(1)}, bf16[192,768]{1,0:T(8,128)(2,1)S(1)}, u32[]{:S(2)}, u32[]{:S(2)}) %collective-permute-start.37) | collective-permute-done | bytes 294944 | tf_op jit(solution)/shard_map/ppermute | solution.py:167
  121.1 2.9 %collective-permute-start.42 = (bf16[96,768]{1,0:T(8,128)(2,1)S(1)}, bf16[96,768]{1,0:T(8,128)(2,1)S(1)}, u32[]{:S(2)}, u32[]{:S(2)}) collective-permute-start(bf16[96,768]{1,0:T(8,128)(2,1)S(1)} %get-tuple-element.505), channel_id=1, source_target_pairs={{0,2},{1,3},{2,0},{3,1},{4,6},{5,7},{6,4},{7,5},{8,10},{9,11},{10,... | collective-permute-start | bytes 442376 | tf_op jit(solution)/shard_map/ppermute | solution.py:167
  124.1 7.4 %collective-permute-done.40.refs_2_ = bf16[192,768]{1,0:T(8,128)(2,1)S(1)} collective-permute-done((bf16[192,768]{1,0:T(8,128)(2,1)S(1)}, bf16[192,768]{1,0:T(8,128)(2,1)S(1)}, u32[]{:S(2)}, u32[]{:S(2)}) %collective-permute-start.40) | collective-permute-done | bytes 294944 | tf_op jit(solution)/shard_map/ppermute | solution.py:167
  132.7 1.5 shard_map.349
  135.5 2.0 %collective-permute-start.45 = (bf16[48,768]{1,0:T(8,128)(2,1)S(1)}, bf16[48,768]{1,0:T(8,128)(2,1)S(1)}, u32[]{:S(2)}, u32[]{:S(2)}) collective-permute-start(bf16[48,768]{1,0:T(8,128)(2,1)S(1)} %get-tuple-element.511.refs_1_), channel_id=1, source_target_pairs={{0,8},{4,12},{8,0},{12,4},{1,9},{5,13},{9,1},{13,5},{2,10},{6,14},... | collective-permute-start | bytes 221192 | tf_op jit(solution)/shard_map/ppermute | solution.py:149
  138.0 2.2 %collective-permute-done.45.refs_2_ = bf16[48,768]{1,0:T(8,128)(2,1)S(1)} collective-permute-done((bf16[48,768]{1,0:T(8,128)(2,1)S(1)}, bf16[48,768]{1,0:T(8,128)(2,1)S(1)}, u32[]{:S(2)}, u32[]{:S(2)}) %collective-permute-start.45) | collective-permute-done | bytes 73760 | tf_op jit(solution)/shard_map/ppermute | solution.py:149
  140.2 2.9 %collective-permute-start.46 = (bf16[48,768]{1,0:T(8,128)(2,1)S(1)}, bf16[48,768]{1,0:T(8,128)(2,1)S(1)}, u32[]{:S(2)}, u32[]{:S(2)}) collective-permute-start(bf16[48,768]{1,0:T(8,128)(2,1)S(1)} %get-tuple-element.518.refs_8_), channel_id=1, source_target_pairs={{0,16},{1,17},{2,18},{3,19},{4,20},{5,21},{6,22},{7,23},{8,24},{9,... | collective-permute-start | bytes 221192 | tf_op jit(solution)/shard_map/ppermute | solution.py:161
  143.2 1.5 shard_map.355
  145.1 1.4 shard_map.356
  148.3 1.6 shard_map.357
  150.0 1.8 %collective-permute-start.50 = (bf16[2,208,384]{2,1,0:T(8,128)(2,1)S(1)}, bf16[2,208,384]{2,1,0:T(8,128)(2,1)S(1)}, u32[]{:S(2)}, u32[]{:S(2)}) collective-permute-start(bf16[2,208,384]{2,1,0:T(8,128)(2,1)S(1)} %get-tuple-element.535), channel_id=1, source_target_pairs={{0,8},{4,12},{8,0},{12,4},{1,9},{5,13},{9,1},{13,5},{2,10},{6,14},... | collective-permute-start | bytes 958472 | tf_op jit(solution)/shard_map/ppermute | solution.py:149
  151.8 1.7 shard_map.359
  154.9 4.8 %collective-permute-done.50.refs_2_ = bf16[2,208,384]{2,1,0:T(8,128)(2,1)S(1)} collective-permute-done((bf16[2,208,384]{2,1,0:T(8,128)(2,1)S(1)}, bf16[2,208,384]{2,1,0:T(8,128)(2,1)S(1)}, u32[]{:S(2)}, u32[]{:S(2)}) %collective-permute-start.50) | collective-permute-done | bytes 319520 | tf_op jit(solution)/shard_map/ppermute | solution.py:149
  161.0 1.4 collective-permute-done.51.refs_2_
  162.5 3.7 %collective-permute-start.55 = (bf16[384,768]{1,0:T(8,128)(2,1)S(1)}, bf16[384,768]{1,0:T(8,128)(2,1)S(1)}, u32[]{:S(2)}, u32[]{:S(2)}) collective-permute-start(bf16[384,768]{1,0:T(8,128)(2,1)S(1)} %get-tuple-element.552.refs_1_), channel_id=1, source_target_pairs={{0,16},{1,17},{2,18},{3,19},{4,20},{5,21},{6,22},{7,23},{8,24},{9,... | collective-permute-start | bytes 1769480 | tf_op jit(solution)/shard_map/ppermute | solution.py:161
  166.8 1.6 shard_map.364
  168.4 5.6 %collective-permute-done.54.refs_2_ = bf16[2,208,384]{2,1,0:T(8,128)(2,1)S(1)} collective-permute-done((bf16[2,208,384]{2,1,0:T(8,128)(2,1)S(1)}, bf16[2,208,384]{2,1,0:T(8,128)(2,1)S(1)}, u32[]{:S(2)}, u32[]{:S(2)}) %collective-permute-start.54) | collective-permute-done | bytes 319520 | tf_op jit(solution)/shard_map/ppermute | solution.py:149
  175.1 2.2 %collective-permute-done.55.refs_2_ = bf16[384,768]{1,0:T(8,128)(2,1)S(1)} collective-permute-done((bf16[384,768]{1,0:T(8,128)(2,1)S(1)}, bf16[384,768]{1,0:T(8,128)(2,1)S(1)}, u32[]{:S(2)}, u32[]{:S(2)}) %collective-permute-start.55) | collective-permute-done | bytes 589856 | tf_op jit(solution)/shard_map/ppermute | solution.py:161
  177.3 1.6 shard_map.366
  (186 shorter events, 52.9 us)
Async XLA Ops:
  2.3 26.4 %collective-permute-start.5 = (bf16[592,768]{1,0:T(8,128)(2,1)S(1)}, bf16[592,768]{1,0:T(8,128)(2,1)S(1)}, u32[]{:S(2)}, u32[]{:S(2)}) collective-permute-start(bf16[592,768]{1,0:T(8,128)(2,1)S(1)} %get-tuple-element.305), channel_id=1, source_target_pairs={{16,0},{17,1},{18,2},{19,3},{20,4},{21,5},{22,6},{23,7},{24,8},{25... | collective-permute-start | bytes 2727944 | tf_op jit(solution)/shard_map/ppermute | solution.py:164
  3.6 29.4 %collective-permute-start.7 = (bf16[192,768]{1,0:T(8,128)(2,1)}, bf16[192,768]{1,0:T(8,128)(2,1)S(1)}, u32[]{:S(2)}, u32[]{:S(2)}) collective-permute-start(bf16[192,768]{1,0:T(8,128)(2,1)} %bitcast.27), channel_id=1, source_target_pairs={{16,0},{17,1},{18,2},{19,3},{20,4},{21,5},{22,6},{23,7},{24,8},{25... | collective-permute-start | bytes 884744 | tf_op jit(solution)/shard_map/ppermute | solution.py:164
  5.7 10.3 %collective-permute-start = (bf16[8,768]{1,0:T(8,128)(2,1)S(1)}, bf16[8,768]{1,0:T(8,128)(2,1)S(1)}, u32[]{:S(2)}, u32[]{:S(2)}) collective-permute-start(bf16[8,768]{1,0:T(8,128)(2,1)S(1)} %slice_bitcast_fusion.refs_2_.refs_3_), channel_id=1, source_target_pairs={{0,1},{1,0},{2,3},{3,2},{4,5},{5,4},{6,7},{7,6},{8,9},{9,8},{10,11... | collective-permute-start | bytes 36872 | tf_op jit(solution)/shard_map/ppermute | solution.py:167
  8.7 7.3 %collective-permute-start.1 = (bf16[8,768]{1,0:T(8,128)(2,1)S(1)}, bf16[8,768]{1,0:T(8,128)(2,1)S(1)}, u32[]{:S(2)}, u32[]{:S(2)}) collective-permute-start(bf16[8,768]{1,0:T(8,128)(2,1)S(1)} %slice_bitcast_fusion.refs_2_.refs_3_), channel_id=1, source_target_pairs={{0,2},{1,3},{2,0},{3,1},{4,6},{5,7},{6,4},{7,5},{8,10},{9,11},{10,... | collective-permute-start | bytes 36872 | tf_op jit(solution)/shard_map/ppermute | solution.py:167
  11.3 5.5 %collective-permute-start.2 = (bf16[8,768]{1,0:T(8,128)(2,1)S(1)}, bf16[8,768]{1,0:T(8,128)(2,1)S(1)}, u32[]{:S(2)}, u32[]{:S(2)}) collective-permute-start(bf16[8,768]{1,0:T(8,128)(2,1)S(1)} %slice_bitcast_fusion.refs_2_.refs_3_), channel_id=1, source_target_pairs={{0,3},{1,2},{2,1},{3,0},{4,7},{5,6},{6,5},{7,4},{8,11},{9,10},{10,... | collective-permute-start | bytes 36872 | tf_op jit(solution)/shard_map/ppermute | solution.py:167
  20.2 3.8 %collective-permute-start.4 = (f32[8,768]{1,0:T(8,128)S(1)}, f32[8,768]{1,0:T(8,128)S(1)}, u32[]{:S(2)}, u32[]{:S(2)}) collective-permute-start(f32[8,768]{1,0:T(8,128)S(1)} %get-tuple-element.299.refs_1_), channel_id=1, source_target_pairs={{0,8},{4,12},{8,0},{12,4},{1,9},{5,13},{9,1},{13,5},{2,10},{6,14},... | collective-permute-start | bytes 73736 | tf_op jit(solution)/shard_map/ppermute | solution.py:149
  24.0 6.5 %collective-permute-start.6 = (f32[8,768]{1,0:T(8,128)S(1)}, f32[8,768]{1,0:T(8,128)S(1)}, u32[]{:S(2)}, u32[]{:S(2)}) collective-permute-start(f32[8,768]{1,0:T(8,128)S(1)} %get-tuple-element.308.refs_2_), channel_id=1, source_target_pairs={{0,16},{1,17},{2,18},{3,19},{4,20},{5,21},{6,22},{7,23},{8,24},{9,... | collective-permute-start | bytes 73736 | tf_op jit(solution)/shard_map/ppermute | solution.py:161
  36.3 7.3 %collective-permute-start.9 = (bf16[208,768]{1,0:T(8,128)(2,1)S(1)}, bf16[208,768]{1,0:T(8,128)(2,1)S(1)}, u32[]{:S(2)}, u32[]{:S(2)}) collective-permute-start(bf16[208,768]{1,0:T(8,128)(2,1)S(1)} %get-tuple-element.340), channel_id=1, source_target_pairs={{0,4},{4,0},{8,12},{12,8},{1,5},{5,1},{9,13},{13,9},{2,6},{6,2},{1... | collective-permute-start | bytes 958472 | tf_op jit(solution)/shard_map/ppermute | solution.py:149
  36.5 7.5 %collective-permute-start.10 = (bf16[112,768]{1,0:T(8,128)(2,1)S(1)}, bf16[112,768]{1,0:T(8,128)(2,1)S(1)}, u32[]{:S(2)}, u32[]{:S(2)}) collective-permute-start(bf16[112,768]{1,0:T(8,128)(2,1)S(1)} %get-tuple-element.343), channel_id=1, source_target_pairs={{0,8},{4,12},{8,0},{12,4},{1,9},{5,13},{9,1},{13,5},{2,10},{6,14},... | collective-permute-start | bytes 516104 | tf_op jit(solution)/shard_map/ppermute | solution.py:149
  38.9 8.1 %collective-permute-start.11 = (bf16[96,768]{1,0:T(8,128)(2,1)S(1)}, bf16[96,768]{1,0:T(8,128)(2,1)S(1)}, u32[]{:S(2)}, u32[]{:S(2)}) collective-permute-start(bf16[96,768]{1,0:T(8,128)(2,1)S(1)} %get-tuple-element.345), channel_id=1, source_target_pairs={{0,8},{4,12},{8,0},{12,4},{1,9},{5,13},{9,1},{13,5},{2,10},{6,14},... | collective-permute-start | bytes 442376 | tf_op jit(solution)/shard_map/ppermute | solution.py:149
  44.3 11.2 %collective-permute-start.14 = (bf16[112,768]{1,0:T(8,128)(2,1)S(1)}, bf16[112,768]{1,0:T(8,128)(2,1)S(1)}, u32[]{:S(2)}, u32[]{:S(2)}) collective-permute-start(bf16[112,768]{1,0:T(8,128)(2,1)S(1)} %get-tuple-element.347.refs_7_), channel_id=1, source_target_pairs={{0,8},{4,12},{8,0},{12,4},{1,9},{5,13},{9,1},{13,5},{2,10},{6,14},... | collective-permute-start | bytes 516104 | tf_op jit(solution)/shard_map/ppermute | solution.py:149
  47.2 5.5 %collective-permute-start.12 = (bf16[208,768]{1,0:T(8,128)(2,1)S(1)}, bf16[208,768]{1,0:T(8,128)(2,1)S(1)}, u32[]{:S(2)}, u32[]{:S(2)}) collective-permute-start(bf16[208,768]{1,0:T(8,128)(2,1)S(1)} %get-tuple-element.354.refs_1_), channel_id=1, source_target_pairs={{0,4},{4,0},{8,12},{12,8},{1,5},{5,1},{9,13},{13,9},{2,6},{6,2},{1... | collective-permute-start | bytes 958472 | tf_op jit(solution)/shard_map/ppermute | solution.py:149
  47.3 12.0 %collective-permute-start.17 = (bf16[208,768]{1,0:T(8,128)(2,1)S(1)}, bf16[208,768]{1,0:T(8,128)(2,1)S(1)}, u32[]{:S(2)}, u32[]{:S(2)}) collective-permute-start(bf16[208,768]{1,0:T(8,128)(2,1)S(1)} %get-tuple-element.354.refs_1_), channel_id=1, source_target_pairs={{0,16},{16,0},{1,17},{17,1},{2,18},{18,2},{3,19},{19,3},{4,20},{20... | collective-permute-start | bytes 958472 | tf_op jit(solution)/shard_map/ppermute | solution.py:158
  48.6 6.9 %collective-permute-start.15 = (bf16[96,768]{1,0:T(8,128)(2,1)S(1)}, bf16[96,768]{1,0:T(8,128)(2,1)S(1)}, u32[]{:S(2)}, u32[]{:S(2)}) collective-permute-start(bf16[96,768]{1,0:T(8,128)(2,1)S(1)} %get-tuple-element.365), channel_id=1, source_target_pairs={{0,8},{4,12},{8,0},{12,4},{1,9},{5,13},{9,1},{13,5},{2,10},{6,14},... | collective-permute-start | bytes 442376 | tf_op jit(solution)/shard_map/ppermute | solution.py:149
  55.8 12.9 %collective-permute-start.21 = (bf16[208,768]{1,0:T(8,128)(2,1)S(1)}, bf16[208,768]{1,0:T(8,128)(2,1)S(1)}, u32[]{:S(2)}, u32[]{:S(2)}) collective-permute-start(bf16[208,768]{1,0:T(8,128)(2,1)S(1)} %get-tuple-element.367.refs_1_.refs_2_), channel_id=1, source_target_pairs={{0,16},{16,0},{1,17},{17,1},{2,18},{18,2},{3,19},{19,3},{4,20},{20... | collective-permute-start | bytes 958472 | tf_op jit(solution)/shard_map/ppermute | solution.py:158
  59.3 4.2 %collective-permute-start.19 = (bf16[208,768]{1,0:T(8,128)(2,1)S(1)}, bf16[208,768]{1,0:T(8,128)(2,1)S(1)}, u32[]{:S(2)}, u32[]{:S(2)}) collective-permute-start(bf16[208,768]{1,0:T(8,128)(2,1)S(1)} %get-tuple-element.376.refs_1_.refs_6_), channel_id=1, source_target_pairs={{0,4},{4,0},{8,12},{12,8},{1,5},{5,1},{9,13},{13,9},{2,6},{6,2},{1... | collective-permute-start | bytes 958472 | tf_op jit(solution)/shard_map/ppermute | solution.py:149
  60.9 7.3 %collective-permute-start.20 = (bf16[112,768]{1,0:T(8,128)(2,1)S(1)}, bf16[112,768]{1,0:T(8,128)(2,1)S(1)}, u32[]{:S(2)}, u32[]{:S(2)}) collective-permute-start(bf16[112,768]{1,0:T(8,128)(2,1)S(1)} %get-tuple-element.389), channel_id=1, source_target_pairs={{0,8},{4,12},{8,0},{12,4},{1,9},{5,13},{9,1},{13,5},{2,10},{6,14},... | collective-permute-start | bytes 516104 | tf_op jit(solution)/shard_map/ppermute | solution.py:149
  61.4 9.2 %collective-permute-start.22 = (bf16[96,768]{1,0:T(8,128)(2,1)S(1)}, bf16[96,768]{1,0:T(8,128)(2,1)S(1)}, u32[]{:S(2)}, u32[]{:S(2)}) collective-permute-start(bf16[96,768]{1,0:T(8,128)(2,1)S(1)} %get-tuple-element.392), channel_id=1, source_target_pairs={{0,8},{4,12},{8,0},{12,4},{1,9},{5,13},{9,1},{13,5},{2,10},{6,14},... | collective-permute-start | bytes 442376 | tf_op jit(solution)/shard_map/ppermute | solution.py:149
  68.7 12.7 %collective-permute-start.25 = (bf16[112,768]{1,0:T(8,128)(2,1)S(1)}, bf16[112,768]{1,0:T(8,128)(2,1)S(1)}, u32[]{:S(2)}, u32[]{:S(2)}) collective-permute-start(bf16[112,768]{1,0:T(8,128)(2,1)S(1)} %get-tuple-element.394.refs_7_), channel_id=1, source_target_pairs={{0,8},{4,12},{8,0},{12,4},{1,9},{5,13},{9,1},{13,5},{2,10},{6,14},... | collective-permute-start | bytes 516104 | tf_op jit(solution)/shard_map/ppermute | solution.py:149
  71.0 8.0 %collective-permute-start.24 = (bf16[208,768]{1,0:T(8,128)(2,1)S(1)}, bf16[208,768]{1,0:T(8,128)(2,1)S(1)}, u32[]{:S(2)}, u32[]{:S(2)}) collective-permute-start(bf16[208,768]{1,0:T(8,128)(2,1)S(1)} %get-tuple-element.416.refs_1_.refs_7_), channel_id=1, source_target_pairs={{0,4},{4,0},{8,12},{12,8},{1,5},{5,1},{9,13},{13,9},{2,6},{6,2},{1... | collective-permute-start | bytes 958472 | tf_op jit(solution)/shard_map/ppermute | solution.py:149
  71.0 10.4 %collective-permute-start.26 = (bf16[96,768]{1,0:T(8,128)(2,1)S(1)}, bf16[96,768]{1,0:T(8,128)(2,1)S(1)}, u32[]{:S(2)}, u32[]{:S(2)}) collective-permute-start(bf16[96,768]{1,0:T(8,128)(2,1)S(1)} %get-tuple-element.434), channel_id=1, source_target_pairs={{0,8},{4,12},{8,0},{12,4},{1,9},{5,13},{9,1},{13,5},{2,10},{6,14},... | collective-permute-start | bytes 442376 | tf_op jit(solution)/shard_map/ppermute | solution.py:149
  73.9 10.2 %collective-permute-start.27 = (bf16[192,768]{1,0:T(8,128)(2,1)S(1)}, bf16[192,768]{1,0:T(8,128)(2,1)S(1)}, u32[]{:S(2)}, u32[]{:S(2)}) collective-permute-start(bf16[192,768]{1,0:T(8,128)(2,1)S(1)} %get-tuple-element.442), channel_id=1, source_target_pairs={{0,1},{1,0},{2,3},{3,2},{4,5},{5,4},{6,7},{7,6},{8,9},{9,8},{10,11... | collective-permute-start | bytes 884744 | tf_op jit(solution)/shard_map/ppermute | solution.py:167
  81.5 5.5 %collective-permute-start.28 = (bf16[208,768]{1,0:T(8,128)(2,1)S(1)}, bf16[208,768]{1,0:T(8,128)(2,1)S(1)}, u32[]{:S(2)}, u32[]{:S(2)}) collective-permute-start(bf16[208,768]{1,0:T(8,128)(2,1)S(1)} %get-tuple-element.436.refs_1_.refs_8_), channel_id=1, source_target_pairs={{0,4},{4,0},{8,12},{12,8},{1,5},{5,1},{9,13},{13,9},{2,6},{6,2},{1... | collective-permute-start | bytes 958472 | tf_op jit(solution)/shard_map/ppermute | solution.py:149
  81.6 12.6 %collective-permute-start.30 = (bf16[384,384]{1,0:T(8,128)(2,1)S(1)}, bf16[384,384]{1,0:T(8,128)(2,1)S(1)}, u32[]{:S(2)}, u32[]{:S(2)}) collective-permute-start(bf16[384,384]{1,0:T(8,128)(2,1)S(1)} %get-tuple-element.467), channel_id=1, source_target_pairs={{0,1},{1,0},{2,3},{3,2},{4,5},{5,4},{6,7},{7,6},{8,9},{9,8},{10,11... | collective-permute-start | bytes 884744 | tf_op jit(solution)/shard_map/ppermute | solution.py:167
  84.2 10.1 %collective-permute-start.31 = (bf16[96,768]{1,0:T(8,128)(2,1)S(1)}, bf16[96,768]{1,0:T(8,128)(2,1)S(1)}, u32[]{:S(2)}, u32[]{:S(2)}) collective-permute-start(bf16[96,768]{1,0:T(8,128)(2,1)S(1)} %get-tuple-element.470), channel_id=1, source_target_pairs={{0,2},{1,3},{2,0},{3,1},{4,6},{5,7},{6,4},{7,5},{8,10},{9,11},{10,... | collective-permute-start | bytes 442376 | tf_op jit(solution)/shard_map/ppermute | solution.py:167
  90.8 15.7 %collective-permute-start.33 = (bf16[384,768]{1,0:T(8,128)(2,1)S(1)}, bf16[384,768]{1,0:T(8,128)(2,1)S(1)}, u32[]{:S(2)}, u32[]{:S(2)}) collective-permute-start(bf16[384,768]{1,0:T(8,128)(2,1)S(1)} %get-tuple-element.475), channel_id=1, source_target_pairs={{0,16},{16,0},{1,17},{17,1},{2,18},{18,2},{3,19},{19,3},{4,20},{20... | collective-permute-start | bytes 1769480 | tf_op jit(solution)/shard_map/ppermute | solution.py:158
  91.3 4.2 %collective-permute-start.32 = (bf16[32,768]{1,0:T(8,128)(2,1)S(1)}, bf16[32,768]{1,0:T(8,128)(2,1)S(1)}, u32[]{:S(2)}, u32[]{:S(2)}) collective-permute-start(bf16[32,768]{1,0:T(8,128)(2,1)S(1)} %get-tuple-element.472.refs_1_), channel_id=1, source_target_pairs={{0,8},{4,12},{8,0},{12,4},{1,9},{5,13},{9,1},{13,5},{2,10},{6,14},... | collective-permute-start | bytes 147464 | tf_op jit(solution)/shard_map/ppermute | solution.py:149
  94.3 14.1 %collective-permute-start.34 = (bf16[192,384]{1,0:T(8,128)(2,1)S(1)}, bf16[192,384]{1,0:T(8,128)(2,1)S(1)}, u32[]{:S(2)}, u32[]{:S(2)}) collective-permute-start(bf16[192,384]{1,0:T(8,128)(2,1)S(1)} %get-tuple-element.478), channel_id=1, source_target_pairs={{0,2},{1,3},{2,0},{3,1},{4,6},{5,7},{6,4},{7,5},{8,10},{9,11},{10,... | collective-permute-start | bytes 442376 | tf_op jit(solution)/shard_map/ppermute | solution.py:167
  95.5 13.0 %collective-permute-start.35 = (bf16[32,768]{1,0:T(8,128)(2,1)S(1)}, bf16[32,768]{1,0:T(8,128)(2,1)S(1)}, u32[]{:S(2)}, u32[]{:S(2)}) collective-permute-start(bf16[32,768]{1,0:T(8,128)(2,1)S(1)} %get-tuple-element.480.refs_1_), channel_id=1, source_target_pairs={{0,16},{16,0},{1,17},{17,1},{2,18},{18,2},{3,19},{19,3},{4,20},{20... | collective-permute-start | bytes 147464 | tf_op jit(solution)/shard_map/ppermute | solution.py:158
  97.2 12.4 %collective-permute-start.36 = (bf16[96,768]{1,0:T(8,128)(2,1)S(1)}, bf16[96,768]{1,0:T(8,128)(2,1)S(1)}, u32[]{:S(2)}, u32[]{:S(2)}) collective-permute-start(bf16[96,768]{1,0:T(8,128)(2,1)S(1)} %get-tuple-element.482.refs_1_), channel_id=1, source_target_pairs={{0,2},{1,3},{2,0},{3,1},{4,6},{5,7},{6,4},{7,5},{8,10},{9,11},{10,... | collective-permute-start | bytes 442376 | tf_op jit(solution)/shard_map/ppermute | solution.py:167
  106.8 13.2 %collective-permute-start.37 = (bf16[192,768]{1,0:T(8,128)(2,1)S(1)}, bf16[192,768]{1,0:T(8,128)(2,1)S(1)}, u32[]{:S(2)}, u32[]{:S(2)}) collective-permute-start(bf16[192,768]{1,0:T(8,128)(2,1)S(1)} %get-tuple-element.485), channel_id=1, source_target_pairs={{0,1},{1,0},{2,3},{3,2},{4,5},{5,4},{6,7},{7,6},{8,9},{9,8},{10,11... | collective-permute-start | bytes 884744 | tf_op jit(solution)/shard_map/ppermute | solution.py:167
  108.5 12.5 %collective-permute-start.38 = (bf16[32,768]{1,0:T(8,128)(2,1)S(1)}, bf16[32,768]{1,0:T(8,128)(2,1)S(1)}, u32[]{:S(2)}, u32[]{:S(2)}) collective-permute-start(bf16[32,768]{1,0:T(8,128)(2,1)S(1)} %get-tuple-element.487.refs_1_), channel_id=1, source_target_pairs={{0,1},{1,0},{2,3},{3,2},{4,5},{5,4},{6,7},{7,6},{8,9},{9,8},{10,11... | collective-permute-start | bytes 147464 | tf_op jit(solution)/shard_map/ppermute | solution.py:167
  109.0 15.0 %collective-permute-start.39 = (bf16[192,384]{1,0:T(8,128)(2,1)S(1)}, bf16[192,384]{1,0:T(8,128)(2,1)S(1)}, u32[]{:S(2)}, u32[]{:S(2)}) collective-permute-start(bf16[192,384]{1,0:T(8,128)(2,1)S(1)} %get-tuple-element.489.refs_1_), channel_id=1, source_target_pairs={{0,2},{1,3},{2,0},{3,1},{4,6},{5,7},{6,4},{7,5},{8,10},{9,11},{10,... | collective-permute-start | bytes 442376 | tf_op jit(solution)/shard_map/ppermute | solution.py:167
  109.6 21.9 %collective-permute-start.40 = (bf16[192,768]{1,0:T(8,128)(2,1)S(1)}, bf16[192,768]{1,0:T(8,128)(2,1)S(1)}, u32[]{:S(2)}, u32[]{:S(2)}) collective-permute-start(bf16[192,768]{1,0:T(8,128)(2,1)S(1)} %get-tuple-element.491.refs_1_), channel_id=1, source_target_pairs={{0,1},{1,0},{2,3},{3,2},{4,5},{5,4},{6,7},{7,6},{8,9},{9,8},{10,11... | collective-permute-start | bytes 884744 | tf_op jit(solution)/shard_map/ppermute | solution.py:167
  121.0 10.6 %collective-permute-start.41 = (bf16[64,768]{1,0:T(8,128)(2,1)S(1)}, bf16[64,768]{1,0:T(8,128)(2,1)S(1)}, u32[]{:S(2)}, u32[]{:S(2)}) collective-permute-start(bf16[64,768]{1,0:T(8,128)(2,1)S(1)} %get-tuple-element.493.refs_1_), channel_id=1, source_target_pairs={{0,2},{1,3},{2,0},{3,1},{4,6},{5,7},{6,4},{7,5},{8,10},{9,11},{10,... | collective-permute-start | bytes 294920 | tf_op jit(solution)/shard_map/ppermute | solution.py:167
  121.1 13.7 %collective-permute-start.42 = (bf16[96,768]{1,0:T(8,128)(2,1)S(1)}, bf16[96,768]{1,0:T(8,128)(2,1)S(1)}, u32[]{:S(2)}, u32[]{:S(2)}) collective-permute-start(bf16[96,768]{1,0:T(8,128)(2,1)S(1)} %get-tuple-element.505), channel_id=1, source_target_pairs={{0,2},{1,3},{2,0},{3,1},{4,6},{5,7},{6,4},{7,5},{8,10},{9,11},{10,... | collective-permute-start | bytes 442376 | tf_op jit(solution)/shard_map/ppermute | solution.py:167
  124.0 13.9 %collective-permute-start.44 = (bf16[384,384]{1,0:T(8,128)(2,1)S(1)}, bf16[384,384]{1,0:T(8,128)(2,1)S(1)}, u32[]{:S(2)}, u32[]{:S(2)}) collective-permute-start(bf16[384,384]{1,0:T(8,128)(2,1)S(1)} %get-tuple-element.509.refs_1_), channel_id=1, source_target_pairs={{0,1},{1,0},{2,3},{3,2},{4,5},{5,4},{6,7},{7,6},{8,9},{9,8},{10,11... | collective-permute-start | bytes 884744 | tf_op jit(solution)/shard_map/ppermute | solution.py:167
  131.5 16.7 %collective-permute-start.47 = (bf16[384,768]{1,0:T(8,128)(2,1)S(1)}, bf16[384,768]{1,0:T(8,128)(2,1)S(1)}, u32[]{:S(2)}, u32[]{:S(2)}) collective-permute-start(bf16[384,768]{1,0:T(8,128)(2,1)S(1)} %get-tuple-element.522.refs_1_), channel_id=1, source_target_pairs={{0,16},{16,0},{1,17},{17,1},{2,18},{18,2},{3,19},{19,3},{4,20},{20... | collective-permute-start | bytes 1769480 | tf_op jit(solution)/shard_map/ppermute | solution.py:158
  134.8 18.7 %collective-permute-start.49 = (bf16[96,768]{1,0:T(8,128)(2,1)S(1)}, bf16[96,768]{1,0:T(8,128)(2,1)S(1)}, u32[]{:S(2)}, u32[]{:S(2)}) collective-permute-start(bf16[96,768]{1,0:T(8,128)(2,1)S(1)} %get-tuple-element.532.refs_1_), channel_id=1, source_target_pairs={{0,2},{1,3},{2,0},{3,1},{4,6},{5,7},{6,4},{7,5},{8,10},{9,11},{10,... | collective-permute-start | bytes 442376 | tf_op jit(solution)/shard_map/ppermute | solution.py:167
  135.5 4.6 %collective-permute-start.45 = (bf16[48,768]{1,0:T(8,128)(2,1)S(1)}, bf16[48,768]{1,0:T(8,128)(2,1)S(1)}, u32[]{:S(2)}, u32[]{:S(2)}) collective-permute-start(bf16[48,768]{1,0:T(8,128)(2,1)S(1)} %get-tuple-element.511.refs_1_), channel_id=1, source_target_pairs={{0,8},{4,12},{8,0},{12,4},{1,9},{5,13},{9,1},{13,5},{2,10},{6,14},... | collective-permute-start | bytes 221192 | tf_op jit(solution)/shard_map/ppermute | solution.py:149
  140.2 4.9 %collective-permute-start.46 = (bf16[48,768]{1,0:T(8,128)(2,1)S(1)}, bf16[48,768]{1,0:T(8,128)(2,1)S(1)}, u32[]{:S(2)}, u32[]{:S(2)}) collective-permute-start(bf16[48,768]{1,0:T(8,128)(2,1)S(1)} %get-tuple-element.518.refs_8_), channel_id=1, source_target_pairs={{0,16},{1,17},{2,18},{3,19},{4,20},{5,21},{6,22},{7,23},{8,24},{9,... | collective-permute-start | bytes 221192 | tf_op jit(solution)/shard_map/ppermute | solution.py:161
  144.7 5.2 %collective-permute-start.48 = (bf16[2,2,208,384]{3,2,1,0:T(8,128)(2,1)S(1)}, bf16[2,2,208,384]{3,2,1,0:T(8,128)(2,1)S(1)}, u32[]{:S(2)}, u32[]{:S(2)}) collective-permute-start(bf16[2,2,208,384]{3,2,1,0:T(8,128)(2,1)S(1)} %get-tuple-element.525), channel_id=1, source_target_pairs={{0,4},{4,0},{8,12},{12,8},{1,5},{5,1},{9,13},{13,9},{2,6},{6,2},{1... | collective-permute-start | bytes 1916936 | tf_op jit(solution)/shard_map/ppermute | solution.py:149
  144.7 22.0 %collective-permute-start.53 = (bf16[768,384]{1,0:T(8,128)(2,1)S(1)}, bf16[768,384]{1,0:T(8,128)(2,1)S(1)}, u32[]{:S(2)}, u32[]{:S(2)}) collective-permute-start(bf16[768,384]{1,0:T(8,128)(2,1)S(1)} %get-tuple-element.543.refs_1_), channel_id=1, source_target_pairs={{0,16},{16,0},{1,17},{17,1},{2,18},{18,2},{3,19},{19,3},{4,20},{20... | collective-permute-start | bytes 1769480 | tf_op jit(solution)/shard_map/ppermute | solution.py:158
  150.0 9.7 %collective-permute-start.50 = (bf16[2,208,384]{2,1,0:T(8,128)(2,1)S(1)}, bf16[2,208,384]{2,1,0:T(8,128)(2,1)S(1)}, u32[]{:S(2)}, u32[]{:S(2)}) collective-permute-start(bf16[2,208,384]{2,1,0:T(8,128)(2,1)S(1)} %get-tuple-element.535), channel_id=1, source_target_pairs={{0,8},{4,12},{8,0},{12,4},{1,9},{5,13},{9,1},{13,5},{2,10},{6,14},... | collective-permute-start | bytes 958472 | tf_op jit(solution)/shard_map/ppermute | solution.py:149
  153.6 8.9 %collective-permute-start.51 = (bf16[192,768]{1,0:T(8,128)(2,1)S(1)}, bf16[192,768]{1,0:T(8,128)(2,1)S(1)}, u32[]{:S(2)}, u32[]{:S(2)}) collective-permute-start(bf16[192,768]{1,0:T(8,128)(2,1)S(1)} %get-tuple-element.538.refs_1_), channel_id=1, source_target_pairs={{0,1},{1,0},{2,3},{3,2},{4,5},{5,4},{6,7},{7,6},{8,9},{9,8},{10,11... | collective-permute-start | bytes 884744 | tf_op jit(solution)/shard_map/ppermute | solution.py:167
  154.9 11.3 %collective-permute-start.52 = (bf16[2,2,208,384]{3,2,1,0:T(8,128)(2,1)S(1)}, bf16[2,2,208,384]{3,2,1,0:T(8,128)(2,1)S(1)}, u32[]{:S(2)}, u32[]{:S(2)}) collective-permute-start(bf16[2,2,208,384]{3,2,1,0:T(8,128)(2,1)S(1)} %get-tuple-element.541), channel_id=1, source_target_pairs={{0,4},{4,0},{8,12},{12,8},{1,5},{5,1},{9,13},{13,9},{2,6},{6,2},{1... | collective-permute-start | bytes 1916936 | tf_op jit(solution)/shard_map/ppermute | solution.py:149
  162.5 14.8 %collective-permute-start.55 = (bf16[384,768]{1,0:T(8,128)(2,1)S(1)}, bf16[384,768]{1,0:T(8,128)(2,1)S(1)}, u32[]{:S(2)}, u32[]{:S(2)}) collective-permute-start(bf16[384,768]{1,0:T(8,128)(2,1)S(1)} %get-tuple-element.552.refs_1_), channel_id=1, source_target_pairs={{0,16},{1,17},{2,18},{3,19},{4,20},{5,21},{6,22},{7,23},{8,24},{9,... | collective-permute-start | bytes 1769480 | tf_op jit(solution)/shard_map/ppermute | solution.py:161
  166.4 7.6 %collective-permute-start.54 = (bf16[2,208,384]{2,1,0:T(8,128)(2,1)S(1)}, bf16[2,208,384]{2,1,0:T(8,128)(2,1)S(1)}, u32[]{:S(2)}, u32[]{:S(2)}) collective-permute-start(bf16[2,208,384]{2,1,0:T(8,128)(2,1)S(1)} %get-tuple-element.546), channel_id=1, source_target_pairs={{0,8},{4,12},{8,0},{12,4},{1,9},{5,13},{9,1},{13,5},{2,10},{6,14},... | collective-permute-start | bytes 958472 | tf_op jit(solution)/shard_map/ppermute | solution.py:149
  (28 other events, 161.7 us)
